TPU v7x, 32 devices: a whole 2x2x4 slice. The times are simulated.
32 devices in a mesh: dp: 4 (over z), row: 4 (over x, core), col: 2 (over y).
Axes of the slice: x: 2, y: 2, z: 4, core: 2. Of those that a mesh axis runs over, the one named last changes fastest.
Arguments:
- latent: bfloat16 [8, 64, 64, 16], P('dp', 'row', 'col'), may hold values from -6 to 6
- skip_input: bfloat16 [8, 64, 64, 1408], P('dp', 'row', 'col'), may hold values from -6 to 6
- text_states: bfloat16 [8, 333, 1024], P('dp'), may hold values from -6 to 6
- timesteps: int32 [8], P('dp'), may hold values from 0 to 999
- image_sides: int32 [8], P('dp'), may hold values from 32 to 64, as said below
- cotangent: bfloat16 [8, 64, 64, 32], P('dp', 'row', 'col'), may hold values from -6 to 6
- w_patch: bfloat16 [1408, 16], P(('row', 'col'), 'dp'), may hold values from -1.5 to 1.5
- w_skip: bfloat16 [2816, 1408], P(('row', 'col'), 'dp'), may hold values from -0.109375 to 0.109375
- w_time: bfloat16 [256, 1408], P(('row', 'col'), 'dp'), may hold values from -0.375 to 0.375
- w_shift: bfloat16 [1408, 1408], P(('row', 'col'), 'dp'), may hold values from -0.15625 to 0.15625
- w_qkv: bfloat16 [1408, 4224], P(('row', 'col'), 'dp'), may hold values from -0.15625 to 0.15625
- w_out: bfloat16 [1408, 1408], P(('row', 'col'), 'dp'), may hold values from -2.5 to 2.5
- w_query: bfloat16 [1408, 1408], P(('row', 'col'), 'dp'), may hold values from -0.15625 to 0.15625
- w_text: bfloat16 [1024, 2816], P(('row', 'col'), 'dp'), may hold values from -0.1875 to 0.1875
- w_cross: bfloat16 [1408, 1408], P(('row', 'col'), 'dp'), may hold values from -0.625 to 0.625
- w_up: bfloat16 [1408, 6144], P(('row', 'col'), 'dp'), may hold values from -0.15625 to 0.15625
- w_down: bfloat16 [6144, 1408], P(('row', 'col'), 'dp'), may hold values from -0.078125 to 0.078125
- w_final: bfloat16 [1408, 32], P(('row', 'col'), 'dp'), may hold values from -0.15625 to 0.15625
- norm_params: bfloat16 [1408, 12], P(('row', 'col'), 'dp'), as said below
Outputs:
- prediction: bfloat16 [8, 64, 64, 32], P('dp', 'row', 'col')
- latent_grad: float32 [8, 64, 64, 16], P('dp', 'row', 'col')
- skip_grad: float32 [8, 64, 64, 1408], P('dp', 'row', 'col')
- text_grad: float32 [8, 333, 1024], P('dp', None, ('row', 'col'))
- w_patch_grad: float32 [1408, 16], P(('row', 'col'), 'dp')
- w_skip_grad: float32 [2816, 1408], P(('row', 'col'), 'dp')
- w_time_grad: float32 [256, 1408], P(('row', 'col'), 'dp')
- w_shift_grad: float32 [1408, 1408], P(('row', 'col'), 'dp')
- w_qkv_grad: float32 [1408, 4224], P(('row', 'col'), 'dp')
- w_out_grad: float32 [1408, 1408], P(('row', 'col'), 'dp')
- w_query_grad: float32 [1408, 1408], P(('row', 'col'), 'dp')
- w_text_grad: float32 [1024, 2816], P(('row', 'col'), 'dp')
- w_cross_grad: float32 [1408, 1408], P(('row', 'col'), 'dp')
- w_up_grad: float32 [1408, 6144], P(('row', 'col'), 'dp')
- w_down_grad: float32 [6144, 1408], P(('row', 'col'), 'dp')
- w_final_grad: float32 [1408, 32], P(('row', 'col'), 'dp')
- norm_params_grad: float32 [1408, 12], P(('row', 'col'), 'dp')
Inputs may be any that keep to these rules, and one draw needn't show every extreme that they name: `image_sides`: in each aligned run of 2 images, one image drawn from the seed has side 64; an image of side s has its first s grid rows and first s grid columns valid. `norm_params`: even columns are gains near 1, odd columns biases.
All inputs are finite; a program needn't handle non-finite values.
Results may differ from a plain program's by a relative error of at most 0.02.
Values may be sent and summed in bfloat16 or wider, within the bound.
No kernel may reach another device: no remote copies, remote signals or barrier semaphores. Data moves between devices by JAX's collectives and lax.ppermute only.
A program may use at most 896 MiB of HBM per device.

v0:
```python
import math

import jax
import jax.numpy as jnp
from jax import lax
from jax.sharding import PartitionSpec as P

HEADS = 16
FREQ = 256


EPSILON = 1e-06


def layer_norm(values_in):
    centred = values_in - jnp.mean(values_in, axis=-1, keepdims=True)
    inverse = lax.rsqrt(jnp.mean(centred * centred, axis=-1, keepdims=True) + EPSILON)
    return (centred * inverse, inverse)


def norm_back(grad_normed, normed, inverse):
    mean_grad = jnp.mean(grad_normed, axis=-1, keepdims=True)
    mean_cross = jnp.mean(grad_normed * normed, axis=-1, keepdims=True)
    return inverse * (grad_normed - mean_grad - normed * mean_cross)


def turn_half(piece_half, cosine, sine_tab):
    quarter = cosine.shape[-1]
    lower = piece_half[..., :quarter]
    higher = piece_half[..., quarter:]
    return jnp.concatenate(
        [lower * cosine - higher * sine_tab, higher * cosine + lower * sine_tab], axis=-1
    )


def rotate(values_in, tables, signum):
    cos_row, sin_row, cos_col, sin_col = tables
    half_dim = values_in.shape[-1] // 2
    return jnp.concatenate(
        [
            turn_half(values_in[..., :half_dim], cos_row, signum * sin_row),
            turn_half(values_in[..., half_dim:], cos_col, signum * sin_col),
        ],
        axis=-1,
    )


def rope_tables(row_pos, col_pos, head_size):
    quarter = head_size // 4
    frequency = jnp.exp(jnp.arange(quarter, dtype=jnp.float32) * (-math.log(10000.0) / quarter))
    row_ang = row_pos.astype(jnp.float32)[:, None, None] * frequency
    col_ang = col_pos.astype(jnp.float32)[:, None, None] * frequency
    return (jnp.cos(row_ang), jnp.sin(row_ang), jnp.cos(col_ang), jnp.sin(col_ang))


def time_embed(step_values, freq_count):
    half_dim = freq_count // 2
    rate_list = jnp.exp(jnp.arange(half_dim, dtype=jnp.float32) * (-math.log(10000.0) / half_dim))
    angles = step_values.astype(jnp.float32)[..., None] * rate_list
    return jnp.concatenate([jnp.cos(angles), jnp.sin(angles)], axis=-1)


def gelu_tanh(inputs):
    return jax.nn.gelu(inputs, approximate=True)


def plain_dot(left_mat, right_mat):
    return jnp.dot(left_mat, right_mat, preferred_element_type=jnp.float32)


def left_dot(left_mat, right_mat):
    return lax.dot_general(
        left_mat, right_mat, (((0,), (0,)), ((), ())), preferred_element_type=jnp.float32
    )


def right_dot(left_mat, right_mat):
    return lax.dot_general(
        left_mat, right_mat, (((1,), (1,)), ((), ())), preferred_element_type=jnp.float32
    )


def block_size(key_count):
    block_len = key_count
    while block_len > 1024 and block_len % 2 == 0:
        block_len = block_len // 2
    return block_len


def local(
    latent,
    skip_input,
    text_states,
    timesteps,
    image_sides,
    cotangent,
    w_patch,
    w_skip,
    w_time,
    w_shift,
    w_qkv,
    w_out,
    w_query,
    w_text,
    w_cross,
    w_up,
    w_down,
    w_final,
    norm_params,
):
    widened = (
        lax.all_gather(w_patch, "dp", axis=1, tiled=True),
        lax.all_gather(w_skip, "dp", axis=1, tiled=True),
        lax.all_gather(w_time, "dp", axis=1, tiled=True),
        lax.all_gather(w_shift, "dp", axis=1, tiled=True),
        lax.all_gather(w_qkv, "dp", axis=1, tiled=True),
        lax.all_gather(w_out, "dp", axis=1, tiled=True),
        lax.all_gather(w_query, "dp", axis=1, tiled=True),
        lax.all_gather(w_text, "dp", axis=1, tiled=True),
        lax.all_gather(w_cross, "dp", axis=1, tiled=True),
        lax.all_gather(w_up, "dp", axis=1, tiled=True),
        lax.all_gather(w_down, "dp", axis=1, tiled=True),
        lax.all_gather(w_final, "dp", axis=1, tiled=True),
        lax.all_gather(norm_params, "dp", axis=1, tiled=True),
    )
    gathered = (
        lax.all_gather(widened[0], ("row", "col"), axis=0, tiled=True),
        lax.all_gather(widened[1], ("row", "col"), axis=0, tiled=True),
        lax.all_gather(widened[2], ("row", "col"), axis=0, tiled=True),
        lax.all_gather(widened[3], ("row", "col"), axis=0, tiled=True),
        lax.all_gather(widened[4], ("row", "col"), axis=0, tiled=True),
        lax.all_gather(widened[5], ("row", "col"), axis=0, tiled=True),
        lax.all_gather(widened[6], ("row", "col"), axis=0, tiled=True),
        lax.all_gather(widened[7], ("row", "col"), axis=0, tiled=True),
        lax.all_gather(widened[8], ("row", "col"), axis=0, tiled=True),
        lax.all_gather(widened[9], ("row", "col"), axis=0, tiled=True),
        lax.all_gather(widened[10], ("row", "col"), axis=0, tiled=True),
        lax.all_gather(widened[11], ("row", "col"), axis=0, tiled=True),
        lax.all_gather(widened[12], ("row", "col"), axis=0, tiled=True),
    )
    (
        f_patch,
        f_skip,
        f_time,
        f_shift,
        f_qkv,
        f_out,
        f_query,
        f_text,
        f_cross,
        f_up,
        f_down,
        f_final,
        f_norms,
    ) = gathered
    part_text = widened[7]
    images, rows_tile, cols_tile, patch_width = latent.shape
    tile_len = rows_tile * cols_tile
    row_count = images * tile_len
    model_width = f_qkv.shape[0]
    head_count = HEADS
    head_dim = model_width // head_count
    text_len = text_states.shape[1]
    grid_devices = lax.axis_size(("row", "col"))
    col_devices = lax.axis_size("col")
    grid_at = lax.axis_index(("row", "col"))
    row_at = lax.axis_index("row")
    col_at = lax.axis_index("col")
    score_scale = head_dim ** (-0.5)
    positions = jnp.arange(tile_len, dtype=jnp.int32)
    row_pos = row_at * rows_tile + positions // cols_tile
    col_pos = col_at * cols_tile + positions % cols_tile
    query_ok = (row_pos[None, :] < image_sides[:, None]) & (col_pos[None, :] < image_sides[:, None])
    keep_rows = query_ok.astype(jnp.float32).reshape(row_count, 1)
    tables = rope_tables(row_pos, col_pos, head_dim)
    norm_f = f_norms.astype(jnp.float32)

    def valid_keys(offset, block_len):
        index_list = offset + jnp.arange(block_len, dtype=jnp.int32)
        source = index_list // tile_len
        within = index_list % tile_len
        key_row = source // col_devices * rows_tile + within // cols_tile
        key_col = source % col_devices * cols_tile + within % cols_tile
        return (key_row[None, :] < image_sides[:, None]) & (key_col[None, :] < image_sides[:, None])

    patch_rows = latent.reshape(row_count, patch_width)
    patch_feat = right_dot(patch_rows, f_patch)
    skip_rows = skip_input.reshape(row_count, model_width).astype(jnp.float32)
    gain_skip = jnp.concatenate([norm_f[:, 8], norm_f[:, 10]])
    bias_skip = jnp.concatenate([norm_f[:, 9], norm_f[:, 11]])
    joined, joined_inv = layer_norm(jnp.concatenate([patch_feat, skip_rows], axis=-1))
    skip_in = (joined * gain_skip + bias_skip).astype(jnp.bfloat16)
    residual = plain_dot(skip_in, f_skip)
    embedding = time_embed(timesteps, FREQ).astype(jnp.bfloat16)
    time_pre = plain_dot(embedding, f_time)
    time_float, silu_pull = jax.vjp(jax.nn.silu, time_pre)
    time_act = time_float.astype(jnp.bfloat16)
    time_shift = plain_dot(time_act, f_shift)
    first_z, first_inv = layer_norm(residual)
    first_pre = (first_z * norm_f[:, 0] + norm_f[:, 1]).reshape(
        images, tile_len, model_width
    ) + time_shift[:, None, :]
    first_in = first_pre.reshape(row_count, model_width).astype(jnp.bfloat16)
    qkv = plain_dot(first_in, f_qkv)
    query_z, query_inv = layer_norm(
        qkv[:, :model_width].reshape(images, tile_len, head_count, head_dim)
    )
    key_z, key_inv = layer_norm(
        qkv[:, model_width : 2 * model_width].reshape(images, tile_len, head_count, head_dim)
    )
    queries = rotate(query_z, tables, 1.0).astype(jnp.bfloat16)
    queries_h = jnp.transpose(queries, (0, 2, 1, 3))
    keys = rotate(key_z, tables, 1.0).astype(jnp.bfloat16).reshape(images, tile_len, model_width)
    values = qkv[:, 2 * model_width :].astype(jnp.bfloat16).reshape(images, tile_len, model_width)
    start_carry = (
        jnp.full((images, head_count, tile_len), -1e30, jnp.float32),
        jnp.zeros((images, head_count, tile_len), jnp.float32),
        jnp.zeros((images, head_count, tile_len, head_dim), jnp.float32),
    )
    key_rows = lax.all_gather(keys, ("row", "col"), axis=1, tiled=True)
    value_rows = lax.all_gather(values, ("row", "col"), axis=1, tiled=True)
    key_count = key_rows.shape[1]
    block_len = block_size(key_count)

    def forward_block_step(block_index, running):
        running_max, weight_sum, accum_sum = running
        offset = block_index * block_len
        key_blk = lax.dynamic_slice_in_dim(key_rows, offset, block_len, 1).reshape(
            images, block_len, head_count, head_dim
        )
        value_blk = lax.dynamic_slice_in_dim(value_rows, offset, block_len, 1).reshape(
            images, block_len, head_count, head_dim
        )
        key_ok = valid_keys(offset, block_len)
        scores = (
            jnp.einsum("ihqe,ikhe->ihqk", queries_h, key_blk, preferred_element_type=jnp.float32)
            * score_scale
        )
        scores = jnp.where(key_ok[:, None, None, :], scores, -jnp.inf)
        new_max = jnp.maximum(running_max, jnp.max(scores, axis=-1))
        weight = jnp.exp(scores - new_max[..., None])
        rescale = jnp.exp(running_max - new_max)
        weight_sum = weight_sum * rescale + jnp.sum(weight, axis=-1)
        accum_sum = accum_sum * rescale[..., None] + jnp.einsum(
            "ihqk,ikhe->ihqe",
            weight.astype(jnp.bfloat16),
            value_blk,
            preferred_element_type=jnp.float32,
        )
        return (new_max, weight_sum, accum_sum)

    running_max, weight_sum, accum_sum = lax.fori_loop(
        0, key_count // block_len, forward_block_step, start_carry
    )
    attended = accum_sum / weight_sum[..., None]
    log_sum = running_max + jnp.log(weight_sum)
    att_low = (
        jnp.transpose(attended, (0, 2, 1, 3)).reshape(row_count, model_width).astype(jnp.bfloat16)
    )
    residual_two = residual + plain_dot(att_low, f_out)
    third_z, third_inv = layer_norm(residual_two)
    third_in = (third_z * norm_f[:, 2] + norm_f[:, 3]).astype(jnp.bfloat16)
    cross_pre = plain_dot(third_in, f_query)
    cq_z, cq_inv = layer_norm(cross_pre.reshape(images, tile_len, head_count, head_dim))
    cross_queries = cq_z.astype(jnp.bfloat16)
    text_kv = jnp.einsum("itc,cd->itd", text_states, f_text, preferred_element_type=jnp.float32)
    ck_z, ck_inv = layer_norm(
        text_kv[..., :model_width].reshape(images, text_len, head_count, head_dim)
    )
    cross_keys = ck_z.astype(jnp.bfloat16)
    cross_values = (
        text_kv[..., model_width:]
        .astype(jnp.bfloat16)
        .reshape(images, text_len, head_count, head_dim)
    )

    def cross_softmax():
        scores = (
            jnp.einsum(
                "iqhe,ikhe->ihqk", cross_queries, cross_keys, preferred_element_type=jnp.float32
            )
            * score_scale
        )
        return jax.nn.softmax(scores, axis=-1)

    crossed = jnp.einsum(
        "ihqk,ikhe->iqhe",
        cross_softmax().astype(jnp.bfloat16),
        cross_values,
        preferred_element_type=jnp.float32,
    )
    cross_low = crossed.reshape(row_count, model_width).astype(jnp.bfloat16)
    residual_three = residual_two + plain_dot(cross_low, f_cross)
    second_z, second_inv = layer_norm(residual_three)
    second_in = (second_z * norm_f[:, 4] + norm_f[:, 5]).astype(jnp.bfloat16)
    up_pre = plain_dot(second_in, f_up)
    hidden_float, gelu_pull = jax.vjp(gelu_tanh, up_pre)
    hidden_act = hidden_float.astype(jnp.bfloat16)
    residual_four = residual_three + plain_dot(hidden_act, f_down)
    last_z, last_inv = layer_norm(residual_four)
    last_in = (last_z * norm_f[:, 6] + norm_f[:, 7]).astype(jnp.bfloat16)
    produced = plain_dot(last_in, f_final)
    prediction = (
        (produced * keep_rows)
        .astype(jnp.bfloat16)
        .reshape(images, rows_tile, cols_tile, produced.shape[1])
    )
    grad_out = (
        cotangent.reshape(row_count, produced.shape[1]).astype(jnp.float32) * keep_rows
    ).astype(jnp.bfloat16)
    d_final = left_dot(last_in, grad_out)
    grad_last = right_dot(grad_out, f_final)
    gain_final = jnp.sum(grad_last * last_z, axis=0)
    bias_final = jnp.sum(grad_last, axis=0)
    grad_four = norm_back(grad_last * norm_f[:, 6], last_z, last_inv)
    low_four = grad_four.astype(jnp.bfloat16)
    d_down = left_dot(hidden_act, low_four)
    grad_hidden = right_dot(low_four, f_down)
    grad_up = gelu_pull(grad_hidden)[0].astype(jnp.bfloat16)
    d_up = left_dot(second_in, grad_up)
    grad_second = right_dot(grad_up, f_up)
    gain_second = jnp.sum(grad_second * second_z, axis=0)
    bias_second = jnp.sum(grad_second, axis=0)
    grad_three = grad_four + norm_back(grad_second * norm_f[:, 4], second_z, second_inv)
    low_three = grad_three.astype(jnp.bfloat16)
    d_cross = left_dot(cross_low, low_three)
    grad_crossed = (
        right_dot(low_three, f_cross)
        .astype(jnp.bfloat16)
        .reshape(images, tile_len, head_count, head_dim)
    )
    cross_probs = cross_softmax()
    cross_delta = jnp.transpose(
        jnp.sum(grad_crossed.astype(jnp.float32) * crossed, axis=-1), (0, 2, 1)
    )
    grad_probs = jnp.einsum(
        "iqhe,ikhe->ihqk", grad_crossed, cross_values, preferred_element_type=jnp.float32
    )
    grad_cscore = (cross_probs * (grad_probs - cross_delta[..., None])).astype(jnp.bfloat16)
    grad_cq = score_scale * jnp.einsum(
        "ihqk,ikhe->iqhe", grad_cscore, cross_keys, preferred_element_type=jnp.float32
    )
    part_ckey = score_scale * jnp.einsum(
        "ihqk,iqhe->ikhe", grad_cscore, cross_queries, preferred_element_type=jnp.float32
    )
    part_cvalue = jnp.einsum(
        "ihqk,iqhe->ikhe",
        cross_probs.astype(jnp.bfloat16),
        grad_crossed,
        preferred_element_type=jnp.float32,
    )
    grad_cross_q = (
        norm_back(grad_cq, cq_z, cq_inv).reshape(row_count, model_width).astype(jnp.bfloat16)
    )
    d_query = left_dot(third_in, grad_cross_q)
    grad_third = right_dot(grad_cross_q, f_query)
    gain_third = jnp.sum(grad_third * third_z, axis=0)
    bias_third = jnp.sum(grad_third, axis=0)
    grad_two = grad_three + norm_back(grad_third * norm_f[:, 2], third_z, third_inv)
    sum_ckey, sum_cvalue = lax.psum((part_ckey, part_cvalue), ("row", "col"))
    low_two = grad_two.astype(jnp.bfloat16)
    d_out = left_dot(att_low, low_two)
    grad_att = (
        right_dot(low_two, f_out)
        .astype(jnp.bfloat16)
        .reshape(images, tile_len, head_count, head_dim)
    )
    grad_att_h = jnp.transpose(grad_att, (0, 2, 1, 3))
    delta_rows = jnp.sum(grad_att_h.astype(jnp.float32) * attended, axis=-1)
    back_carry = (
        jnp.zeros((images, head_count, tile_len, head_dim), jnp.float32),
        jnp.zeros((images, tile_len * grid_devices, model_width), jnp.float32),
        jnp.zeros((images, tile_len * grid_devices, model_width), jnp.float32),
    )
    backward_key_rows = lax.all_gather(keys, ("row", "col"), axis=1, tiled=True)
    backward_value_rows = lax.all_gather(values, ("row", "col"), axis=1, tiled=True)
    key_count = backward_key_rows.shape[1]
    backward_block_len = block_size(key_count)

    def backward_block_step(block_index, running):
        grad_query, grad_key_all, grad_value_all = running
        offset = block_index * backward_block_len
        key_blk = lax.dynamic_slice_in_dim(
            backward_key_rows, offset, backward_block_len, 1
        ).reshape(images, backward_block_len, head_count, head_dim)
        value_blk = lax.dynamic_slice_in_dim(
            backward_value_rows, offset, backward_block_len, 1
        ).reshape(images, backward_block_len, head_count, head_dim)
        key_ok = valid_keys(offset, backward_block_len)
        scores = (
            jnp.einsum("ihqe,ikhe->ihqk", queries_h, key_blk, preferred_element_type=jnp.float32)
            * score_scale
        )
        scores = jnp.where(key_ok[:, None, None, :], scores, -jnp.inf)
        attn_probs = jnp.exp(scores - log_sum[..., None])
        grad_prob = jnp.einsum(
            "ihqe,ikhe->ihqk", grad_att_h, value_blk, preferred_element_type=jnp.float32
        )
        grad_score = (attn_probs * (grad_prob - delta_rows[..., None])).astype(jnp.bfloat16)
        grad_query = grad_query + score_scale * jnp.einsum(
            "ihqk,ikhe->ihqe", grad_score, key_blk, preferred_element_type=jnp.float32
        )
        key_part = score_scale * jnp.einsum(
            "ihqk,ihqe->ikhe", grad_score, queries_h, preferred_element_type=jnp.float32
        )
        value_part = jnp.einsum(
            "ihqk,ihqe->ikhe",
            attn_probs.astype(jnp.bfloat16),
            grad_att_h,
            preferred_element_type=jnp.float32,
        )
        grad_key_all = lax.dynamic_update_slice_in_dim(
            grad_key_all, key_part.reshape(images, backward_block_len, model_width), offset, 1
        )
        grad_value_all = lax.dynamic_update_slice_in_dim(
            grad_value_all, value_part.reshape(images, backward_block_len, model_width), offset, 1
        )
        return (grad_query, grad_key_all, grad_value_all)

    grad_query, grad_key_all, grad_value_all = lax.fori_loop(
        0, key_count // backward_block_len, backward_block_step, back_carry
    )
    grad_key_own, grad_value_own = (
        lax.psum_scatter(grad_key_all, ("row", "col"), scatter_dimension=1, tiled=True),
        lax.psum_scatter(grad_value_all, ("row", "col"), scatter_dimension=1, tiled=True),
    )
    grad_qn = rotate(jnp.transpose(grad_query, (0, 2, 1, 3)), tables, -1.0)
    grad_kn = rotate(grad_key_own.reshape(images, tile_len, head_count, head_dim), tables, -1.0)
    grad_qkv = jnp.concatenate(
        [
            norm_back(grad_qn, query_z, query_inv).reshape(row_count, model_width),
            norm_back(grad_kn, key_z, key_inv).reshape(row_count, model_width),
            grad_value_own.reshape(row_count, model_width),
        ],
        axis=-1,
    ).astype(jnp.bfloat16)
    d_qkv = left_dot(first_in, grad_qkv)
    grad_first = right_dot(grad_qkv, f_qkv)
    gain_first = jnp.sum(grad_first * first_z, axis=0)
    bias_first = jnp.sum(grad_first, axis=0)
    part_shift = jnp.sum(grad_first.reshape(images, tile_len, model_width), axis=1)
    grad_one = grad_two + norm_back(grad_first * norm_f[:, 0], first_z, first_inv)
    shift_grad = lax.psum(part_shift, ("row", "col"))
    grad_ckey = norm_back(sum_ckey, ck_z, ck_inv).reshape(images, text_len, model_width)
    grad_kv = jnp.concatenate(
        [grad_ckey, sum_cvalue.reshape(images, text_len, model_width)], axis=-1
    ).astype(jnp.bfloat16)
    text_slice = text_states.shape[2] // grid_devices
    text_cols = lax.dynamic_slice_in_dim(text_states, grid_at * text_slice, text_slice, 2)
    d_text_w = jnp.einsum("itc,itd->cd", text_cols, grad_kv, preferred_element_type=jnp.float32)
    text_grad = jnp.einsum("itd,cd->itc", grad_kv, part_text, preferred_element_type=jnp.float32)
    shift_low = shift_grad.astype(jnp.bfloat16)
    shift_slice = model_width // grid_devices
    act_cols = lax.dynamic_slice_in_dim(time_act, grid_at * shift_slice, shift_slice, 1)
    d_shift_w = jnp.einsum("ic,id->cd", act_cols, shift_low, preferred_element_type=jnp.float32)
    grad_time_act = right_dot(shift_low, f_shift)
    grad_time_pre = silu_pull(grad_time_act)[0].astype(jnp.bfloat16)
    freq_slice = embedding.shape[1] // grid_devices
    embed_cols = lax.dynamic_slice_in_dim(embedding, grid_at * freq_slice, freq_slice, 1)
    d_time_w = jnp.einsum(
        "ic,id->cd", embed_cols, grad_time_pre, preferred_element_type=jnp.float32
    )
    low_one = grad_one.astype(jnp.bfloat16)
    d_skip_w = left_dot(skip_in, low_one)
    grad_skip_in = right_dot(low_one, f_skip)
    gain_skips = jnp.sum(grad_skip_in * joined, axis=0)
    bias_skips = jnp.sum(grad_skip_in, axis=0)
    grad_joined = norm_back(grad_skip_in * gain_skip, joined, joined_inv)
    skip_grad = grad_joined[:, model_width:].reshape(images, rows_tile, cols_tile, model_width)
    grad_patch = grad_joined[:, :model_width].astype(jnp.bfloat16)
    d_patch = left_dot(grad_patch, patch_rows)
    latent_grad = plain_dot(grad_patch, f_patch).reshape(images, rows_tile, cols_tile, patch_width)
    d_norms = jnp.stack(
        [
            gain_first,
            bias_first,
            gain_third,
            bias_third,
            gain_second,
            bias_second,
            gain_final,
            bias_final,
            gain_skips[:model_width],
            bias_skips[:model_width],
            gain_skips[model_width:],
            bias_skips[model_width:],
        ],
        axis=1,
    )
    tile_done = (
        lax.psum_scatter(d_patch, ("row", "col"), scatter_dimension=0, tiled=True),
        lax.psum_scatter(d_skip_w, ("row", "col"), scatter_dimension=0, tiled=True),
        lax.psum_scatter(d_qkv, ("row", "col"), scatter_dimension=0, tiled=True),
        lax.psum_scatter(d_out, ("row", "col"), scatter_dimension=0, tiled=True),
        lax.psum_scatter(d_query, ("row", "col"), scatter_dimension=0, tiled=True),
        lax.psum_scatter(d_cross, ("row", "col"), scatter_dimension=0, tiled=True),
        lax.psum_scatter(d_up, ("row", "col"), scatter_dimension=0, tiled=True),
        lax.psum_scatter(d_down, ("row", "col"), scatter_dimension=0, tiled=True),
        lax.psum_scatter(d_final, ("row", "col"), scatter_dimension=0, tiled=True),
        lax.psum_scatter(d_norms, ("row", "col"), scatter_dimension=0, tiled=True),
    )
    reduced = (
        lax.psum_scatter(
            tile_done[0].astype(jnp.bfloat16), "dp", scatter_dimension=1, tiled=True
        ).astype(jnp.float32),
        lax.psum_scatter(
            tile_done[1].astype(jnp.bfloat16), "dp", scatter_dimension=1, tiled=True
        ).astype(jnp.float32),
        lax.psum_scatter(
            tile_done[2].astype(jnp.bfloat16), "dp", scatter_dimension=1, tiled=True
        ).astype(jnp.float32),
        lax.psum_scatter(
            tile_done[3].astype(jnp.bfloat16), "dp", scatter_dimension=1, tiled=True
        ).astype(jnp.float32),
        lax.psum_scatter(
            tile_done[4].astype(jnp.bfloat16), "dp", scatter_dimension=1, tiled=True
        ).astype(jnp.float32),
        lax.psum_scatter(
            tile_done[5].astype(jnp.bfloat16), "dp", scatter_dimension=1, tiled=True
        ).astype(jnp.float32),
        lax.psum_scatter(
            tile_done[6].astype(jnp.bfloat16), "dp", scatter_dimension=1, tiled=True
        ).astype(jnp.float32),
        lax.psum_scatter(
            tile_done[7].astype(jnp.bfloat16), "dp", scatter_dimension=1, tiled=True
        ).astype(jnp.float32),
        lax.psum_scatter(
            tile_done[8].astype(jnp.bfloat16), "dp", scatter_dimension=1, tiled=True
        ).astype(jnp.float32),
        lax.psum_scatter(
            tile_done[9].astype(jnp.bfloat16), "dp", scatter_dimension=1, tiled=True
        ).astype(jnp.float32),
        lax.psum_scatter(
            d_time_w.astype(jnp.bfloat16), "dp", scatter_dimension=1, tiled=True
        ).astype(jnp.float32),
        lax.psum_scatter(
            d_shift_w.astype(jnp.bfloat16), "dp", scatter_dimension=1, tiled=True
        ).astype(jnp.float32),
        lax.psum_scatter(
            d_text_w.astype(jnp.bfloat16), "dp", scatter_dimension=1, tiled=True
        ).astype(jnp.float32),
    )
    return (
        prediction,
        latent_grad,
        skip_grad,
        text_grad,
        reduced[0],
        reduced[1],
        reduced[10],
        reduced[11],
        reduced[2],
        reduced[3],
        reduced[4],
        reduced[12],
        reduced[5],
        reduced[6],
        reduced[7],
        reduced[8],
        reduced[9],
    )


def solution(mesh):
    return jax.shard_map(
        local,
        mesh=mesh,
        in_specs=(
            P("dp", "row", "col", None),
            P("dp", "row", "col", None),
            P("dp", None, None),
            P("dp"),
            P("dp"),
            P("dp", "row", "col", None),
            P(("row", "col"), "dp"),
            P(("row", "col"), "dp"),
            P(("row", "col"), "dp"),
            P(("row", "col"), "dp"),
            P(("row", "col"), "dp"),
            P(("row", "col"), "dp"),
            P(("row", "col"), "dp"),
            P(("row", "col"), "dp"),
            P(("row", "col"), "dp"),
            P(("row", "col"), "dp"),
            P(("row", "col"), "dp"),
            P(("row", "col"), "dp"),
            P(("row", "col"), "dp"),
        ),
        out_specs=(
            P("dp", "row", "col", None),
            P("dp", "row", "col", None),
            P("dp", "row", "col", None),
            P("dp", None, ("row", "col")),
            P(("row", "col"), "dp"),
            P(("row", "col"), "dp"),
            P(("row", "col"), "dp"),
            P(("row", "col"), "dp"),
            P(("row", "col"), "dp"),
            P(("row", "col"), "dp"),
            P(("row", "col"), "dp"),
            P(("row", "col"), "dp"),
            P(("row", "col"), "dp"),
            P(("row", "col"), "dp"),
            P(("row", "col"), "dp"),
            P(("row", "col"), "dp"),
            P(("row", "col"), "dp"),
        ),
        check_vma=False,
    )
```

profile of v0, /device:TPU:0, one launch (start us, length us, event | category | flops | bytes accessed | tf_op | source)
XLA Modules:
  0.0 4093.2 jit_solution(15417110918744314412)
XLA Ops:
  8.0 20.2 all-gather.5
  30.8 38.0 all_gather.90
  171.7 23.9 all_gather.93
  501.2 122.9 %all-gather.32.cloned.1.call-done = bf16[2,4096,1408]{1,2,0:T(8,128)(2,1)} async-done(((bf16[2,512,1408]{1,2,0:T(8,128)(2,1)}), bf16[2,4096,1408]{1,2,0:T(8,128)(2,1)}) %all-gather.32.cloned.1.call-update) | async-done | bytes 23068688 | tf_op jit(solution)/shard_map/all_gather | solution.py:220
  624.1 370.3 %while.42 = (s32[]{:T(128)}, f32[2,16,512]{2,1,0:T(8,128)S(1)}, f32[2,16,512]{2,1,0:T(8,128)S(1)}, f32[2,16,512,88]{2,3,1,0:T(8,128)}, s32[2]{0:T(128)S(1)}, /*i...) while((s32[]{:T(128)}, f32[2,16,512]{2,1,0:T(8,128)S(1)}, ...), condition=%wide.region_12.13_spmd.clone, body=%wide.region_9.12_spmd.clone.sunk | while | flops 6094606336 | bytes 251420880 | solution.py:252
  634.3 29.1 bitcast_reduce_fusion.4
  663.4 21.9 fusion.260
  685.3 29.2 fusion.262
  724.7 30.4 bitcast_reduce_fusion.4
  755.0 21.4 fusion.260
  776.5 32.9 fusion.262
  819.4 30.5 bitcast_reduce_fusion.4
  850.0 21.4 fusion.260
  871.4 33.1 fusion.262
  914.7 28.2 bitcast_reduce_fusion.4
  943.0 21.4 fusion.260
  964.4 29.8 fusion.262
  1097.8 27.1 fusion.140
  1124.9 29.2 fusion.161
  1162.6 41.2 %fusion.51 = bf16[1024,6144]{1,0:T(8,128)(2,1)} fusion(f32[1024,6144]{1,0:T(8,128)} %fusion.140, bf16[6144,1408]{0,1:T(8,128)(2,1)} %all-gather.50.cloned.1.call-done, f32[1024,1408]{1,0:T(8,128)} %get-tuple-element.973), kind=kOutput, calls=%fused_computation.106 | convolution fusion | flops 17844011008 | bytes 60817408 | tf_op jit(solution)/shard_map/dot_general | solution.py:78
  1203.8 30.9 multiply_reduce_fusion.6
  1372.1 627.1 %while.43 = (s32[]{:T(128)}, f32[2,16,512,88]{2,3,1,0:T(8,128)}, f32[2,4096,1408]{1,2,0:T(8,128)}, f32[2,4096,1408]{1,2,0:T(8,128)}, s32[2]{0:T(128)}, /*index=5...) while((s32[]{:T(128)}, f32[2,16,512,88]{2,3,1,0:T(8,128)}, ...), condition=%wide.region_36.37_spmd.clone, body=%wide.region_35.36_spmd.clone.sunk | while | flops 14939035648 | bytes 457922816 | solution.py:420
  1384.6 25.1 fusion.273
  1409.7 28.7 fusion.276
  1438.4 43.8 %multiply_convert_fusion.13 = bf16[2,16,1024,512]{3,2,1,0:T(8,128)(2,1)} fusion(f32[2,16,1024,512]{3,2,1,0:T(8,128)} %fusion.273, f32[2,16,512]{2,1,0:T(8,128)S(1)} %get-tuple-element.1246, f32[2,16,512]{2,1,0:T(8,128)S(1)} %get-tuple-element.1243, pred[2,1024]{1,0:T(4,128)(4,1)S(1)} %compare_and_fusion.5, bf16[2,1024,16,88]{1,3,2,0:T(8,128)(2,1)} %bitcast.347, ...), kind=kOutput, calls=%fused_computation.51.clone.1 | convolution fusion | flops 3053453312 | bytes 109447168 | tf_op jit(solution)/shard_map/while/body/eval_jaxpr/ihqe,ikhe->ihqk/dot_general | solution.py:396
  1540.0 25.1 fusion.273
  1565.1 28.7 fusion.276
  1593.8 43.8 %multiply_convert_fusion.13 = bf16[2,16,1024,512]{3,2,1,0:T(8,128)(2,1)} fusion(f32[2,16,1024,512]{3,2,1,0:T(8,128)} %fusion.273, f32[2,16,512]{2,1,0:T(8,128)S(1)} %get-tuple-element.1246, f32[2,16,512]{2,1,0:T(8,128)S(1)} %get-tuple-element.1243, pred[2,1024]{1,0:T(4,128)(4,1)S(1)} %compare_and_fusion.5, bf16[2,1024,16,88]{1,3,2,0:T(8,128)(2,1)} %bitcast.347, ...), kind=kOutput, calls=%fused_computation.51.clone.1 | convolution fusion | flops 3053453312 | bytes 109447168 | tf_op jit(solution)/shard_map/while/body/eval_jaxpr/ihqe,ikhe->ihqk/dot_general | solution.py:396
  1637.6 18.1 select_add_fusion.2
  1697.0 25.1 fusion.273
  1722.1 28.7 fusion.276
  1750.8 43.8 %multiply_convert_fusion.13 = bf16[2,16,1024,512]{3,2,1,0:T(8,128)(2,1)} fusion(f32[2,16,1024,512]{3,2,1,0:T(8,128)} %fusion.273, f32[2,16,512]{2,1,0:T(8,128)S(1)} %get-tuple-element.1246, f32[2,16,512]{2,1,0:T(8,128)S(1)} %get-tuple-element.1243, pred[2,1024]{1,0:T(4,128)(4,1)S(1)} %compare_and_fusion.5, bf16[2,1024,16,88]{1,3,2,0:T(8,128)(2,1)} %bitcast.347, ...), kind=kOutput, calls=%fused_computation.51.clone.1 | convolution fusion | flops 3053453312 | bytes 109447168 | tf_op jit(solution)/shard_map/while/body/eval_jaxpr/ihqe,ikhe->ihqk/dot_general | solution.py:396
  1794.6 18.1 select_add_fusion.2
  1854.1 25.1 fusion.273
  1879.2 28.7 fusion.276
  1907.9 43.8 %multiply_convert_fusion.13 = bf16[2,16,1024,512]{3,2,1,0:T(8,128)(2,1)} fusion(f32[2,16,1024,512]{3,2,1,0:T(8,128)} %fusion.273, f32[2,16,512]{2,1,0:T(8,128)S(1)} %get-tuple-element.1246, f32[2,16,512]{2,1,0:T(8,128)S(1)} %get-tuple-element.1243, pred[2,1024]{1,0:T(4,128)(4,1)S(1)} %compare_and_fusion.5, bf16[2,1024,16,88]{1,3,2,0:T(8,128)(2,1)} %bitcast.347, ...), kind=kOutput, calls=%fused_computation.51.clone.1 | convolution fusion | flops 3053453312 | bytes 109447168 | tf_op jit(solution)/shard_map/while/body/eval_jaxpr/ihqe,ikhe->ihqk/dot_general | solution.py:396
  2044.7 37.0 fusion.80
  2094.0 27.9 fusion.139
  2210.4 54.7 %reduce-scatter.48.cloned.1.call-done = f32[2,512,1408]{1,2,0:T(8,128)} async-done(((f32[2,4096,1408]{1,2,0:T(8,128)}), f32[2,512,1408]{1,2,0:T(8,128)}) %reduce-scatter.48.cloned.1.call-update) | async-done | bytes 5767184 | tf_op jit(solution)/shard_map/reduce_scatter | solution.py:425
  2270.9 262.5 %reduce-scatter.46.cloned.1.call-done = f32[2,512,1408]{1,2,0:T(8,128)} async-done(((f32[2,4096,1408]{1,2,0:T(8,128)}), f32[2,512,1408]{1,2,0:T(8,128)}) %reduce-scatter.46.cloned.1.call-update) | async-done | bytes 5767184 | tf_op jit(solution)/shard_map/reduce_scatter | solution.py:424
  2583.1 23.8 multiply_convert_fusion.4
  2606.9 22.2 multiply_reduce_fusion.8
  2638.3 18.7 fusion.137
  2657.2 20.2 fusion.68
  2681.7 35.8 reduce-scatter.60.cloned.1.call-done
  2719.9 70.1 %reduce-scatter.54.cloned.1.call-done = f32[176,1408]{1,0:T(8,128)} async-done(((f32[1408,1408]{1,0:T(8,128)}), f32[176,1408]{1,0:T(8,128)}) %reduce-scatter.54.cloned.1.call-update) | async-done | bytes 991248 | tf_op jit(solution)/shard_map/reduce_scatter | solution.py:494
  2792.5 212.1 %reduce-scatter.66.cloned.1.call-done = f32[768,1408]{1,0:T(8,128)} async-done(((f32[6144,1408]{1,0:T(8,128)}), f32[768,1408]{1,0:T(8,128)}) %reduce-scatter.66.cloned.1.call-update) | async-done | bytes 4325392 | tf_op jit(solution)/shard_map/reduce_scatter | solution.py:498
  3025.7 65.1 %all-reduce.7.cloned.1.call-done = f32[2,333,16,88]{1,3,2,0:T(8,128)} async-done(((f32[2,333,16,88]{1,3,2,0:T(8,128)}), f32[2,333,16,88]{1,3,2,0:T(8,128)}) %all-reduce.7.cloned.1.call-update) | async-done | bytes 3750928 | tf_op jit(solution)/shard_map/psum | solution.py:360
  3095.8 209.7 %reduce-scatter.62.cloned.1.call-done = f32[176,6144]{1,0:T(8,128)} async-done(((f32[1408,6144]{1,0:T(8,128)}), f32[176,6144]{1,0:T(8,128)}) %reduce-scatter.62.cloned.1.call-update) | async-done | bytes 4325392 | tf_op jit(solution)/shard_map/reduce_scatter | solution.py:497
  3312.3 18.2 multiply_reduce_fusion.1
  3331.9 278.7 %all-reduce.8 = (bf16[2,333,16,88]{1,3,2,0:T(8,128)(2,1)}, bf16[2,1408]{1,0:T(2,128)(2,1)S(1)}) all-reduce(f32[2,333,16,88]{1,3,2,0:T(8,128)} %convolution_bitcast_fusion.1, f32[2,1408]{1,0:T(2,128)S(1)} %bitcast_reduce_fusion.1), channel_id=1, replica_groups=mesh['dp'=4,'row'=4,'col'=2] {'row','col'}, use_global_device_ids=true, to_apply=%region_56.57 | all-reduce | flops 940544 | bytes 5643264 | tf_op jit(solution)/shard_map/psum | solution.py:360
  3653.8 22.3 reduce-scatter.52.cloned.1.call-done
  3699.0 22.4 reduce-scatter.82.cloned.1.call-done
  3723.2 22.4 reduce-scatter.84.cloned.1.call-done
  3747.4 22.9 reduce-scatter.80.cloned.1.call-done
  3772.1 44.3 %reduce-scatter.86.cloned.1.call-done = bf16[352,768]{1,0:T(8,128)(2,1)} async-done(((bf16[1408,768]{1,0:T(8,128)(2,1)}), bf16[352,768]{1,0:T(8,128)(2,1)}) %reduce-scatter.86.cloned.1.call-update) | async-done | bytes 540688
  3818.9 44.2 %reduce-scatter.64.cloned.1.call-done = bf16[176,1536]{1,0:T(8,128)(2,1)} async-done(((bf16[176,6144]{1,0:T(8,128)(2,1)}), bf16[176,1536]{1,0:T(8,128)(2,1)}) %reduce-scatter.64.cloned.1.call-update) | async-done | bytes 540688 | tf_op jit(solution)/shard_map/reduce_scatter | solution.py:521
  3876.3 24.2 reduce-scatter.90.cloned.1.call-done
  3901.4 37.4 reduce-scatter.70.cloned.1.call-done
  3939.8 18.8 all-reduce.3
  3963.8 21.7 reduce-scatter.76.cloned.1.call-done
  3987.2 22.0 reduce-scatter.58.cloned.1.call-done
  4010.9 27.3 reduce-scatter.72.cloned.1.call-done
  4040.2 44.0 %reduce-scatter.78.cloned.1.call-done = bf16[1056,176]{1,0:T(8,128)(2,1)} async-done(((bf16[4224,176]{1,0:T(8,128)(2,1)}), bf16[1056,176]{1,0:T(8,128)(2,1)}) %reduce-scatter.78.cloned.1.call-update) | async-done | bytes 371728
  (722 shorter events, 1254.0 us)
Async XLA Ops:
  7.2 63.6 %all-gather.52.cloned.1.call-start = ((), (), s32[]{:S(2)}) async-start(), calls=%async_computation.49 | async-start | bytes 2027520 | tf_op jit(solution)/shard_map/all_gather | solution.py:116
  7.9 197.4 %all-gather.28.cloned.1.call-start = ((), (), s32[]{:S(2)}) async-start(), calls=%async_computation.24 | async-start | bytes 4460544 | tf_op jit(solution)/shard_map/all_gather | solution.py:130
  29.6 178.5 %all-gather.26.cloned.1.call-start = ((), (), s32[]{:S(2)}) async-start(), calls=%async_computation.23 | async-start | bytes 8921088 | tf_op jit(solution)/shard_map/all_gather | solution.py:128
  70.7 40.4 copy-start.127
  70.8 52.3 %copy-start.17 = (bf16[2,16,32,1408]{3,2,1,0:T(8,128)(2,1)S(1)}, bf16[2,16,32,1408]{3,2,1,0:T(8,128)(2,1)}, u32[]{:S(2)}) copy-start(bf16[2,16,32,1408]{3,2,1,0:T(8,128)(2,1)} %param.24) | copy-start | bytes 8650756
  70.8 166.0 %all-gather.30.cloned.1.call-start = ((), (), s32[]{:S(2)}) async-start(), calls=%async_computation.25 | async-start | bytes 13381632 | tf_op jit(solution)/shard_map/all_gather | solution.py:131
  74.2 82.4 %copy-start.101 = (bf16[32,352]{1,0:T(8,128)(2,1)S(1)}, bf16[32,352]{1,0:T(8,128)(2,1)}, u32[]{:S(2)}) copy-start(bf16[32,352]{1,0:T(8,128)(2,1)} %param.31) | copy-start | bytes 67588
  74.2 96.0 %copy-start.72 = (bf16[2,16,32,16]{2,3,1,0:T(8,128)(2,1)S(1)}, bf16[2,16,32,16]{2,3,1,0:T(8,128)(2,1)}, u32[]{:S(2)}) copy-start(bf16[2,16,32,16]{2,3,1,0:T(8,128)(2,1)} %param.23) | copy-start | bytes 98308
  78.2 302.1 %all-gather.44.cloned.1.call-start = ((), (), s32[]{:S(2)}) async-start(), calls=%async_computation.32 | async-start | bytes 2703360 | tf_op jit(solution)/shard_map/all_gather | solution.py:121
  78.8 334.6 %all-gather.48.cloned.1.call-start = ((), (), s32[]{:S(2)}) async-start(), calls=%async_computation.34 | async-start | bytes 2703360 | tf_op jit(solution)/shard_map/all_gather | solution.py:122
  79.4 334.2 %all-gather.38.cloned.1.call-start = ((), (), s32[]{:S(2)}) async-start(), calls=%async_computation.29 | async-start | bytes 6488064 | tf_op jit(solution)/shard_map/all_gather | solution.py:134
  99.2 402.0 %all-gather.34.cloned.1.call-start = ((), (), s32[]{:S(2)}) async-start(), calls=%async_computation.27 | async-start | bytes 25952256 | tf_op jit(solution)/shard_map/all_gather | solution.py:221
  156.6 42.7 %copy-start.58 = (bf16[1408,16]{0,1:T(8,128)(2,1)}, bf16[1408,16]{0,1:T(8,128)(2,1)S(1)}, u32[]{:S(2)}) copy-start(bf16[1408,16]{0,1:T(8,128)(2,1)S(1)} %reshape.969) | copy-start | bytes 135172
  170.8 33.7 copy-start.5
  171.7 51.9 %copy-start.73 = (f32[1408]{0:T(1024)}, f32[1408]{0:T(1024)S(1)}, u32[]{:S(2)}) copy-start(f32[1408]{0:T(1024)S(1)} %get-tuple-element.878) | copy-start | bytes 16900
  171.7 36.4 copy-start.81
  171.7 36.4 copy-start.109
  223.6 30.2 copy-start.91
  262.9 361.2 %all-gather.32.cloned.1.call-start = ((), (), s32[]{:S(2)}) async-start(), calls=%async_computation.26 | async-start | bytes 25952256 | tf_op jit(solution)/shard_map/all_gather | solution.py:220
  264.1 205.4 %copy-start.36 = (f32[512,22]{0,1:T(8,128)}, f32[512,22]{0,1:T(8,128)S(1)}, u32[]{:S(2)}) copy-start(f32[512,22]{0,1:T(8,128)S(1)} %get-tuple-element.997) | copy-start | bytes 135172
  264.1 205.4 %copy-start.38 = (f32[512,22]{0,1:T(8,128)}, f32[512,22]{0,1:T(8,128)S(1)}, u32[]{:S(2)}) copy-start(f32[512,22]{0,1:T(8,128)S(1)} %get-tuple-element.1004) | copy-start | bytes 135172
  327.6 35.3 copy-start.71
  327.6 680.2 %all-gather.36.cloned.1.call-start = ((), (), s32[]{:S(2)}) async-start(), calls=%async_computation.28 | async-start | bytes 4460544 | tf_op jit(solution)/shard_map/all_gather | solution.py:132
  343.9 37.2 copy-start.80
  343.9 37.9 copy-start.125
  343.9 68.6 %copy-start.64 = (bf16[2,16,32,32]{3,2,1,0:T(8,128)(2,1)S(1)}, bf16[2,16,32,32]{3,2,1,0:T(8,128)(2,1)}, u32[]{:S(2)}) copy-start(bf16[2,16,32,32]{3,2,1,0:T(8,128)(2,1)} %param.28) | copy-start | bytes 196612
  345.4 675.4 %all-gather.40.cloned.1.call-start = ((), (), s32[]{:S(2)}) async-start(), calls=%async_computation.30 | async-start | bytes 4460544 | tf_op jit(solution)/shard_map/all_gather | solution.py:133
  361.6 52.0 %copy-start.35 = (bf16[2,333,1024]{2,0,1:T(2,128)(2,1)S(1)}, bf16[2,333,1024]{2,0,1:T(2,128)(2,1)}, u32[]{:S(2)}) copy-start(bf16[2,333,1024]{2,0,1:T(2,128)(2,1)} %param.25) | copy-start | bytes 4091908
  362.8 721.7 %all-gather.42.cloned.1.call-start = ((), (), s32[]{:S(2)}) async-start(), calls=%async_computation.31 | async-start | bytes 4460544 | tf_op jit(solution)/shard_map/all_gather | solution.py:135
  380.3 717.5 %all-gather.46.cloned.1.call-start = ((), (), s32[]{:S(2)}) async-start(), calls=%async_computation.33 | async-start | bytes 19464192 | tf_op jit(solution)/shard_map/all_gather | solution.py:136
  381.1 743.8 %all-gather.50.cloned.1.call-start = ((), (), s32[]{:S(2)}) async-start(), calls=%async_computation.35 | async-start | bytes 19464192 | tf_op jit(solution)/shard_map/all_gather | solution.py:137
  413.5 1851.6 %reduce-scatter.48.cloned.1.call-start = ((), (), s32[]{:S(2)}) async-start(), calls=%async_computation.37 | async-start | bytes 51904512 | tf_op jit(solution)/shard_map/reduce_scatter | solution.py:425
  1094.0 140.7 %copy-start.86 = (f32[1024]{0:T(1024)}, f32[1024]{0:T(1024)S(1)}, u32[]{:S(2)}) copy-start(f32[1024]{0:T(1024)S(1)} %broadcast_multiply_fusion.22) | copy-start | bytes 12292
  1097.1 137.6 %copy-start.104 = (f32[1024]{0:T(1024)}, f32[1024]{0:T(1024)S(1)}, u32[]{:S(2)}) copy-start(f32[1024]{0:T(1024)S(1)} %add_rsqrt_fusion.5) | copy-start | bytes 12292
  1999.2 534.2 %reduce-scatter.46.cloned.1.call-start = ((), (), s32[]{:S(2)}) async-start(), calls=%async_computation.36 | async-start | bytes 51904512 | tf_op jit(solution)/shard_map/reduce_scatter | solution.py:424
  1999.8 677.6 %reduce-scatter.88.cloned.1.call-start = ((), (), s32[]{:S(2)}) async-start(), calls=%async_computation.59 | async-start | bytes 811008
  2003.2 675.9 %reduce-scatter.56.cloned.1.call-start = ((), (), s32[]{:S(2)}) async-start(), calls=%async_computation.42 | async-start | bytes 8921088 | tf_op jit(solution)/shard_map/reduce_scatter | solution.py:495
  2017.3 700.2 %reduce-scatter.60.cloned.1.call-start = ((), (), s32[]{:S(2)}) async-start(), calls=%async_computation.44 | async-start | bytes 8921088 | tf_op jit(solution)/shard_map/reduce_scatter | solution.py:496
  2030.9 759.1 %reduce-scatter.54.cloned.1.call-start = ((), (), s32[]{:S(2)}) async-start(), calls=%async_computation.41 | async-start | bytes 8921088 | tf_op jit(solution)/shard_map/reduce_scatter | solution.py:494
  2044.6 960.0 %reduce-scatter.66.cloned.1.call-start = ((), (), s32[]{:S(2)}) async-start(), calls=%async_computation.47 | async-start | bytes 38928384 | tf_op jit(solution)/shard_map/reduce_scatter | solution.py:498
  2081.7 1009.1 %all-reduce.7.cloned.1.call-start = ((), (), s32[]{:S(2)}) async-start(), calls=%async_computation.38 | async-start | bytes 8650752 | tf_op jit(solution)/shard_map/psum | solution.py:360
  2093.9 1211.5 %reduce-scatter.62.cloned.1.call-start = ((), (), s32[]{:S(2)}) async-start(), calls=%async_computation.45 | async-start | bytes 38928384 | tf_op jit(solution)/shard_map/reduce_scatter | solution.py:497
  2121.9 1528.4 %reduce-scatter.50.cloned.1.call-start = ((), (), s32[]{:S(2)}) async-start(), calls=%async_computation.39 | async-start | bytes 17842176 | tf_op jit(solution)/shard_map/reduce_scatter | solution.py:492
  2657.1 1018.9 %reduce-scatter.52.cloned.1.call-start = ((), (), s32[]{:S(2)}) async-start(), calls=%async_computation.40 | async-start | bytes 26763264 | tf_op jit(solution)/shard_map/reduce_scatter | solution.py:493
  2677.3 1020.4 %reduce-scatter.68.cloned.1.call-start = ((), (), s32[]{:S(2)}) async-start(), calls=%async_computation.48 | async-start | bytes 20480 | tf_op jit(solution)/shard_map/reduce_scatter | solution.py:527
  2679.0 1042.4 %reduce-scatter.82.cloned.1.call-start = ((), (), s32[]{:S(2)}) async-start(), calls=%async_computation.56 | async-start | bytes 901120
  2681.6 1063.9 %reduce-scatter.84.cloned.1.call-start = ((), (), s32[]{:S(2)}) async-start(), calls=%async_computation.57 | async-start | bytes 901120
  2719.9 1050.4 %reduce-scatter.80.cloned.1.call-start = ((), (), s32[]{:S(2)}) async-start(), calls=%async_computation.55 | async-start | bytes 901120
  2792.4 1023.9 %reduce-scatter.86.cloned.1.call-start = ((), (), s32[]{:S(2)}) async-start(), calls=%async_computation.58 | async-start | bytes 2703360
  3012.9 850.3 %reduce-scatter.64.cloned.1.call-start = ((), (), s32[]{:S(2)}) async-start(), calls=%async_computation.46 | async-start | bytes 2703360 | tf_op jit(solution)/shard_map/reduce_scatter | solution.py:521
  3016.3 74.5 %copy-start.43 = (f32[2,333,16]{1,2,0:T(8,128)S(1)}, f32[2,333,16]{1,2,0:T(8,128)}, u32[]{:S(2)}) copy-start(f32[2,333,16]{1,2,0:T(8,128)} %copy-done.40) | copy-start | bytes 127876
  3016.3 74.5 %copy-start.53 = (f32[2,333,16]{1,2,0:T(8,128)S(1)}, f32[2,333,16]{1,2,0:T(8,128)}, u32[]{:S(2)}) copy-start(f32[2,333,16]{1,2,0:T(8,128)} %add_rsqrt_fusion.3) | copy-start | bytes 127876
  3095.7 216.6 %copy-start.24 = (bf16[1024,1408]{1,0:T(8,128)(2,1)S(1)}, bf16[1024,1408]{1,0:T(8,128)(2,1)}, u32[]{:S(2)}) copy-start(bf16[1024,1408]{1,0:T(8,128)(2,1)} %copy-done.23) | copy-start | bytes 8650756
  3309.3 591.1 %reduce-scatter.90.cloned.1.call-start = ((), (), s32[]{:S(2)}) async-start(), calls=%async_computation.60 | async-start | bytes 811008
  3610.7 328.1 %reduce-scatter.70.cloned.1.call-start = ((), (), s32[]{:S(2)}) async-start(), calls=%async_computation.50 | async-start | bytes 811008
  3627.7 334.5 %reduce-scatter.74.cloned.1.call-start = ((), (), s32[]{:S(2)}) async-start(), calls=%async_computation.52 | async-start | bytes 450560
  3632.3 353.2 %reduce-scatter.76.cloned.1.call-start = ((), (), s32[]{:S(2)}) async-start(), calls=%async_computation.53 | async-start | bytes 901120
  3634.6 374.6 %reduce-scatter.58.cloned.1.call-start = ((), (), s32[]{:S(2)}) async-start(), calls=%async_computation.43 | async-start | bytes 901120 | tf_op jit(solution)/shard_map/reduce_scatter | solution.py:539
  3650.2 388.0 %reduce-scatter.72.cloned.1.call-start = ((), (), s32[]{:S(2)}) async-start(), calls=%async_computation.51 | async-start | bytes 1351680
  3653.4 29.6 copy-start.130
  3653.4 31.5 copy-start.8
  3653.4 31.5 copy-start.61
  3653.5 31.5 copy-start.68
  3653.5 430.7 %reduce-scatter.78.cloned.1.call-start = ((), (), s32[]{:S(2)}) async-start(), calls=%async_computation.54 | async-start | bytes 2703360
  (119 other events, 978.6 us)
Sparse Core Ops, SparseCore 0:
  9.6 59.5 all-gather.51
  71.7 34.2 all-gather.27
  108.4 52.9 all-gather.25
  163.2 73.5 all-gather.29
  238.2 47.2 all-gather.43
  286.9 45.9 all-gather.47
  335.3 42.0 all-gather.37
  379.4 121.8 all-gather.33
  503.1 120.9 all-gather.31
  626.5 35.7 all-gather.35
  664.7 35.7 all-gather.39
  702.8 35.7 all-gather.41
  740.5 92.0 all-gather.45
  834.3 91.6 all-gather.49
  1999.3 265.7 reduce-scatter.47
  2269.0 264.3 reduce-scatter.45
  2536.9 34.7 reduce-scatter.87
  2575.2 69.0 reduce-scatter.55
  2648.4 69.0 reduce-scatter.59
  2720.9 69.0 reduce-scatter.53
  2794.1 210.4 reduce-scatter.65
  3008.3 82.4 all-reduce.6
  3094.9 210.5 reduce-scatter.61
  3309.5 174.6 reduce-scatter.49
  3487.8 188.2 reduce-scatter.51
  3678.8 18.8 reduce-scatter.67
  3700.4 20.9 reduce-scatter.81
  3723.7 21.8 reduce-scatter.83
  3748.5 21.7 reduce-scatter.79
  3772.4 43.8 reduce-scatter.85
  3818.8 44.2 reduce-scatter.63
  3866.3 34.1 reduce-scatter.89
  3904.0 34.7 reduce-scatter.69
  3941.7 20.4 reduce-scatter.73
  3964.5 20.9 reduce-scatter.75
  3987.6 21.6 reduce-scatter.57
  4011.4 26.7 reduce-scatter.71
  4040.5 43.5 reduce-scatter.77
where the time goes:
time: 4100 us; the launch traced here: 4090 us
  waiting for transfers between devices  1420 us (35%)
  matrix products  1260 us (31%)
  blocking collectives  545 us (13%)
  local copies, waits for them, and re-layouts  495 us (12%)
  other arithmetic  348 us (8%)
    psum x1, blocking collectives, local(): sum_ckey, sum_cvalue = lax.psum((part_ckey, part_cvalue), ('row', 'col'))  279 us
    unnamed x49, waiting for transfers between devices  272 us
    reduce_scatter x1, waiting for transfers between devices, local(): lax.psum_scatter(grad_key_all, ('row', 'col'), scatter_dimension=1, tiled...  263 us
    reduce_scatter x1, waiting for transfers between devices, local(): lax.psum_scatter(d_down, ('row', 'col'), scatter_dimension=0, tiled=True)  212 us
    reduce_scatter x1, waiting for transfers between devices, local(): lax.psum_scatter(d_up, ('row', 'col'), scatter_dimension=0, tiled=True)  210 us
    dot_general x4, matrix products, backward_block_step(): jnp.einsum('ihqe,ikhe->ihqk', grad_att_h, value_blk, preferred_element_ty...  175 us
    dot_general x9, matrix products, right_dot(): lax.dot_general(left_mat, right_mat, (((1,), (1,)), ((), ())), preferred_...  143 us
    dot_general x7, matrix products, left_dot(): lax.dot_general(left_mat, right_mat, (((0,), (0,)), ((), ())), preferred_...  140 us
  transfers between devices with their start and end apart: 38, of which 24 were waited for; matrix products, arithmetic and copies ran while one was open for 29% of the time, Pallas kernels for 0%

commit v1 on v0

--- a/solution.py
+++ b/solution.py
@@ -1,8 +1,11 @@
+import functools
 import math
 
 import jax
 import jax.numpy as jnp
 from jax import lax
+from jax.experimental import pallas as pl
+from jax.experimental.pallas import tpu as pltpu
 from jax.sharding import PartitionSpec as P
 
 HEADS = 16
@@ -87,7 +90,7 @@
     return block_len
 
 
-def local(
+def local_gathered(
     latent,
     skip_input,
     text_states,
@@ -561,9 +564,848 @@
     )
 
 
+TILE = ("row", "col")
+EVERY = ("dp", "row", "col")
+LOG2E = math.log2(math.e)
+F32 = jnp.float32
+BF16 = jnp.bfloat16
+VMEM_BYTES = 56 * 2**20
+
+
+def kernel_call(body, flops, moved, **options):
+    return pl.pallas_call(
+        body,
+        compiler_params=pltpu.CompilerParams(vmem_limit_bytes=VMEM_BYTES),
+        cost_estimate=pl.CostEstimate(flops=flops, bytes_accessed=moved, transcendentals=0),
+        **options,
+    )
+
+
+def pair_swap(values_in):
+    quarter = values_in.shape[0] // 4
+    parts = [values_in[at * quarter : (at + 1) * quarter] for at in (1, 0, 3, 2)]
+    return jnp.concatenate(parts, axis=0)
+
+
+def column_norm(values_in):
+    centred = values_in - jnp.mean(values_in, axis=0, keepdims=True)
+    inverse = lax.rsqrt(jnp.mean(centred * centred, axis=0, keepdims=True) + EPSILON)
+    return (centred * inverse, inverse)
+
+
+def column_norm_back(grad_normed, normed, inverse):
+    mean_grad = jnp.mean(grad_normed, axis=0, keepdims=True)
+    mean_cross = jnp.mean(grad_normed * normed, axis=0, keepdims=True)
+    return inverse * (grad_normed - mean_grad - normed * mean_cross)
+
+
+def minus_pieces(row_values):
+    high = row_values.astype(BF16).astype(F32)
+    rest = row_values - high
+    middle = rest.astype(BF16).astype(F32)
+    lower = rest - middle
+    at = lax.broadcasted_iota(jnp.int32, (8, row_values.shape[1]), 0)
+    zero = jnp.zeros((8, row_values.shape[1]), F32)
+    picked = jnp.where(at == 0, high, jnp.where(at == 1, middle, jnp.where(at == 2, lower, zero)))
+    return -picked
+
+
+def piece_flags(width):
+    return (lax.broadcasted_iota(jnp.int32, (8, width), 0) < 3).astype(F32)
+
+
+def head_norm_body(
+    query_scale, rows_ref, weight_ref, cos_ref, sin_ref, ok_ref, out_ref, inv_ref
+):
+    groups, _, heads, head_dim, _ = out_ref.shape
+    part = pl.program_id(0)
+    made = jnp.dot(rows_ref[...], weight_ref[...], preferred_element_type=F32).T
+    valid = ok_ref[...]
+
+    @pl.when(part < 2)
+    def _():
+        factor = jnp.where(part == 0, query_scale, valid)
+        cosine, sine = cos_ref[...] * factor, sin_ref[...] * factor
+        for group in range(groups):
+            for head in range(heads):
+                at = (group * heads + head) * head_dim
+                normed, inverse = column_norm(made[at : at + head_dim])
+                turned = normed * cosine + pair_swap(normed) * sine
+                out_ref[group, 0, head] = turned.astype(BF16)
+                inv_ref[group, 0, head : head + 1] = inverse
+
+    @pl.when(part == 2)
+    def _():
+        for group in range(groups):
+            for head in range(heads):
+                at = (group * heads + head) * head_dim
+                out_ref[group, 0, head] = (made[at : at + head_dim] * valid).astype(BF16)
+                inv_ref[group, 0, head : head + 1] = valid
+
+
+def head_norm(rows, weight, tables, valid, groups, head_dim, query_scale):
+    tile_len, depth = rows.shape
+    width = weight.shape[1] // 3
+    heads = width // groups // head_dim
+    table = pl.BlockSpec((head_dim, tile_len), lambda p: (0, 0))
+    return kernel_call(
+        functools.partial(head_norm_body, query_scale),
+        6 * tile_len * depth * width,
+        6 * depth * width,
+        grid=(3,),
+        in_specs=[
+            pl.BlockSpec((tile_len, depth), lambda p: (0, 0)),
+            pl.BlockSpec((depth, width), lambda p: (0, p)),
+            table,
+            table,
+            pl.BlockSpec((1, tile_len), lambda p: (0, 0)),
+        ],
+        out_specs=[
+            pl.BlockSpec((groups, 1, heads, head_dim, tile_len), lambda p: (0, p, 0, 0, 0)),
+            pl.BlockSpec((groups, 1, heads, tile_len), lambda p: (0, p, 0, 0)),
+        ],
+        out_shape=[
+            jax.ShapeDtypeStruct((groups, 3, heads, head_dim, tile_len), BF16),
+            jax.ShapeDtypeStruct((groups, 3, heads, tile_len), F32),
+        ],
+    )(rows, weight, *tables, valid)
+
+
+def head_back_body(
+    query_scale, grad_ref, own_ref, inv_ref, cos_ref, sin_ref, ok_ref, *others
+):
+    out_ref = others[-1]
+    heads, head_dim = own_ref.shape[2], own_ref.shape[3]
+    cosine, sine, valid = cos_ref[...], sin_ref[...], ok_ref[...]
+
+    def unturn(values_in):
+        return values_in * cosine - pair_swap(values_in) * sine
+
+    for part in range(3):
+        pieces = []
+        for head in range(heads):
+            grad = grad_ref[0, part, head].astype(F32)
+            if part > 0:
+                grad = grad * valid
+            if part < 2:
+                normed = unturn(own_ref[0, part, head].astype(F32))
+                if part == 0:
+                    normed = normed * (1.0 / query_scale)
+                inverse = inv_ref[0, part, head : head + 1]
+                grad = column_norm_back(unturn(grad), normed, inverse)
+            pieces.append(grad)
+        out_ref[part, 0] = jnp.concatenate(pieces, axis=0).astype(BF16)
+
+
+def head_back(grads, own, inverses, tables, valid, query_scale, image, images, before):
+    groups, _, heads, head_dim, tile_len = own.shape
+    group_rows = heads * head_dim
+    stacked = pl.BlockSpec((1, 3, heads, head_dim, tile_len), lambda g: (g, 0, 0, 0, 0))
+    table = pl.BlockSpec((head_dim, tile_len), lambda g: (0, 0))
+    earlier = () if before is None else (before,)
+    return kernel_call(
+        functools.partial(head_back_body, query_scale),
+        0,
+        6 * own.size,
+        grid=(groups,),
+        in_specs=[
+            stacked,
+            stacked,
+            pl.BlockSpec((1, 3, heads, tile_len), lambda g: (g, 0, 0, 0)),
+            table,
+            table,
+            pl.BlockSpec((1, tile_len), lambda g: (0, 0)),
+        ]
+        + [pl.BlockSpec(memory_space=pl.ANY)] * len(earlier),
+        out_specs=pl.BlockSpec((3, 1, group_rows, tile_len), lambda g: (0, g, 0, image)),
+        out_shape=jax.ShapeDtypeStruct((3, groups, group_rows, images * tile_len), BF16),
+        input_output_aliases={6: 0} if earlier else {},
+    )(grads, own, inverses, *tables, valid, *earlier)
+
+
+def attend_body(query_ref, key_ref, value_ref, ok_ref, out_ref, lse_ref, key_nat, value_ext):
+    tiles, tile_len, head_dim = key_ref.shape[0], key_ref.shape[-1], key_ref.shape[-2]
+
+    @pl.when(pl.program_id(1) == 0)
+    def _():
+        for tile in range(tiles):
+            key_nat[tile * tile_len : (tile + 1) * tile_len, :] = key_ref[tile, 0, 0].T
+            value_ext[tile] = jnp.concatenate(
+                [value_ref[tile, 0, 0].astype(F32), ok_ref[tile]], axis=0
+            ).astype(BF16)
+
+    query = query_ref[0, 0, 0]
+
+    def step(tile, total):
+        rows = pl.ds(pl.multiple_of(tile * tile_len, tile_len), tile_len)
+        scores = jnp.dot(key_nat[rows, :], query, preferred_element_type=F32)
+        weight = jnp.exp2(scores).astype(BF16)
+        return total + jnp.dot(value_ext[tile], weight, preferred_element_type=F32)
+
+    start = jnp.zeros((head_dim + 8, tile_len), F32)
+    total = lax.fori_loop(0, tiles, step, start, unroll=8)
+    weight_sum = total[head_dim : head_dim + 1]
+    out_ref[0, 0] = (total[:head_dim] / weight_sum).astype(BF16)
+    lse_ref[0, 0] = jnp.log2(weight_sum)
+
+
+def attend(qkv, flags):
+    tiles, _, heads, head_dim, tile_len = qkv.shape
+    return kernel_call(
+        attend_body,
+        1024 * heads * tiles**2 * tile_len**2,
+        8 * qkv.size,
+        grid=(heads, tiles),
+        in_specs=[
+            pl.BlockSpec((1, 1, 1, head_dim, tile_len), lambda h, t: (t, 0, h, 0, 0)),
+            pl.BlockSpec((tiles, 1, 1, head_dim, tile_len), lambda h, t: (0, 1, h, 0, 0)),
+            pl.BlockSpec((tiles, 1, 1, head_dim, tile_len), lambda h, t: (0, 2, h, 0, 0)),
+            pl.BlockSpec((tiles, 8, tile_len), lambda h, t: (0, 0, 0)),
+        ],
+        out_specs=[
+            pl.BlockSpec((1, 1, head_dim, tile_len), lambda h, t: (t, h, 0, 0)),
+            pl.BlockSpec((1, 1, 1, tile_len), lambda h, t: (t, h, 0, 0)),
+        ],
+        out_shape=[
+            jax.ShapeDtypeStruct((tiles, heads, head_dim, tile_len), BF16),
+            jax.ShapeDtypeStruct((tiles, heads, 1, tile_len), F32),
+        ],
+        scratch_shapes=[
+            pltpu.VMEM((tiles * tile_len, head_dim), BF16),
+            pltpu.VMEM((tiles, head_dim + 8, tile_len), BF16),
+        ],
+    )(qkv, qkv, qkv, flags)
+
+
+def attend_back_body(
+    score_scale,
+    query_ref,
+    key_ref,
+    value_ref,
+    grad_ref,
+    att_ref,
+    lse_ref,
+    out_ref,
+    key_nat,
+    value_nat,
+    key_sum,
+    value_sum,
+):
+    tiles, tile_len, head_dim = key_ref.shape[0], key_ref.shape[-1], key_ref.shape[-2]
+    at = pl.program_id(1)
+
+    @pl.when(at == 0)
+    def _():
+        ones = piece_flags(tile_len)
+        for tile in range(tiles):
+            rows = slice(tile * tile_len, (tile + 1) * tile_len)
+            for source, kept in ((key_ref, key_nat), (value_ref, value_nat)):
+                wide = jnp.concatenate([source[tile, 0, 0].astype(F32), ones], axis=0)
+                kept[rows, :] = wide.T.astype(BF16)
+        key_sum[...] = jnp.zeros_like(key_sum)
+        value_sum[...] = jnp.zeros_like(value_sum)
+
+    query = query_ref[0, 0, 0].astype(F32)
+    grad = grad_ref[0, 0].astype(F32)
+    delta = jnp.sum(grad * att_ref[0, 0].astype(F32), axis=0, keepdims=True)
+    query_ext = jnp.concatenate([query, minus_pieces(lse_ref[0, 0])], axis=0)
+    grad_ext = jnp.concatenate([grad, minus_pieces(delta)], axis=0)
+    query_cols, grad_cols = query_ext.astype(BF16), grad_ext.astype(BF16)
+    query_nat, grad_nat = query_ext.T.astype(BF16), grad_ext.T.astype(BF16)
+
+    def step(tile, total):
+        rows = pl.ds(pl.multiple_of(tile * tile_len, tile_len), tile_len)
+        scores = jnp.dot(key_nat[rows, :], query_cols, preferred_element_type=F32)
+        probs = jnp.exp2(scores)
+        grad_probs = jnp.dot(value_nat[rows, :], grad_cols, preferred_element_type=F32)
+        grad_scores = (probs * grad_probs).astype(BF16)
+        value_sum[rows, :] += jnp.dot(probs.astype(BF16), grad_nat, preferred_element_type=F32)
+        key_sum[rows, :] += jnp.dot(grad_scores, query_nat, preferred_element_type=F32)
+        return total + jnp.dot(key_ref[tile, 0, 0], grad_scores, preferred_element_type=F32)
+
+    start = jnp.zeros((head_dim, tile_len), F32)
+    total = lax.fori_loop(0, tiles, step, start, unroll=8)
+    out_ref[at, 0, 0] = (total * score_scale).astype(BF16)
+
+    @pl.when(at == tiles - 1)
+    def _():
+        for tile in range(tiles):
+            rows = slice(tile * tile_len, (tile + 1) * tile_len)
+            key_grad = key_sum[rows, :].T[:head_dim] * (1.0 / LOG2E)
+            out_ref[tile, 1, 0] = key_grad.astype(BF16)
+            out_ref[tile, 2, 0] = value_sum[rows, :].T[:head_dim].astype(BF16)
+
+
+def attend_back(qkv, grad_att, att, lse, score_scale):
+    tiles, _, heads, head_dim, tile_len = qkv.shape
+    one = pl.BlockSpec((1, 1, head_dim, tile_len), lambda h, t: (t, h, 0, 0))
+    return kernel_call(
+        functools.partial(attend_back_body, score_scale),
+        2560 * heads * tiles**2 * tile_len**2,
+        8 * qkv.size,
+        grid=(heads, tiles),
+        in_specs=[
+            pl.BlockSpec((1, 1, 1, head_dim, tile_len), lambda h, t: (t, 0, h, 0, 0)),
+            pl.BlockSpec((tiles, 1, 1, head_dim, tile_len), lambda h, t: (0, 1, h, 0, 0)),
+            pl.BlockSpec((tiles, 1, 1, head_dim, tile_len), lambda h, t: (0, 2, h, 0, 0)),
+            one,
+            one,
+            pl.BlockSpec((1, 1, 1, tile_len), lambda h, t: (t, h, 0, 0)),
+        ],
+        out_specs=pl.BlockSpec(
+            (tiles, 3, 1, head_dim, tile_len), lambda h, t: (0, 0, h, 0, 0)
+        ),
+        out_shape=jax.ShapeDtypeStruct(qkv.shape, BF16),
+        scratch_shapes=[
+            pltpu.VMEM((tiles * tile_len, head_dim + 8), BF16),
+            pltpu.VMEM((tiles * tile_len, head_dim + 8), BF16),
+            pltpu.VMEM((tiles * tile_len, head_dim + 8), F32),
+            pltpu.VMEM((tiles * tile_len, head_dim + 8), F32),
+        ],
+    )(qkv, qkv, qkv, grad_att, att, lse)
+
+
+def cross_body(text_len, query_scale, pre_ref, kv_ref, att_ref, query_ref, inv_ref, lse_ref):
+    head_dim, text_pad = kv_ref.shape[2], kv_ref.shape[3]
+    normed, inverse = column_norm(pre_ref[0])
+    query = (normed * query_scale).astype(BF16)
+    query_ref[0] = query
+    inv_ref[0] = inverse
+    key = column_norm(kv_ref[0, 0])[0].astype(BF16)
+    at = lax.broadcasted_iota(jnp.int32, (8, text_pad), 0)
+    text_at = lax.broadcasted_iota(jnp.int32, (8, text_pad), 1)
+    flags = ((at == 0) & (text_at < text_len)).astype(F32)
+    value_ext = jnp.concatenate([kv_ref[1, 0], flags], axis=0).astype(BF16)
+    scores = jnp.dot(key.T, query, preferred_element_type=F32)
+    weight = jnp.exp2(scores).astype(BF16)
+    total = jnp.dot(value_ext, weight, preferred_element_type=F32)
+    weight_sum = total[head_dim : head_dim + 1]
+    att_ref[0] = (total[:head_dim] / weight_sum).astype(BF16)
+    lse_ref[0] = jnp.log2(weight_sum)
+
+
+def cross_attend(pre, text_kv, images, text_len, query_scale):
+    heads, head_dim, tokens = pre.shape
+    tile_len, text_pad = tokens // images, text_kv.shape[3] // images
+    wide = pl.BlockSpec((1, head_dim, tile_len), lambda i, h: (h, 0, i))
+    row = pl.BlockSpec((1, 1, tile_len), lambda i, h: (h, 0, i))
+    return kernel_call(
+        functools.partial(cross_body, text_len, query_scale),
+        1024 * heads * tokens * text_pad,
+        8 * pre.size,
+        grid=(images, heads),
+        in_specs=[wide, pl.BlockSpec((2, 1, head_dim, text_pad), lambda i, h: (0, h, 0, i))],
+        out_specs=[wide, wide, row, row],
+        out_shape=[
+            jax.ShapeDtypeStruct(pre.shape, BF16),
+            jax.ShapeDtypeStruct(pre.shape, BF16),
+            jax.ShapeDtypeStruct((heads, 1, tokens), F32),
+            jax.ShapeDtypeStruct((heads, 1, tokens), F32),
+        ],
+    )(pre, text_kv)
+
+
+def cross_back_body(
+    query_scale,
+    score_scale,
+    query_ref,
+    kv_ref,
+    grad_ref,
+    att_ref,
+    inv_ref,
+    lse_ref,
+    out_ref,
+    key_ref,
+    value_ref,
+):
+    head_dim, text_pad = kv_ref.shape[2], kv_ref.shape[3]
+    query = query_ref[0].astype(F32)
+    grad = grad_ref[0].astype(F32)
+    delta = jnp.sum(grad * att_ref[0].astype(F32), axis=0, keepdims=True)
+    query_ext = jnp.concatenate([query, minus_pieces(lse_ref[0])], axis=0).astype(BF16)
+    grad_ext = jnp.concatenate([grad, minus_pieces(delta)], axis=0).astype(BF16)
+    ones = piece_flags(text_pad)
+    key = column_norm(kv_ref[0, 0])[0].astype(BF16)
+    key_ext = jnp.concatenate([key.astype(F32), ones], axis=0).T.astype(BF16)
+    value_ext = jnp.concatenate([kv_ref[1, 0], ones], axis=0).T.astype(BF16)
+    probs = jnp.exp2(jnp.dot(key_ext, query_ext, preferred_element_type=F32))
+    grad_probs = jnp.dot(value_ext, grad_ext, preferred_element_type=F32)
+    grad_scores = (probs * grad_probs).astype(BF16)
+    value_grad = right_dot(grad_ext, probs.astype(BF16))[:head_dim]
+    key_grad = right_dot(query_ext, grad_scores)[:head_dim]
+    key_ref[0] = (key_grad * (1.0 / LOG2E)).astype(BF16)
+    value_ref[0] = value_grad.astype(BF16)
+    query_grad = jnp.dot(key, grad_scores, preferred_element_type=F32) * score_scale
+    normed = query * (1.0 / query_scale)
+    out_ref[0] = column_norm_back(query_grad, normed, inv_ref[0]).astype(BF16)
+
+
+def cross_back(query, text_kv, grad, att, inverse, lse, images, query_scale, score_scale):
+    heads, head_dim, tokens = query.shape
+    tile_len, text_pad = tokens // images, text_kv.shape[3] // images
+    wide = pl.BlockSpec((1, head_dim, tile_len), lambda i, h: (h, 0, i))
+    row = pl.BlockSpec((1, 1, tile_len), lambda i, h: (h, 0, i))
+    text = pl.BlockSpec((2, 1, head_dim, text_pad), lambda i, h: (0, h, 0, i))
+    text_out = pl.BlockSpec((1, head_dim, text_pad), lambda i, h: (h, 0, i))
+    return kernel_call(
+        functools.partial(cross_back_body, query_scale, score_scale),
+        2560 * heads * tokens * text_pad,
+        16 * query.size,
+        grid=(images, heads),
+        in_specs=[wide, text, wide, wide, row, row],
+        out_specs=[
+            wide,
+            text_out,
+            text_out,
+        ],
+        out_shape=[
+            jax.ShapeDtypeStruct(query.shape, BF16),
+            jax.ShapeDtypeStruct((heads, head_dim, images * text_pad), BF16),
+            jax.ShapeDtypeStruct((heads, head_dim, images * text_pad), BF16),
+        ],
+    )(query, text_kv, grad, att, inverse, lse)
+
+
+def swap_tiles(values_in):
+    return lax.all_to_all(values_in, TILE, split_axis=0, concat_axis=0, tiled=True)
+
+
+def shift_pairs(devices, step):
+    return [(at, (at + step) % devices) for at in range(devices)]
+
+
+def fetch(weight):
+    devices = lax.axis_size("dp")
+    return [weight] + [
+        lax.ppermute(weight, "dp", shift_pairs(devices, step)) for step in range(1, devices)
+    ]
+
+
+def widen(pieces, first=None):
+    devices, me = lax.axis_size("dp"), lax.axis_index("dp")
+    if first is not None:
+        pieces = after(first, *pieces)
+    return jnp.concatenate(
+        [lax.select_n((me - at) % devices, *pieces) for at in range(devices)], axis=1
+    )
+
+
+def narrow_blocks(blocks):
+    devices, me = lax.axis_size("dp"), lax.axis_index("dp")
+    total = lax.select_n(me, *blocks).astype(F32)
+    for step in range(1, devices):
+        sent = lax.select_n((me + step) % devices, *blocks)
+        total = total + lax.ppermute(sent, "dp", shift_pairs(devices, step)).astype(F32)
+    return total
+
+
+def narrow(weight_grad):
+    return narrow_blocks(jnp.split(weight_grad, lax.axis_size("dp"), axis=1))
+
+
+def narrow_three(weight_grads):
+    devices = lax.axis_size("dp")
+    weight_grads = jnp.split(weight_grads, 3, axis=1)
+    split = [jnp.split(weight_grad, devices, axis=1) for weight_grad in weight_grads]
+    return narrow_blocks([jnp.concatenate(blocks, axis=1) for blocks in zip(*split)])
+
+
+def sum_tiles(part_sums):
+    devices, me = lax.axis_size(TILE), lax.axis_index(TILE)
+    blocks = jnp.split(part_sums, devices, axis=0)
+    total = lax.select_n(me, *blocks)
+    for step in range(1, devices):
+        sent = lax.select_n((me + step) % devices, *blocks)
+        total = total + lax.ppermute(sent, TILE, shift_pairs(devices, step))
+    return total
+
+
+def total_tiles(part_sum):
+    devices = lax.axis_size(TILE)
+    total = part_sum
+    for step in range(1, devices):
+        total = total + lax.ppermute(part_sum, TILE, shift_pairs(devices, step))
+    return total
+
+
+def over_tiles(weight_grad):
+    return lax.optimization_barrier(
+        lax.psum_scatter(weight_grad, TILE, scatter_dimension=0, tiled=True)
+    )
+
+
+def tiles_whole(weight):
+    return lax.all_gather(weight, TILE, axis=0, tiled=True)
+
+
+def after(first, *values_in):
+    return lax.optimization_barrier((first, *values_in))[1:]
+
+
+def dot_over(left_mat, right_mat, left_axis, right_axis):
+    return lax.dot_general(
+        left_mat,
+        right_mat,
+        (((left_axis,), (right_axis,)), ((), ())),
+        preferred_element_type=F32,
+    )
+
+
+def local_heads(
+    latent,
+    skip_input,
+    text_states,
+    timesteps,
+    image_sides,
+    cotangent,
+    w_patch,
+    w_skip,
+    w_time,
+    w_shift,
+    w_qkv,
+    w_out,
+    w_query,
+    w_text,
+    w_cross,
+    w_up,
+    w_down,
+    w_final,
+    norm_params,
+):
+    dp_devices = lax.axis_size("dp")
+    grid_devices = lax.axis_size(TILE)
+    col_devices = lax.axis_size("col")
+    grid_at = lax.axis_index(TILE)
+    row_at = lax.axis_index("row")
+    col_at = lax.axis_index("col")
+    images, rows_tile, cols_tile, patch_width = latent.shape
+    tile_len = rows_tile * cols_tile
+    row_count = images * tile_len
+    out_width = cotangent.shape[3]
+
+    part_skip = widen(fetch(w_skip))
+    small = jnp.concatenate([w_patch, w_final, norm_params], axis=1)
+    small_widths = (w_patch.shape[1], w_final.shape[1], norm_params.shape[1])
+    cuts = (0, small_widths[0], sum(small_widths[:2]), sum(small_widths))
+    part_small = widen(fetch(small))
+    part_time, part_shift_w = widen(fetch(w_time)), widen(fetch(w_shift))
+    f_small = tiles_whole(part_small).reshape(-1, dp_devices, sum(small_widths))
+    f_patch, f_final, f_norms = (
+        f_small[:, :, cuts[at] : cuts[at + 1]].reshape(f_small.shape[0], -1) for at in range(3)
+    )
+    f_skip = tiles_whole(part_skip)
+    held_qkv = fetch(w_qkv)
+    held_out, held_query, held_cross = fetch(w_out), fetch(w_query), fetch(w_cross)
+    held_text = fetch(w_text)
+    held_up, held_down = fetch(w_up), fetch(w_down)
+    model_width = skip_input.shape[3]
+    head_count = HEADS
+    head_dim = model_width // head_count
+    text_len = text_states.shape[1]
+    text_pad = -(-text_len // 128) * 128
+    score_scale = head_dim ** (-0.5)
+    query_scale = score_scale * LOG2E
+    positions = jnp.arange(tile_len, dtype=jnp.int32)
+    row_pos = row_at * rows_tile + positions // cols_tile
+    col_pos = col_at * cols_tile + positions % cols_tile
+    query_ok = (row_pos[None, :] < image_sides[:, None]) & (col_pos[None, :] < image_sides[:, None])
+    valid = query_ok.astype(F32)
+    keep_rows = query_ok.astype(F32).reshape(row_count, 1)
+    tile_list = jnp.arange(grid_devices, dtype=jnp.int32)[:, None]
+    key_row = tile_list // col_devices * rows_tile + (positions // cols_tile)[None, :]
+    key_col = tile_list % col_devices * cols_tile + (positions % cols_tile)[None, :]
+    sides = image_sides[:, None, None]
+    key_ok = ((key_row[None] < sides) & (key_col[None] < sides)).astype(F32)
+    flags = jnp.concatenate(
+        [key_ok[:, :, None, :], jnp.zeros((images, grid_devices, 7, tile_len), F32)], axis=2
+    )
+    cos_row, sin_row, cos_col, sin_col = (
+        jnp.transpose(table[:, 0, :]) for table in rope_tables(row_pos, col_pos, head_dim)
+    )
+    tables = (
+        jnp.concatenate([cos_row, cos_row, cos_col, cos_col], axis=0),
+        jnp.concatenate([-sin_row, sin_row, -sin_col, sin_col], axis=0),
+    )
+    norm_f = f_norms.astype(F32)
+
+    embedding = time_embed(timesteps, FREQ).astype(BF16)
+    freq_slice = part_time.shape[0]
+    shift_slice = part_shift_w.shape[0]
+    embed_cols = lax.dynamic_slice_in_dim(embedding, grid_at * freq_slice, freq_slice, 1)
+    time_pre = total_tiles(plain_dot(embed_cols, part_time))
+    time_float, silu_pull = jax.vjp(jax.nn.silu, time_pre)
+    time_act = time_float.astype(BF16)
+    act_cols = lax.dynamic_slice_in_dim(time_act, grid_at * shift_slice, shift_slice, 1)
+    time_shift = total_tiles(plain_dot(act_cols, part_shift_w))
+
+    patch_rows = latent.reshape(row_count, patch_width)
+    patch_feat = right_dot(patch_rows, f_patch)
+    skip_rows = skip_input.reshape(row_count, model_width).astype(F32)
+    gain_skip = jnp.concatenate([norm_f[:, 8], norm_f[:, 10]])
+    bias_skip = jnp.concatenate([norm_f[:, 9], norm_f[:, 11]])
+    joined, joined_inv = layer_norm(jnp.concatenate([patch_feat, skip_rows], axis=-1))
+    skip_in = (joined * gain_skip + bias_skip).astype(BF16)
+    f_qkv = tiles_whole(widen(held_qkv, skip_in))
+    part_three = [widen(held, skip_in) for held in (held_out, held_query, held_cross)]
+    f_three = tiles_whole(jnp.concatenate(part_three, axis=1))
+    f_out, f_query, f_cross = jnp.split(f_three, 3, axis=1)
+    residual = plain_dot(skip_in, f_skip)
+    first_z, first_inv = layer_norm(residual)
+    first_pre = (first_z * norm_f[:, 0] + norm_f[:, 1]).reshape(
+        images, tile_len, model_width
+    ) + time_shift[:, None, :]
+    first_in = first_pre.reshape(row_count, model_width).astype(BF16)
+    f_up = tiles_whole(widen(held_up, first_in))
+    part_text = widen(held_text, first_in)
+    f_text = tiles_whole(part_text)
+    first_rows = first_in.reshape(images, tile_len, model_width)
+    own_qkv, qk_inv, tile_qkv, tile_att, tile_lse, att_rows = [], [], [], [], [], []
+    for image in range(images):
+        rows = first_rows[image]
+        own, inverses = head_norm(
+            rows,
+            f_qkv,
+            tables,
+            valid[image : image + 1],
+            grid_devices,
+            head_dim,
+            query_scale,
+        )
+        own_qkv.append(own)
+        qk_inv.append(inverses)
+        tile_qkv.append(swap_tiles(own))
+    for image in range(images):
+        att, lse = attend(tile_qkv[image], flags[image])
+        tile_att.append(att)
+        tile_lse.append(lse)
+        own_att = swap_tiles(att).reshape(model_width, tile_len)
+        att_rows.append(jnp.transpose(own_att))
+    att_low = jnp.concatenate(att_rows, axis=0)
+    residual_two = residual + plain_dot(att_low, f_out)
+    f_down = tiles_whole(widen(held_down, residual_two))
+
+    third_z, third_inv = layer_norm(residual_two)
+    third_in = (third_z * norm_f[:, 2] + norm_f[:, 3]).astype(BF16)
+    cross_pre = dot_over(f_query, third_in, 0, 1).reshape(head_count, head_dim, row_count)
+    text_rows = jnp.pad(text_states, ((0, 0), (0, text_pad - text_len), (0, 0)))
+    text_rows = text_rows.reshape(images * text_pad, -1)
+    text_kv = dot_over(f_text, text_rows, 0, 1).reshape(2, head_count, head_dim, images * text_pad)
+    crossed, cross_queries, cq_inv, cross_lse = cross_attend(
+        cross_pre, text_kv, images, text_len, query_scale
+    )
+    cross_cols = crossed.reshape(model_width, row_count)
+    residual_three = residual_two + left_dot(cross_cols, f_cross)
+    second_z, second_inv = layer_norm(residual_three)
+    second_in = (second_z * norm_f[:, 4] + norm_f[:, 5]).astype(BF16)
+    up_pre = plain_dot(second_in, f_up)
+    hidden_float, gelu_pull = jax.vjp(gelu_tanh, up_pre)
+    hidden_act = hidden_float.astype(BF16)
+    residual_four = residual_three + plain_dot(hidden_act, f_down)
+    last_z, last_inv = layer_norm(residual_four)
+    last_in = (last_z * norm_f[:, 6] + norm_f[:, 7]).astype(BF16)
+    produced = plain_dot(last_in, f_final)
+    prediction = (
+        (produced * keep_rows).astype(BF16).reshape(images, rows_tile, cols_tile, out_width)
+    )
+
+    grad_out = (cotangent.reshape(row_count, out_width).astype(F32) * keep_rows).astype(BF16)
+    d_final = left_dot(last_in, grad_out)
+    grad_last = right_dot(grad_out, f_final)
+    gain_final = jnp.sum(grad_last * last_z, axis=0)
+    bias_final = jnp.sum(grad_last, axis=0)
+    grad_four = norm_back(grad_last * norm_f[:, 6], last_z, last_inv)
+    low_four = grad_four.astype(BF16)
+    d_down = left_dot(hidden_act, low_four).astype(BF16)
+    d_down, low_four = lax.optimization_barrier((d_down, low_four))
+    t_down = over_tiles(d_down)
+    grad_hidden = right_dot(low_four, f_down)
+    grad_up = gelu_pull(grad_hidden)[0].astype(BF16)
+    d_up = left_dot(second_in, grad_up).astype(BF16)
+    d_up, grad_up = lax.optimization_barrier((d_up, grad_up))
+    t_up = over_tiles(d_up)
+    grad_second = right_dot(grad_up, f_up)
+    gain_second = jnp.sum(grad_second * second_z, axis=0)
+    bias_second = jnp.sum(grad_second, axis=0)
+    grad_three = grad_four + norm_back(grad_second * norm_f[:, 4], second_z, second_inv)
+    low_three = grad_three.astype(BF16)
+    d_cross = plain_dot(cross_cols, low_three).astype(BF16)
+    down_grad = narrow(t_down)
+    grad_crossed = dot_over(f_cross, low_three, 1, 1).astype(BF16)
+    t_down, grad_crossed = lax.optimization_barrier((t_down, grad_crossed))
+    grad_cross_q, d_text_key, d_text_value = cross_back(
+        cross_queries,
+        text_kv,
+        grad_crossed.reshape(head_count, head_dim, row_count),
+        crossed,
+        cq_inv,
+        cross_lse,
+        images,
+        query_scale,
+        score_scale,
+    )
+    grad_cross_q = grad_cross_q.reshape(model_width, row_count)
+    d_query = dot_over(third_in, grad_cross_q, 0, 1).astype(BF16)
+    grad_third = dot_over(grad_cross_q, f_query, 0, 1)
+    gain_third = jnp.sum(grad_third * third_z, axis=0)
+    bias_third = jnp.sum(grad_third, axis=0)
+    grad_two = grad_three + norm_back(grad_third * norm_f[:, 2], third_z, third_inv)
+    low_two = grad_two.astype(BF16)
+    low_two_rows = low_two.reshape(images, tile_len, model_width)
+    tile_grads = []
+    for image in range(images):
+        grad_att = dot_over(f_out, low_two_rows[image], 1, 1).astype(BF16)
+        tile_grads.append(swap_tiles(grad_att.reshape(tile_att[image].shape)))
+    d_out = left_dot(att_low, low_two).astype(BF16)
+    d_joint = jnp.concatenate(
+        [
+            d_out,
+            d_query,
+            d_cross,
+            d_text_key.reshape(model_width, -1),
+            d_text_value.reshape(model_width, -1),
+        ],
+        axis=1,
+    )
+    t_joint = over_tiles(d_joint)
+    own_grads = []
+    tile_back = None
+    for image in range(images):
+        if tile_back is not None:
+            t_up, down_grad, tile_grads[image], tile_back = lax.optimization_barrier(
+                (t_up, down_grad, tile_grads[image], tile_back)
+            )
+            own_grads.append(swap_tiles(tile_back))
+        tile_back = attend_back(
+            tile_qkv[image], tile_grads[image], tile_att[image], tile_lse[image], score_scale
+        )
+    own_grads.append(swap_tiles(tile_back))
+    up_grad = narrow(t_up)
+    t_joint, up_grad, own_grads[-1] = lax.optimization_barrier((t_joint, up_grad, own_grads[-1]))
+    joint_grad = narrow_three(t_joint[:, : 3 * model_width])
+    sum_text_kv = t_joint[:, 3 * model_width :].astype(F32)
+    sum_text_kv = jnp.transpose(
+        sum_text_kv.reshape(-1, head_dim, 2, images * text_pad), (2, 0, 1, 3)
+    )
+    group_heads = head_count // grid_devices
+    own_key = lax.dynamic_slice_in_dim(text_kv[0], grid_at * group_heads, group_heads, 0)
+    ck_z, ck_inv = layer_norm(jnp.swapaxes(own_key, 1, 2))
+    grad_ckey = jnp.swapaxes(norm_back(jnp.swapaxes(sum_text_kv[0], 1, 2), ck_z, ck_inv), 1, 2)
+    grad_kv = tiles_whole(jnp.stack([grad_ckey, sum_text_kv[1]]).astype(BF16)[None])
+    grad_qkv = None
+    for image in range(images):
+        grad_qkv = head_back(
+            own_grads[image],
+            own_qkv[image],
+            qk_inv[image],
+            tables,
+            valid[image : image + 1],
+            query_scale,
+            image,
+            images,
+            grad_qkv,
+        )
+    grad_qkv = grad_qkv.reshape(3 * model_width, row_count)
+    d_qkv = dot_over(first_in, grad_qkv, 0, 1).astype(BF16)
+    d_qkv, grad_qkv = lax.optimization_barrier((d_qkv, grad_qkv))
+    t_qkv = over_tiles(d_qkv)
+    grad_first = dot_over(grad_qkv, f_qkv, 0, 1)
+    joint_grad, grad_first = lax.optimization_barrier((joint_grad, grad_first))
+    out_grad, query_w_grad, cross_grad = jnp.split(joint_grad, 3, axis=1)
+    gain_first = jnp.sum(grad_first * first_z, axis=0)
+    bias_first = jnp.sum(grad_first, axis=0)
+    part_shift = jnp.sum(grad_first.reshape(images, tile_len, model_width), axis=1)
+    grad_one = grad_two + norm_back(grad_first * norm_f[:, 0], first_z, first_inv)
+
+    low_one = grad_one.astype(BF16)
+    d_skip_w = left_dot(skip_in, low_one).astype(BF16)
+    d_skip_w, low_one = lax.optimization_barrier((d_skip_w, low_one))
+    t_qkv, d_skip_w = lax.optimization_barrier((t_qkv, d_skip_w))
+    qkv_grad = narrow(t_qkv)
+    t_skip = over_tiles(d_skip_w)
+
+    grad_kv = jnp.transpose(grad_kv, (1, 0, 2, 3, 4)).reshape(2 * model_width, images * text_pad)
+    text_slice = text_states.shape[2] // grid_devices
+    text_cols = lax.dynamic_slice_in_dim(text_rows, grid_at * text_slice, text_slice, 1)
+    text_w_grad = narrow(dot_over(text_cols, grad_kv, 0, 1).astype(BF16))
+    text_grad = dot_over(grad_kv, part_text, 0, 1).reshape(images, text_pad, text_slice)
+    text_grad = text_grad[:, :text_len]
+
+    shift_low = total_tiles(part_shift).astype(BF16)
+    shift_w_grad = narrow(left_dot(act_cols, shift_low).astype(BF16))
+    grad_time_act = lax.all_gather(right_dot(shift_low, part_shift_w), TILE, axis=1, tiled=True)
+    grad_time_pre = silu_pull(grad_time_act)[0].astype(BF16)
+    time_w_grad = narrow(left_dot(embed_cols, grad_time_pre).astype(BF16))
+
+    grad_skip_in = right_dot(low_one, f_skip)
+    gain_skips = jnp.sum(grad_skip_in * joined, axis=0)
+    bias_skips = jnp.sum(grad_skip_in, axis=0)
+    grad_joined = norm_back(grad_skip_in * gain_skip, joined, joined_inv)
+    qkv_grad, grad_joined = lax.optimization_barrier((qkv_grad, grad_joined))
+    skip_grad = grad_joined[:, model_width:].reshape(images, rows_tile, cols_tile, model_width)
+    grad_patch = grad_joined[:, :model_width].astype(BF16)
+    d_patch = left_dot(grad_patch, patch_rows)
+    latent_grad = plain_dot(grad_patch, f_patch).reshape(images, rows_tile, cols_tile, patch_width)
+    d_norms = jnp.stack(
+        [
+            gain_first,
+            bias_first,
+            gain_third,
+            bias_third,
+            gain_second,
+            bias_second,
+            gain_final,
+            bias_final,
+            gain_skips[:model_width],
+            bias_skips[:model_width],
+            gain_skips[model_width:],
+            bias_skips[model_width:],
+        ],
+        axis=1,
+    )
+    small_grads = jnp.concatenate(
+        [
+            grad.reshape(model_width, dp_devices, -1)
+            for grad in (d_patch, d_final, d_norms)
+        ],
+        axis=2,
+    )
+    small_grads = narrow(sum_tiles(small_grads.reshape(model_width, -1)))
+    skip_w_grad = narrow(t_skip)
+    patch_grad, final_grad, norms_grad = (
+        small_grads[:, cuts[at] : cuts[at + 1]] for at in range(3)
+    )
+    return (
+        prediction,
+        latent_grad,
+        skip_grad,
+        text_grad,
+        patch_grad,
+        skip_w_grad,
+        time_w_grad,
+        shift_w_grad,
+        qkv_grad,
+        out_grad,
+        query_w_grad,
+        text_w_grad,
+        cross_grad,
+        up_grad,
+        down_grad,
+        final_grad,
+        norms_grad,
+    )
+
+
+def local(sizes, latent, *others):
+    grid_devices = sizes["row"] * sizes["col"]
+    tile_len = latent.shape[1] * latent.shape[2]
+    if HEADS % grid_devices == 0 and tile_len % 128 == 0:
+        return local_heads(latent, *others)
+    return local_gathered(latent, *others)
+
+
 def solution(mesh):
     return jax.shard_map(
-        local,
+        functools.partial(local, mesh.shape),
         mesh=mesh,
         in_specs=(
             P("dp", "row", "col", None),

time: 4100 us -> 1600 us (0.39)
  waiting for transfers between devices: 1420 us -> 273 us
  matrix products: 1260 us -> 378 us
  blocking collectives: 545 us -> 33.8 us
  Pallas kernels: 0 us -> 380 us
  local copies, waits for them, and re-layouts: 495 us -> 179 us
  other arithmetic: 348 us -> 124 us
  starting transfers between devices: 1.82 us -> 195 us
    reduce_scatter x12 -> x3, waiting for transfers between devices: 944 us -> 2.27 us  [over_tiles(): lax.psum_scatter(weight_grad, TILE, scatter_dimension=0, tiled=True)]
    dot_general x38 -> x11, matrix products: 835 us -> 105 us  [dot_over(): lax.dot_general(left_mat, right_mat, (((left_axis,), (right_axis,)), ((),...]
    pallas_call x0 -> x10, Pallas kernels: none -> 380 us  [the longest x2 178 us: attend_back(): kernel_call(functools.partial(attend_back_body, score_scale), 2560 * head...]
    psum x1 -> x0, blocking collectives: 279 us -> none  [local(): sum_ckey, sum_cvalue = lax.psum((part_ckey, part_cvalue), ('row', 'col'))]
    unnamed x49 -> x14, waiting for transfers between devices: 272 us -> 0.21 us
    all_gather x14 -> x2, blocking collectives: 248 us -> 33.8 us  [the longest x1 17.5 us: tiles_whole(): return lax.all_gather(weight, TILE, axis=0, tiled=True)]
    ppermute x0 -> x88, waiting for transfers between devices: none -> 169 us  [the longest x27 84.9 us: narrow_blocks(): lax.ppermute(sent, 'dp', shift_pairs(devices, step)).astype(F32)]
    ppermute x0 -> x88, starting transfers between devices: none -> 160 us  [the longest x27 68.5 us: narrow_blocks(): lax.ppermute(sent, 'dp', shift_pairs(devices, step)).astype(F32)]
  transfers between devices with their start and end apart: 38 -> 108, of which waited for: 24 -> 28; matrix products, arithmetic and copies ran while one was open for 29% -> 36% of each run, Pallas kernels for 0% -> 23%
where the time goes in v1:
time: 1600 us; the launch traced here: 1580 us
  Pallas kernels  380 us (24%)
  matrix products  378 us (24%)
  waiting for transfers between devices  273 us (17%)
  starting transfers between devices  195 us (12%)
  local copies, waits for them, and re-layouts  179 us (11%)
  other arithmetic  124 us (8%)
  blocking collectives  33.8 us (2%)
  between operations  17.4 us (1%)
    pallas_call x2, Pallas kernels, attend_back(): kernel_call(functools.partial(attend_back_body, score_scale), 2560 * head...  178 us
    dot_general x11, matrix products, dot_over(): lax.dot_general(left_mat, right_mat, (((left_axis,), (right_axis,)), ((),...  105 us
    dot_general x6, matrix products, right_dot(): lax.dot_general(left_mat, right_mat, (((1,), (1,)), ((), ())), preferred_...  94.1 us
    dot_general x9, matrix products, plain_dot(): return jnp.dot(left_mat, right_mat, preferred_element_type=jnp.float32)  91.8 us
    pallas_call x2, Pallas kernels, attend(): kernel_call(attend_body, 1024 * heads * tiles ** 2 * tile_len ** 2, 8 * q...  89.7 us
    all_to_all x8, waiting for transfers between devices, swap_tiles(): lax.all_to_all(values_in, TILE, split_axis=0, concat_axis=0, tiled=True)  87.8 us
    dot_general x9, matrix products, left_dot(): lax.dot_general(left_mat, right_mat, (((0,), (0,)), ((), ())), preferred_...  87.7 us
    ppermute x27, waiting for transfers between devices, narrow_blocks(): lax.ppermute(sent, 'dp', shift_pairs(devices, step)).astype(F32)  84.9 us
  transfers between devices with their start and end apart: 108, of which 28 were waited for; matrix products, arithmetic and copies ran while one was open for 36% of the time, Pallas kernels for 23%

profile of v1, /device:TPU:0, one launch (start us, length us, event | category | flops | bytes accessed | tf_op | source)
XLA Modules:
  0.0 1580.7 jit_solution(14101479573935320033)
XLA Ops:
  14.3 5.7 collective-permute-done.3
  20.0 10.7 collective-permute-done.4
  37.4 5.7 collective-permute-start
  56.8 17.5 %all-gather = bf16[8,176,60]{1,2,0:T(8,128)(2,1)S(1)} all-gather(bf16[1,176,60]{1,2,0:T(8,128)(2,1)S(1)} %maximum_bitcast_fusion), channel_id=1, replica_groups=mesh['dp'=4,'row'=4,'col'=2] {'row','col'}, dimensions={0}, use_global_device_ids=true | all-gather | bytes 190080 | tf_op jit(solution)/shard_map/all_gather | solution.py:1038
  83.2 7.0 add_convert_fusion
  103.5 4.9 collective-permute-done.36
  108.4 6.9 collective-permute-start.29
  120.0 5.8 collective-permute-done.33
  125.8 5.8 collective-permute-done.30
  177.3 14.2 fusion.98
  204.5 12.8 collective-permute-done.41
  217.3 21.5 %collective-permute-done.42 = bf16[176,1536]{1,0:T(8,128)(2,1)S(1)} collective-permute-done((bf16[176,1536]{1,0:T(8,128)(2,1)}, bf16[176,1536]{1,0:T(8,128)(2,1)S(1)}, u32[]{:S(2)}, u32[]{:S(2)}) %collective-permute-start.42) | collective-permute-done | bytes 540704 | tf_op jit(solution)/shard_map/ppermute | solution.py:980
  246.1 15.0 shard_map.314
  266.1 14.8 shard_map.316
  280.8 46.3 %all-to-all-done.query_ref.key_ref.value_ref = bf16[8,3,2,88,512]{4,3,2,1,0:T(8,128)(2,1)} async-done(((bf16[8,3,2,88,512]{4,3,2,1,0:T(8,128)(2,1)}), bf16[8,3,2,88,512]{4,3,2,1,0:T(8,128)(2,1)}, u32[]{:S(2)}, u32[]{:S(2)}) %all-to-all-start) | async-done | bytes 4325408 | tf_op jit(solution)/shard_map/all_to_all | solution.py:970
  332.5 44.8 %shard_map.315 = (bf16[8,2,88,512]{3,2,1,0:T(8,128)(2,1)}, f32[8,2,1,512]{3,2,1,0:T(1,128)}) custom-call(bf16[8,3,2,88,512]{4,3,2,1,0:T(8,128)(2,1)} %all-to-all-done.query_ref.key_ref.value_ref, bf16[8,3,2,88,512]{4,3,2,1,0:T(8,128)(2,1)} %all-to-all-done.query_ref.key_ref.value_ref, bf16[8,3,2,88,512]{4,3,2,1,0:T(8,128)(2,1)} %all-to-all-done.query_ref.key_ref.value_ref, ...), custom_call_target="tpu_custom_call" | custom-call | flops 34359738368 | bytes 17301504 | tf_op jit(solution)/shard_map/pallas_call | solution.py:754
  377.4 20.8 %all-to-all-done.2.query_ref.key_ref.value_ref = bf16[8,3,2,88,512]{4,3,2,1,0:T(8,128)(2,1)} async-done(((bf16[8,3,2,88,512]{4,3,2,1,0:T(8,128)(2,1)}), bf16[8,3,2,88,512]{4,3,2,1,0:T(8,128)(2,1)}, u32[]{:S(2)}, u32[]{:S(2)}) %all-to-all-start.2) | async-done | bytes 4325408 | tf_op jit(solution)/shard_map/all_to_all | solution.py:970
  401.9 44.9 %shard_map.317 = (bf16[8,2,88,512]{3,2,1,0:T(8,128)(2,1)}, f32[8,2,1,512]{3,2,1,0:T(1,128)}) custom-call(bf16[8,3,2,88,512]{4,3,2,1,0:T(8,128)(2,1)} %all-to-all-done.2.query_ref.key_ref.value_ref, bf16[8,3,2,88,512]{4,3,2,1,0:T(8,128)(2,1)} %all-to-all-done.2.query_ref.key_ref.value_ref, ...), custom_call_target="tpu_custom_call" | custom-call | flops 34359738368 | bytes 17301504 | tf_op jit(solution)/shard_map/pallas_call | solution.py:754
  456.5 20.8 %all-to-all-done.3 = bf16[8,2,88,512]{3,2,1,0:T(8,128)(2,1)S(1)} async-done(((bf16[8,2,88,512]{3,2,1,0:T(8,128)(2,1)}), bf16[8,2,88,512]{3,2,1,0:T(8,128)(2,1)S(1)}, u32[]{:S(2)}, u32[]{:S(2)}) %all-to-all-start.3) | async-done | bytes 1441824 | tf_op jit(solution)/shard_map/all_to_all | solution.py:970
  477.3 10.5 fusion.99
  495.8 9.6 fusion.105
  506.1 9.3 fusion.17
  515.5 27.9 %shard_map.318 = (bf16[16,88,1024]{2,1,0:T(8,128)(2,1)}, bf16[16,88,1024]{2,1,0:T(8,128)(2,1)}, f32[16,1,1024]{2,1,0:T(1,128)}, f32[16,1,1024]{2,1,0:T(1,128)}) custom-call(f32[16,88,1024]{2,1,0:T(8,128)} %bitcast.236, f32[2,16,88,768]{3,2,1,0:T(8,128)} %bitcast.217), custom_call_target="tpu_custom_call" | custom-call | flops 6442450944 | bytes 11534336 | tf_op jit(solution)/shard_map/pallas_call | solution.py:892
  543.3 8.5 fusion.100
  555.2 27.6 %fusion.88 = f32[1024,6144]{1,0:T(8,128)} fusion(bf16[1408,6144]{1,0:T(8,128)(2,1)} %all-gather.18.cloned.1.call-done, f32[1024,1408]{1,0:T(8,128)} %copy-done.6, f32[1408]{0:T(1024)S(1)} %copy-done.120, f32[1408]{0:T(1024)S(1)} %copy-done.91, f32[1024]{0:T(1024)S(1)} %add_rsqrt_fusion.2, f32[1024]{0:T(1024)S(1)} %broadcast_multiply_fusion.12), kind=kOutput, calls=%fused_computation.332 | convolution fusion | flops 17723949056 | bytes 48253952 | tf_op jit(solution)/shard_map/dot_general | solution.py:71
  582.8 14.0 all-gather.20.cloned.1.call-done
  596.8 28.8 %fusion.101 = (f32[1024]{0:T(1024)S(1)}, f32[1024,1408]{1,0:T(8,128)S(1)}) fusion(f32[1024,1408]{1,0:T(8,128)} %copy-done.6, bf16[6144,1408]{0,1:T(8,128)(2,1)} %all-gather.20.cloned.1.call-done, f32[1024,6144]{1,0:T(8,128)} %fusion.88), kind=kOutput, calls=%fused_computation.345 | convolution fusion | flops 17776246784 | bytes 54005760 | tf_op jit(solution)/shard_map/dot_general | solution.py:71
  634.2 29.9 %convolution_convert_fusion = bf16[6144,1408]{1,0:T(8,128)(2,1)} fusion(bf16[1024,1408]{1,0:T(8,128)(2,1)S(1)} %get-tuple-element.115, f32[1024,6144]{1,0:T(8,128)} %fusion.88), kind=kOutput, calls=%fused_computation.10 | convolution fusion | flops 17782013952 | bytes 45350912 | tf_op jit(solution)/shard_map/dot_general | solution.py:75
  664.3 40.0 %fusion.6 = bf16[1024,6144]{1,0:T(8,128)(2,1)} fusion(f32[1024,6144]{1,0:T(8,128)} %fusion.88, bf16[1024,1408]{1,0:T(8,128)(2,1)S(1)} %get-tuple-element.115, bf16[6144,1408]{0,1:T(8,128)(2,1)} %all-gather.20.cloned.1.call-done), kind=kOutput, calls=%fused_computation.8 | convolution fusion | flops 17842569216 | bytes 57933824 | tf_op jit(solution)/shard_map/dot_general | solution.py:81
  704.3 26.5 %convolution_convert_fusion.1 = bf16[1408,6144]{1,0:T(8,128)(2,1)} fusion(bf16[1024,6144]{1,0:T(8,128)(2,1)} %fusion.6, f32[1024,1408]{1,0:T(8,128)} %copy-done.6, f32[1408]{0:T(1024)S(1)} %copy-done.121, f32[1408]{0:T(1024)S(1)} %copy-done.92, f32[1024]{0:T(1024)S(1)} %copy-done.107, f32[1024]{0:T(1024)S(1)} %copy-done.86), kind=kOutput, calls=%fused_computation.11 | convolution fusion | flops 17732599808 | bytes 35671040 | tf_op jit(solution)/shard_map/dot_general | solution.py:75
  730.9 31.8 %multiply_reduce_fusion.5 = (f32[1408]{0:T(1024)}, f32[1024]{0:T(1024)S(1)}, f32[1024]{0:T(1024)S(1)}, f32[1408]{0:T(1024)}, f32[1024,1408]{1,0:T(8,128)}) fusion(f32[1024,1408]{1,0:T(8,128)} %copy-done.6, f32[1024]{0:T(1024)S(1)} %copy-done.107, f32[1024]{0:T(1024)S(1)} %copy-done.86, f32[1408]{0:T(1024)S(1)} %copy-done.92, bf16[1024,6144]{1,0:T(8,128)(2,1)} %fusion.6, ...), kind=kOutput, calls=%fused_computation.32 | convolution fusion | flops 17729710080 | bytes 41452032 | tf_op jit(solution)/shard_map/dot_general | solution.py:81
  762.6 7.4 multiply_add_fusion.1
  772.5 8.2 convolution_convert_fusion.7
  783.0 33.9 %shard_map.319 = (bf16[16,88,1024]{2,1,0:T(8,128)(2,1)}, bf16[16,88,768]{2,1,0:T(8,128)(2,1)}, bf16[16,88,768]{2,1,0:T(8,128)(2,1)}) custom-call(bf16[16,88,1024]{2,1,0:T(8,128)(2,1)} %get-tuple-element.117.query_ref, f32[2,16,88,768]{3,2,1,0:T(8,128)} %bitcast.218, bf16[16,88,1024]{2,1,0:T(8,128)(2,1)} %bitcast.241, ...), custom_call_target="tpu_custom_call" | custom-call | flops 16106127360 | bytes 23068672 | tf_op jit(solution)/shard_map/pallas_call | solution.py:950
  825.6 11.8 multiply_reduce_fusion.6
  837.4 5.7 fusion.89
  844.8 6.4 fusion.9
  851.2 6.8 fusion.7
  858.1 6.5 fusion.8
  868.4 21.6 %copy.184 = bf16[1408,5760]{1,0:T(8,128)(2,1)} copy(bf16[1408,5760]{0,1:T(8,128)(2,1)} %constant_dynamic-update-slice_fusion) | data formatting | bytes 32440320
  890.2 6.6 fusion.27
  910.9 6.1 fusion.24
  920.3 22.4 %collective-permute-done.48 = bf16[768,352]{0,1:T(8,128)(2,1)} collective-permute-done((bf16[768,352]{0,1:T(8,128)(2,1)}, bf16[768,352]{0,1:T(8,128)(2,1)}, u32[]{:S(2)}, u32[]{:S(2)}) %collective-permute-start.48) | collective-permute-done | bytes 540704 | tf_op jit(solution)/shard_map/ppermute | solution.py:998
  953.3 89.1 %shard_map.320 = bf16[8,3,2,88,512]{4,3,2,1,0:T(8,128)(2,1)} custom-call(bf16[8,3,2,88,512]{4,3,2,1,0:T(8,128)(2,1)} %all-to-all-done.query_ref.key_ref.value_ref, bf16[8,3,2,88,512]{4,3,2,1,0:T(8,128)(2,1)} %all-to-all-done.query_ref.key_ref.value_ref, bf16[8,3,2,88,512]{4,3,2,1,0:T(8,128)(2,1)} %all-to-all-done.query_ref.key_ref.value_ref, ...), custom_call_target="tpu_custom_call" | custom-call | flops 85899345920 | bytes 17301504 | tf_op jit(solution)/shard_map/pallas_call | solution.py:842
  1047.2 89.1 %shard_map.321 = bf16[8,3,2,88,512]{4,3,2,1,0:T(8,128)(2,1)} custom-call(bf16[8,3,2,88,512]{4,3,2,1,0:T(8,128)(2,1)} %all-to-all-done.2.query_ref.key_ref.value_ref, bf16[8,3,2,88,512]{4,3,2,1,0:T(8,128)(2,1)} %all-to-all-done.2.query_ref.key_ref.value_ref, bf16[8,3,2,88,512]{4,3,2,1,0:T(8,128)(2,1)} %all-to-all-done.2.query_ref.key_ref.value_ref, ...), custom_call_target="tpu_custom_call" | custom-call | flops 85899345920 | bytes 17301504 | tf_op jit(solution)/shard_map/pallas_call | solution.py:842
  1141.2 10.8 collective-permute-start.50
  1154.9 12.3 collective-permute-done.50
  1167.2 22.9 %collective-permute-done.51 = bf16[176,1536]{1,0:T(8,128)(2,1)S(1)} collective-permute-done((bf16[176,1536]{1,0:T(8,128)(2,1)S(1)}, bf16[176,1536]{1,0:T(8,128)(2,1)S(1)}, u32[]{:S(2)}, u32[]{:S(2)}) %collective-permute-start.51) | collective-permute-done | bytes 540704 | tf_op jit(solution)/shard_map/ppermute | solution.py:998
  1191.6 10.1 shard_map.322.others_0_
  1206.0 10.3 shard_map.323
  1216.3 19.8 %convolution_convert_fusion.2 = bf16[1408,4224]{1,0:T(8,128)(2,1)} fusion(bf16[1024,1408]{1,0:T(8,128)(2,1)S(1)} %copy-done.12, bf16[4224,1024]{1,0:T(8,128)(2,1)} %bitcast.196), kind=kOutput, calls=%fused_computation.12 | convolution fusion | flops 12186206208 | bytes 23429120 | tf_op jit(solution)/shard_map/dot_general | solution.py:1046
  1266.0 12.0 collective-permute-start.53
  1289.7 20.8 %fusion.106 = f32[1024,1408]{1,0:T(8,128)} fusion(bf16[4224,1024]{1,0:T(8,128)(2,1)} %bitcast.197, bf16[1408,4224]{1,0:T(8,128)(2,1)} %all-gather.12.cloned.1.call-done.weight_ref), kind=kOutput, calls=%fused_computation.350 | convolution fusion | flops 12180258816 | bytes 26312704 | tf_op jit(solution)/shard_map/dot_general | solution.py:1046
  1337.1 10.9 convolution_convert_fusion.3
  1348.0 15.6 fusion.102
  1363.7 12.0 copy.161
  1379.6 13.1 multiply_reduce_fusion
  1393.0 11.6 subtract_multiply_fusion
  1409.6 16.2 %all-gather.1 = f32[8,176,2]{1,2,0:T(2,128)S(1)} all-gather(f32[1,176,2]{1,2,0:T(2,128)S(1)} %convolution_bitcast_fusion), channel_id=1, replica_groups=mesh['dp'=4,'row'=4,'col'=2] {'row','col'}, dimensions={0}, use_global_device_ids=true | all-gather | bytes 12672 | tf_op jit(solution)/shard_map/all_gather | solution.py:1335
  1459.9 6.4 copy.166
  1485.3 15.7 collective-permute-done.57
  1530.5 8.2 collective-permute-start.66
  1554.9 6.1 slice.173
  1561.0 6.4 copy.163
  (733 shorter events, 410.0 us)
Async XLA Ops:
  7.2 170.1 %all-gather.10.cloned.1.call-start = ((), (), s32[]{:S(2)}) async-start(), calls=%async_computation.13 | async-start | bytes 8921088 | tf_op jit(solution)/shard_map/all_gather | solution.py:1038
  10.3 20.4 %collective-permute-start.4 = (bf16[352,352]{1,0:T(8,128)(2,1)}, bf16[352,352]{1,0:T(8,128)(2,1)S(1)}, u32[]{:S(2)}, u32[]{:S(2)}) collective-permute-start(bf16[352,352]{1,0:T(8,128)(2,1)} %param.26), channel_id=1, source_target_pairs={{0,16},{8,24},{16,0},{24,8},{1,17},{9,25},{17,1},{25,9},{2,18},{10... | collective-permute-start | bytes 743432 | tf_op jit(solution)/shard_map/ppermute | solution.py:980
  12.9 18.6 %collective-permute-start.5 = (bf16[352,352]{1,0:T(8,128)(2,1)}, bf16[352,352]{1,0:T(8,128)(2,1)}, u32[]{:S(2)}, u32[]{:S(2)}) collective-permute-start(bf16[352,352]{1,0:T(8,128)(2,1)} %param.26), channel_id=1, source_target_pairs={{0,24},{8,0},{16,8},{24,16},{1,25},{9,1},{17,9},{25,17},{2,26},{10... | collective-permute-start | bytes 743432 | tf_op jit(solution)/shard_map/ppermute | solution.py:980
  36.0 210.1 %all-gather.12.cloned.1.call-start = ((), (), s32[]{:S(2)}) async-start(), calls=%async_computation.14 | async-start | bytes 13381632 | tf_op jit(solution)/shard_map/all_gather | solution.py:1038
  45.4 44.8 %collective-permute-start.26 = (bf16[176,1056]{1,0:T(8,128)(2,1)}, bf16[176,1056]{1,0:T(8,128)(2,1)}, u32[]{:S(2)}, u32[]{:S(2)}) collective-permute-start(bf16[176,1056]{1,0:T(8,128)(2,1)} %param.29), channel_id=1, source_target_pairs={{0,8},{8,16},{16,24},{24,0},{1,9},{9,17},{17,25},{25,1},{2,10},{10... | collective-permute-start | bytes 1115144 | tf_op jit(solution)/shard_map/ppermute | solution.py:980
  47.3 43.0 %collective-permute-start.27 = (bf16[176,1056]{1,0:T(8,128)(2,1)}, bf16[176,1056]{1,0:T(8,128)(2,1)}, u32[]{:S(2)}, u32[]{:S(2)}) collective-permute-start(bf16[176,1056]{1,0:T(8,128)(2,1)} %param.29), channel_id=1, source_target_pairs={{0,16},{8,24},{16,0},{24,8},{1,17},{9,25},{17,1},{25,9},{2,18},{10... | collective-permute-start | bytes 1115144 | tf_op jit(solution)/shard_map/ppermute | solution.py:980
  53.6 36.7 %collective-permute-start.28 = (bf16[176,1056]{1,0:T(8,128)(2,1)S(1)}, bf16[176,1056]{1,0:T(8,128)(2,1)S(1)}, u32[]{:S(2)}, u32[]{:S(2)}) collective-permute-start(bf16[176,1056]{1,0:T(8,128)(2,1)S(1)} %copy-done.58), channel_id=1, source_target_pairs={{0,24},{8,0},{16,8},{24,16},{1,25},{9,1},{17,9},{25,17},{2,26},{10... | collective-permute-start | bytes 1115144 | tf_op jit(solution)/shard_map/ppermute | solution.py:980
  94.6 362.0 %all-gather.14.cloned.1.call-start = ((), (), s32[]{:S(2)}) async-start(), calls=%async_computation.15 | async-start | bytes 13381632 | tf_op jit(solution)/shard_map/all_gather | solution.py:1038
  97.4 17.9 %collective-permute-start.37 = (bf16[176,352]{1,0:T(8,128)(2,1)S(1)}, bf16[176,352]{1,0:T(8,128)(2,1)S(1)}, u32[]{:S(2)}, u32[]{:S(2)}) collective-permute-start(bf16[176,352]{1,0:T(8,128)(2,1)S(1)} %copy-done.70), channel_id=1, source_target_pairs={{0,24},{8,0},{16,8},{24,16},{1,25},{9,1},{17,9},{25,17},{2,26},{10... | collective-permute-start | bytes 371720 | tf_op jit(solution)/shard_map/ppermute | solution.py:980
  99.3 19.5 %collective-permute-start.32 = (bf16[176,352]{1,0:T(8,128)(2,1)S(1)}, bf16[176,352]{1,0:T(8,128)(2,1)S(1)}, u32[]{:S(2)}, u32[]{:S(2)}) collective-permute-start(bf16[176,352]{1,0:T(8,128)(2,1)S(1)} %copy-done.71), channel_id=1, source_target_pairs={{0,8},{8,16},{16,24},{24,0},{1,9},{9,17},{17,25},{25,1},{2,10},{10... | collective-permute-start | bytes 371720 | tf_op jit(solution)/shard_map/ppermute | solution.py:980
  99.5 26.3 %collective-permute-start.33 = (bf16[176,352]{1,0:T(8,128)(2,1)S(1)}, bf16[176,352]{1,0:T(8,128)(2,1)S(1)}, u32[]{:S(2)}, u32[]{:S(2)}) collective-permute-start(bf16[176,352]{1,0:T(8,128)(2,1)S(1)} %copy-done.71), channel_id=1, source_target_pairs={{0,16},{8,24},{16,0},{24,8},{1,17},{9,25},{17,1},{25,9},{2,18},{10... | collective-permute-start | bytes 371720 | tf_op jit(solution)/shard_map/ppermute | solution.py:980
  103.0 22.7 %collective-permute-start.34 = (bf16[176,352]{1,0:T(8,128)(2,1)S(1)}, bf16[176,352]{1,0:T(8,128)(2,1)S(1)}, u32[]{:S(2)}, u32[]{:S(2)}) collective-permute-start(bf16[176,352]{1,0:T(8,128)(2,1)S(1)} %copy-done.71), channel_id=1, source_target_pairs={{0,24},{8,0},{16,8},{24,16},{1,25},{9,1},{17,9},{25,17},{2,26},{10... | collective-permute-start | bytes 371720 | tf_op jit(solution)/shard_map/ppermute | solution.py:980
  108.4 17.4 %collective-permute-start.29 = (bf16[176,352]{1,0:T(8,128)(2,1)S(1)}, bf16[176,352]{1,0:T(8,128)(2,1)S(1)}, u32[]{:S(2)}, u32[]{:S(2)}) collective-permute-start(bf16[176,352]{1,0:T(8,128)(2,1)S(1)} %copy-done.72), channel_id=1, source_target_pairs={{0,8},{8,16},{16,24},{24,0},{1,9},{9,17},{17,25},{25,1},{2,10},{10... | collective-permute-start | bytes 371720 | tf_op jit(solution)/shard_map/ppermute | solution.py:980
  135.7 360.1 %all-gather.16.cloned.1.call-start = ((), (), s32[]{:S(2)}) async-start(), calls=%async_computation.16 | async-start | bytes 6488064 | tf_op jit(solution)/shard_map/all_gather | solution.py:1038
  171.7 22.3 %collective-permute-start.38 = (bf16[128,704]{1,0:T(8,128)(2,1)}, bf16[128,704]{1,0:T(8,128)(2,1)S(1)}, u32[]{:S(2)}, u32[]{:S(2)}) collective-permute-start(bf16[128,704]{1,0:T(8,128)(2,1)} %copy.132), channel_id=1, source_target_pairs={{0,8},{8,16},{16,24},{24,0},{1,9},{9,17},{17,25},{25,1},{2,10},{10... | collective-permute-start | bytes 540680 | tf_op jit(solution)/shard_map/ppermute | solution.py:980
  174.8 19.2 %collective-permute-start.39 = (bf16[128,704]{1,0:T(8,128)(2,1)}, bf16[128,704]{1,0:T(8,128)(2,1)S(1)}, u32[]{:S(2)}, u32[]{:S(2)}) collective-permute-start(bf16[128,704]{1,0:T(8,128)(2,1)} %copy.132), channel_id=1, source_target_pairs={{0,16},{8,24},{16,0},{24,8},{1,17},{9,25},{17,1},{25,9},{2,18},{10... | collective-permute-start | bytes 540680 | tf_op jit(solution)/shard_map/ppermute | solution.py:980
  176.1 18.6 %collective-permute-start.40 = (bf16[128,704]{1,0:T(8,128)(2,1)}, bf16[128,704]{1,0:T(8,128)(2,1)}, u32[]{:S(2)}, u32[]{:S(2)}) collective-permute-start(bf16[128,704]{1,0:T(8,128)(2,1)} %copy.132), channel_id=1, source_target_pairs={{0,24},{8,0},{16,8},{24,16},{1,25},{9,1},{17,9},{25,17},{2,26},{10... | collective-permute-start | bytes 540680 | tf_op jit(solution)/shard_map/ppermute | solution.py:980
  199.9 355.2 %all-gather.18.cloned.1.call-start = ((), (), s32[]{:S(2)}) async-start(), calls=%async_computation.17 | async-start | bytes 19464192 | tf_op jit(solution)/shard_map/all_gather | solution.py:1038
  200.0 17.4 %collective-permute-start.41 = (bf16[176,1536]{1,0:T(8,128)(2,1)}, bf16[176,1536]{1,0:T(8,128)(2,1)S(1)}, u32[]{:S(2)}, u32[]{:S(2)}) collective-permute-start(bf16[176,1536]{1,0:T(8,128)(2,1)} %param.34), channel_id=1, source_target_pairs={{0,8},{8,16},{16,24},{24,0},{1,9},{9,17},{17,25},{25,1},{2,10},{10... | collective-permute-start | bytes 1622024 | tf_op jit(solution)/shard_map/ppermute | solution.py:980
  201.1 37.8 %collective-permute-start.42 = (bf16[176,1536]{1,0:T(8,128)(2,1)}, bf16[176,1536]{1,0:T(8,128)(2,1)S(1)}, u32[]{:S(2)}, u32[]{:S(2)}) collective-permute-start(bf16[176,1536]{1,0:T(8,128)(2,1)} %param.34), channel_id=1, source_target_pairs={{0,16},{8,24},{16,0},{24,8},{1,17},{9,25},{17,1},{25,9},{2,18},{10... | collective-permute-start | bytes 1622024 | tf_op jit(solution)/shard_map/ppermute | solution.py:980
  202.9 35.9 %collective-permute-start.43 = (bf16[176,1536]{1,0:T(8,128)(2,1)}, bf16[176,1536]{1,0:T(8,128)(2,1)S(1)}, u32[]{:S(2)}, u32[]{:S(2)}) collective-permute-start(bf16[176,1536]{1,0:T(8,128)(2,1)} %param.34), channel_id=1, source_target_pairs={{0,24},{8,0},{16,8},{24,16},{1,25},{9,1},{17,9},{25,17},{2,26},{10... | collective-permute-start | bytes 1622024 | tf_op jit(solution)/shard_map/ppermute | solution.py:980
  261.2 65.9 %all-to-all-start = ((bf16[8,3,2,88,512]{4,3,2,1,0:T(8,128)(2,1)}), bf16[8,3,2,88,512]{4,3,2,1,0:T(8,128)(2,1)}, u32[]{:S(2)}, u32[]{:S(2)}) async-start(bf16[8,3,2,88,512]{4,3,2,1,0:T(8,128)(2,1)} %get-tuple-element.86.own_ref), calls=%async_computation | async-start | bytes 8650752 | tf_op jit(solution)/shard_map/all_to_all | solution.py:970
  327.1 71.0 %all-to-all-start.2 = ((bf16[8,3,2,88,512]{4,3,2,1,0:T(8,128)(2,1)}), bf16[8,3,2,88,512]{4,3,2,1,0:T(8,128)(2,1)}, u32[]{:S(2)}, u32[]{:S(2)}) async-start(bf16[8,3,2,88,512]{4,3,2,1,0:T(8,128)(2,1)} %get-tuple-element.88.own_ref), calls=%async_computation.2 | async-start | bytes 8650752 | tf_op jit(solution)/shard_map/all_to_all | solution.py:970
  398.1 48.7 %all-to-all-start.1 = ((bf16[8,2,88,512]{3,2,1,0:T(8,128)(2,1)}), bf16[8,2,88,512]{3,2,1,0:T(8,128)(2,1)S(1)}, u32[]{:S(2)}, u32[]{:S(2)}) async-start(bf16[8,2,88,512]{3,2,1,0:T(8,128)(2,1)} %get-tuple-element.87.att_ref), calls=%async_computation.1 | async-start | bytes 2883584 | tf_op jit(solution)/shard_map/all_to_all | solution.py:970
  446.9 30.4 %all-to-all-start.3 = ((bf16[8,2,88,512]{3,2,1,0:T(8,128)(2,1)}), bf16[8,2,88,512]{3,2,1,0:T(8,128)(2,1)S(1)}, u32[]{:S(2)}, u32[]{:S(2)}) async-start(bf16[8,2,88,512]{3,2,1,0:T(8,128)(2,1)} %get-tuple-element.89.att_ref), calls=%async_computation.3 | async-start | bytes 2883584 | tf_op jit(solution)/shard_map/all_to_all | solution.py:970
  451.0 145.8 %all-gather.20.cloned.1.call-start = ((), (), s32[]{:S(2)}) async-start(), calls=%async_computation.18 | async-start | bytes 19464192 | tf_op jit(solution)/shard_map/all_gather | solution.py:1038
  451.1 36.8 %collective-permute-start.44 = (bf16[768,352]{0,1:T(8,128)(2,1)S(1)}, bf16[768,352]{0,1:T(8,128)(2,1)}, u32[]{:S(2)}, u32[]{:S(2)}) collective-permute-start(bf16[768,352]{0,1:T(8,128)(2,1)S(1)} %copy-done.55), channel_id=1, source_target_pairs={{0,8},{8,16},{16,24},{24,0},{1,9},{9,17},{17,25},{25,1},{2,10},{10... | collective-permute-start | bytes 1622024 | tf_op jit(solution)/shard_map/ppermute | solution.py:980
  452.7 38.3 %collective-permute-start.45 = (bf16[768,352]{0,1:T(8,128)(2,1)S(1)}, bf16[768,352]{0,1:T(8,128)(2,1)}, u32[]{:S(2)}, u32[]{:S(2)}) collective-permute-start(bf16[768,352]{0,1:T(8,128)(2,1)S(1)} %copy-done.55), channel_id=1, source_target_pairs={{0,16},{8,24},{16,0},{24,8},{1,17},{9,25},{17,1},{25,9},{2,18},{10... | collective-permute-start | bytes 1622024 | tf_op jit(solution)/shard_map/ppermute | solution.py:980
  455.1 35.9 %collective-permute-start.46 = (bf16[768,352]{0,1:T(8,128)(2,1)S(1)}, bf16[768,352]{0,1:T(8,128)(2,1)}, u32[]{:S(2)}, u32[]{:S(2)}) collective-permute-start(bf16[768,352]{0,1:T(8,128)(2,1)S(1)} %copy-done.55), channel_id=1, source_target_pairs={{0,24},{8,0},{16,8},{24,16},{1,25},{9,1},{17,9},{25,17},{2,26},{10... | collective-permute-start | bytes 1622024 | tf_op jit(solution)/shard_map/ppermute | solution.py:980
  494.1 288.9 %reduce-scatter.10.cloned.1.call-start = ((), (), s32[]{:S(2)}) async-start(), calls=%async_computation.19 | async-start | bytes 19464192 | tf_op jit(solution)/shard_map/reduce_scatter | solution.py:1033
  664.2 246.6 %reduce-scatter.12.cloned.1.call-start = ((), (), s32[]{:S(2)}) async-start(), calls=%async_computation.20 | async-start | bytes 19464192 | tf_op jit(solution)/shard_map/reduce_scatter | solution.py:1033
  730.8 470.9 %reduce-scatter.16.cloned.1.call-start = ((), (), s32[]{:S(2)}) async-start(), calls=%async_computation.23 | async-start | bytes 18247680
  896.7 52.7 %all-to-all-start.5 = ((bf16[8,2,88,512]{3,2,1,0:T(8,128)(2,1)}), bf16[8,2,88,512]{3,2,1,0:T(8,128)(2,1)}, u32[]{:S(2)}, u32[]{:S(2)}) async-start(bf16[8,2,88,512]{3,2,1,0:T(8,128)(2,1)} %bitcast.227), calls=%async_computation.7 | async-start | bytes 2883584 | tf_op jit(solution)/shard_map/all_to_all | solution.py:970
  905.0 37.8 %collective-permute-start.48 = (bf16[768,352]{0,1:T(8,128)(2,1)}, bf16[768,352]{0,1:T(8,128)(2,1)}, u32[]{:S(2)}, u32[]{:S(2)}) collective-permute-start(bf16[768,352]{0,1:T(8,128)(2,1)} %copy.144), channel_id=1, source_target_pairs={{0,16},{8,24},{16,0},{24,8},{1,17},{9,25},{17,1},{25,9},{2,18},{10... | collective-permute-start | bytes 1622024 | tf_op jit(solution)/shard_map/ppermute | solution.py:998
  909.0 35.1 %collective-permute-start.49 = (bf16[768,352]{0,1:T(8,128)(2,1)}, bf16[768,352]{0,1:T(8,128)(2,1)}, u32[]{:S(2)}, u32[]{:S(2)}) collective-permute-start(bf16[768,352]{0,1:T(8,128)(2,1)} %copy.146), channel_id=1, source_target_pairs={{0,24},{8,0},{16,8},{24,16},{1,25},{9,1},{17,9},{25,17},{2,26},{10... | collective-permute-start | bytes 1622024 | tf_op jit(solution)/shard_map/ppermute | solution.py:998
  949.5 93.0 %all-to-all-start.4 = ((bf16[8,2,88,512]{3,2,1,0:T(8,128)(2,1)}), bf16[8,2,88,512]{3,2,1,0:T(8,128)(2,1)S(1)}, u32[]{:S(2)}, u32[]{:S(2)}) async-start(bf16[8,2,88,512]{3,2,1,0:T(8,128)(2,1)} %bitcast.228), calls=%async_computation.6 | async-start | bytes 2883584 | tf_op jit(solution)/shard_map/all_to_all | solution.py:970
  1042.5 93.9 %all-to-all-start.7 = ((bf16[8,3,2,88,512]{4,3,2,1,0:T(8,128)(2,1)}), bf16[8,3,2,88,512]{4,3,2,1,0:T(8,128)(2,1)}, u32[]{:S(2)}, u32[]{:S(2)}) async-start(bf16[8,3,2,88,512]{4,3,2,1,0:T(8,128)(2,1)} %shard_map.320), calls=%async_computation.9 | async-start | bytes 8650752 | tf_op jit(solution)/shard_map/all_to_all | solution.py:970
  1136.3 69.7 %all-to-all-start.6 = ((bf16[8,3,2,88,512]{4,3,2,1,0:T(8,128)(2,1)}), bf16[8,3,2,88,512]{4,3,2,1,0:T(8,128)(2,1)}, u32[]{:S(2)}, u32[]{:S(2)}) async-start(bf16[8,3,2,88,512]{4,3,2,1,0:T(8,128)(2,1)} %shard_map.321), calls=%async_computation.8 | async-start | bytes 8650752 | tf_op jit(solution)/shard_map/all_to_all | solution.py:970
  1141.0 234.7 %reduce-scatter.18.cloned.1.call-start = ((), (), s32[]{:S(2)}) async-start(), calls=%async_computation.24 | async-start | bytes 13381632
  1141.2 26.0 %collective-permute-start.50 = (bf16[176,1536]{1,0:T(8,128)(2,1)S(1)}, bf16[176,1536]{1,0:T(8,128)(2,1)S(1)}, u32[]{:S(2)}, u32[]{:S(2)}) collective-permute-start(bf16[176,1536]{1,0:T(8,128)(2,1)S(1)} %get-tuple-element.271), channel_id=1, source_target_pairs={{0,8},{8,16},{16,24},{24,0},{1,9},{9,17},{17,25},{25,1},{2,10},{10... | collective-permute-start | bytes 1622024 | tf_op jit(solution)/shard_map/ppermute | solution.py:998
  1152.1 38.0 %collective-permute-start.51 = (bf16[176,1536]{1,0:T(8,128)(2,1)S(1)}, bf16[176,1536]{1,0:T(8,128)(2,1)S(1)}, u32[]{:S(2)}, u32[]{:S(2)}) collective-permute-start(bf16[176,1536]{1,0:T(8,128)(2,1)S(1)} %get-tuple-element.272), channel_id=1, source_target_pairs={{0,16},{8,24},{16,0},{24,8},{1,17},{9,25},{17,1},{25,9},{2,18},{10... | collective-permute-start | bytes 1622024 | tf_op jit(solution)/shard_map/ppermute | solution.py:998
  1154.7 35.5 %collective-permute-start.52 = (bf16[176,1536]{1,0:T(8,128)(2,1)S(1)}, bf16[176,1536]{1,0:T(8,128)(2,1)S(1)}, u32[]{:S(2)}, u32[]{:S(2)}) collective-permute-start(bf16[176,1536]{1,0:T(8,128)(2,1)S(1)} %select_select_fusion.9), channel_id=1, source_target_pairs={{0,24},{8,0},{16,8},{24,16},{1,25},{9,1},{17,9},{25,17},{2,26},{10... | collective-permute-start | bytes 1622024 | tf_op jit(solution)/shard_map/ppermute | solution.py:998
  1236.2 209.1 %all-gather.22.cloned.1.call-start = ((), (), s32[]{:S(2)}) async-start(), calls=%async_computation.21 | async-start | bytes 4866048 | tf_op jit(solution)/shard_map/all_gather | solution.py:1038
  1266.0 44.5 %collective-permute-start.53 = (bf16[176,1056]{1,0:T(8,128)(2,1)}, bf16[176,1056]{1,0:T(8,128)(2,1)}, u32[]{:S(2)}, u32[]{:S(2)}) collective-permute-start(bf16[176,1056]{1,0:T(8,128)(2,1)} %copy.149), channel_id=1, source_target_pairs={{0,8},{8,16},{16,24},{24,0},{1,9},{9,17},{17,25},{25,1},{2,10},{10... | collective-permute-start | bytes 1115144 | tf_op jit(solution)/shard_map/ppermute | solution.py:998
  1280.8 31.7 %collective-permute-start.54 = (bf16[176,1056]{1,0:T(8,128)(2,1)}, bf16[176,1056]{1,0:T(8,128)(2,1)}, u32[]{:S(2)}, u32[]{:S(2)}) collective-permute-start(bf16[176,1056]{1,0:T(8,128)(2,1)} %copy.151), channel_id=1, source_target_pairs={{0,16},{8,24},{16,0},{24,8},{1,17},{9,25},{17,1},{25,9},{2,18},{10... | collective-permute-start | bytes 1115144 | tf_op jit(solution)/shard_map/ppermute | solution.py:998
  1283.6 31.0 %collective-permute-start.55 = (bf16[176,1056]{1,0:T(8,128)(2,1)}, bf16[176,1056]{1,0:T(8,128)(2,1)}, u32[]{:S(2)}, u32[]{:S(2)}) collective-permute-start(bf16[176,1056]{1,0:T(8,128)(2,1)} %copy.153), channel_id=1, source_target_pairs={{0,24},{8,0},{16,8},{24,16},{1,25},{9,1},{17,9},{25,17},{2,26},{10... | collective-permute-start | bytes 1115144 | tf_op jit(solution)/shard_map/ppermute | solution.py:998
  1289.7 253.1 %reduce-scatter.14.cloned.1.call-start = ((), (), s32[]{:S(2)}) async-start(), calls=%async_computation.22 | async-start | bytes 8921088 | tf_op jit(solution)/shard_map/reduce_scatter | solution.py:1033
  1323.6 81.0 %collective-permute-start.72 = (f32[2,1408]{1,0:T(2,128)S(1)}, f32[2,1408]{1,0:T(2,128)S(1)}, u32[]{:S(2)}, u32[]{:S(2)}) collective-permute-start(f32[2,1408]{1,0:T(2,128)S(1)} %bitcast_reduce_fusion), channel_id=1, source_target_pairs={{0,1},{1,2},{2,3},{3,4},{4,5},{5,6},{6,7},{7,0},{8,9},{9,10},{10,1... | collective-permute-start | bytes 33800 | tf_op jit(solution)/shard_map/ppermute | solution.py:1027
  1325.3 80.1 %collective-permute-start.73 = (f32[2,1408]{1,0:T(2,128)S(1)}, f32[2,1408]{1,0:T(2,128)S(1)}, u32[]{:S(2)}, u32[]{:S(2)}) collective-permute-start(f32[2,1408]{1,0:T(2,128)S(1)} %bitcast_reduce_fusion), channel_id=1, source_target_pairs={{0,2},{1,3},{2,4},{3,5},{4,6},{5,7},{6,0},{7,1},{8,10},{9,11},{10,... | collective-permute-start | bytes 33800 | tf_op jit(solution)/shard_map/ppermute | solution.py:1027
  1325.3 83.3 %collective-permute-start.74 = (f32[2,1408]{1,0:T(2,128)S(1)}, f32[2,1408]{1,0:T(2,128)S(1)}, u32[]{:S(2)}, u32[]{:S(2)}) collective-permute-start(f32[2,1408]{1,0:T(2,128)S(1)} %bitcast_reduce_fusion), channel_id=1, source_target_pairs={{0,3},{1,4},{2,5},{3,6},{4,7},{5,0},{6,1},{7,2},{8,11},{9,12},{10,... | collective-permute-start | bytes 33800 | tf_op jit(solution)/shard_map/ppermute | solution.py:1027
  1327.0 81.6 %collective-permute-start.75 = (f32[2,1408]{1,0:T(2,128)S(1)}, f32[2,1408]{1,0:T(2,128)S(1)}, u32[]{:S(2)}, u32[]{:S(2)}) collective-permute-start(f32[2,1408]{1,0:T(2,128)S(1)} %bitcast_reduce_fusion), channel_id=1, source_target_pairs={{0,4},{1,5},{2,6},{3,7},{4,0},{5,1},{6,2},{7,3},{8,12},{9,13},{10,... | collective-permute-start | bytes 33800 | tf_op jit(solution)/shard_map/ppermute | solution.py:1027
  1327.3 81.4 %collective-permute-start.76 = (f32[2,1408]{1,0:T(2,128)S(1)}, f32[2,1408]{1,0:T(2,128)S(1)}, u32[]{:S(2)}, u32[]{:S(2)}) collective-permute-start(f32[2,1408]{1,0:T(2,128)S(1)} %bitcast_reduce_fusion), channel_id=1, source_target_pairs={{0,5},{1,6},{2,7},{3,0},{4,1},{5,2},{6,3},{7,4},{8,13},{9,14},{10,... | collective-permute-start | bytes 33800 | tf_op jit(solution)/shard_map/ppermute | solution.py:1027
  1453.4 21.8 %collective-permute-start.85 = (bf16[128,704]{1,0:T(8,128)(2,1)}, bf16[128,704]{1,0:T(8,128)(2,1)}, u32[]{:S(2)}, u32[]{:S(2)}) collective-permute-start(bf16[128,704]{1,0:T(8,128)(2,1)} %get-tuple-element.300), channel_id=1, source_target_pairs={{0,8},{8,16},{16,24},{24,0},{1,9},{9,17},{17,25},{25,1},{2,10},{10... | collective-permute-start | bytes 540680 | tf_op jit(solution)/shard_map/ppermute | solution.py:998
  1456.7 24.0 %collective-permute-start.86 = (bf16[128,704]{1,0:T(8,128)(2,1)}, bf16[128,704]{1,0:T(8,128)(2,1)}, u32[]{:S(2)}, u32[]{:S(2)}) collective-permute-start(bf16[128,704]{1,0:T(8,128)(2,1)} %get-tuple-element.301), channel_id=1, source_target_pairs={{0,16},{8,24},{16,0},{24,8},{1,17},{9,25},{17,1},{25,9},{2,18},{10... | collective-permute-start | bytes 540680 | tf_op jit(solution)/shard_map/ppermute | solution.py:998
  1458.4 22.3 %collective-permute-start.87 = (bf16[128,704]{1,0:T(8,128)(2,1)}, bf16[128,704]{1,0:T(8,128)(2,1)}, u32[]{:S(2)}, u32[]{:S(2)}) collective-permute-start(bf16[128,704]{1,0:T(8,128)(2,1)} %select_select_fusion.31), channel_id=1, source_target_pairs={{0,24},{8,0},{16,8},{24,16},{1,25},{9,1},{17,9},{25,17},{2,26},{10... | collective-permute-start | bytes 540680 | tf_op jit(solution)/shard_map/ppermute | solution.py:998
  1472.1 28.9 %collective-permute-start.57 = (bf16[176,1056]{1,0:T(8,128)(2,1)}, bf16[176,1056]{1,0:T(8,128)(2,1)}, u32[]{:S(2)}, u32[]{:S(2)}) collective-permute-start(bf16[176,1056]{1,0:T(8,128)(2,1)} %copy.157), channel_id=1, source_target_pairs={{0,16},{8,24},{16,0},{24,8},{1,17},{9,25},{17,1},{25,9},{2,18},{10... | collective-permute-start | bytes 1115144 | tf_op jit(solution)/shard_map/ppermute | solution.py:998
  1475.1 27.1 %collective-permute-start.58 = (bf16[176,1056]{1,0:T(8,128)(2,1)}, bf16[176,1056]{1,0:T(8,128)(2,1)}, u32[]{:S(2)}, u32[]{:S(2)}) collective-permute-start(bf16[176,1056]{1,0:T(8,128)(2,1)} %copy.159), channel_id=1, source_target_pairs={{0,24},{8,0},{16,8},{24,16},{1,25},{9,1},{17,9},{25,17},{2,26},{10... | collective-permute-start | bytes 1115144 | tf_op jit(solution)/shard_map/ppermute | solution.py:998
  1512.4 17.5 %collective-permute-start.61 = (f32[176,60]{0,1:T(8,128)S(1)}, f32[176,60]{0,1:T(8,128)S(1)}, u32[]{:S(2)}, u32[]{:S(2)}) collective-permute-start(f32[176,60]{0,1:T(8,128)S(1)} %select_n.2918), channel_id=1, source_target_pairs={{0,3},{1,4},{2,5},{3,6},{4,7},{5,0},{6,1},{7,2},{8,11},{9,12},{10,... | collective-permute-start | bytes 126728 | tf_op jit(solution)/shard_map/ppermute | solution.py:1019
  1530.5 18.9 %collective-permute-start.66 = (f32[176,15]{0,1:T(8,128)}, f32[176,15]{0,1:T(8,128)}, u32[]{:S(2)}, u32[]{:S(2)}) collective-permute-start(f32[176,15]{0,1:T(8,128)} %get-tuple-element.330), channel_id=1, source_target_pairs={{0,8},{8,16},{16,24},{24,0},{1,9},{9,17},{17,25},{25,1},{2,10},{10... | collective-permute-start | bytes 31688 | tf_op jit(solution)/shard_map/ppermute | solution.py:998
  1538.7 29.9 %collective-permute-start.67 = (f32[176,15]{0,1:T(8,128)S(1)}, f32[176,15]{0,1:T(8,128)}, u32[]{:S(2)}, u32[]{:S(2)}) collective-permute-start(f32[176,15]{0,1:T(8,128)S(1)} %get-tuple-element.331), channel_id=1, source_target_pairs={{0,16},{8,24},{16,0},{24,8},{1,17},{9,25},{17,1},{25,9},{2,18},{10... | collective-permute-start | bytes 31688 | tf_op jit(solution)/shard_map/ppermute | solution.py:998
  1542.7 25.9 %collective-permute-start.68 = (f32[176,15]{0,1:T(8,128)}, f32[176,15]{0,1:T(8,128)}, u32[]{:S(2)}, u32[]{:S(2)}) collective-permute-start(f32[176,15]{0,1:T(8,128)} %select_select_fusion.72), channel_id=1, source_target_pairs={{0,24},{8,0},{16,8},{24,16},{1,25},{9,1},{17,9},{25,17},{2,26},{10... | collective-permute-start | bytes 31688 | tf_op jit(solution)/shard_map/ppermute | solution.py:998
  1547.4 23.8 %collective-permute-start.69 = (bf16[352,352]{1,0:T(8,128)(2,1)}, bf16[352,352]{1,0:T(8,128)(2,1)S(1)}, u32[]{:S(2)}, u32[]{:S(2)}) collective-permute-start(bf16[352,352]{1,0:T(8,128)(2,1)} %get-tuple-element.294), channel_id=1, source_target_pairs={{0,8},{8,16},{16,24},{24,0},{1,9},{9,17},{17,25},{25,1},{2,10},{10... | collective-permute-start | bytes 743432 | tf_op jit(solution)/shard_map/ppermute | solution.py:998
  1549.4 21.8 %collective-permute-start.70 = (bf16[352,352]{1,0:T(8,128)(2,1)}, bf16[352,352]{1,0:T(8,128)(2,1)S(1)}, u32[]{:S(2)}, u32[]{:S(2)}) collective-permute-start(bf16[352,352]{1,0:T(8,128)(2,1)} %get-tuple-element.295), channel_id=1, source_target_pairs={{0,16},{8,24},{16,0},{24,8},{1,17},{9,25},{17,1},{25,9},{2,18},{10... | collective-permute-start | bytes 743432 | tf_op jit(solution)/shard_map/ppermute | solution.py:998
  1549.4 21.8 %collective-permute-start.71 = (bf16[352,352]{1,0:T(8,128)(2,1)}, bf16[352,352]{1,0:T(8,128)(2,1)}, u32[]{:S(2)}, u32[]{:S(2)}) collective-permute-start(bf16[352,352]{1,0:T(8,128)(2,1)} %select_select_fusion.24), channel_id=1, source_target_pairs={{0,24},{8,0},{16,8},{24,16},{1,25},{9,1},{17,9},{25,17},{2,26},{10... | collective-permute-start | bytes 743432 | tf_op jit(solution)/shard_map/ppermute | solution.py:998
  (187 other events, 3375.8 us)
Sparse Core Ops, SparseCore 0:
  36.1 58.0 all-gather.9
  96.2 69.9 all-gather.11
  168.1 69.2 all-gather.13
  239.1 66.5 all-gather.15
  307.4 172.2 all-gather.17
  494.3 102.4 all-gather.19
  664.3 118.6 reduce-scatter.9
  787.1 118.5 reduce-scatter.11
  909.4 134.0 reduce-scatter.15
  1236.3 100.2 reduce-scatter.17
  1339.1 37.2 all-gather.21
  1379.8 69.3 reduce-scatter.13

commit v2 on v1

--- a/solution.py
+++ b/solution.py
@@ -5,6 +5,7 @@
 import jax.numpy as jnp
 from jax import lax
 from jax.experimental import pallas as pl
+from jax.experimental.layout import Layout, with_layout_constraint
 from jax.experimental.pallas import tpu as pltpu
 from jax.sharding import PartitionSpec as P
 
@@ -735,15 +736,17 @@
             ).astype(BF16)
 
     query = query_ref[0, 0, 0]
-
-    def step(tile, total):
-        rows = pl.ds(pl.multiple_of(tile * tile_len, tile_len), tile_len)
-        scores = jnp.dot(key_nat[rows, :], query, preferred_element_type=F32)
-        weight = jnp.exp2(scores).astype(BF16)
-        return total + jnp.dot(value_ext[tile], weight, preferred_element_type=F32)
-
-    start = jnp.zeros((head_dim + 8, tile_len), F32)
-    total = lax.fori_loop(0, tiles, step, start, unroll=8)
+    total = jnp.zeros((head_dim + 8, tile_len), F32)
+    held = None
+    for tile in range(tiles + 1):
+        scores = None
+        if tile < tiles:
+            rows = slice(tile * tile_len, (tile + 1) * tile_len)
+            scores = jnp.dot(key_nat[rows, :], query, preferred_element_type=F32)
+        if held is not None:
+            weight = jnp.exp2(held).astype(BF16)
+            total = total + jnp.dot(value_ext[tile - 1], weight, preferred_element_type=F32)
+        held = scores
     weight_sum = total[head_dim : head_dim + 1]
     out_ref[0, 0] = (total[:head_dim] / weight_sum).astype(BF16)
     lse_ref[0, 0] = jnp.log2(weight_sum)
@@ -867,34 +870,36 @@
 
 def cross_body(text_len, query_scale, pre_ref, kv_ref, att_ref, query_ref, inv_ref, lse_ref):
     head_dim, text_pad = kv_ref.shape[2], kv_ref.shape[3]
-    normed, inverse = column_norm(pre_ref[0])
-    query = (normed * query_scale).astype(BF16)
-    query_ref[0] = query
-    inv_ref[0] = inverse
-    key = column_norm(kv_ref[0, 0])[0].astype(BF16)
     at = lax.broadcasted_iota(jnp.int32, (8, text_pad), 0)
     text_at = lax.broadcasted_iota(jnp.int32, (8, text_pad), 1)
     flags = ((at == 0) & (text_at < text_len)).astype(F32)
-    value_ext = jnp.concatenate([kv_ref[1, 0], flags], axis=0).astype(BF16)
-    scores = jnp.dot(key.T, query, preferred_element_type=F32)
-    weight = jnp.exp2(scores).astype(BF16)
-    total = jnp.dot(value_ext, weight, preferred_element_type=F32)
-    weight_sum = total[head_dim : head_dim + 1]
-    att_ref[0] = (total[:head_dim] / weight_sum).astype(BF16)
-    lse_ref[0] = jnp.log2(weight_sum)
+    for head in range(pre_ref.shape[0]):
+        normed, inverse = column_norm(pre_ref[head])
+        query = (normed * query_scale).astype(BF16)
+        query_ref[head] = query
+        inv_ref[head] = inverse
+        key = column_norm(kv_ref[0, head])[0].astype(BF16)
+        value_ext = jnp.concatenate([kv_ref[1, head], flags], axis=0).astype(BF16)
+        scores = jnp.dot(key.T, query, preferred_element_type=F32)
+        weight = jnp.exp2(scores).astype(BF16)
+        total = jnp.dot(value_ext, weight, preferred_element_type=F32)
+        weight_sum = total[head_dim : head_dim + 1]
+        att_ref[head] = (total[:head_dim] / weight_sum).astype(BF16)
+        lse_ref[head] = jnp.log2(weight_sum)
 
 
 def cross_attend(pre, text_kv, images, text_len, query_scale):
     heads, head_dim, tokens = pre.shape
     tile_len, text_pad = tokens // images, text_kv.shape[3] // images
-    wide = pl.BlockSpec((1, head_dim, tile_len), lambda i, h: (h, 0, i))
-    row = pl.BlockSpec((1, 1, tile_len), lambda i, h: (h, 0, i))
+    block = math.gcd(heads, 4)
+    wide = pl.BlockSpec((block, head_dim, tile_len), lambda i, h: (h, 0, i))
+    row = pl.BlockSpec((block, 1, tile_len), lambda i, h: (h, 0, i))
     return kernel_call(
         functools.partial(cross_body, text_len, query_scale),
         1024 * heads * tokens * text_pad,
         8 * pre.size,
-        grid=(images, heads),
-        in_specs=[wide, pl.BlockSpec((2, 1, head_dim, text_pad), lambda i, h: (0, h, 0, i))],
+        grid=(images, heads // block),
+        in_specs=[wide, pl.BlockSpec((2, block, head_dim, text_pad), lambda i, h: (0, h, 0, i))],
         out_specs=[wide, wide, row, row],
         out_shape=[
             jax.ShapeDtypeStruct(pre.shape, BF16),
@@ -919,39 +924,41 @@
     value_ref,
 ):
     head_dim, text_pad = kv_ref.shape[2], kv_ref.shape[3]
-    query = query_ref[0].astype(F32)
-    grad = grad_ref[0].astype(F32)
-    delta = jnp.sum(grad * att_ref[0].astype(F32), axis=0, keepdims=True)
-    query_ext = jnp.concatenate([query, minus_pieces(lse_ref[0])], axis=0).astype(BF16)
-    grad_ext = jnp.concatenate([grad, minus_pieces(delta)], axis=0).astype(BF16)
     ones = piece_flags(text_pad)
-    key = column_norm(kv_ref[0, 0])[0].astype(BF16)
-    key_ext = jnp.concatenate([key.astype(F32), ones], axis=0).T.astype(BF16)
-    value_ext = jnp.concatenate([kv_ref[1, 0], ones], axis=0).T.astype(BF16)
-    probs = jnp.exp2(jnp.dot(key_ext, query_ext, preferred_element_type=F32))
-    grad_probs = jnp.dot(value_ext, grad_ext, preferred_element_type=F32)
-    grad_scores = (probs * grad_probs).astype(BF16)
-    value_grad = right_dot(grad_ext, probs.astype(BF16))[:head_dim]
-    key_grad = right_dot(query_ext, grad_scores)[:head_dim]
-    key_ref[0] = (key_grad * (1.0 / LOG2E)).astype(BF16)
-    value_ref[0] = value_grad.astype(BF16)
-    query_grad = jnp.dot(key, grad_scores, preferred_element_type=F32) * score_scale
-    normed = query * (1.0 / query_scale)
-    out_ref[0] = column_norm_back(query_grad, normed, inv_ref[0]).astype(BF16)
+    for head in range(query_ref.shape[0]):
+        query = query_ref[head].astype(F32)
+        grad = grad_ref[head].astype(F32)
+        delta = jnp.sum(grad * att_ref[head].astype(F32), axis=0, keepdims=True)
+        query_ext = jnp.concatenate([query, minus_pieces(lse_ref[head])], axis=0).astype(BF16)
+        grad_ext = jnp.concatenate([grad, minus_pieces(delta)], axis=0).astype(BF16)
+        key = column_norm(kv_ref[0, head])[0].astype(BF16)
+        key_ext = jnp.concatenate([key.astype(F32), ones], axis=0).T.astype(BF16)
+        value_ext = jnp.concatenate([kv_ref[1, head], ones], axis=0).T.astype(BF16)
+        probs = jnp.exp2(jnp.dot(key_ext, query_ext, preferred_element_type=F32))
+        grad_probs = jnp.dot(value_ext, grad_ext, preferred_element_type=F32)
+        grad_scores = (probs * grad_probs).astype(BF16)
+        value_grad = right_dot(grad_ext, probs.astype(BF16))[:head_dim]
+        key_grad = right_dot(query_ext, grad_scores)[:head_dim]
+        key_ref[head] = (key_grad * (1.0 / LOG2E)).astype(BF16)
+        value_ref[head] = value_grad.astype(BF16)
+        query_grad = jnp.dot(key, grad_scores, preferred_element_type=F32) * score_scale
+        normed = query * (1.0 / query_scale)
+        out_ref[head] = column_norm_back(query_grad, normed, inv_ref[head]).astype(BF16)
 
 
 def cross_back(query, text_kv, grad, att, inverse, lse, images, query_scale, score_scale):
     heads, head_dim, tokens = query.shape
     tile_len, text_pad = tokens // images, text_kv.shape[3] // images
-    wide = pl.BlockSpec((1, head_dim, tile_len), lambda i, h: (h, 0, i))
-    row = pl.BlockSpec((1, 1, tile_len), lambda i, h: (h, 0, i))
-    text = pl.BlockSpec((2, 1, head_dim, text_pad), lambda i, h: (0, h, 0, i))
-    text_out = pl.BlockSpec((1, head_dim, text_pad), lambda i, h: (h, 0, i))
+    block = math.gcd(heads, 4)
+    wide = pl.BlockSpec((block, head_dim, tile_len), lambda i, h: (h, 0, i))
+    row = pl.BlockSpec((block, 1, tile_len), lambda i, h: (h, 0, i))
+    text = pl.BlockSpec((2, block, head_dim, text_pad), lambda i, h: (0, h, 0, i))
+    text_out = pl.BlockSpec((block, head_dim, text_pad), lambda i, h: (h, 0, i))
     return kernel_call(
         functools.partial(cross_back_body, query_scale, score_scale),
         2560 * heads * tokens * text_pad,
         16 * query.size,
-        grid=(images, heads),
+        grid=(images, heads // block),
         in_specs=[wide, text, wide, wide, row, row],
         out_specs=[
             wide,
@@ -964,6 +971,86 @@
             jax.ShapeDtypeStruct((heads, head_dim, images * text_pad), BF16),
         ],
     )(query, text_kv, grad, att, inverse, lse)
+
+
+def join_norm_body(patch_ref, skip_ref, weight_ref, gain_ref, bias_ref, z_ref, inv_ref, in_ref):
+    width = skip_ref.shape[1]
+    patch_feat = right_dot(patch_ref[...], weight_ref[...])
+    joined = jnp.concatenate([patch_feat, skip_ref[...].astype(F32)], axis=1)
+    normed, inverse = layer_norm(joined)
+    z_ref[...] = normed
+    inv_ref[...] = inverse
+    in_ref[...] = (normed * gain_ref[...] + bias_ref[...]).astype(BF16)
+
+
+def join_norm(patch_rows, skip_rows, f_patch, gain, bias):
+    tokens, width = skip_rows.shape
+    block = math.gcd(tokens, 256)
+    rows = lambda columns: pl.BlockSpec((block, columns), lambda t: (t, 0))
+    fixed = lambda shape: pl.BlockSpec(shape, lambda t: (0, 0))
+    return kernel_call(
+        join_norm_body,
+        64 * tokens * width,
+        16 * tokens * width,
+        grid=(tokens // block,),
+        in_specs=[
+            rows(patch_rows.shape[1]),
+            rows(width),
+            fixed(f_patch.shape),
+            fixed(gain.shape),
+            fixed(bias.shape),
+        ],
+        out_specs=[rows(2 * width), rows(1), rows(2 * width)],
+        out_shape=[
+            jax.ShapeDtypeStruct((tokens, 2 * width), F32),
+            jax.ShapeDtypeStruct((tokens, 1), F32),
+            jax.ShapeDtypeStruct((tokens, 2 * width), BF16),
+        ],
+    )(patch_rows, skip_rows, f_patch, gain, bias)
+
+
+def join_back_body(low_ref, weight_ref, z_ref, inv_ref, gain_ref, skip_ref, patch_ref, sums_ref):
+    width = skip_ref.shape[1]
+    grad, normed = right_dot(low_ref[...], weight_ref[...]), z_ref[...]
+
+    @pl.when(pl.program_id(0) == 0)
+    def _():
+        sums_ref[...] = jnp.zeros_like(sums_ref)
+
+    sums_ref[0:1] += jnp.sum(grad * normed, axis=0, keepdims=True)
+    sums_ref[1:2] += jnp.sum(grad, axis=0, keepdims=True)
+    back = norm_back(grad * gain_ref[...], normed, inv_ref[...])
+    patch_ref[...] = back[:, :width].astype(BF16)
+    skip_ref[...] = back[:, width:]
+
+
+def join_back(low_rows, f_skip, normed, inverse, gain):
+    tokens, width = low_rows.shape
+    block = math.gcd(tokens, 256)
+    rows = lambda columns: pl.BlockSpec((block, columns), lambda t: (t, 0))
+    fixed = lambda shape: pl.BlockSpec(shape, lambda t: (0, 0))
+    return kernel_call(
+        join_back_body,
+        4 * tokens * width * width,
+        18 * tokens * width,
+        grid=(tokens // block,),
+        in_specs=[rows(width), fixed(f_skip.shape), rows(2 * width), rows(1), fixed(gain.shape)],
+        out_specs=[rows(width), rows(width), fixed((2, 2 * width))],
+        out_shape=[
+            jax.ShapeDtypeStruct((tokens, width), F32),
+            jax.ShapeDtypeStruct((tokens, width), BF16),
+            jax.ShapeDtypeStruct((2, 2 * width), F32),
+        ],
+    )(low_rows, f_skip, normed, inverse, gain)
+
+
+def gelu_and_slope(inputs):
+    scale, cubic = math.sqrt(2.0 / math.pi), 0.044715
+    square = inputs * inputs
+    curve = jnp.tanh(scale * inputs * (1.0 + cubic * square))
+    half = 0.5 * (1.0 + curve)
+    bend = 0.5 * inputs * (1.0 - curve * curve) * (scale * (1.0 + 3.0 * cubic * square))
+    return ((inputs * half).astype(BF16), (half + bend).astype(BF16))
 
 
 def swap_tiles(values_in):
@@ -990,41 +1077,50 @@
     )
 
 
-def narrow_blocks(blocks):
+def narrow_blocks(blocks, first=None):
     devices, me = lax.axis_size("dp"), lax.axis_index("dp")
-    total = lax.select_n(me, *blocks).astype(F32)
+    received = []
     for step in range(1, devices):
         sent = lax.select_n((me + step) % devices, *blocks)
-        total = total + lax.ppermute(sent, "dp", shift_pairs(devices, step)).astype(F32)
+        received.append(lax.ppermute(sent, "dp", shift_pairs(devices, step)))
+    if first is not None:
+        received = after(first, *received)
+    total = lax.select_n(me, *blocks).astype(F32)
+    for piece in received:
+        total = total + piece.astype(F32)
     return total
 
 
-def narrow(weight_grad):
-    return narrow_blocks(jnp.split(weight_grad, lax.axis_size("dp"), axis=1))
-
-
-def narrow_three(weight_grads):
+def narrow(weight_grad, first=None):
+    return narrow_blocks(jnp.split(weight_grad, lax.axis_size("dp"), axis=1), first)
+
+
+def by_device(weight_grads, parts):
     devices = lax.axis_size("dp")
-    weight_grads = jnp.split(weight_grads, 3, axis=1)
     split = [jnp.split(weight_grad, devices, axis=1) for weight_grad in weight_grads]
-    return narrow_blocks([jnp.concatenate(blocks, axis=1) for blocks in zip(*split)])
+    return [jnp.concatenate(blocks, axis=parts) for blocks in zip(*split)]
 
 
 def sum_tiles(part_sums):
     devices, me = lax.axis_size(TILE), lax.axis_index(TILE)
-    blocks = jnp.split(part_sums, devices, axis=0)
-    total = lax.select_n(me, *blocks)
-    for step in range(1, devices):
-        sent = lax.select_n((me + step) % devices, *blocks)
-        total = total + lax.ppermute(sent, TILE, shift_pairs(devices, step))
+    total, step = part_sums, devices // 2
+    while step > 0:
+        pairs = [(at, at ^ step) for at in range(devices)]
+        lower, upper = jnp.split(total, 2, axis=0)
+        high = (me // step) % 2 == 1
+        sent = jnp.where(high, lower, upper)
+        total = jnp.where(high, upper, lower) + lax.ppermute(sent, TILE, pairs)
+        step //= 2
     return total
 
 
 def total_tiles(part_sum):
     devices = lax.axis_size(TILE)
-    total = part_sum
-    for step in range(1, devices):
-        total = total + lax.ppermute(part_sum, TILE, shift_pairs(devices, step))
+    total, step = part_sum, 1
+    while step < devices:
+        pairs = [(at, at ^ step) for at in range(devices)]
+        total = total + lax.ppermute(total, TILE, pairs)
+        step *= 2
     return total
 
 
@@ -1087,15 +1183,20 @@
     small = jnp.concatenate([w_patch, w_final, norm_params], axis=1)
     small_widths = (w_patch.shape[1], w_final.shape[1], norm_params.shape[1])
     cuts = (0, small_widths[0], sum(small_widths[:2]), sum(small_widths))
-    part_small = widen(fetch(small))
-    part_time, part_shift_w = widen(fetch(w_time)), widen(fetch(w_shift))
+    early = [jnp.pad(small, ((0, 0), (0, w_shift.shape[1] - small.shape[1]))), w_time, w_shift]
+    ends = (small.shape[0], small.shape[0] + w_time.shape[0])
+    part_small, part_time, part_shift_w = jnp.split(
+        widen(fetch(jnp.concatenate(early, axis=0))), ends, axis=0
+    )
+    part_small = part_small.reshape(small.shape[0], dp_devices, -1)[:, :, : small.shape[1]]
+    part_small = part_small.reshape(small.shape[0], -1)
     f_small = tiles_whole(part_small).reshape(-1, dp_devices, sum(small_widths))
     f_patch, f_final, f_norms = (
         f_small[:, :, cuts[at] : cuts[at + 1]].reshape(f_small.shape[0], -1) for at in range(3)
     )
     f_skip = tiles_whole(part_skip)
     held_qkv = fetch(w_qkv)
-    held_out, held_query, held_cross = fetch(w_out), fetch(w_query), fetch(w_cross)
+    held_three = fetch(jnp.concatenate([w_out, w_query, w_cross], axis=1))
     held_text = fetch(w_text)
     held_up, held_down = fetch(w_up), fetch(w_down)
     model_width = skip_input.shape[3]
@@ -1139,15 +1240,14 @@
     time_shift = total_tiles(plain_dot(act_cols, part_shift_w))
 
     patch_rows = latent.reshape(row_count, patch_width)
-    patch_feat = right_dot(patch_rows, f_patch)
-    skip_rows = skip_input.reshape(row_count, model_width).astype(F32)
-    gain_skip = jnp.concatenate([norm_f[:, 8], norm_f[:, 10]])
-    bias_skip = jnp.concatenate([norm_f[:, 9], norm_f[:, 11]])
-    joined, joined_inv = layer_norm(jnp.concatenate([patch_feat, skip_rows], axis=-1))
-    skip_in = (joined * gain_skip + bias_skip).astype(BF16)
+    skip_rows = skip_input.reshape(row_count, model_width)
+    gain_skip = jnp.concatenate([norm_f[:, 8], norm_f[:, 10]])[None]
+    bias_skip = jnp.concatenate([norm_f[:, 9], norm_f[:, 11]])[None]
+    joined, joined_inv, skip_in = join_norm(patch_rows, skip_rows, f_patch, gain_skip, bias_skip)
     f_qkv = tiles_whole(widen(held_qkv, skip_in))
-    part_three = [widen(held, skip_in) for held in (held_out, held_query, held_cross)]
-    f_three = tiles_whole(jnp.concatenate(part_three, axis=1))
+    part_three = widen(held_three, skip_in).reshape(-1, dp_devices, 3, w_out.shape[1])
+    part_three = jnp.swapaxes(part_three, 1, 2).reshape(part_three.shape[0], -1)
+    f_three = tiles_whole(part_three)
     f_out, f_query, f_cross = jnp.split(f_three, 3, axis=1)
     residual = plain_dot(skip_in, f_skip)
     first_z, first_inv = layer_norm(residual)
@@ -1155,7 +1255,6 @@
         images, tile_len, model_width
     ) + time_shift[:, None, :]
     first_in = first_pre.reshape(row_count, model_width).astype(BF16)
-    f_up = tiles_whole(widen(held_up, first_in))
     part_text = widen(held_text, first_in)
     f_text = tiles_whole(part_text)
     first_rows = first_in.reshape(images, tile_len, model_width)
@@ -1174,6 +1273,7 @@
         own_qkv.append(own)
         qk_inv.append(inverses)
         tile_qkv.append(swap_tiles(own))
+    f_up = tiles_whole(widen(held_up, tile_qkv[0]))
     for image in range(images):
         att, lse = attend(tile_qkv[image], flags[image])
         tile_att.append(att)
@@ -1198,8 +1298,7 @@
     second_z, second_inv = layer_norm(residual_three)
     second_in = (second_z * norm_f[:, 4] + norm_f[:, 5]).astype(BF16)
     up_pre = plain_dot(second_in, f_up)
-    hidden_float, gelu_pull = jax.vjp(gelu_tanh, up_pre)
-    hidden_act = hidden_float.astype(BF16)
+    hidden_act, slope = lax.optimization_barrier(gelu_and_slope(up_pre))
     residual_four = residual_three + plain_dot(hidden_act, f_down)
     last_z, last_inv = layer_norm(residual_four)
     last_in = (last_z * norm_f[:, 6] + norm_f[:, 7]).astype(BF16)
@@ -1219,7 +1318,7 @@
     d_down, low_four = lax.optimization_barrier((d_down, low_four))
     t_down = over_tiles(d_down)
     grad_hidden = right_dot(low_four, f_down)
-    grad_up = gelu_pull(grad_hidden)[0].astype(BF16)
+    grad_up = (grad_hidden * slope).astype(BF16)
     d_up = left_dot(second_in, grad_up).astype(BF16)
     d_up, grad_up = lax.optimization_barrier((d_up, grad_up))
     t_up = over_tiles(d_up)
@@ -1229,7 +1328,6 @@
     grad_three = grad_four + norm_back(grad_second * norm_f[:, 4], second_z, second_inv)
     low_three = grad_three.astype(BF16)
     d_cross = plain_dot(cross_cols, low_three).astype(BF16)
-    down_grad = narrow(t_down)
     grad_crossed = dot_over(f_cross, low_three, 1, 1).astype(BF16)
     t_down, grad_crossed = lax.optimization_barrier((t_down, grad_crossed))
     grad_cross_q, d_text_key, d_text_value = cross_back(
@@ -1266,33 +1364,27 @@
         ],
         axis=1,
     )
+    d_joint = with_layout_constraint(d_joint, Layout(major_to_minor=(0, 1)))
+    d_joint, tile_grads[0] = lax.optimization_barrier((d_joint, tile_grads[0]))
     t_joint = over_tiles(d_joint)
-    own_grads = []
-    tile_back = None
+    own_grads, grad_qkv, tile_back = [], None, None
     for image in range(images):
         if tile_back is not None:
-            t_up, down_grad, tile_grads[image], tile_back = lax.optimization_barrier(
-                (t_up, down_grad, tile_grads[image], tile_back)
+            down_grad = narrow(t_down, tile_back)
+            down_grad, tile_grads[image], tile_back = lax.optimization_barrier(
+                (down_grad, tile_grads[image], tile_back)
             )
             own_grads.append(swap_tiles(tile_back))
         tile_back = attend_back(
             tile_qkv[image], tile_grads[image], tile_att[image], tile_lse[image], score_scale
         )
     own_grads.append(swap_tiles(tile_back))
-    up_grad = narrow(t_up)
-    t_joint, up_grad, own_grads[-1] = lax.optimization_barrier((t_joint, up_grad, own_grads[-1]))
-    joint_grad = narrow_three(t_joint[:, : 3 * model_width])
-    sum_text_kv = t_joint[:, 3 * model_width :].astype(F32)
-    sum_text_kv = jnp.transpose(
-        sum_text_kv.reshape(-1, head_dim, 2, images * text_pad), (2, 0, 1, 3)
-    )
-    group_heads = head_count // grid_devices
-    own_key = lax.dynamic_slice_in_dim(text_kv[0], grid_at * group_heads, group_heads, 0)
-    ck_z, ck_inv = layer_norm(jnp.swapaxes(own_key, 1, 2))
-    grad_ckey = jnp.swapaxes(norm_back(jnp.swapaxes(sum_text_kv[0], 1, 2), ck_z, ck_inv), 1, 2)
-    grad_kv = tiles_whole(jnp.stack([grad_ckey, sum_text_kv[1]]).astype(BF16)[None])
-    grad_qkv = None
     for image in range(images):
+        if image == images - 1:
+            up_grad = narrow(t_up, tile_back)
+            t_joint, up_grad, own_grads[-1], grad_qkv = lax.optimization_barrier(
+                (t_joint, up_grad, own_grads[-1], grad_qkv)
+            )
         grad_qkv = head_back(
             own_grads[image],
             own_qkv[image],
@@ -1304,13 +1396,23 @@
             images,
             grad_qkv,
         )
+    sum_text_kv = t_joint[:, 3 * model_width :].astype(F32)
+    sum_text_kv = jnp.transpose(
+        sum_text_kv.reshape(-1, head_dim, 2, images * text_pad), (2, 0, 1, 3)
+    )
+    group_heads = head_count // grid_devices
+    own_key = lax.dynamic_slice_in_dim(text_kv[0], grid_at * group_heads, group_heads, 0)
+    ck_z, ck_inv = layer_norm(jnp.swapaxes(own_key, 1, 2))
+    grad_ckey = jnp.swapaxes(norm_back(jnp.swapaxes(sum_text_kv[0], 1, 2), ck_z, ck_inv), 1, 2)
+    grad_kv = tiles_whole(jnp.stack([grad_ckey, sum_text_kv[1]]).astype(BF16)[None])
+    grad_kv, grad_qkv = lax.optimization_barrier((grad_kv, grad_qkv))
     grad_qkv = grad_qkv.reshape(3 * model_width, row_count)
     d_qkv = dot_over(first_in, grad_qkv, 0, 1).astype(BF16)
     d_qkv, grad_qkv = lax.optimization_barrier((d_qkv, grad_qkv))
     t_qkv = over_tiles(d_qkv)
     grad_first = dot_over(grad_qkv, f_qkv, 0, 1)
-    joint_grad, grad_first = lax.optimization_barrier((joint_grad, grad_first))
-    out_grad, query_w_grad, cross_grad = jnp.split(joint_grad, 3, axis=1)
+    joint_blocks = by_device(jnp.split(t_joint[:, : 3 * model_width], 3, axis=1), 1)
+    joint_grad = narrow_blocks(joint_blocks, grad_first)
     gain_first = jnp.sum(grad_first * first_z, axis=0)
     bias_first = jnp.sum(grad_first, axis=0)
     part_shift = jnp.sum(grad_first.reshape(images, tile_len, model_width), axis=1)
@@ -1319,30 +1421,44 @@
     low_one = grad_one.astype(BF16)
     d_skip_w = left_dot(skip_in, low_one).astype(BF16)
     d_skip_w, low_one = lax.optimization_barrier((d_skip_w, low_one))
-    t_qkv, d_skip_w = lax.optimization_barrier((t_qkv, d_skip_w))
-    qkv_grad = narrow(t_qkv)
+    skip_grad, grad_patch, skip_sums = join_back(low_one, f_skip, joined, joined_inv, gain_skip)
+    t_qkv, d_skip_w, joint_grad, skip_sums = lax.optimization_barrier(
+        (t_qkv, d_skip_w, joint_grad, skip_sums)
+    )
+    out_grad, query_w_grad, cross_grad = jnp.split(joint_grad, 3, axis=1)
     t_skip = over_tiles(d_skip_w)
 
     grad_kv = jnp.transpose(grad_kv, (1, 0, 2, 3, 4)).reshape(2 * model_width, images * text_pad)
     text_slice = text_states.shape[2] // grid_devices
     text_cols = lax.dynamic_slice_in_dim(text_rows, grid_at * text_slice, text_slice, 1)
-    text_w_grad = narrow(dot_over(text_cols, grad_kv, 0, 1).astype(BF16))
+    d_text = dot_over(text_cols, grad_kv, 0, 1).astype(BF16)
     text_grad = dot_over(grad_kv, part_text, 0, 1).reshape(images, text_pad, text_slice)
     text_grad = text_grad[:, :text_len]
 
     shift_low = total_tiles(part_shift).astype(BF16)
-    shift_w_grad = narrow(left_dot(act_cols, shift_low).astype(BF16))
-    grad_time_act = lax.all_gather(right_dot(shift_low, part_shift_w), TILE, axis=1, tiled=True)
+    d_shift = left_dot(act_cols, shift_low).astype(BF16)
+    grad_time_act = total_tiles(
+        lax.dynamic_update_slice_in_dim(
+            jnp.zeros_like(time_pre), right_dot(shift_low, part_shift_w), grid_at * shift_slice, 1
+        )
+    )
     grad_time_pre = silu_pull(grad_time_act)[0].astype(BF16)
-    time_w_grad = narrow(left_dot(embed_cols, grad_time_pre).astype(BF16))
-
-    grad_skip_in = right_dot(low_one, f_skip)
-    gain_skips = jnp.sum(grad_skip_in * joined, axis=0)
-    bias_skips = jnp.sum(grad_skip_in, axis=0)
-    grad_joined = norm_back(grad_skip_in * gain_skip, joined, joined_inv)
-    qkv_grad, grad_joined = lax.optimization_barrier((qkv_grad, grad_joined))
-    skip_grad = grad_joined[:, model_width:].reshape(images, rows_tile, cols_tile, model_width)
-    grad_patch = grad_joined[:, :model_width].astype(BF16)
+    d_time = left_dot(embed_cols, grad_time_pre).astype(BF16)
+    late, width = [], w_shift.shape[1]
+    for at in range(dp_devices):
+        pair = d_text[:, 2 * at * width : 2 * (at + 1) * width]
+        own = slice(at * width, (at + 1) * width)
+        late.append(
+            jnp.concatenate([pair[:, :width], pair[:, width:], d_time[:, own], d_shift[:, own]])
+        )
+    late = narrow_blocks(late)
+    qkv_grad = narrow(t_qkv, late)
+    rows = d_text.shape[0]
+    text_w_grad = jnp.concatenate([late[:rows], late[rows : 2 * rows]], axis=1)
+    time_w_grad, shift_w_grad = jnp.split(late[2 * rows :], [d_time.shape[0]], axis=0)
+
+    skip_grad = skip_grad.reshape(images, rows_tile, cols_tile, model_width)
+    gain_skips, bias_skips = skip_sums[0], skip_sums[1]
     d_patch = left_dot(grad_patch, patch_rows)
     latent_grad = plain_dot(grad_patch, f_patch).reshape(images, rows_tile, cols_tile, patch_width)
     d_norms = jnp.stack(

time: 1600 us -> 1480 us (0.925)
  waiting for transfers between devices: 273 us -> 356 us
  local copies, waits for them, and re-layouts: 179 us -> 101 us
  other arithmetic: 124 us -> 68.1 us
  starting transfers between devices: 195 us -> 157 us
  blocking collectives: 33.8 us -> 17.7 us
    ppermute x55 -> x36, starting transfers between devices: 96.9 us -> 52.8 us  [the longest x21 40.9 us: narrow_blocks(): received.append(lax.ppermute(sent, 'dp', shift_pairs(devices, step)))]
    all_gather x7, waiting for transfers between devices: 14 us -> 55.4 us  [tiles_whole(): return lax.all_gather(weight, TILE, axis=0, tiled=True)]
    pallas_call x0 -> x2, Pallas kernels: none -> 33.6 us  [the longest x1 24 us: join_back(): kernel_call(join_back_body, 4 * tokens * width * width, 18 * tokens * wid...]
    ppermute x55 -> x36, waiting for transfers between devices: 85.6 us -> 119 us  [the longest x21 98.9 us: narrow_blocks(): received.append(lax.ppermute(sent, 'dp', shift_pairs(devices, step)))]
    dot_general x6 -> x4, matrix products: 94.1 us -> 65.4 us  [right_dot(): lax.dot_general(left_mat, right_mat, (((1,), (1,)), ((), ())), preferred_...]
    unnamed x302 -> x250, local copies, waits for them, and re-layouts: 52.9 us -> 27.6 us
    pallas_call x2, Pallas kernels: 89.7 us -> 68.5 us  [attend(): kernel_call(attend_body, 1024 * heads * tiles ** 2 * tile_len ** 2, 8 * q...]
    slice x6 -> x5, local copies, waits for them, and re-layouts: 20.5 us -> 1.26 us  [the longest x1 0.93 us: local_heads(): pair[:, :width]]
  transfers between devices with their start and end apart: 108 -> 77, of which waited for: 28 -> 38; matrix products, arithmetic and copies ran while one was open for 36% -> 30% of each run, Pallas kernels for 23% -> 25%
where the time goes in v2:
time: 1480 us; the launch traced here: 1460 us
  matrix products  378 us (26%)
  Pallas kernels  368 us (25%)
  waiting for transfers between devices  356 us (24%)
  starting transfers between devices  157 us (11%)
  local copies, waits for them, and re-layouts  101 us (7%)
  other arithmetic  68.1 us (5%)
  blocking collectives  17.7 us (1%)
  between operations  16.8 us (1%)
    pallas_call x2, Pallas kernels, attend_back(): kernel_call(functools.partial(attend_back_body, score_scale), 2560 * head...  178 us
    dot_general x11, matrix products, dot_over(): lax.dot_general(left_mat, right_mat, (((left_axis,), (right_axis,)), ((),...  116 us
    dot_general x9, matrix products, plain_dot(): return jnp.dot(left_mat, right_mat, preferred_element_type=jnp.float32)  105 us
    ppermute x21, waiting for transfers between devices, narrow_blocks(): received.append(lax.ppermute(sent, 'dp', shift_pairs(devices, step)))  98.9 us
    dot_general x9, matrix products, left_dot(): lax.dot_general(left_mat, right_mat, (((0,), (0,)), ((), ())), preferred_...  91.5 us
    ppermute x21, waiting for transfers between devices, fetch(): lax.ppermute(weight, 'dp', shift_pairs(devices, step))  88.3 us
    all_to_all x8, waiting for transfers between devices, swap_tiles(): lax.all_to_all(values_in, TILE, split_axis=0, concat_axis=0, tiled=True)  77.7 us
    pallas_call x2, Pallas kernels, attend(): kernel_call(attend_body, 1024 * heads * tiles ** 2 * tile_len ** 2, 8 * q...  68.5 us
  transfers between devices with their start and end apart: 77, of which 38 were waited for; matrix products, arithmetic and copies ran while one was open for 30% of the time, Pallas kernels for 25%

profile of v2, /device:TPU:0, one launch (start us, length us, event | category | flops | bytes accessed | tf_op | source)
XLA Modules:
  0.0 1462.5 jit_solution(13357696509537329789)
XLA Ops:
  14.3 5.7 collective-permute-done.3
  20.1 10.8 collective-permute-done.4
  35.6 6.3 collective-permute-start
  53.7 8.5 collective-permute-done.1
  62.9 17.7 %all-gather = bf16[8,176,60]{1,2,0:T(8,128)(2,1)S(1)} all-gather(bf16[1,176,60]{1,2,0:T(8,128)(2,1)S(1)} %reshape.645), channel_id=1, replica_groups=mesh['dp'=4,'row'=4,'col'=2] {'row','col'}, dimensions={0}, use_global_device_ids=true | all-gather | bytes 190080 | tf_op jit(solution)/shard_map/all_gather | solution.py:1134
  84.1 9.6 shard_map.314
  100.7 21.2 %collective-permute-start.15 = (bf16[176,1056]{1,0:T(8,128)(2,1)S(1)}, bf16[176,1056]{1,0:T(8,128)(2,1)S(1)}, u32[]{:S(2)}, u32[]{:S(2)}) collective-permute-start(bf16[176,1056]{1,0:T(8,128)(2,1)S(1)} %concatenate.108), channel_id=1, source_target_pairs={{0,8},{8,16},{16,24},{24,0},{1,9},{9,17},{17,25},{25,1},{2,10},{10... | collective-permute-start | bytes 1115144 | tf_op jit(solution)/shard_map/ppermute | solution.py:1067
  124.4 7.3 collective-permute-done.15
  131.7 11.3 collective-permute-done.16
  143.0 5.8 collective-permute-done.17
  151.9 5.6 reshape.621
  181.4 8.7 collective-permute-start.18
  193.7 15.2 %fusion.104 = (f32[1024]{0:T(1024)S(1)}, f32[1024,1408]{1,0:T(8,128)S(1)}) fusion(bf16[1024,2816]{1,0:T(8,128)(2,1)} %get-tuple-element.97, bf16[2816,1408]{1,0:T(8,128)(2,1)} %all-gather.9.cloned.1.call-done.weight_ref), kind=kOutput, calls=%fused_computation.312 | convolution fusion | flops 8121613312 | bytes 19468288 | tf_op jit(solution)/shard_map/dot_general | solution.py:72
  220.7 15.9 %shard_map.315 = (bf16[8,3,2,88,512]{4,3,2,1,0:T(8,128)(2,1)}, f32[8,3,2,512]{3,2,1,0:T(2,128)}) custom-call(bf16[512,1408]{1,0:T(8,128)(2,1)} %get-tuple-element.267.rows_ref, bf16[1408,4224]{1,0:T(8,128)(2,1)} %all-gather.11.cloned.1.call-done.weight_ref, f32[88,512]{1,0:T(8,128)} %pad_maximum_fusion.14.cos_ref, f32[88,512]{1,0:T(8,128)} %pad_maximum_fusion.15.sin_ref, ...), custom_call_target="tpu_custom_call" | custom-call | flops 6090129408 | bytes 11894784 | tf_op jit(solution)/shard_map/pallas_call | solution.py:652
  246.4 12.0 collective-permute-done.21
  258.5 22.6 %collective-permute-done.22 = bf16[176,1536]{1,0:T(8,128)(2,1)S(1)} collective-permute-done((bf16[176,1536]{1,0:T(8,128)(2,1)S(1)}, bf16[176,1536]{1,0:T(8,128)(2,1)S(1)}, u32[]{:S(2)}, u32[]{:S(2)}) %collective-permute-start.22) | collective-permute-done | bytes 540704 | tf_op jit(solution)/shard_map/ppermute | solution.py:1067
  281.1 21.4 %all-to-all-done.query_ref.key_ref.value_ref = bf16[8,3,2,88,512]{4,3,2,1,0:T(8,128)(2,1)} async-done(((bf16[8,3,2,88,512]{4,3,2,1,0:T(8,128)(2,1)}), bf16[8,3,2,88,512]{4,3,2,1,0:T(8,128)(2,1)}, u32[]{:S(2)}, u32[]{:S(2)}) %all-to-all-start) | async-done | bytes 4325408 | tf_op jit(solution)/shard_map/all_to_all | solution.py:1057
  304.6 15.2 %shard_map.317 = (bf16[8,3,2,88,512]{4,3,2,1,0:T(8,128)(2,1)}, f32[8,3,2,512]{3,2,1,0:T(2,128)}) custom-call(bf16[512,1408]{1,0:T(8,128)(2,1)} %get-tuple-element.268.rows_ref, bf16[1408,4224]{1,0:T(8,128)(2,1)} %all-gather.11.cloned.1.call-done.weight_ref, f32[88,512]{1,0:T(8,128)} %pad_maximum_fusion.14.cos_ref, f32[88,512]{1,0:T(8,128)} %pad_maximum_fusion.15.sin_ref, ...), custom_call_target="tpu_custom_call" | custom-call | flops 6090129408 | bytes 11894784 | tf_op jit(solution)/shard_map/pallas_call | solution.py:652
  325.2 34.0 %shard_map.316 = (bf16[8,2,88,512]{3,2,1,0:T(8,128)(2,1)}, f32[8,2,1,512]{3,2,1,0:T(1,128)}) custom-call(bf16[8,3,2,88,512]{4,3,2,1,0:T(8,128)(2,1)} %all-to-all-done.query_ref.key_ref.value_ref, bf16[8,3,2,88,512]{4,3,2,1,0:T(8,128)(2,1)} %all-to-all-done.query_ref.key_ref.value_ref, bf16[8,3,2,88,512]{4,3,2,1,0:T(8,128)(2,1)} %all-to-all-done.query_ref.key_ref.value_ref, ...), custom_call_target="tpu_custom_call" | custom-call | flops 34359738368 | bytes 17301504 | tf_op jit(solution)/shard_map/pallas_call | solution.py:757
  359.3 27.8 %all-to-all-done.2.query_ref.key_ref.value_ref = bf16[8,3,2,88,512]{4,3,2,1,0:T(8,128)(2,1)} async-done(((bf16[8,3,2,88,512]{4,3,2,1,0:T(8,128)(2,1)}), bf16[8,3,2,88,512]{4,3,2,1,0:T(8,128)(2,1)}, u32[]{:S(2)}, u32[]{:S(2)}) %all-to-all-start.2) | async-done | bytes 4325408 | tf_op jit(solution)/shard_map/all_to_all | solution.py:1057
  390.7 34.5 %shard_map.318 = (bf16[8,2,88,512]{3,2,1,0:T(8,128)(2,1)}, f32[8,2,1,512]{3,2,1,0:T(1,128)}) custom-call(bf16[8,3,2,88,512]{4,3,2,1,0:T(8,128)(2,1)} %all-to-all-done.2.query_ref.key_ref.value_ref, bf16[8,3,2,88,512]{4,3,2,1,0:T(8,128)(2,1)} %all-to-all-done.2.query_ref.key_ref.value_ref, ...), custom_call_target="tpu_custom_call" | custom-call | flops 34359738368 | bytes 17301504 | tf_op jit(solution)/shard_map/pallas_call | solution.py:757
  434.8 22.5 %all-to-all-done.3 = bf16[8,2,88,512]{3,2,1,0:T(8,128)(2,1)S(1)} async-done(((bf16[8,2,88,512]{3,2,1,0:T(8,128)(2,1)}), bf16[8,2,88,512]{3,2,1,0:T(8,128)(2,1)S(1)}, u32[]{:S(2)}, u32[]{:S(2)}) %all-to-all-start.3) | async-done | bytes 1441824 | tf_op jit(solution)/shard_map/all_to_all | solution.py:1057
  457.3 10.5 fusion.105
  474.1 9.9 fusion.108
  484.8 9.4 fusion.10
  494.2 14.6 shard_map.319
  508.7 9.2 fusion.106
  521.2 39.8 %add_convert_fusion = (bf16[1024,6144]{1,0:T(8,128)(2,1)}, bf16[1024,6144]{1,0:T(8,128)(2,1)}) fusion(bf16[1408,6144]{1,0:T(8,128)(2,1)} %all-gather.17.cloned.1.call-done, f32[1024,1408]{1,0:T(8,128)} %copy-done.4, f32[1408]{0:T(1024)S(1)} %copy-done.98, f32[1408]{0:T(1024)S(1)} %copy-done.70, f32[1024]{0:T(1024)S(1)} %add_rsqrt_fusion.2, ...), kind=kOutput, calls=%fused_computation.1 | convolution fusion | flops 17843486720 | bytes 48253952 | tf_op jit(solution)/shard_map/dot_general | solution.py:72
  561.0 29.5 %all-gather.19.cloned.1.call-done = bf16[6144,1408]{0,1:T(8,128)(2,1)} async-done(((bf16[768,1408]{0,1:T(8,128)(2,1)}), bf16[6144,1408]{0,1:T(8,128)(2,1)}) %all-gather.19.cloned.1.call-update) | async-done | bytes 17301520 | tf_op jit(solution)/shard_map/all_gather | solution.py:1134
  590.5 28.8 %fusion.107 = (f32[1024]{0:T(1024)S(1)}, f32[1024,1408]{1,0:T(8,128)S(1)}) fusion(f32[1024,1408]{1,0:T(8,128)} %copy-done.4, bf16[1024,6144]{1,0:T(8,128)(2,1)} %get-tuple-element.119, bf16[6144,1408]{0,1:T(8,128)(2,1)} %all-gather.19.cloned.1.call-done), kind=kOutput, calls=%fused_computation.315 | convolution fusion | flops 17719623680 | bytes 41422848 | tf_op jit(solution)/shard_map/dot_general | solution.py:72
  629.5 27.9 %convolution_convert_fusion = bf16[6144,1408]{1,0:T(8,128)(2,1)} fusion(bf16[1024,6144]{1,0:T(8,128)(2,1)} %get-tuple-element.119, bf16[1024,1408]{1,0:T(8,128)(2,1)S(1)} %get-tuple-element.124), kind=kOutput, calls=%fused_computation.5 | convolution fusion | flops 17725390848 | bytes 32768000 | tf_op jit(solution)/shard_map/dot_general | solution.py:76
  659.2 30.5 %multiply_convert_fusion = bf16[1024,6144]{1,0:T(8,128)(2,1)} fusion(bf16[1024,6144]{1,0:T(8,128)(2,1)} %get-tuple-element.125, bf16[1024,1408]{1,0:T(8,128)(2,1)S(1)} %copy-done.29, bf16[6144,1408]{0,1:T(8,128)(2,1)} %all-gather.19.cloned.1.call-done), kind=kOutput, calls=%fused_computation | convolution fusion | flops 17735614464 | bytes 45350912 | tf_op jit(solution)/shard_map/dot_general | solution.py:82
  689.8 25.9 %convolution_convert_fusion.1 = bf16[1408,6144]{1,0:T(8,128)(2,1)} fusion(bf16[1024,6144]{1,0:T(8,128)(2,1)} %multiply_convert_fusion, f32[1024,1408]{1,0:T(8,128)} %copy-done.4, f32[1408]{0:T(1024)S(1)} %copy-done.98, f32[1408]{0:T(1024)S(1)} %copy-done.70, f32[1024]{0:T(1024)S(1)} %add_rsqrt_fusion.2, f32[1024]{0:T(1024)S(1)} %broadcast_multiply_fusion.12), kind=kOutput, calls=%fused_computation.6 | convolution fusion | flops 17732599808 | bytes 35671040 | tf_op jit(solution)/shard_map/dot_general | solution.py:76
  715.7 31.5 %multiply_reduce_fusion.1 = (f32[1408]{0:T(1024)}, f32[1024]{0:T(1024)S(1)}, f32[1024]{0:T(1024)S(1)}, f32[1408]{0:T(1024)}, f32[1024,1408]{1,0:T(8,128)}) fusion(f32[1024,1408]{1,0:T(8,128)} %copy-done.4, f32[1024]{0:T(1024)S(1)} %add_rsqrt_fusion.2, f32[1024]{0:T(1024)S(1)} %broadcast_multiply_fusion.12, f32[1408]{0:T(1024)S(1)} %copy-done.70, ...), kind=kOutput, calls=%fused_computation.19 | convolution fusion | flops 17729710080 | bytes 41452032 | tf_op jit(solution)/shard_map/dot_general | solution.py:82
  747.2 7.7 multiply_add_fusion.1
  757.4 8.6 convolution_convert_fusion.7
  766.0 10.2 reduce-scatter.6.cloned.1.call-done
  776.2 21.4 %shard_map.320 = (bf16[16,88,1024]{2,1,0:T(8,128)(2,1)}, bf16[16,88,768]{2,1,0:T(8,128)(2,1)}, bf16[16,88,768]{2,1,0:T(8,128)(2,1)}) custom-call(bf16[16,88,1024]{2,1,0:T(8,128)(2,1)} %get-tuple-element.127.query_ref, f32[2,16,88,768]{3,2,1,0:T(8,128)} %bitcast.191, bf16[16,88,1024]{2,1,0:T(8,128)(2,1)} %bitcast.214, ...), custom_call_target="tpu_custom_call" | custom-call | flops 16106127360 | bytes 23068672 | tf_op jit(solution)/shard_map/pallas_call | solution.py:957
  797.7 11.4 multiply_reduce_fusion.2
  812.7 6.8 fusion.17
  823.8 8.3 fusion.2
  832.1 9.9 fusion.1
  842.1 6.2 fusion
  852.2 6.0 all-to-all-done.4.grad_ref
  867.4 6.4 fusion.20
  878.0 89.1 %shard_map.321 = bf16[8,3,2,88,512]{4,3,2,1,0:T(8,128)(2,1)} custom-call(bf16[8,3,2,88,512]{4,3,2,1,0:T(8,128)(2,1)} %all-to-all-done.query_ref.key_ref.value_ref, bf16[8,3,2,88,512]{4,3,2,1,0:T(8,128)(2,1)} %all-to-all-done.query_ref.key_ref.value_ref, bf16[8,3,2,88,512]{4,3,2,1,0:T(8,128)(2,1)} %all-to-all-done.query_ref.key_ref.value_ref, ...), custom_call_target="tpu_custom_call" | custom-call | flops 85899345920 | bytes 17301504 | tf_op jit(solution)/shard_map/pallas_call | solution.py:845
  979.3 89.2 %shard_map.322 = bf16[8,3,2,88,512]{4,3,2,1,0:T(8,128)(2,1)} custom-call(bf16[8,3,2,88,512]{4,3,2,1,0:T(8,128)(2,1)} %all-to-all-done.2.query_ref.key_ref.value_ref, bf16[8,3,2,88,512]{4,3,2,1,0:T(8,128)(2,1)} %all-to-all-done.2.query_ref.key_ref.value_ref, bf16[8,3,2,88,512]{4,3,2,1,0:T(8,128)(2,1)} %all-to-all-done.2.query_ref.key_ref.value_ref, ...), custom_call_target="tpu_custom_call" | custom-call | flops 85899345920 | bytes 17301504 | tf_op jit(solution)/shard_map/pallas_call | solution.py:845
  1087.2 9.8 collective-permute-done.30
  1096.9 10.2 collective-permute-done.32
  1107.2 23.7 %collective-permute-done.31 = bf16[176,1536]{1,0:T(8,128)(2,1)S(1)} collective-permute-done((bf16[176,1536]{1,0:T(8,128)(2,1)S(1)}, bf16[176,1536]{1,0:T(8,128)(2,1)S(1)}, u32[]{:S(2)}, u32[]{:S(2)}) %collective-permute-start.31) | collective-permute-done | bytes 540704 | tf_op jit(solution)/shard_map/ppermute | solution.py:1085
  1132.4 10.1 shard_map.323.others_0_
  1147.3 10.4 shard_map.324
  1157.6 25.8 %all-gather.21.cloned.1.call-done = bf16[8,2,2,88,768]{4,3,2,1,0:T(8,128)(2,1)} async-done(((bf16[1,2,2,88,768]{4,3,2,1,0:T(8,128)(2,1)}), bf16[8,2,2,88,768]{4,3,2,1,0:T(8,128)(2,1)}) %all-gather.21.cloned.1.call-update) | async-done | bytes 4325392 | tf_op jit(solution)/shard_map/all_gather | solution.py:1134
  1183.5 19.8 %convolution_convert_fusion.2 = bf16[1408,4224]{1,0:T(8,128)(2,1)} fusion(bf16[1024,1408]{1,0:T(8,128)(2,1)S(1)} %copy-done.13, bf16[4224,1024]{1,0:T(8,128)(2,1)} %bitcast.165), kind=kOutput, calls=%fused_computation.7 | convolution fusion | flops 12186206208 | bytes 23429120 | tf_op jit(solution)/shard_map/dot_general | solution.py:1142
  1216.1 27.3 %multiply_reduce_fusion.3 = (f32[1408]{0:T(1024)}, f32[1024]{0:T(1024)S(1)}, f32[1024]{0:T(1024)S(1)}, f32[1408]{0:T(1024)}, f32[1024,1408]{1,0:T(8,128)S(1)}) fusion(f32[1024,1408]{1,0:T(8,128)} %copy-done, f32[1024]{0:T(1024)S(1)} %copy-done.65, f32[1024]{0:T(1024)S(1)} %copy-done.63, f32[1408]{0:T(1024)S(1)} %copy-done.61, ...), kind=kOutput, calls=%fused_computation.21 | convolution fusion | flops 12193230848 | bytes 32113152 | tf_op jit(solution)/shard_map/dot_general | solution.py:1142
  1247.4 13.8 convolution_convert_fusion.3
  1263.8 24.0 %shard_map.325 = (f32[1024,1408]{1,0:T(8,128)}, bf16[1024,1408]{1,0:T(8,128)(2,1)}, f32[2,2816]{1,0:T(2,128)}) custom-call(bf16[1024,1408]{1,0:T(8,128)(2,1)} %copy-done.27, bf16[2816,1408]{1,0:T(8,128)(2,1)} %all-gather.9.cloned.1.call-done.weight_ref, f32[1024,2816]{1,0:T(8,128)} %get-tuple-element.157.z_ref, f32[1024,1]{1,0:T(8,128)} %get-tuple-element.158.inv_ref, ...), custom_call_target="tpu_custom_call" | custom-call | flops 8120172544 | bytes 25952256 | tf_op jit(solution)/shard_map/pallas_call | solution.py:1032
  1305.4 5.5 copy.108
  1311.0 6.7 copy.121
  1355.8 11.4 collective-permute-done.52
  1381.9 8.2 collective-permute-start.54
  1395.3 22.3 %collective-permute-done.39 = f32[176,15]{0,1:T(8,128)S(1)} collective-permute-done((f32[176,15]{0,1:T(8,128)S(1)}, f32[176,15]{0,1:T(8,128)S(1)}, u32[]{:S(2)}, u32[]{:S(2)}) %collective-permute-start.39) | collective-permute-done | bytes 10592 | tf_op jit(solution)/shard_map/ppermute | solution.py:1085
  1418.6 8.0 collective-permute-done.40
  1444.6 9.2 collective-permute-done.43
  (588 shorter events, 311.1 us)
Async XLA Ops:
  7.2 186.5 %all-gather.9.cloned.1.call-start = ((), (), s32[]{:S(2)}) async-start(), calls=%async_computation.13 | async-start | bytes 8921088 | tf_op jit(solution)/shard_map/all_gather | solution.py:1134
  7.3 12.8 collective-permute-start.3
  10.4 20.4 %collective-permute-start.4 = (bf16[352,352]{1,0:T(8,128)(2,1)}, bf16[352,352]{1,0:T(8,128)(2,1)S(1)}, u32[]{:S(2)}, u32[]{:S(2)}) collective-permute-start(bf16[352,352]{1,0:T(8,128)(2,1)} %param.26), channel_id=1, source_target_pairs={{0,16},{8,24},{16,0},{24,8},{1,17},{9,25},{17,1},{25,9},{2,18},{10... | collective-permute-start | bytes 743432 | tf_op jit(solution)/shard_map/ppermute | solution.py:1067
  13.0 17.9 %collective-permute-start.5 = (bf16[352,352]{1,0:T(8,128)(2,1)}, bf16[352,352]{1,0:T(8,128)(2,1)S(1)}, u32[]{:S(2)}, u32[]{:S(2)}) collective-permute-start(bf16[352,352]{1,0:T(8,128)(2,1)} %param.26), channel_id=1, source_target_pairs={{0,24},{8,0},{16,8},{24,16},{1,25},{9,1},{17,9},{25,17},{2,26},{10... | collective-permute-start | bytes 743432 | tf_op jit(solution)/shard_map/ppermute | solution.py:1067
  33.5 187.2 %all-gather.11.cloned.1.call-start = ((), (), s32[]{:S(2)}) async-start(), calls=%async_computation.14 | async-start | bytes 13381632 | tf_op jit(solution)/shard_map/all_gather | solution.py:1134
  35.6 14.9 %collective-permute-start = (bf16[384,352]{0,1:T(8,128)(2,1)S(1)}, bf16[384,352]{0,1:T(8,128)(2,1)S(1)}, u32[]{:S(2)}, u32[]{:S(2)}) collective-permute-start(bf16[384,352]{0,1:T(8,128)(2,1)S(1)} %pad_maximum_fusion.13), channel_id=1, source_target_pairs={{0,8},{8,16},{16,24},{24,0},{1,9},{9,17},{17,25},{25,1},{2,10},{10... | collective-permute-start | bytes 811016 | tf_op jit(solution)/shard_map/ppermute | solution.py:1067
  41.9 20.2 %collective-permute-start.1 = (bf16[384,352]{0,1:T(8,128)(2,1)S(1)}, bf16[384,352]{0,1:T(8,128)(2,1)S(1)}, u32[]{:S(2)}, u32[]{:S(2)}) collective-permute-start(bf16[384,352]{0,1:T(8,128)(2,1)S(1)} %pad_maximum_fusion.13), channel_id=1, source_target_pairs={{0,16},{8,24},{16,0},{24,8},{1,17},{9,25},{17,1},{25,9},{2,18},{10... | collective-permute-start | bytes 811016 | tf_op jit(solution)/shard_map/ppermute | solution.py:1067
  43.5 18.6 %collective-permute-start.2 = (bf16[384,352]{0,1:T(8,128)(2,1)S(1)}, bf16[384,352]{0,1:T(8,128)(2,1)S(1)}, u32[]{:S(2)}, u32[]{:S(2)}) collective-permute-start(bf16[384,352]{0,1:T(8,128)(2,1)S(1)} %pad_maximum_fusion.13), channel_id=1, source_target_pairs={{0,24},{8,0},{16,8},{24,16},{1,25},{9,1},{17,9},{25,17},{2,26},{10... | collective-permute-start | bytes 811016 | tf_op jit(solution)/shard_map/ppermute | solution.py:1067
  44.4 49.3 %collective-permute-start.12 = (bf16[176,1056]{1,0:T(8,128)(2,1)S(1)}, bf16[176,1056]{1,0:T(8,128)(2,1)S(1)}, u32[]{:S(2)}, u32[]{:S(2)}) collective-permute-start(bf16[176,1056]{1,0:T(8,128)(2,1)S(1)} %copy-done.53), channel_id=1, source_target_pairs={{0,8},{8,16},{16,24},{24,0},{1,9},{9,17},{17,25},{25,1},{2,10},{10... | collective-permute-start | bytes 1115144 | tf_op jit(solution)/shard_map/ppermute | solution.py:1067
  45.6 48.2 %collective-permute-start.13 = (bf16[176,1056]{1,0:T(8,128)(2,1)S(1)}, bf16[176,1056]{1,0:T(8,128)(2,1)S(1)}, u32[]{:S(2)}, u32[]{:S(2)}) collective-permute-start(bf16[176,1056]{1,0:T(8,128)(2,1)S(1)} %copy-done.53), channel_id=1, source_target_pairs={{0,16},{8,24},{16,0},{24,8},{1,17},{9,25},{17,1},{25,9},{2,18},{10... | collective-permute-start | bytes 1115144 | tf_op jit(solution)/shard_map/ppermute | solution.py:1067
  50.5 43.2 %collective-permute-start.14 = (bf16[176,1056]{1,0:T(8,128)(2,1)S(1)}, bf16[176,1056]{1,0:T(8,128)(2,1)S(1)}, u32[]{:S(2)}, u32[]{:S(2)}) collective-permute-start(bf16[176,1056]{1,0:T(8,128)(2,1)S(1)} %copy-done.53), channel_id=1, source_target_pairs={{0,24},{8,0},{16,8},{24,16},{1,25},{9,1},{17,9},{25,17},{2,26},{10... | collective-permute-start | bytes 1115144 | tf_op jit(solution)/shard_map/ppermute | solution.py:1067
  99.4 335.4 %all-gather.13.cloned.1.call-start = ((), (), s32[]{:S(2)}) async-start(), calls=%async_computation.15 | async-start | bytes 13381632 | tf_op jit(solution)/shard_map/all_gather | solution.py:1134
  100.7 30.9 %collective-permute-start.15 = (bf16[176,1056]{1,0:T(8,128)(2,1)S(1)}, bf16[176,1056]{1,0:T(8,128)(2,1)S(1)}, u32[]{:S(2)}, u32[]{:S(2)}) collective-permute-start(bf16[176,1056]{1,0:T(8,128)(2,1)S(1)} %concatenate.108), channel_id=1, source_target_pairs={{0,8},{8,16},{16,24},{24,0},{1,9},{9,17},{17,25},{25,1},{2,10},{10... | collective-permute-start | bytes 1115144 | tf_op jit(solution)/shard_map/ppermute | solution.py:1067
  121.9 21.1 %collective-permute-start.16 = (bf16[176,1056]{1,0:T(8,128)(2,1)S(1)}, bf16[176,1056]{1,0:T(8,128)(2,1)S(1)}, u32[]{:S(2)}, u32[]{:S(2)}) collective-permute-start(bf16[176,1056]{1,0:T(8,128)(2,1)S(1)} %concatenate.108), channel_id=1, source_target_pairs={{0,16},{8,24},{16,0},{24,8},{1,17},{9,25},{17,1},{25,9},{2,18},{10... | collective-permute-start | bytes 1115144 | tf_op jit(solution)/shard_map/ppermute | solution.py:1067
  121.9 26.9 %collective-permute-start.17 = (bf16[176,1056]{1,0:T(8,128)(2,1)S(1)}, bf16[176,1056]{1,0:T(8,128)(2,1)S(1)}, u32[]{:S(2)}, u32[]{:S(2)}) collective-permute-start(bf16[176,1056]{1,0:T(8,128)(2,1)S(1)} %concatenate.108), channel_id=1, source_target_pairs={{0,24},{8,0},{16,8},{24,16},{1,25},{9,1},{17,9},{25,17},{2,26},{10... | collective-permute-start | bytes 1115144 | tf_op jit(solution)/shard_map/ppermute | solution.py:1067
  163.6 310.6 %all-gather.15.cloned.1.call-start = ((), (), s32[]{:S(2)}) async-start(), calls=%async_computation.16 | async-start | bytes 6488064 | tf_op jit(solution)/shard_map/all_gather | solution.py:1134
  179.4 14.3 collective-permute-start.11
  181.4 30.0 %collective-permute-start.18 = (bf16[128,704]{1,0:T(8,128)(2,1)}, bf16[128,704]{1,0:T(8,128)(2,1)S(1)}, u32[]{:S(2)}, u32[]{:S(2)}) collective-permute-start(bf16[128,704]{1,0:T(8,128)(2,1)} %copy.90), channel_id=1, source_target_pairs={{0,8},{8,16},{16,24},{24,0},{1,9},{9,17},{17,25},{25,1},{2,10},{10... | collective-permute-start | bytes 540680 | tf_op jit(solution)/shard_map/ppermute | solution.py:1067
  190.1 21.3 %collective-permute-start.19 = (bf16[128,704]{1,0:T(8,128)(2,1)}, bf16[128,704]{1,0:T(8,128)(2,1)}, u32[]{:S(2)}, u32[]{:S(2)}) collective-permute-start(bf16[128,704]{1,0:T(8,128)(2,1)} %copy.90), channel_id=1, source_target_pairs={{0,16},{8,24},{16,0},{24,8},{1,17},{9,25},{17,1},{25,9},{2,18},{10... | collective-permute-start | bytes 540680 | tf_op jit(solution)/shard_map/ppermute | solution.py:1067
  193.4 18.6 %collective-permute-start.20 = (bf16[128,704]{1,0:T(8,128)(2,1)}, bf16[128,704]{1,0:T(8,128)(2,1)}, u32[]{:S(2)}, u32[]{:S(2)}) collective-permute-start(bf16[128,704]{1,0:T(8,128)(2,1)} %copy.90), channel_id=1, source_target_pairs={{0,24},{8,0},{16,8},{24,16},{1,25},{9,1},{17,9},{25,17},{2,26},{10... | collective-permute-start | bytes 540680 | tf_op jit(solution)/shard_map/ppermute | solution.py:1067
  236.6 65.9 %all-to-all-start = ((bf16[8,3,2,88,512]{4,3,2,1,0:T(8,128)(2,1)}), bf16[8,3,2,88,512]{4,3,2,1,0:T(8,128)(2,1)}, u32[]{:S(2)}, u32[]{:S(2)}) async-start(bf16[8,3,2,88,512]{4,3,2,1,0:T(8,128)(2,1)} %get-tuple-element.102.own_ref), calls=%async_computation | async-start | bytes 8650752 | tf_op jit(solution)/shard_map/all_to_all | solution.py:1057
  241.3 279.8 %all-gather.17.cloned.1.call-start = ((), (), s32[]{:S(2)}) async-start(), calls=%async_computation.17 | async-start | bytes 19464192 | tf_op jit(solution)/shard_map/all_gather | solution.py:1134
  241.4 17.1 %collective-permute-start.21 = (bf16[176,1536]{1,0:T(8,128)(2,1)S(1)}, bf16[176,1536]{1,0:T(8,128)(2,1)S(1)}, u32[]{:S(2)}, u32[]{:S(2)}) collective-permute-start(bf16[176,1536]{1,0:T(8,128)(2,1)S(1)} %copy-done.49), channel_id=1, source_target_pairs={{0,8},{8,16},{16,24},{24,0},{1,9},{9,17},{17,25},{25,1},{2,10},{10... | collective-permute-start | bytes 1622024 | tf_op jit(solution)/shard_map/ppermute | solution.py:1067
  243.6 37.4 %collective-permute-start.22 = (bf16[176,1536]{1,0:T(8,128)(2,1)S(1)}, bf16[176,1536]{1,0:T(8,128)(2,1)S(1)}, u32[]{:S(2)}, u32[]{:S(2)}) collective-permute-start(bf16[176,1536]{1,0:T(8,128)(2,1)S(1)} %copy-done.49), channel_id=1, source_target_pairs={{0,16},{8,24},{16,0},{24,8},{1,17},{9,25},{17,1},{25,9},{2,18},{10... | collective-permute-start | bytes 1622024 | tf_op jit(solution)/shard_map/ppermute | solution.py:1067
  243.6 37.4 %collective-permute-start.23 = (bf16[176,1536]{1,0:T(8,128)(2,1)S(1)}, bf16[176,1536]{1,0:T(8,128)(2,1)S(1)}, u32[]{:S(2)}, u32[]{:S(2)}) collective-permute-start(bf16[176,1536]{1,0:T(8,128)(2,1)S(1)} %copy-done.49), channel_id=1, source_target_pairs={{0,24},{8,0},{16,8},{24,16},{1,25},{9,1},{17,9},{25,17},{2,26},{10... | collective-permute-start | bytes 1622024 | tf_op jit(solution)/shard_map/ppermute | solution.py:1067
  319.8 67.3 %all-to-all-start.2 = ((bf16[8,3,2,88,512]{4,3,2,1,0:T(8,128)(2,1)}), bf16[8,3,2,88,512]{4,3,2,1,0:T(8,128)(2,1)}, u32[]{:S(2)}, u32[]{:S(2)}) async-start(bf16[8,3,2,88,512]{4,3,2,1,0:T(8,128)(2,1)} %get-tuple-element.104.own_ref), calls=%async_computation.2 | async-start | bytes 8650752 | tf_op jit(solution)/shard_map/all_to_all | solution.py:1057
  387.1 38.1 %all-to-all-start.1 = ((bf16[8,2,88,512]{3,2,1,0:T(8,128)(2,1)}), bf16[8,2,88,512]{3,2,1,0:T(8,128)(2,1)S(1)}, u32[]{:S(2)}, u32[]{:S(2)}) async-start(bf16[8,2,88,512]{3,2,1,0:T(8,128)(2,1)} %get-tuple-element.103.att_ref), calls=%async_computation.1 | async-start | bytes 2883584 | tf_op jit(solution)/shard_map/all_to_all | solution.py:1057
  425.2 32.0 %all-to-all-start.3 = ((bf16[8,2,88,512]{3,2,1,0:T(8,128)(2,1)}), bf16[8,2,88,512]{3,2,1,0:T(8,128)(2,1)S(1)}, u32[]{:S(2)}, u32[]{:S(2)}) async-start(bf16[8,2,88,512]{3,2,1,0:T(8,128)(2,1)} %get-tuple-element.105.att_ref), calls=%async_computation.3 | async-start | bytes 2883584 | tf_op jit(solution)/shard_map/all_to_all | solution.py:1057
  429.4 161.1 %all-gather.19.cloned.1.call-start = ((), (), s32[]{:S(2)}) async-start(), calls=%async_computation.18 | async-start | bytes 19464192 | tf_op jit(solution)/shard_map/all_gather | solution.py:1134
  429.4 38.4 %collective-permute-start.24 = (bf16[768,352]{0,1:T(8,128)(2,1)S(1)}, bf16[768,352]{0,1:T(8,128)(2,1)}, u32[]{:S(2)}, u32[]{:S(2)}) collective-permute-start(bf16[768,352]{0,1:T(8,128)(2,1)S(1)} %copy-done.50), channel_id=1, source_target_pairs={{0,8},{8,16},{16,24},{24,0},{1,9},{9,17},{17,25},{25,1},{2,10},{10... | collective-permute-start | bytes 1622024 | tf_op jit(solution)/shard_map/ppermute | solution.py:1067
  431.0 38.4 %collective-permute-start.25 = (bf16[768,352]{0,1:T(8,128)(2,1)S(1)}, bf16[768,352]{0,1:T(8,128)(2,1)}, u32[]{:S(2)}, u32[]{:S(2)}) collective-permute-start(bf16[768,352]{0,1:T(8,128)(2,1)S(1)} %copy-done.50), channel_id=1, source_target_pairs={{0,16},{8,24},{16,0},{24,8},{1,17},{9,25},{17,1},{25,9},{2,18},{10... | collective-permute-start | bytes 1622024 | tf_op jit(solution)/shard_map/ppermute | solution.py:1067
  433.4 36.0 %collective-permute-start.26 = (bf16[768,352]{0,1:T(8,128)(2,1)S(1)}, bf16[768,352]{0,1:T(8,128)(2,1)}, u32[]{:S(2)}, u32[]{:S(2)}) collective-permute-start(bf16[768,352]{0,1:T(8,128)(2,1)S(1)} %copy-done.50), channel_id=1, source_target_pairs={{0,24},{8,0},{16,8},{24,16},{1,25},{9,1},{17,9},{25,17},{2,26},{10... | collective-permute-start | bytes 1622024 | tf_op jit(solution)/shard_map/ppermute | solution.py:1067
  472.5 303.7 %reduce-scatter.6.cloned.1.call-start = ((), (), s32[]{:S(2)}) async-start(), calls=%async_computation.19 | async-start | bytes 19464192 | tf_op jit(solution)/shard_map/reduce_scatter | solution.py:1129
  657.4 420.7 %reduce-scatter.10.cloned.1.call-start = ((), (), s32[]{:S(2)}) async-start(), calls=%async_computation.21 | async-start | bytes 19464192 | tf_op jit(solution)/shard_map/reduce_scatter | solution.py:1129
  819.4 38.7 %all-to-all-start.4 = ((bf16[8,2,88,512]{3,2,1,0:T(8,128)(2,1)}), bf16[8,2,88,512]{3,2,1,0:T(8,128)(2,1)}, u32[]{:S(2)}, u32[]{:S(2)}) async-start(bf16[8,2,88,512]{3,2,1,0:T(8,128)(2,1)} %bitcast.201), calls=%async_computation.5 | async-start | bytes 2883584 | tf_op jit(solution)/shard_map/all_to_all | solution.py:1057
  823.7 318.7 %reduce-scatter.8.cloned.1.call-start = ((), (), s32[]{:S(2)}) async-start(), calls=%async_computation.20 | async-start | bytes 18247680 | tf_op jit(solution)/shard_map/reduce_scatter | solution.py:1129
  860.0 107.1 %collective-permute-start.27 = (bf16[768,352]{0,1:T(8,128)(2,1)}, bf16[768,352]{0,1:T(8,128)(2,1)S(1)}, u32[]{:S(2)}, u32[]{:S(2)}) collective-permute-start(bf16[768,352]{0,1:T(8,128)(2,1)} %copy.101), channel_id=1, source_target_pairs={{0,8},{8,16},{16,24},{24,0},{1,9},{9,17},{17,25},{25,1},{2,10},{10... | collective-permute-start | bytes 1622024 | tf_op jit(solution)/shard_map/ppermute | solution.py:1085
  862.6 104.5 %collective-permute-start.29 = (bf16[768,352]{0,1:T(8,128)(2,1)}, bf16[768,352]{0,1:T(8,128)(2,1)}, u32[]{:S(2)}, u32[]{:S(2)}) collective-permute-start(bf16[768,352]{0,1:T(8,128)(2,1)} %copy.103), channel_id=1, source_target_pairs={{0,24},{8,0},{16,8},{24,16},{1,25},{9,1},{17,9},{25,17},{2,26},{10... | collective-permute-start | bytes 1622024 | tf_op jit(solution)/shard_map/ppermute | solution.py:1085
  866.7 100.4 %collective-permute-start.28 = (bf16[768,352]{0,1:T(8,128)(2,1)}, bf16[768,352]{0,1:T(8,128)(2,1)}, u32[]{:S(2)}, u32[]{:S(2)}) collective-permute-start(bf16[768,352]{0,1:T(8,128)(2,1)} %copy.102), channel_id=1, source_target_pairs={{0,16},{8,24},{16,0},{24,8},{1,17},{9,25},{17,1},{25,9},{2,18},{10... | collective-permute-start | bytes 1622024 | tf_op jit(solution)/shard_map/ppermute | solution.py:1085
  873.8 100.5 %all-to-all-start.5 = ((bf16[8,2,88,512]{3,2,1,0:T(8,128)(2,1)}), bf16[8,2,88,512]{3,2,1,0:T(8,128)(2,1)}, u32[]{:S(2)}, u32[]{:S(2)}) async-start(bf16[8,2,88,512]{3,2,1,0:T(8,128)(2,1)} %bitcast.200), calls=%async_computation.8 | async-start | bytes 2883584 | tf_op jit(solution)/shard_map/all_to_all | solution.py:1057
  974.3 94.2 %all-to-all-start.7 = ((bf16[8,3,2,88,512]{4,3,2,1,0:T(8,128)(2,1)}), bf16[8,3,2,88,512]{4,3,2,1,0:T(8,128)(2,1)}, u32[]{:S(2)}, u32[]{:S(2)}) async-start(bf16[8,3,2,88,512]{4,3,2,1,0:T(8,128)(2,1)} %shard_map.321), calls=%async_computation.10 | async-start | bytes 8650752 | tf_op jit(solution)/shard_map/all_to_all | solution.py:1057
  1068.5 74.0 %all-to-all-start.6 = ((bf16[8,3,2,88,512]{4,3,2,1,0:T(8,128)(2,1)}), bf16[8,3,2,88,512]{4,3,2,1,0:T(8,128)(2,1)}, u32[]{:S(2)}, u32[]{:S(2)}) async-start(bf16[8,3,2,88,512]{4,3,2,1,0:T(8,128)(2,1)} %shard_map.322), calls=%async_computation.9 | async-start | bytes 8650752 | tf_op jit(solution)/shard_map/all_to_all | solution.py:1057
  1073.1 110.3 %all-gather.21.cloned.1.call-start = ((), (), s32[]{:S(2)}) async-start(), calls=%async_computation.22 | async-start | bytes 4866048 | tf_op jit(solution)/shard_map/all_gather | solution.py:1134
  1079.9 17.0 %collective-permute-start.30 = (bf16[176,1536]{1,0:T(8,128)(2,1)S(1)}, bf16[176,1536]{1,0:T(8,128)(2,1)S(1)}, u32[]{:S(2)}, u32[]{:S(2)}) collective-permute-start(bf16[176,1536]{1,0:T(8,128)(2,1)S(1)} %get-tuple-element.270), channel_id=1, source_target_pairs={{0,8},{8,16},{16,24},{24,0},{1,9},{9,17},{17,25},{25,1},{2,10},{10... | collective-permute-start | bytes 1622024 | tf_op jit(solution)/shard_map/ppermute | solution.py:1085
  1081.5 25.6 %collective-permute-start.32 = (bf16[176,1536]{1,0:T(8,128)(2,1)S(1)}, bf16[176,1536]{1,0:T(8,128)(2,1)S(1)}, u32[]{:S(2)}, u32[]{:S(2)}) collective-permute-start(bf16[176,1536]{1,0:T(8,128)(2,1)S(1)} %get-tuple-element.269), channel_id=1, source_target_pairs={{0,24},{8,0},{16,8},{24,16},{1,25},{9,1},{17,9},{25,17},{2,26},{10... | collective-permute-start | bytes 1622024 | tf_op jit(solution)/shard_map/ppermute | solution.py:1085
  1085.5 45.5 %collective-permute-start.31 = (bf16[176,1536]{1,0:T(8,128)(2,1)S(1)}, bf16[176,1536]{1,0:T(8,128)(2,1)S(1)}, u32[]{:S(2)}, u32[]{:S(2)}) collective-permute-start(bf16[176,1536]{1,0:T(8,128)(2,1)S(1)} %select_select_fusion.4), channel_id=1, source_target_pairs={{0,16},{8,24},{16,0},{24,8},{1,17},{9,25},{17,1},{25,9},{2,18},{10... | collective-permute-start | bytes 1622024 | tf_op jit(solution)/shard_map/ppermute | solution.py:1085
  1147.1 146.2 %reduce-scatter.12.cloned.1.call-start = ((), (), s32[]{:S(2)}) async-start(), calls=%async_computation.23 | async-start | bytes 13381632 | tf_op jit(solution)/shard_map/reduce_scatter | solution.py:1129
  1203.4 226.5 %reduce-scatter.14.cloned.1.call-start = ((), (), s32[]{:S(2)}) async-start(), calls=%async_computation.24 | async-start | bytes 8921088 | tf_op jit(solution)/shard_map/reduce_scatter | solution.py:1129
  1210.4 33.0 %collective-permute-start.33 = (bf16[176,1056]{1,0:T(8,128)(2,1)}, bf16[176,1056]{1,0:T(8,128)(2,1)}, u32[]{:S(2)}, u32[]{:S(2)}) collective-permute-start(bf16[176,1056]{1,0:T(8,128)(2,1)} %get-tuple-element.295), channel_id=1, source_target_pairs={{0,8},{8,16},{16,24},{24,0},{1,9},{9,17},{17,25},{25,1},{2,10},{10... | collective-permute-start | bytes 1115144 | tf_op jit(solution)/shard_map/ppermute | solution.py:1085
  1211.9 31.5 %collective-permute-start.34 = (bf16[176,1056]{1,0:T(8,128)(2,1)}, bf16[176,1056]{1,0:T(8,128)(2,1)}, u32[]{:S(2)}, u32[]{:S(2)}) collective-permute-start(bf16[176,1056]{1,0:T(8,128)(2,1)} %get-tuple-element.294), channel_id=1, source_target_pairs={{0,16},{8,24},{16,0},{24,8},{1,17},{9,25},{17,1},{25,9},{2,18},{10... | collective-permute-start | bytes 1115144 | tf_op jit(solution)/shard_map/ppermute | solution.py:1085
  1214.4 29.0 %collective-permute-start.35 = (bf16[176,1056]{1,0:T(8,128)(2,1)}, bf16[176,1056]{1,0:T(8,128)(2,1)}, u32[]{:S(2)}, u32[]{:S(2)}) collective-permute-start(bf16[176,1056]{1,0:T(8,128)(2,1)} %get-tuple-element.293), channel_id=1, source_target_pairs={{0,24},{8,0},{16,8},{24,16},{1,25},{9,1},{17,9},{25,17},{2,26},{10... | collective-permute-start | bytes 1115144 | tf_op jit(solution)/shard_map/ppermute | solution.py:1085
  1297.9 19.8 %collective-permute-start.45 = (f32[2,1408]{1,0:T(2,128)S(1)}, f32[2,1408]{1,0:T(2,128)S(1)}, u32[]{:S(2)}, u32[]{:S(2)}) collective-permute-start(f32[2,1408]{1,0:T(2,128)S(1)} %bitcast_reduce_fusion), channel_id=1, source_target_pairs={{0,1},{1,0},{2,3},{3,2},{4,5},{5,4},{6,7},{7,6},{8,9},{9,8},{10,11... | collective-permute-start | bytes 33800 | tf_op jit(solution)/shard_map/ppermute | solution.py:1122
  1340.0 15.9 %collective-permute-start.51 = (bf16[464,352]{1,0:T(8,128)(2,1)S(1)}, bf16[464,352]{1,0:T(8,128)(2,1)S(1)}, u32[]{:S(2)}, u32[]{:S(2)}) collective-permute-start(bf16[464,352]{1,0:T(8,128)(2,1)S(1)} %select_select_fusion.30), channel_id=1, source_target_pairs={{0,8},{8,16},{16,24},{24,0},{1,9},{9,17},{17,25},{25,1},{2,10},{10... | collective-permute-start | bytes 979976 | tf_op jit(solution)/shard_map/ppermute | solution.py:1085
  1344.3 22.9 %collective-permute-start.52 = (bf16[464,352]{1,0:T(8,128)(2,1)S(1)}, bf16[464,352]{1,0:T(8,128)(2,1)S(1)}, u32[]{:S(2)}, u32[]{:S(2)}) collective-permute-start(bf16[464,352]{1,0:T(8,128)(2,1)S(1)} %select_select_fusion.29), channel_id=1, source_target_pairs={{0,16},{8,24},{16,0},{24,8},{1,17},{9,25},{17,1},{25,9},{2,18},{10... | collective-permute-start | bytes 979976 | tf_op jit(solution)/shard_map/ppermute | solution.py:1085
  1346.7 20.6 %collective-permute-start.53 = (bf16[464,352]{1,0:T(8,128)(2,1)S(1)}, bf16[464,352]{1,0:T(8,128)(2,1)S(1)}, u32[]{:S(2)}, u32[]{:S(2)}) collective-permute-start(bf16[464,352]{1,0:T(8,128)(2,1)S(1)} %select_select_fusion.28), channel_id=1, source_target_pairs={{0,24},{8,0},{16,8},{24,16},{1,25},{9,1},{17,9},{25,17},{2,26},{10... | collective-permute-start | bytes 979976 | tf_op jit(solution)/shard_map/ppermute | solution.py:1085
  1380.0 11.6 collective-permute-start.38
  1381.9 48.0 %collective-permute-start.54 = (bf16[176,1056]{1,0:T(8,128)(2,1)S(1)}, bf16[176,1056]{1,0:T(8,128)(2,1)S(1)}, u32[]{:S(2)}, u32[]{:S(2)}) collective-permute-start(bf16[176,1056]{1,0:T(8,128)(2,1)S(1)} %get-tuple-element.305), channel_id=1, source_target_pairs={{0,8},{8,16},{16,24},{24,0},{1,9},{9,17},{17,25},{25,1},{2,10},{10... | collective-permute-start | bytes 1115144 | tf_op jit(solution)/shard_map/ppermute | solution.py:1085
  1390.1 39.8 %collective-permute-start.56 = (bf16[176,1056]{1,0:T(8,128)(2,1)S(1)}, bf16[176,1056]{1,0:T(8,128)(2,1)S(1)}, u32[]{:S(2)}, u32[]{:S(2)}) collective-permute-start(bf16[176,1056]{1,0:T(8,128)(2,1)S(1)} %get-tuple-element.304), channel_id=1, source_target_pairs={{0,24},{8,0},{16,8},{24,16},{1,25},{9,1},{17,9},{25,17},{2,26},{10... | collective-permute-start | bytes 1115144 | tf_op jit(solution)/shard_map/ppermute | solution.py:1085
  1390.2 39.7 %collective-permute-start.55 = (bf16[176,1056]{1,0:T(8,128)(2,1)S(1)}, bf16[176,1056]{1,0:T(8,128)(2,1)S(1)}, u32[]{:S(2)}, u32[]{:S(2)}) collective-permute-start(bf16[176,1056]{1,0:T(8,128)(2,1)S(1)} %select_select_fusion.15), channel_id=1, source_target_pairs={{0,16},{8,24},{16,0},{24,8},{1,17},{9,25},{17,1},{25,9},{2,18},{10... | collective-permute-start | bytes 1115144 | tf_op jit(solution)/shard_map/ppermute | solution.py:1085
  1391.7 25.8 %collective-permute-start.39 = (f32[176,15]{0,1:T(8,128)S(1)}, f32[176,15]{0,1:T(8,128)S(1)}, u32[]{:S(2)}, u32[]{:S(2)}) collective-permute-start(f32[176,15]{0,1:T(8,128)S(1)} %get-tuple-element.345), channel_id=1, source_target_pairs={{0,8},{8,16},{16,24},{24,0},{1,9},{9,17},{17,25},{25,1},{2,10},{10... | collective-permute-start | bytes 31688 | tf_op jit(solution)/shard_map/ppermute | solution.py:1085
  1392.9 33.8 %collective-permute-start.40 = (f32[176,15]{0,1:T(8,128)S(1)}, f32[176,15]{0,1:T(8,128)S(1)}, u32[]{:S(2)}, u32[]{:S(2)}) collective-permute-start(f32[176,15]{0,1:T(8,128)S(1)} %get-tuple-element.346), channel_id=1, source_target_pairs={{0,16},{8,24},{16,0},{24,8},{1,17},{9,25},{17,1},{25,9},{2,18},{10... | collective-permute-start | bytes 31688 | tf_op jit(solution)/shard_map/ppermute | solution.py:1085
  1433.2 11.4 collective-permute-start.42
  1435.7 18.1 %collective-permute-start.43 = (bf16[352,352]{1,0:T(8,128)(2,1)S(1)}, bf16[352,352]{1,0:T(8,128)(2,1)S(1)}, u32[]{:S(2)}, u32[]{:S(2)}) collective-permute-start(bf16[352,352]{1,0:T(8,128)(2,1)S(1)} %get-tuple-element.315), channel_id=1, source_target_pairs={{0,16},{8,24},{16,0},{24,8},{1,17},{9,25},{17,1},{25,9},{2,18},{10... | collective-permute-start | bytes 743432 | tf_op jit(solution)/shard_map/ppermute | solution.py:1085
  1437.2 16.6 %collective-permute-start.44 = (bf16[352,352]{1,0:T(8,128)(2,1)S(1)}, bf16[352,352]{1,0:T(8,128)(2,1)S(1)}, u32[]{:S(2)}, u32[]{:S(2)}) collective-permute-start(bf16[352,352]{1,0:T(8,128)(2,1)S(1)} %select_select_fusion.31), channel_id=1, source_target_pairs={{0,24},{8,0},{16,8},{24,16},{1,25},{9,1},{17,9},{25,17},{2,26},{10... | collective-permute-start | bytes 743432 | tf_op jit(solution)/shard_map/ppermute | solution.py:1085
  (132 other events, 1686.1 us)
Sparse Core Ops, SparseCore 0:
  33.6 59.1 all-gather.8
  99.5 87.6 all-gather.10
  189.1 92.3 all-gather.12
  283.2 95.5 all-gather.14
  380.5 116.4 all-gather.16
  498.8 91.6 all-gather.18
  657.6 118.5 reduce-scatter.5
  780.2 141.0 reduce-scatter.9
  925.0 178.5 reduce-scatter.7
  1147.2 36.2 all-gather.20
  1203.5 89.7 reduce-scatter.11
  1296.7 69.4 reduce-scatter.13

commit v3 on v2

--- a/solution.py
+++ b/solution.py
@@ -1068,13 +1068,15 @@
     ]
 
 
-def widen(pieces, first=None):
+def widen(pieces, first=None, joined=1):
     devices, me = lax.axis_size("dp"), lax.axis_index("dp")
     if first is not None:
         pieces = after(first, *pieces)
-    return jnp.concatenate(
-        [lax.select_n((me - at) % devices, *pieces) for at in range(devices)], axis=1
-    )
+    slots = [lax.select_n((me - at) % devices, *pieces) for at in range(devices)]
+    if joined > 1:
+        split = [jnp.split(slot, joined, axis=1) for slot in slots]
+        slots = [each for group in zip(*split) for each in group]
+    return jnp.concatenate(slots, axis=1)
 
 
 def narrow_blocks(blocks, first=None):
@@ -1179,7 +1181,10 @@
     row_count = images * tile_len
     out_width = cotangent.shape[3]
 
-    part_skip = widen(fetch(w_skip))
+    f_skip = lax.all_gather(w_skip, EVERY, axis=0, tiled=True).reshape(
+        dp_devices, -1, w_skip.shape[1]
+    )
+    f_skip = jnp.swapaxes(f_skip, 0, 1).reshape(f_skip.shape[1], -1)
     small = jnp.concatenate([w_patch, w_final, norm_params], axis=1)
     small_widths = (w_patch.shape[1], w_final.shape[1], norm_params.shape[1])
     cuts = (0, small_widths[0], sum(small_widths[:2]), sum(small_widths))
@@ -1194,7 +1199,6 @@
     f_patch, f_final, f_norms = (
         f_small[:, :, cuts[at] : cuts[at + 1]].reshape(f_small.shape[0], -1) for at in range(3)
     )
-    f_skip = tiles_whole(part_skip)
     held_qkv = fetch(w_qkv)
     held_three = fetch(jnp.concatenate([w_out, w_query, w_cross], axis=1))
     held_text = fetch(w_text)
@@ -1245,8 +1249,7 @@
     bias_skip = jnp.concatenate([norm_f[:, 9], norm_f[:, 11]])[None]
     joined, joined_inv, skip_in = join_norm(patch_rows, skip_rows, f_patch, gain_skip, bias_skip)
     f_qkv = tiles_whole(widen(held_qkv, skip_in))
-    part_three = widen(held_three, skip_in).reshape(-1, dp_devices, 3, w_out.shape[1])
-    part_three = jnp.swapaxes(part_three, 1, 2).reshape(part_three.shape[0], -1)
+    part_three = widen(held_three, skip_in, 3)
     f_three = tiles_whole(part_three)
     f_out, f_query, f_cross = jnp.split(f_three, 3, axis=1)
     residual = plain_dot(skip_in, f_skip)
@@ -1329,7 +1332,6 @@
     low_three = grad_three.astype(BF16)
     d_cross = plain_dot(cross_cols, low_three).astype(BF16)
     grad_crossed = dot_over(f_cross, low_three, 1, 1).astype(BF16)
-    t_down, grad_crossed = lax.optimization_barrier((t_down, grad_crossed))
     grad_cross_q, d_text_key, d_text_value = cross_back(
         cross_queries,
         text_kv,
@@ -1341,6 +1343,7 @@
         query_scale,
         score_scale,
     )
+    t_down, grad_cross_q = lax.optimization_barrier((t_down, grad_cross_q))
     grad_cross_q = grad_cross_q.reshape(model_width, row_count)
     d_query = dot_over(third_in, grad_cross_q, 0, 1).astype(BF16)
     grad_third = dot_over(grad_cross_q, f_query, 0, 1)
@@ -1382,8 +1385,8 @@
     for image in range(images):
         if image == images - 1:
             up_grad = narrow(t_up, tile_back)
-            t_joint, up_grad, own_grads[-1], grad_qkv = lax.optimization_barrier(
-                (t_joint, up_grad, own_grads[-1], grad_qkv)
+            up_grad, own_grads[-1], grad_qkv = lax.optimization_barrier(
+                (up_grad, own_grads[-1], grad_qkv)
             )
         grad_qkv = head_back(
             own_grads[image],
@@ -1404,8 +1407,8 @@
     own_key = lax.dynamic_slice_in_dim(text_kv[0], grid_at * group_heads, group_heads, 0)
     ck_z, ck_inv = layer_norm(jnp.swapaxes(own_key, 1, 2))
     grad_ckey = jnp.swapaxes(norm_back(jnp.swapaxes(sum_text_kv[0], 1, 2), ck_z, ck_inv), 1, 2)
-    grad_kv = tiles_whole(jnp.stack([grad_ckey, sum_text_kv[1]]).astype(BF16)[None])
-    grad_kv, grad_qkv = lax.optimization_barrier((grad_kv, grad_qkv))
+    grad_kv = jnp.stack([grad_ckey, sum_text_kv[1]]).astype(BF16)
+    grad_kv = tiles_whole(grad_kv.reshape(-1, images * text_pad))
     grad_qkv = grad_qkv.reshape(3 * model_width, row_count)
     d_qkv = dot_over(first_in, grad_qkv, 0, 1).astype(BF16)
     d_qkv, grad_qkv = lax.optimization_barrier((d_qkv, grad_qkv))
@@ -1428,11 +1431,14 @@
     out_grad, query_w_grad, cross_grad = jnp.split(joint_grad, 3, axis=1)
     t_skip = over_tiles(d_skip_w)
 
-    grad_kv = jnp.transpose(grad_kv, (1, 0, 2, 3, 4)).reshape(2 * model_width, images * text_pad)
+    group_shape = (-1, 2, grid_devices, model_width // grid_devices)
     text_slice = text_states.shape[2] // grid_devices
     text_cols = lax.dynamic_slice_in_dim(text_rows, grid_at * text_slice, text_slice, 1)
     d_text = dot_over(text_cols, grad_kv, 0, 1).astype(BF16)
-    text_grad = dot_over(grad_kv, part_text, 0, 1).reshape(images, text_pad, text_slice)
+    d_text = jnp.swapaxes(d_text.reshape(text_slice, grid_devices, 2, -1), 1, 2)
+    d_text = d_text.reshape(text_slice, -1)
+    grouped_text = jnp.swapaxes(part_text.reshape(group_shape), 1, 2).reshape(part_text.shape)
+    text_grad = dot_over(grad_kv, grouped_text, 0, 1).reshape(images, text_pad, text_slice)
     text_grad = text_grad[:, :text_len]
 
     shift_low = total_tiles(part_shift).astype(BF16)
@@ -1451,8 +1457,9 @@
         late.append(
             jnp.concatenate([pair[:, :width], pair[:, width:], d_time[:, own], d_shift[:, own]])
         )
+    qkv_grad = narrow(t_qkv, d_text)
+    qkv_grad, *late = lax.optimization_barrier((qkv_grad, *late))
     late = narrow_blocks(late)
-    qkv_grad = narrow(t_qkv, late)
     rows = d_text.shape[0]
     text_w_grad = jnp.concatenate([late[:rows], late[rows : 2 * rows]], axis=1)
     time_w_grad, shift_w_grad = jnp.split(late[2 * rows :], [d_time.shape[0]], axis=0)

time: 1480 us -> 1470 us (level)
  waiting for transfers between devices: 356 us -> 338 us
    all_gather x7 -> x6, waiting for transfers between devices: 55.4 us -> 29 us  [tiles_whole(): return lax.all_gather(weight, TILE, axis=0, tiled=True)]
    all_to_all x8, waiting for transfers between devices: 77.7 us -> 99.3 us  [swap_tiles(): lax.all_to_all(values_in, TILE, split_axis=0, concat_axis=0, tiled=True)]
    reshape x2, local copies, waits for them, and re-layouts: 9.66 us -> 27.9 us  [the longest x1 16.2 us: local_heads(): lax.all_gather(w_skip, EVERY, axis=0, tiled=True)]
    reduce_scatter x5, waiting for transfers between devices: 15.6 us -> 0.08 us  [over_tiles(): lax.psum_scatter(weight_grad, TILE, scatter_dimension=0, tiled=True)]
    ppermute x21 -> x18, starting transfers between devices: 67.8 us -> 60.4 us  [fetch(): lax.ppermute(weight, 'dp', shift_pairs(devices, step))]
    ppermute x21 -> x18, waiting for transfers between devices: 88.3 us -> 94.9 us  [fetch(): lax.ppermute(weight, 'dp', shift_pairs(devices, step))]
  transfers between devices with their start and end apart: 77 -> 74, of which waited for: 38 -> 34; matrix products, arithmetic and copies ran while one was open for 30% -> 33% of each run, Pallas kernels for 25% -> 25%
where the time goes in v3:
time: 1470 us; the launch traced here: 1460 us
  matrix products  380 us (26%)
  Pallas kernels  367 us (25%)
  waiting for transfers between devices  338 us (23%)
  starting transfers between devices  153 us (10%)
  local copies, waits for them, and re-layouts  107 us (7%)
  other arithmetic  78.9 us (5%)
  blocking collectives  16.9 us (1%)
  between operations  16.5 us (1%)
    pallas_call x2, Pallas kernels, attend_back(): kernel_call(functools.partial(attend_back_body, score_scale), 2560 * head...  178 us
    dot_general x11, matrix products, dot_over(): lax.dot_general(left_mat, right_mat, (((left_axis,), (right_axis,)), ((),...  118 us
    dot_general x9, matrix products, plain_dot(): return jnp.dot(left_mat, right_mat, preferred_element_type=jnp.float32)  105 us
    all_to_all x8, waiting for transfers between devices, swap_tiles(): lax.all_to_all(values_in, TILE, split_axis=0, concat_axis=0, tiled=True)  99.3 us
    ppermute x21, waiting for transfers between devices, narrow_blocks(): received.append(lax.ppermute(sent, 'dp', shift_pairs(devices, step)))  95.9 us
    ppermute x18, waiting for transfers between devices, fetch(): lax.ppermute(weight, 'dp', shift_pairs(devices, step))  94.9 us
    dot_general x9, matrix products, left_dot(): lax.dot_general(left_mat, right_mat, (((0,), (0,)), ((), ())), preferred_...  90.6 us
    pallas_call x2, Pallas kernels, attend(): kernel_call(attend_body, 1024 * heads * tiles ** 2 * tile_len ** 2, 8 * q...  68.2 us
  transfers between devices with their start and end apart: 74, of which 34 were waited for; matrix products, arithmetic and copies ran while one was open for 33% of the time, Pallas kernels for 25%

profile of v3, /device:TPU:0, one launch (start us, length us, event | category | flops | bytes accessed | tf_op | source)
XLA Modules:
  0.0 1455.8 jit_solution(16100739024400253839)
XLA Ops:
  23.3 10.2 collective-permute-start.9
  33.5 14.4 collective-permute-done.1
  48.7 16.9 %all-gather = bf16[8,176,60]{1,2,0:T(8,128)(2,1)S(1)} all-gather(bf16[1,176,60]{1,2,0:T(8,128)(2,1)S(1)} %reshape.628), channel_id=1, replica_groups=mesh['dp'=4,'row'=4,'col'=2] {'row','col'}, dimensions={0}, use_global_device_ids=true | all-gather | bytes 190080 | tf_op jit(solution)/shard_map/all_gather | solution.py:1136
  69.0 9.6 shard_map.314
  85.7 16.0 %collective-permute-start.12 = (bf16[176,1056]{1,0:T(8,128)(2,1)S(1)}, bf16[176,1056]{1,0:T(8,128)(2,1)S(1)}, u32[]{:S(2)}, u32[]{:S(2)}) collective-permute-start(bf16[176,1056]{1,0:T(8,128)(2,1)S(1)} %concatenate.96), channel_id=1, source_target_pairs={{0,8},{8,16},{16,24},{24,0},{1,9},{9,17},{17,25},{25,1},{2,10},{10... | collective-permute-start | bytes 1115144 | tf_op jit(solution)/shard_map/ppermute | solution.py:1067
  105.0 18.4 %collective-permute-done.12 = bf16[176,1056]{1,0:T(8,128)(2,1)S(1)} collective-permute-done((bf16[176,1056]{1,0:T(8,128)(2,1)S(1)}, bf16[176,1056]{1,0:T(8,128)(2,1)S(1)}, u32[]{:S(2)}, u32[]{:S(2)}) %collective-permute-start.12) | collective-permute-done | bytes 371744 | tf_op jit(solution)/shard_map/ppermute | solution.py:1067
  123.4 20.6 %collective-permute-done.13 = bf16[176,1056]{1,0:T(8,128)(2,1)S(1)} collective-permute-done((bf16[176,1056]{1,0:T(8,128)(2,1)S(1)}, bf16[176,1056]{1,0:T(8,128)(2,1)S(1)}, u32[]{:S(2)}, u32[]{:S(2)}) %collective-permute-start.13) | collective-permute-done | bytes 371744 | tf_op jit(solution)/shard_map/ppermute | solution.py:1067
  165.8 9.5 collective-permute-start.15
  177.8 16.2 %copy.158 = bf16[4,2816,352]{1,0,2:T(4,128)(2,1)} copy(bf16[4,2816,352]{2,1,0:T(8,128)(2,1)} %bitcast.180) | data formatting | bytes 15859712 | tf_op jit(solution)/shard_map/reshape | solution.py:1184
  198.5 13.5 fusion.107
  221.0 15.5 %shard_map.315 = (bf16[8,3,2,88,512]{4,3,2,1,0:T(8,128)(2,1)}, f32[8,3,2,512]{3,2,1,0:T(2,128)}) custom-call(bf16[512,1408]{1,0:T(8,128)(2,1)} %get-tuple-element.288.rows_ref, bf16[1408,4224]{1,0:T(8,128)(2,1)} %all-gather.11.cloned.1.call-done.weight_ref, f32[88,512]{1,0:T(8,128)} %pad_maximum_fusion.15.cos_ref, f32[88,512]{1,0:T(8,128)} %pad_maximum_fusion.16.sin_ref, ...), custom_call_target="tpu_custom_call" | custom-call | flops 6090129408 | bytes 11894784 | tf_op jit(solution)/shard_map/pallas_call | solution.py:652
  245.6 12.8 collective-permute-done.18
  258.4 22.6 %collective-permute-done.19 = bf16[176,1536]{1,0:T(8,128)(2,1)S(1)} collective-permute-done((bf16[176,1536]{1,0:T(8,128)(2,1)S(1)}, bf16[176,1536]{1,0:T(8,128)(2,1)S(1)}, u32[]{:S(2)}, u32[]{:S(2)}) %collective-permute-start.19) | collective-permute-done | bytes 540704 | tf_op jit(solution)/shard_map/ppermute | solution.py:1067
  281.0 38.5 %all-to-all-done.query_ref.key_ref.value_ref = bf16[8,3,2,88,512]{4,3,2,1,0:T(8,128)(2,1)} async-done(((bf16[8,3,2,88,512]{4,3,2,1,0:T(8,128)(2,1)}), bf16[8,3,2,88,512]{4,3,2,1,0:T(8,128)(2,1)}, u32[]{:S(2)}, u32[]{:S(2)}) %all-to-all-start) | async-done | bytes 4325408 | tf_op jit(solution)/shard_map/all_to_all | solution.py:1057
  321.6 14.9 %shard_map.317 = (bf16[8,3,2,88,512]{4,3,2,1,0:T(8,128)(2,1)}, f32[8,3,2,512]{3,2,1,0:T(2,128)}) custom-call(bf16[512,1408]{1,0:T(8,128)(2,1)} %get-tuple-element.289.rows_ref, bf16[1408,4224]{1,0:T(8,128)(2,1)} %all-gather.11.cloned.1.call-done.weight_ref, f32[88,512]{1,0:T(8,128)} %pad_maximum_fusion.15.cos_ref, f32[88,512]{1,0:T(8,128)} %pad_maximum_fusion.16.sin_ref, ...), custom_call_target="tpu_custom_call" | custom-call | flops 6090129408 | bytes 11894784 | tf_op jit(solution)/shard_map/pallas_call | solution.py:652
  341.9 34.1 %shard_map.316 = (bf16[8,2,88,512]{3,2,1,0:T(8,128)(2,1)}, f32[8,2,1,512]{3,2,1,0:T(1,128)}) custom-call(bf16[8,3,2,88,512]{4,3,2,1,0:T(8,128)(2,1)} %all-to-all-done.query_ref.key_ref.value_ref, bf16[8,3,2,88,512]{4,3,2,1,0:T(8,128)(2,1)} %all-to-all-done.query_ref.key_ref.value_ref, bf16[8,3,2,88,512]{4,3,2,1,0:T(8,128)(2,1)} %all-to-all-done.query_ref.key_ref.value_ref, ...), custom_call_target="tpu_custom_call" | custom-call | flops 34359738368 | bytes 17301504 | tf_op jit(solution)/shard_map/pallas_call | solution.py:757
  376.0 30.1 %all-to-all-done.2.query_ref.key_ref.value_ref = bf16[8,3,2,88,512]{4,3,2,1,0:T(8,128)(2,1)} async-done(((bf16[8,3,2,88,512]{4,3,2,1,0:T(8,128)(2,1)}), bf16[8,3,2,88,512]{4,3,2,1,0:T(8,128)(2,1)}, u32[]{:S(2)}, u32[]{:S(2)}) %all-to-all-start.2) | async-done | bytes 4325408 | tf_op jit(solution)/shard_map/all_to_all | solution.py:1057
  409.7 34.1 %shard_map.318 = (bf16[8,2,88,512]{3,2,1,0:T(8,128)(2,1)}, f32[8,2,1,512]{3,2,1,0:T(1,128)}) custom-call(bf16[8,3,2,88,512]{4,3,2,1,0:T(8,128)(2,1)} %all-to-all-done.2.query_ref.key_ref.value_ref, bf16[8,3,2,88,512]{4,3,2,1,0:T(8,128)(2,1)} %all-to-all-done.2.query_ref.key_ref.value_ref, ...), custom_call_target="tpu_custom_call" | custom-call | flops 34359738368 | bytes 17301504 | tf_op jit(solution)/shard_map/pallas_call | solution.py:757
  452.6 19.4 %all-to-all-done.3 = bf16[8,2,88,512]{3,2,1,0:T(8,128)(2,1)S(1)} async-done(((bf16[8,2,88,512]{3,2,1,0:T(8,128)(2,1)}), bf16[8,2,88,512]{3,2,1,0:T(8,128)(2,1)S(1)}, u32[]{:S(2)}, u32[]{:S(2)}) %all-to-all-start.3) | async-done | bytes 1441824 | tf_op jit(solution)/shard_map/all_to_all | solution.py:1057
  472.0 10.6 fusion.108
  482.6 5.3 collective-permute-done.22
  492.7 9.9 fusion.111
  503.4 9.3 fusion.10
  512.7 14.6 %shard_map.319 = (bf16[16,88,1024]{2,1,0:T(8,128)(2,1)}, bf16[16,88,1024]{2,1,0:T(8,128)(2,1)}, f32[16,1,1024]{2,1,0:T(1,128)}, f32[16,1,1024]{2,1,0:T(1,128)}) custom-call(f32[16,88,1024]{2,1,0:T(8,128)} %bitcast.213, f32[2,16,88,768]{3,2,1,0:T(8,128)} %bitcast.192), custom_call_target="tpu_custom_call" | custom-call | flops 6442450944 | bytes 11534336 | tf_op jit(solution)/shard_map/pallas_call | solution.py:897
  527.3 9.0 fusion.109
  539.6 39.9 %add_convert_fusion = (bf16[1024,6144]{1,0:T(8,128)(2,1)}, bf16[1024,6144]{1,0:T(8,128)(2,1)}) fusion(bf16[1408,6144]{1,0:T(8,128)(2,1)} %all-gather.17.cloned.1.call-done, f32[1024,1408]{1,0:T(8,128)} %copy-done.4, f32[1408]{0:T(1024)S(1)} %copy-done.81, f32[1408]{0:T(1024)S(1)} %copy-done.56, f32[1024]{0:T(1024)S(1)} %add_rsqrt_fusion.2, ...), kind=kOutput, calls=%fused_computation.1 | convolution fusion | flops 17843486720 | bytes 48253952 | tf_op jit(solution)/shard_map/dot_general | solution.py:72
  579.5 29.0 %all-gather.19.cloned.1.call-done = bf16[6144,1408]{0,1:T(8,128)(2,1)} async-done(((bf16[768,1408]{0,1:T(8,128)(2,1)}), bf16[6144,1408]{0,1:T(8,128)(2,1)}) %all-gather.19.cloned.1.call-update) | async-done | bytes 17301520 | tf_op jit(solution)/shard_map/all_gather | solution.py:1136
  608.5 28.8 %fusion.110 = (f32[1024]{0:T(1024)S(1)}, f32[1024,1408]{1,0:T(8,128)S(1)}) fusion(f32[1024,1408]{1,0:T(8,128)} %copy-done.4, bf16[1024,6144]{1,0:T(8,128)(2,1)} %get-tuple-element.121, bf16[6144,1408]{0,1:T(8,128)(2,1)} %all-gather.19.cloned.1.call-done), kind=kOutput, calls=%fused_computation.314 | convolution fusion | flops 17719623680 | bytes 41422848 | tf_op jit(solution)/shard_map/dot_general | solution.py:72
  647.5 28.0 %convolution_convert_fusion = bf16[6144,1408]{1,0:T(8,128)(2,1)} fusion(bf16[1024,6144]{1,0:T(8,128)(2,1)} %get-tuple-element.121, bf16[1024,1408]{1,0:T(8,128)(2,1)S(1)} %get-tuple-element.126), kind=kOutput, calls=%fused_computation.5 | convolution fusion | flops 17725390848 | bytes 32768000 | tf_op jit(solution)/shard_map/dot_general | solution.py:76
  677.3 30.6 %multiply_convert_fusion = bf16[1024,6144]{1,0:T(8,128)(2,1)} fusion(bf16[1024,6144]{1,0:T(8,128)(2,1)} %get-tuple-element.127, bf16[1024,1408]{1,0:T(8,128)(2,1)S(1)} %copy-done.20, bf16[6144,1408]{0,1:T(8,128)(2,1)} %all-gather.19.cloned.1.call-done), kind=kOutput, calls=%fused_computation | convolution fusion | flops 17735614464 | bytes 45350912 | tf_op jit(solution)/shard_map/dot_general | solution.py:82
  707.8 26.0 %convolution_convert_fusion.1 = bf16[1408,6144]{1,0:T(8,128)(2,1)} fusion(bf16[1024,6144]{1,0:T(8,128)(2,1)} %multiply_convert_fusion, f32[1024,1408]{1,0:T(8,128)} %copy-done.4, f32[1408]{0:T(1024)S(1)} %copy-done.81, f32[1408]{0:T(1024)S(1)} %copy-done.56, f32[1024]{0:T(1024)S(1)} %add_rsqrt_fusion.2, f32[1024]{0:T(1024)S(1)} %broadcast_multiply_fusion.12), kind=kOutput, calls=%fused_computation.6 | convolution fusion | flops 17732599808 | bytes 35671040 | tf_op jit(solution)/shard_map/dot_general | solution.py:76
  733.9 31.5 %multiply_reduce_fusion.1 = (f32[1408]{0:T(1024)}, f32[1024]{0:T(1024)S(1)}, f32[1024]{0:T(1024)S(1)}, f32[1408]{0:T(1024)}, f32[1024,1408]{1,0:T(8,128)}) fusion(f32[1024,1408]{1,0:T(8,128)} %copy-done.4, f32[1024]{0:T(1024)S(1)} %add_rsqrt_fusion.2, f32[1024]{0:T(1024)S(1)} %broadcast_multiply_fusion.12, f32[1408]{0:T(1024)S(1)} %copy-done.56, ...), kind=kOutput, calls=%fused_computation.19 | convolution fusion | flops 17729710080 | bytes 41452032 | tf_op jit(solution)/shard_map/dot_general | solution.py:82
  765.4 7.7 multiply_add_fusion.1
  773.1 10.5 convolution_convert_fusion.7
  783.7 21.3 %shard_map.320 = (bf16[16,88,1024]{2,1,0:T(8,128)(2,1)}, bf16[16,88,768]{2,1,0:T(8,128)(2,1)}, bf16[16,88,768]{2,1,0:T(8,128)(2,1)}) custom-call(bf16[16,88,1024]{2,1,0:T(8,128)(2,1)} %get-tuple-element.130.query_ref, f32[2,16,88,768]{3,2,1,0:T(8,128)} %bitcast.193, bf16[16,88,1024]{2,1,0:T(8,128)(2,1)} %bitcast.218, ...), custom_call_target="tpu_custom_call" | custom-call | flops 16106127360 | bytes 23068672 | tf_op jit(solution)/shard_map/pallas_call | solution.py:957
  805.1 14.3 multiply_reduce_fusion.2
  819.4 6.3 fusion.93
  825.7 6.8 fusion.17
  837.1 8.6 fusion.2
  845.7 9.9 fusion.1
  855.7 6.2 fusion
  865.8 5.4 all-to-all-done.4.grad_ref
  880.2 6.1 fusion.20
  890.6 89.2 %shard_map.321 = bf16[8,3,2,88,512]{4,3,2,1,0:T(8,128)(2,1)} custom-call(bf16[8,3,2,88,512]{4,3,2,1,0:T(8,128)(2,1)} %all-to-all-done.query_ref.key_ref.value_ref, bf16[8,3,2,88,512]{4,3,2,1,0:T(8,128)(2,1)} %all-to-all-done.query_ref.key_ref.value_ref, bf16[8,3,2,88,512]{4,3,2,1,0:T(8,128)(2,1)} %all-to-all-done.query_ref.key_ref.value_ref, ...), custom_call_target="tpu_custom_call" | custom-call | flops 85899345920 | bytes 17301504 | tf_op jit(solution)/shard_map/pallas_call | solution.py:845
  991.6 89.2 %shard_map.322 = bf16[8,3,2,88,512]{4,3,2,1,0:T(8,128)(2,1)} custom-call(bf16[8,3,2,88,512]{4,3,2,1,0:T(8,128)(2,1)} %all-to-all-done.2.query_ref.key_ref.value_ref, bf16[8,3,2,88,512]{4,3,2,1,0:T(8,128)(2,1)} %all-to-all-done.2.query_ref.key_ref.value_ref, bf16[8,3,2,88,512]{4,3,2,1,0:T(8,128)(2,1)} %all-to-all-done.2.query_ref.key_ref.value_ref, ...), custom_call_target="tpu_custom_call" | custom-call | flops 85899345920 | bytes 17301504 | tf_op jit(solution)/shard_map/pallas_call | solution.py:845
  1094.0 10.4 collective-permute-done.27
  1104.4 11.0 collective-permute-done.29
  1115.4 23.2 %collective-permute-done.28 = bf16[176,1536]{1,0:T(8,128)(2,1)S(1)} collective-permute-done((bf16[176,1536]{1,0:T(8,128)(2,1)S(1)}, bf16[176,1536]{1,0:T(8,128)(2,1)S(1)}, u32[]{:S(2)}, u32[]{:S(2)}) %collective-permute-start.28) | collective-permute-done | bytes 540704 | tf_op jit(solution)/shard_map/ppermute | solution.py:1087
  1140.0 10.1 shard_map.323.others_0_
  1150.1 5.8 all-to-all-done.6.grad_ref
  1155.9 10.2 shard_map.324
  1166.2 19.9 %convolution_convert_fusion.2 = bf16[1408,4224]{1,0:T(8,128)(2,1)} fusion(bf16[1024,1408]{1,0:T(8,128)(2,1)S(1)} %copy-done.13, bf16[4224,1024]{1,0:T(8,128)(2,1)} %bitcast.166), kind=kOutput, calls=%fused_computation.7 | convolution fusion | flops 12186206208 | bytes 23429120 | tf_op jit(solution)/shard_map/dot_general | solution.py:1144
  1186.2 11.7 copy.132.weight_ref
  1208.8 24.3 %multiply_reduce_fusion.3 = (f32[1408]{0:T(1024)}, f32[1024]{0:T(1024)S(1)}, f32[1024]{0:T(1024)S(1)}, f32[1408]{0:T(1024)S(1)}, f32[1024,1408]{1,0:T(8,128)S(1)}) fusion(f32[1024,1408]{1,0:T(8,128)} %copy-done, f32[1024]{0:T(1024)S(1)} %copy-done.51, f32[1024]{0:T(1024)S(1)} %copy-done.49, f32[1408]{0:T(1024)S(1)} %copy-done.47, ...), kind=kOutput, calls=%fused_computation.21 | convolution fusion | flops 12193230848 | bytes 32113152 | tf_op jit(solution)/shard_map/dot_general | solution.py:1144
  1233.1 7.7 add_convert_fusion.1.low_ref
  1242.4 14.0 convolution_convert_fusion.3
  1265.7 23.8 %shard_map.325 = (f32[1024,1408]{1,0:T(8,128)}, bf16[1024,1408]{1,0:T(8,128)(2,1)}, f32[2,2816]{1,0:T(2,128)}) custom-call(bf16[1024,1408]{1,0:T(8,128)(2,1)} %copy-done.18, bf16[2816,1408]{1,0:T(8,128)(2,1)} %copy.132.weight_ref, f32[1024,2816]{1,0:T(8,128)} %get-tuple-element.156.z_ref, f32[1024,1]{1,0:T(8,128)} %get-tuple-element.157.inv_ref, ...), custom_call_target="tpu_custom_call" | custom-call | flops 8120172544 | bytes 25952256 | tf_op jit(solution)/shard_map/pallas_call | solution.py:1032
  1336.2 9.1 collective-permute-start.42
  1352.3 13.2 collective-permute-done.36
  1374.2 11.3 collective-permute-done.43
  1395.3 6.5 copy.134
  1405.9 12.6 collective-permute-done.52
  1423.7 7.2 collective-permute-start.39
  1437.8 8.7 collective-permute-done.40
  (535 shorter events, 277.2 us)
Async XLA Ops:
  7.2 170.6 %all-gather.9.cloned.1.call-start = ((), (), s32[]{:S(2)}) async-start(), calls=%async_computation.13 | async-start | bytes 8921088 | tf_op jit(solution)/shard_map/all_gather | solution.py:1184
  7.9 213.1 %all-gather.11.cloned.1.call-start = ((), (), s32[]{:S(2)}) async-start(), calls=%async_computation.14 | async-start | bytes 13381632 | tf_op jit(solution)/shard_map/all_gather | solution.py:1136
  10.8 12.6 collective-permute-start
  13.8 34.1 %collective-permute-start.1 = (bf16[384,352]{0,1:T(8,128)(2,1)S(1)}, bf16[384,352]{0,1:T(8,128)(2,1)S(1)}, u32[]{:S(2)}, u32[]{:S(2)}) collective-permute-start(bf16[384,352]{0,1:T(8,128)(2,1)S(1)} %pad_maximum_fusion.14), channel_id=1, source_target_pairs={{0,16},{8,24},{16,0},{24,8},{1,17},{9,25},{17,1},{25,9},{2,18},{10... | collective-permute-start | bytes 811016 | tf_op jit(solution)/shard_map/ppermute | solution.py:1067
  16.4 31.5 %collective-permute-start.2 = (bf16[384,352]{0,1:T(8,128)(2,1)S(1)}, bf16[384,352]{0,1:T(8,128)(2,1)S(1)}, u32[]{:S(2)}, u32[]{:S(2)}) collective-permute-start(bf16[384,352]{0,1:T(8,128)(2,1)S(1)} %pad_maximum_fusion.14), channel_id=1, source_target_pairs={{0,24},{8,0},{16,8},{24,16},{1,25},{9,1},{17,9},{25,17},{2,26},{10... | collective-permute-start | bytes 811016 | tf_op jit(solution)/shard_map/ppermute | solution.py:1067
  17.8 60.9 %collective-permute-start.10 = (bf16[176,1056]{1,0:T(8,128)(2,1)}, bf16[176,1056]{1,0:T(8,128)(2,1)S(1)}, u32[]{:S(2)}, u32[]{:S(2)}) collective-permute-start(bf16[176,1056]{1,0:T(8,128)(2,1)} %param.29), channel_id=1, source_target_pairs={{0,16},{8,24},{16,0},{24,8},{1,17},{9,25},{17,1},{25,9},{2,18},{10... | collective-permute-start | bytes 1115144 | tf_op jit(solution)/shard_map/ppermute | solution.py:1067
  18.0 60.7 %collective-permute-start.11 = (bf16[176,1056]{1,0:T(8,128)(2,1)}, bf16[176,1056]{1,0:T(8,128)(2,1)S(1)}, u32[]{:S(2)}, u32[]{:S(2)}) collective-permute-start(bf16[176,1056]{1,0:T(8,128)(2,1)} %param.29), channel_id=1, source_target_pairs={{0,24},{8,0},{16,8},{24,16},{1,25},{9,1},{17,9},{25,17},{2,26},{10... | collective-permute-start | bytes 1115144 | tf_op jit(solution)/shard_map/ppermute | solution.py:1067
  23.3 55.4 %collective-permute-start.9 = (bf16[176,1056]{1,0:T(8,128)(2,1)}, bf16[176,1056]{1,0:T(8,128)(2,1)S(1)}, u32[]{:S(2)}, u32[]{:S(2)}) collective-permute-start(bf16[176,1056]{1,0:T(8,128)(2,1)} %param.29), channel_id=1, source_target_pairs={{0,8},{8,16},{16,24},{24,0},{1,9},{9,17},{17,25},{25,1},{2,10},{10... | collective-permute-start | bytes 1115144 | tf_op jit(solution)/shard_map/ppermute | solution.py:1067
  84.3 368.2 %all-gather.13.cloned.1.call-start = ((), (), s32[]{:S(2)}) async-start(), calls=%async_computation.15 | async-start | bytes 13381632 | tf_op jit(solution)/shard_map/all_gather | solution.py:1136
  85.7 37.7 %collective-permute-start.12 = (bf16[176,1056]{1,0:T(8,128)(2,1)S(1)}, bf16[176,1056]{1,0:T(8,128)(2,1)S(1)}, u32[]{:S(2)}, u32[]{:S(2)}) collective-permute-start(bf16[176,1056]{1,0:T(8,128)(2,1)S(1)} %concatenate.96), channel_id=1, source_target_pairs={{0,8},{8,16},{16,24},{24,0},{1,9},{9,17},{17,25},{25,1},{2,10},{10... | collective-permute-start | bytes 1115144 | tf_op jit(solution)/shard_map/ppermute | solution.py:1067
  101.7 42.2 %collective-permute-start.13 = (bf16[176,1056]{1,0:T(8,128)(2,1)S(1)}, bf16[176,1056]{1,0:T(8,128)(2,1)S(1)}, u32[]{:S(2)}, u32[]{:S(2)}) collective-permute-start(bf16[176,1056]{1,0:T(8,128)(2,1)S(1)} %concatenate.96), channel_id=1, source_target_pairs={{0,16},{8,24},{16,0},{24,8},{1,17},{9,25},{17,1},{25,9},{2,18},{10... | collective-permute-start | bytes 1115144 | tf_op jit(solution)/shard_map/ppermute | solution.py:1067
  105.0 38.9 %collective-permute-start.14 = (bf16[176,1056]{1,0:T(8,128)(2,1)S(1)}, bf16[176,1056]{1,0:T(8,128)(2,1)S(1)}, u32[]{:S(2)}, u32[]{:S(2)}) collective-permute-start(bf16[176,1056]{1,0:T(8,128)(2,1)S(1)} %concatenate.96), channel_id=1, source_target_pairs={{0,24},{8,0},{16,8},{24,16},{1,25},{9,1},{17,9},{25,17},{2,26},{10... | collective-permute-start | bytes 1115144 | tf_op jit(solution)/shard_map/ppermute | solution.py:1067
  148.6 344.0 %all-gather.15.cloned.1.call-start = ((), (), s32[]{:S(2)}) async-start(), calls=%async_computation.16 | async-start | bytes 6488064 | tf_op jit(solution)/shard_map/all_gather | solution.py:1136
  164.3 13.5 collective-permute-start.8
  165.8 48.6 %collective-permute-start.15 = (bf16[128,704]{0,1:T(8,128)(2,1)S(1)}, bf16[128,704]{0,1:T(8,128)(2,1)S(1)}, u32[]{:S(2)}, u32[]{:S(2)}) collective-permute-start(bf16[128,704]{0,1:T(8,128)(2,1)S(1)} %copy-done.44), channel_id=1, source_target_pairs={{0,8},{8,16},{16,24},{24,0},{1,9},{9,17},{17,25},{25,1},{2,10},{10... | collective-permute-start | bytes 540680 | tf_op jit(solution)/shard_map/ppermute | solution.py:1067
  175.2 39.2 %collective-permute-start.16 = (bf16[128,704]{0,1:T(8,128)(2,1)S(1)}, bf16[128,704]{0,1:T(8,128)(2,1)S(1)}, u32[]{:S(2)}, u32[]{:S(2)}) collective-permute-start(bf16[128,704]{0,1:T(8,128)(2,1)S(1)} %copy-done.44), channel_id=1, source_target_pairs={{0,16},{8,24},{16,0},{24,8},{1,17},{9,25},{17,1},{25,9},{2,18},{10... | collective-permute-start | bytes 540680 | tf_op jit(solution)/shard_map/ppermute | solution.py:1067
  176.6 37.8 %collective-permute-start.17 = (bf16[128,704]{0,1:T(8,128)(2,1)S(1)}, bf16[128,704]{0,1:T(8,128)(2,1)}, u32[]{:S(2)}, u32[]{:S(2)}) collective-permute-start(bf16[128,704]{0,1:T(8,128)(2,1)S(1)} %copy-done.44), channel_id=1, source_target_pairs={{0,24},{8,0},{16,8},{24,16},{1,25},{9,1},{17,9},{25,17},{2,26},{10... | collective-permute-start | bytes 540680 | tf_op jit(solution)/shard_map/ppermute | solution.py:1067
  236.6 83.0 %all-to-all-start = ((bf16[8,3,2,88,512]{4,3,2,1,0:T(8,128)(2,1)}), bf16[8,3,2,88,512]{4,3,2,1,0:T(8,128)(2,1)}, u32[]{:S(2)}, u32[]{:S(2)}) async-start(bf16[8,3,2,88,512]{4,3,2,1,0:T(8,128)(2,1)} %get-tuple-element.104.own_ref), calls=%async_computation | async-start | bytes 8650752 | tf_op jit(solution)/shard_map/all_to_all | solution.py:1057
  241.3 298.3 %all-gather.17.cloned.1.call-start = ((), (), s32[]{:S(2)}) async-start(), calls=%async_computation.17 | async-start | bytes 19464192 | tf_op jit(solution)/shard_map/all_gather | solution.py:1136
  241.3 17.1 %collective-permute-start.18 = (bf16[176,1536]{1,0:T(8,128)(2,1)S(1)}, bf16[176,1536]{1,0:T(8,128)(2,1)S(1)}, u32[]{:S(2)}, u32[]{:S(2)}) collective-permute-start(bf16[176,1536]{1,0:T(8,128)(2,1)S(1)} %copy-done.36), channel_id=1, source_target_pairs={{0,8},{8,16},{16,24},{24,0},{1,9},{9,17},{17,25},{25,1},{2,10},{10... | collective-permute-start | bytes 1622024 | tf_op jit(solution)/shard_map/ppermute | solution.py:1067
  242.3 38.7 %collective-permute-start.19 = (bf16[176,1536]{1,0:T(8,128)(2,1)S(1)}, bf16[176,1536]{1,0:T(8,128)(2,1)S(1)}, u32[]{:S(2)}, u32[]{:S(2)}) collective-permute-start(bf16[176,1536]{1,0:T(8,128)(2,1)S(1)} %copy-done.36), channel_id=1, source_target_pairs={{0,16},{8,24},{16,0},{24,8},{1,17},{9,25},{17,1},{25,9},{2,18},{10... | collective-permute-start | bytes 1622024 | tf_op jit(solution)/shard_map/ppermute | solution.py:1067
  243.2 37.8 %collective-permute-start.20 = (bf16[176,1536]{1,0:T(8,128)(2,1)S(1)}, bf16[176,1536]{1,0:T(8,128)(2,1)S(1)}, u32[]{:S(2)}, u32[]{:S(2)}) collective-permute-start(bf16[176,1536]{1,0:T(8,128)(2,1)S(1)} %copy-done.36), channel_id=1, source_target_pairs={{0,24},{8,0},{16,8},{24,16},{1,25},{9,1},{17,9},{25,17},{2,26},{10... | collective-permute-start | bytes 1622024 | tf_op jit(solution)/shard_map/ppermute | solution.py:1067
  336.5 69.6 %all-to-all-start.2 = ((bf16[8,3,2,88,512]{4,3,2,1,0:T(8,128)(2,1)}), bf16[8,3,2,88,512]{4,3,2,1,0:T(8,128)(2,1)}, u32[]{:S(2)}, u32[]{:S(2)}) async-start(bf16[8,3,2,88,512]{4,3,2,1,0:T(8,128)(2,1)} %get-tuple-element.106.own_ref), calls=%async_computation.2 | async-start | bytes 8650752 | tf_op jit(solution)/shard_map/all_to_all | solution.py:1057
  406.1 37.7 %all-to-all-start.1 = ((bf16[8,2,88,512]{3,2,1,0:T(8,128)(2,1)}), bf16[8,2,88,512]{3,2,1,0:T(8,128)(2,1)S(1)}, u32[]{:S(2)}, u32[]{:S(2)}) async-start(bf16[8,2,88,512]{3,2,1,0:T(8,128)(2,1)} %get-tuple-element.105.att_ref), calls=%async_computation.1 | async-start | bytes 2883584 | tf_op jit(solution)/shard_map/all_to_all | solution.py:1057
  443.9 28.1 %all-to-all-start.3 = ((bf16[8,2,88,512]{3,2,1,0:T(8,128)(2,1)}), bf16[8,2,88,512]{3,2,1,0:T(8,128)(2,1)S(1)}, u32[]{:S(2)}, u32[]{:S(2)}) async-start(bf16[8,2,88,512]{3,2,1,0:T(8,128)(2,1)} %get-tuple-element.107.att_ref), calls=%async_computation.3 | async-start | bytes 2883584 | tf_op jit(solution)/shard_map/all_to_all | solution.py:1057
  448.0 160.5 %all-gather.19.cloned.1.call-start = ((), (), s32[]{:S(2)}) async-start(), calls=%async_computation.18 | async-start | bytes 19464192 | tf_op jit(solution)/shard_map/all_gather | solution.py:1136
  448.0 34.5 %collective-permute-start.21 = (bf16[768,352]{0,1:T(8,128)(2,1)S(1)}, bf16[768,352]{0,1:T(8,128)(2,1)}, u32[]{:S(2)}, u32[]{:S(2)}) collective-permute-start(bf16[768,352]{0,1:T(8,128)(2,1)S(1)} %copy-done.37), channel_id=1, source_target_pairs={{0,8},{8,16},{16,24},{24,0},{1,9},{9,17},{17,25},{25,1},{2,10},{10... | collective-permute-start | bytes 1622024 | tf_op jit(solution)/shard_map/ppermute | solution.py:1067
  448.7 39.2 %collective-permute-start.22 = (bf16[768,352]{0,1:T(8,128)(2,1)S(1)}, bf16[768,352]{0,1:T(8,128)(2,1)}, u32[]{:S(2)}, u32[]{:S(2)}) collective-permute-start(bf16[768,352]{0,1:T(8,128)(2,1)S(1)} %copy-done.37), channel_id=1, source_target_pairs={{0,16},{8,24},{16,0},{24,8},{1,17},{9,25},{17,1},{25,9},{2,18},{10... | collective-permute-start | bytes 1622024 | tf_op jit(solution)/shard_map/ppermute | solution.py:1067
  451.1 36.8 %collective-permute-start.23 = (bf16[768,352]{0,1:T(8,128)(2,1)S(1)}, bf16[768,352]{0,1:T(8,128)(2,1)}, u32[]{:S(2)}, u32[]{:S(2)}) collective-permute-start(bf16[768,352]{0,1:T(8,128)(2,1)S(1)} %copy-done.37), channel_id=1, source_target_pairs={{0,24},{8,0},{16,8},{24,16},{1,25},{9,1},{17,9},{25,17},{2,26},{10... | collective-permute-start | bytes 1622024 | tf_op jit(solution)/shard_map/ppermute | solution.py:1067
  491.0 314.0 %reduce-scatter.6.cloned.1.call-start = ((), (), s32[]{:S(2)}) async-start(), calls=%async_computation.19 | async-start | bytes 19464192 | tf_op jit(solution)/shard_map/reduce_scatter | solution.py:1131
  675.5 410.0 %reduce-scatter.8.cloned.1.call-start = ((), (), s32[]{:S(2)}) async-start(), calls=%async_computation.20 | async-start | bytes 19464192 | tf_op jit(solution)/shard_map/reduce_scatter | solution.py:1131
  832.5 38.8 %all-to-all-start.4 = ((bf16[8,2,88,512]{3,2,1,0:T(8,128)(2,1)}), bf16[8,2,88,512]{3,2,1,0:T(8,128)(2,1)}, u32[]{:S(2)}, u32[]{:S(2)}) async-start(bf16[8,2,88,512]{3,2,1,0:T(8,128)(2,1)} %bitcast.204), calls=%async_computation.6 | async-start | bytes 2883584 | tf_op jit(solution)/shard_map/all_to_all | solution.py:1057
  836.8 366.8 %reduce-scatter.10.cloned.1.call-start = ((), (), s32[]{:S(2)}) async-start(), calls=%async_computation.21 | async-start | bytes 18247680 | tf_op jit(solution)/shard_map/reduce_scatter | solution.py:1131
  873.1 106.7 %collective-permute-start.24 = (bf16[768,352]{0,1:T(8,128)(2,1)}, bf16[768,352]{0,1:T(8,128)(2,1)S(1)}, u32[]{:S(2)}, u32[]{:S(2)}) collective-permute-start(bf16[768,352]{0,1:T(8,128)(2,1)} %copy.126), channel_id=1, source_target_pairs={{0,8},{8,16},{16,24},{24,0},{1,9},{9,17},{17,25},{25,1},{2,10},{10... | collective-permute-start | bytes 1622024 | tf_op jit(solution)/shard_map/ppermute | solution.py:1087
  875.2 104.6 %collective-permute-start.26 = (bf16[768,352]{0,1:T(8,128)(2,1)}, bf16[768,352]{0,1:T(8,128)(2,1)}, u32[]{:S(2)}, u32[]{:S(2)}) collective-permute-start(bf16[768,352]{0,1:T(8,128)(2,1)} %copy.128), channel_id=1, source_target_pairs={{0,24},{8,0},{16,8},{24,16},{1,25},{9,1},{17,9},{25,17},{2,26},{10... | collective-permute-start | bytes 1622024 | tf_op jit(solution)/shard_map/ppermute | solution.py:1087
  880.0 99.8 %collective-permute-start.25 = (bf16[768,352]{0,1:T(8,128)(2,1)}, bf16[768,352]{0,1:T(8,128)(2,1)}, u32[]{:S(2)}, u32[]{:S(2)}) collective-permute-start(bf16[768,352]{0,1:T(8,128)(2,1)} %copy.127), channel_id=1, source_target_pairs={{0,16},{8,24},{16,0},{24,8},{1,17},{9,25},{17,1},{25,9},{2,18},{10... | collective-permute-start | bytes 1622024 | tf_op jit(solution)/shard_map/ppermute | solution.py:1087
  886.3 100.5 %all-to-all-start.5 = ((bf16[8,2,88,512]{3,2,1,0:T(8,128)(2,1)}), bf16[8,2,88,512]{3,2,1,0:T(8,128)(2,1)}, u32[]{:S(2)}, u32[]{:S(2)}) async-start(bf16[8,2,88,512]{3,2,1,0:T(8,128)(2,1)} %bitcast.203), calls=%async_computation.7 | async-start | bytes 2883584 | tf_op jit(solution)/shard_map/all_to_all | solution.py:1057
  986.8 94.0 %all-to-all-start.7 = ((bf16[8,3,2,88,512]{4,3,2,1,0:T(8,128)(2,1)}), bf16[8,3,2,88,512]{4,3,2,1,0:T(8,128)(2,1)}, u32[]{:S(2)}, u32[]{:S(2)}) async-start(bf16[8,3,2,88,512]{4,3,2,1,0:T(8,128)(2,1)} %shard_map.321), calls=%async_computation.9 | async-start | bytes 8650752 | tf_op jit(solution)/shard_map/all_to_all | solution.py:1057
  1080.8 75.1 %all-to-all-start.6 = ((bf16[8,3,2,88,512]{4,3,2,1,0:T(8,128)(2,1)}), bf16[8,3,2,88,512]{4,3,2,1,0:T(8,128)(2,1)}, u32[]{:S(2)}, u32[]{:S(2)}) async-start(bf16[8,3,2,88,512]{4,3,2,1,0:T(8,128)(2,1)} %shard_map.322), calls=%async_computation.8 | async-start | bytes 8650752 | tf_op jit(solution)/shard_map/all_to_all | solution.py:1057
  1085.4 204.1 %reduce-scatter.12.cloned.1.call-start = ((), (), s32[]{:S(2)}) async-start(), calls=%async_computation.23 | async-start | bytes 13381632 | tf_op jit(solution)/shard_map/reduce_scatter | solution.py:1131
  1087.4 17.0 %collective-permute-start.27 = (bf16[176,1536]{1,0:T(8,128)(2,1)S(1)}, bf16[176,1536]{1,0:T(8,128)(2,1)S(1)}, u32[]{:S(2)}, u32[]{:S(2)}) collective-permute-start(bf16[176,1536]{1,0:T(8,128)(2,1)S(1)} %get-tuple-element.291), channel_id=1, source_target_pairs={{0,8},{8,16},{16,24},{24,0},{1,9},{9,17},{17,25},{25,1},{2,10},{10... | collective-permute-start | bytes 1622024 | tf_op jit(solution)/shard_map/ppermute | solution.py:1087
  1090.8 24.6 %collective-permute-start.29 = (bf16[176,1536]{1,0:T(8,128)(2,1)S(1)}, bf16[176,1536]{1,0:T(8,128)(2,1)S(1)}, u32[]{:S(2)}, u32[]{:S(2)}) collective-permute-start(bf16[176,1536]{1,0:T(8,128)(2,1)S(1)} %get-tuple-element.290), channel_id=1, source_target_pairs={{0,24},{8,0},{16,8},{24,16},{1,25},{9,1},{17,9},{25,17},{2,26},{10... | collective-permute-start | bytes 1622024 | tf_op jit(solution)/shard_map/ppermute | solution.py:1087
  1093.0 45.6 %collective-permute-start.28 = (bf16[176,1536]{1,0:T(8,128)(2,1)S(1)}, bf16[176,1536]{1,0:T(8,128)(2,1)S(1)}, u32[]{:S(2)}, u32[]{:S(2)}) collective-permute-start(bf16[176,1536]{1,0:T(8,128)(2,1)S(1)} %select_select_fusion.4), channel_id=1, source_target_pairs={{0,16},{8,24},{16,0},{24,8},{1,17},{9,25},{17,1},{25,9},{2,18},{10... | collective-permute-start | bytes 1622024 | tf_op jit(solution)/shard_map/ppermute | solution.py:1087
  1186.1 181.4 %all-gather.21.cloned.1.call-start = ((), (), s32[]{:S(2)}) async-start(), calls=%async_computation.22 | async-start | bytes 4866048 | tf_op jit(solution)/shard_map/all_gather | solution.py:1136
  1208.3 212.1 %reduce-scatter.14.cloned.1.call-start = ((), (), s32[]{:S(2)}) async-start(), calls=%async_computation.24 | async-start | bytes 8921088 | tf_op jit(solution)/shard_map/reduce_scatter | solution.py:1131
  1260.6 28.9 %collective-permute-start.30 = (bf16[176,1056]{1,0:T(8,128)(2,1)}, bf16[176,1056]{1,0:T(8,128)(2,1)S(1)}, u32[]{:S(2)}, u32[]{:S(2)}) collective-permute-start(bf16[176,1056]{1,0:T(8,128)(2,1)} %get-tuple-element.316), channel_id=1, source_target_pairs={{0,8},{8,16},{16,24},{24,0},{1,9},{9,17},{17,25},{25,1},{2,10},{10... | collective-permute-start | bytes 1115144 | tf_op jit(solution)/shard_map/ppermute | solution.py:1087
  1261.7 29.8 %collective-permute-start.31 = (bf16[176,1056]{1,0:T(8,128)(2,1)}, bf16[176,1056]{1,0:T(8,128)(2,1)S(1)}, u32[]{:S(2)}, u32[]{:S(2)}) collective-permute-start(bf16[176,1056]{1,0:T(8,128)(2,1)} %get-tuple-element.315), channel_id=1, source_target_pairs={{0,16},{8,24},{16,0},{24,8},{1,17},{9,25},{17,1},{25,9},{2,18},{10... | collective-permute-start | bytes 1115144 | tf_op jit(solution)/shard_map/ppermute | solution.py:1087
  1263.6 27.9 %collective-permute-start.32 = (bf16[176,1056]{1,0:T(8,128)(2,1)S(1)}, bf16[176,1056]{1,0:T(8,128)(2,1)}, u32[]{:S(2)}, u32[]{:S(2)}) collective-permute-start(bf16[176,1056]{1,0:T(8,128)(2,1)S(1)} %get-tuple-element.314), channel_id=1, source_target_pairs={{0,24},{8,0},{16,8},{24,16},{1,25},{9,1},{17,9},{25,17},{2,26},{10... | collective-permute-start | bytes 1115144 | tf_op jit(solution)/shard_map/ppermute | solution.py:1087
  1303.3 4.7 collective-permute-start.46
  1312.5 6.2 collective-permute-start.48
  1325.3 5.9 collective-permute-start.33
  1334.0 12.0 collective-permute-start.35
  1336.2 38.1 %collective-permute-start.42 = (bf16[176,1056]{1,0:T(8,128)(2,1)}, bf16[176,1056]{1,0:T(8,128)(2,1)}, u32[]{:S(2)}, u32[]{:S(2)}) collective-permute-start(bf16[176,1056]{1,0:T(8,128)(2,1)} %get-tuple-element.326), channel_id=1, source_target_pairs={{0,8},{8,16},{16,24},{24,0},{1,9},{9,17},{17,25},{25,1},{2,10},{10... | collective-permute-start | bytes 1115144 | tf_op jit(solution)/shard_map/ppermute | solution.py:1087
  1345.3 29.0 %collective-permute-start.44 = (bf16[176,1056]{1,0:T(8,128)(2,1)}, bf16[176,1056]{1,0:T(8,128)(2,1)}, u32[]{:S(2)}, u32[]{:S(2)}) collective-permute-start(bf16[176,1056]{1,0:T(8,128)(2,1)} %get-tuple-element.325), channel_id=1, source_target_pairs={{0,24},{8,0},{16,8},{24,16},{1,25},{9,1},{17,9},{25,17},{2,26},{10... | collective-permute-start | bytes 1115144 | tf_op jit(solution)/shard_map/ppermute | solution.py:1087
  1346.0 19.5 %collective-permute-start.36 = (f32[176,15]{0,1:T(8,128)S(1)}, f32[176,15]{0,1:T(8,128)S(1)}, u32[]{:S(2)}, u32[]{:S(2)}) collective-permute-start(f32[176,15]{0,1:T(8,128)S(1)} %get-tuple-element.377), channel_id=1, source_target_pairs={{0,8},{8,16},{16,24},{24,0},{1,9},{9,17},{17,25},{25,1},{2,10},{10... | collective-permute-start | bytes 31688 | tf_op jit(solution)/shard_map/ppermute | solution.py:1087
  1348.5 17.2 %collective-permute-start.37 = (f32[176,15]{0,1:T(8,128)S(1)}, f32[176,15]{0,1:T(8,128)S(1)}, u32[]{:S(2)}, u32[]{:S(2)}) collective-permute-start(f32[176,15]{0,1:T(8,128)S(1)} %get-tuple-element.378), channel_id=1, source_target_pairs={{0,16},{8,24},{16,0},{24,8},{1,17},{9,25},{17,1},{25,9},{2,18},{10... | collective-permute-start | bytes 31688 | tf_op jit(solution)/shard_map/ppermute | solution.py:1087
  1349.3 16.4 %collective-permute-start.38 = (f32[176,15]{0,1:T(8,128)S(1)}, f32[176,15]{0,1:T(8,128)S(1)}, u32[]{:S(2)}, u32[]{:S(2)}) collective-permute-start(f32[176,15]{0,1:T(8,128)S(1)} %select_select_fusion.42), channel_id=1, source_target_pairs={{0,24},{8,0},{16,8},{24,16},{1,25},{9,1},{17,9},{25,17},{2,26},{10... | collective-permute-start | bytes 31688 | tf_op jit(solution)/shard_map/ppermute | solution.py:1087
  1365.5 20.1 %collective-permute-start.43 = (bf16[176,1056]{1,0:T(8,128)(2,1)}, bf16[176,1056]{1,0:T(8,128)(2,1)}, u32[]{:S(2)}, u32[]{:S(2)}) collective-permute-start(bf16[176,1056]{1,0:T(8,128)(2,1)} %select_select_fusion.15), channel_id=1, source_target_pairs={{0,16},{8,24},{16,0},{24,8},{1,17},{9,25},{17,1},{25,9},{2,18},{10... | collective-permute-start | bytes 1115144 | tf_op jit(solution)/shard_map/ppermute | solution.py:1087
  1391.5 14.5 collective-permute-start.51
  1391.5 27.1 %collective-permute-start.52 = (bf16[464,352]{1,0:T(8,128)(2,1)}, bf16[464,352]{1,0:T(8,128)(2,1)S(1)}, u32[]{:S(2)}, u32[]{:S(2)}) collective-permute-start(bf16[464,352]{1,0:T(8,128)(2,1)} %get-tuple-element.329), channel_id=1, source_target_pairs={{0,16},{8,24},{16,0},{24,8},{1,17},{9,25},{17,1},{25,9},{2,18},{10... | collective-permute-start | bytes 979976 | tf_op jit(solution)/shard_map/ppermute | solution.py:1087
  1392.9 25.7 %collective-permute-start.53 = (bf16[464,352]{1,0:T(8,128)(2,1)}, bf16[464,352]{1,0:T(8,128)(2,1)S(1)}, u32[]{:S(2)}, u32[]{:S(2)}) collective-permute-start(bf16[464,352]{1,0:T(8,128)(2,1)} %get-tuple-element.328), channel_id=1, source_target_pairs={{0,24},{8,0},{16,8},{24,16},{1,25},{9,1},{17,9},{25,17},{2,26},{10... | collective-permute-start | bytes 979976 | tf_op jit(solution)/shard_map/ppermute | solution.py:1087
  1423.7 14.1 collective-permute-start.39
  1430.9 15.7 %collective-permute-start.40 = (bf16[352,352]{1,0:T(8,128)(2,1)S(1)}, bf16[352,352]{1,0:T(8,128)(2,1)S(1)}, u32[]{:S(2)}, u32[]{:S(2)}) collective-permute-start(bf16[352,352]{1,0:T(8,128)(2,1)S(1)} %get-tuple-element.335), channel_id=1, source_target_pairs={{0,16},{8,24},{16,0},{24,8},{1,17},{9,25},{17,1},{25,9},{2,18},{10... | collective-permute-start | bytes 743432 | tf_op jit(solution)/shard_map/ppermute | solution.py:1087
  1430.9 16.6 %collective-permute-start.41 = (bf16[352,352]{1,0:T(8,128)(2,1)S(1)}, bf16[352,352]{1,0:T(8,128)(2,1)S(1)}, u32[]{:S(2)}, u32[]{:S(2)}) collective-permute-start(bf16[352,352]{1,0:T(8,128)(2,1)S(1)} %select_select_fusion.31), channel_id=1, source_target_pairs={{0,24},{8,0},{16,8},{24,16},{1,25},{9,1},{17,9},{25,17},{2,26},{10... | collective-permute-start | bytes 743432 | tf_op jit(solution)/shard_map/ppermute | solution.py:1087
  (102 other events, 1274.2 us)
Sparse Core Ops, SparseCore 0:
  10.9 132.3 all-gather.8
  145.3 67.9 all-gather.10
  215.1 109.6 all-gather.12
  327.1 81.7 all-gather.14
  410.6 105.1 all-gather.16
  517.6 90.8 all-gather.18
  675.6 118.5 reduce-scatter.5
  798.3 148.5 reduce-scatter.7
  950.6 204.9 reduce-scatter.9
  1186.3 88.9 reduce-scatter.11
  1277.7 37.4 all-gather.20
  1318.7 69.1 reduce-scatter.13

commit v4 on v3

--- a/solution.py
+++ b/solution.py
@@ -1181,10 +1181,7 @@
     row_count = images * tile_len
     out_width = cotangent.shape[3]
 
-    f_skip = lax.all_gather(w_skip, EVERY, axis=0, tiled=True).reshape(
-        dp_devices, -1, w_skip.shape[1]
-    )
-    f_skip = jnp.swapaxes(f_skip, 0, 1).reshape(f_skip.shape[1], -1)
+    f_skip = tiles_whole(widen(fetch(w_skip)))
     small = jnp.concatenate([w_patch, w_final, norm_params], axis=1)
     small_widths = (w_patch.shape[1], w_final.shape[1], norm_params.shape[1])
     cuts = (0, small_widths[0], sum(small_widths[:2]), sum(small_widths))
@@ -1249,15 +1246,14 @@
     bias_skip = jnp.concatenate([norm_f[:, 9], norm_f[:, 11]])[None]
     joined, joined_inv, skip_in = join_norm(patch_rows, skip_rows, f_patch, gain_skip, bias_skip)
     f_qkv = tiles_whole(widen(held_qkv, skip_in))
-    part_three = widen(held_three, skip_in, 3)
-    f_three = tiles_whole(part_three)
-    f_out, f_query, f_cross = jnp.split(f_three, 3, axis=1)
     residual = plain_dot(skip_in, f_skip)
     first_z, first_inv = layer_norm(residual)
     first_pre = (first_z * norm_f[:, 0] + norm_f[:, 1]).reshape(
         images, tile_len, model_width
     ) + time_shift[:, None, :]
     first_in = first_pre.reshape(row_count, model_width).astype(BF16)
+    f_three = tiles_whole(widen(held_three, first_in, 3))
+    f_out, f_query, f_cross = jnp.split(f_three, 3, axis=1)
     part_text = widen(held_text, first_in)
     f_text = tiles_whole(part_text)
     first_rows = first_in.reshape(images, tile_len, model_width)
@@ -1276,6 +1272,7 @@
         own_qkv.append(own)
         qk_inv.append(inverses)
         tile_qkv.append(swap_tiles(own))
+    tile_qkv[0], own_qkv[-1] = lax.optimization_barrier((tile_qkv[0], own_qkv[-1]))
     f_up = tiles_whole(widen(held_up, tile_qkv[0]))
     for image in range(images):
         att, lse = attend(tile_qkv[image], flags[image])
@@ -1408,7 +1405,7 @@
     ck_z, ck_inv = layer_norm(jnp.swapaxes(own_key, 1, 2))
     grad_ckey = jnp.swapaxes(norm_back(jnp.swapaxes(sum_text_kv[0], 1, 2), ck_z, ck_inv), 1, 2)
     grad_kv = jnp.stack([grad_ckey, sum_text_kv[1]]).astype(BF16)
-    grad_kv = tiles_whole(grad_kv.reshape(-1, images * text_pad))
+    grad_kv = grad_kv.reshape(-1, images * text_pad)
     grad_qkv = grad_qkv.reshape(3 * model_width, row_count)
     d_qkv = dot_over(first_in, grad_qkv, 0, 1).astype(BF16)
     d_qkv, grad_qkv = lax.optimization_barrier((d_qkv, grad_qkv))
@@ -1425,20 +1422,24 @@
     d_skip_w = left_dot(skip_in, low_one).astype(BF16)
     d_skip_w, low_one = lax.optimization_barrier((d_skip_w, low_one))
     skip_grad, grad_patch, skip_sums = join_back(low_one, f_skip, joined, joined_inv, gain_skip)
-    t_qkv, d_skip_w, joint_grad, skip_sums = lax.optimization_barrier(
-        (t_qkv, d_skip_w, joint_grad, skip_sums)
-    )
+    t_qkv, d_skip_w, joint_grad = lax.optimization_barrier((t_qkv, d_skip_w, joint_grad))
     out_grad, query_w_grad, cross_grad = jnp.split(joint_grad, 3, axis=1)
     t_skip = over_tiles(d_skip_w)
 
-    group_shape = (-1, 2, grid_devices, model_width // grid_devices)
     text_slice = text_states.shape[2] // grid_devices
-    text_cols = lax.dynamic_slice_in_dim(text_rows, grid_at * text_slice, text_slice, 1)
-    d_text = dot_over(text_cols, grad_kv, 0, 1).astype(BF16)
-    d_text = jnp.swapaxes(d_text.reshape(text_slice, grid_devices, 2, -1), 1, 2)
-    d_text = d_text.reshape(text_slice, -1)
-    grouped_text = jnp.swapaxes(part_text.reshape(group_shape), 1, 2).reshape(part_text.shape)
-    text_grad = dot_over(grad_kv, grouped_text, 0, 1).reshape(images, text_pad, text_slice)
+    own_cols = lax.dynamic_slice_in_dim(
+        f_text.reshape(f_text.shape[0], 2, -1), grid_at * group_heads * head_dim, group_heads * head_dim, 2
+    ).reshape(f_text.shape[0], -1)
+    text_parts = jnp.concatenate(
+        [dot_over(text_rows, grad_kv, 0, 1).astype(BF16), plain_dot(own_cols, grad_kv).astype(BF16)],
+        axis=1,
+    )
+    text_parts = swap_tiles(text_parts.reshape(grid_devices, text_slice, -1))
+    own_width = own_cols.shape[1]
+    d_text = text_parts[:, :, :own_width].reshape(grid_devices, text_slice, 2, -1)
+    d_text = jnp.transpose(d_text, (1, 2, 0, 3)).reshape(text_slice, -1)
+    text_grad = jnp.sum(text_parts[:, :, own_width:].astype(F32), axis=0)
+    text_grad = jnp.transpose(text_grad).reshape(images, text_pad, text_slice)
     text_grad = text_grad[:, :text_len]
 
     shift_low = total_tiles(part_shift).astype(BF16)
@@ -1450,20 +1451,6 @@
     )
     grad_time_pre = silu_pull(grad_time_act)[0].astype(BF16)
     d_time = left_dot(embed_cols, grad_time_pre).astype(BF16)
-    late, width = [], w_shift.shape[1]
-    for at in range(dp_devices):
-        pair = d_text[:, 2 * at * width : 2 * (at + 1) * width]
-        own = slice(at * width, (at + 1) * width)
-        late.append(
-            jnp.concatenate([pair[:, :width], pair[:, width:], d_time[:, own], d_shift[:, own]])
-        )
-    qkv_grad = narrow(t_qkv, d_text)
-    qkv_grad, *late = lax.optimization_barrier((qkv_grad, *late))
-    late = narrow_blocks(late)
-    rows = d_text.shape[0]
-    text_w_grad = jnp.concatenate([late[:rows], late[rows : 2 * rows]], axis=1)
-    time_w_grad, shift_w_grad = jnp.split(late[2 * rows :], [d_time.shape[0]], axis=0)
-
     skip_grad = skip_grad.reshape(images, rows_tile, cols_tile, model_width)
     gain_skips, bias_skips = skip_sums[0], skip_sums[1]
     d_patch = left_dot(grad_patch, patch_rows)
@@ -1492,11 +1479,26 @@
         ],
         axis=2,
     )
-    small_grads = narrow(sum_tiles(small_grads.reshape(model_width, -1)))
+    small_grads = sum_tiles(small_grads.reshape(model_width, -1))
+    late, width = [], w_shift.shape[1]
+    small_width = sum(small_widths)
+    for at in range(dp_devices):
+        pair = d_text[:, 2 * at * width : 2 * (at + 1) * width]
+        own = slice(at * width, (at + 1) * width)
+        few = small_grads[:, at * small_width : (at + 1) * small_width].astype(BF16)
+        few = jnp.pad(few, ((0, 0), (0, width - small_width)))
+        late.append(
+            jnp.concatenate([pair[:, :width], pair[:, width:], d_time[:, own], d_shift[:, own], few])
+        )
+    qkv_grad = narrow(t_qkv, d_text)
+    qkv_grad, *late = lax.optimization_barrier((qkv_grad, *late))
+    late = narrow_blocks(late)
+    rows = d_text.shape[0]
+    text_w_grad = jnp.concatenate([late[:rows], late[rows : 2 * rows]], axis=1)
+    ends = (d_time.shape[0], d_time.shape[0] + d_shift.shape[0])
+    time_w_grad, shift_w_grad, few = jnp.split(late[2 * rows :], ends, axis=0)
     skip_w_grad = narrow(t_skip)
-    patch_grad, final_grad, norms_grad = (
-        small_grads[:, cuts[at] : cuts[at + 1]] for at in range(3)
-    )
+    patch_grad, final_grad, norms_grad = (few[:, cuts[at] : cuts[at + 1]] for at in range(3))
     return (
         prediction,
         latent_grad,

time: 1470 us -> 1530 us (1.041)
  waiting for transfers between devices: 338 us -> 409 us
    all_to_all x8 -> x9, waiting for transfers between devices: 99.3 us -> 183 us  [swap_tiles(): lax.all_to_all(values_in, TILE, split_axis=0, concat_axis=0, tiled=True)]
    ppermute x18 -> x21, waiting for transfers between devices: 94.9 us -> 53.2 us  [fetch(): lax.ppermute(weight, 'dp', shift_pairs(devices, step))]
    reshape x2 -> x0, local copies, waits for them, and re-layouts: 27.9 us -> none  [the longest x1 16.2 us: local_heads(): lax.all_gather(w_skip, EVERY, axis=0, tiled=True)]
    ppermute x3, waiting for transfers between devices: 2.8 us -> 29.2 us  [sum_tiles(): total = jnp.where(high, upper, lower) + lax.ppermute(sent, TILE, pairs)]
    all_gather x6, waiting for transfers between devices: 29 us -> 6.9 us  [tiles_whole(): return lax.all_gather(weight, TILE, axis=0, tiled=True)]
    unnamed x203 -> x216, local copies, waits for them, and re-layouts: 26.6 us -> 42.3 us
    ppermute x21 -> x18, waiting for transfers between devices: 95.9 us -> 107 us  [narrow_blocks(): received.append(lax.ppermute(sent, 'dp', shift_pairs(devices, step)))]
    dot_general x11 -> x10, matrix products: 118 us -> 111 us  [dot_over(): lax.dot_general(left_mat, right_mat, (((left_axis,), (right_axis,)), ((),...]
  transfers between devices with their start and end apart: 74 -> 74, of which waited for: 34 -> 34; matrix products, arithmetic and copies ran while one was open for 33% -> 31% of each run, Pallas kernels for 25% -> 24%
where the time goes in v4:
time: 1530 us; the launch traced here: 1520 us
  waiting for transfers between devices  409 us (27%)
  matrix products  375 us (25%)
  Pallas kernels  366 us (24%)
  starting transfers between devices  153 us (10%)
  local copies, waits for them, and re-layouts  96.9 us (6%)
  other arithmetic  82.4 us (5%)
  blocking collectives  17.8 us (1%)
  between operations  16.2 us (1%)
    all_to_all x9, waiting for transfers between devices, swap_tiles(): lax.all_to_all(values_in, TILE, split_axis=0, concat_axis=0, tiled=True)  183 us
    pallas_call x2, Pallas kernels, attend_back(): kernel_call(functools.partial(attend_back_body, score_scale), 2560 * head...  178 us
    dot_general x10, matrix products, dot_over(): lax.dot_general(left_mat, right_mat, (((left_axis,), (right_axis,)), ((),...  111 us
    dot_general x10, matrix products, plain_dot(): return jnp.dot(left_mat, right_mat, preferred_element_type=jnp.float32)  108 us
    ppermute x18, waiting for transfers between devices, narrow_blocks(): received.append(lax.ppermute(sent, 'dp', shift_pairs(devices, step)))  107 us
    dot_general x9, matrix products, left_dot(): lax.dot_general(left_mat, right_mat, (((0,), (0,)), ((), ())), preferred_...  90.6 us
    pallas_call x2, Pallas kernels, attend(): kernel_call(attend_body, 1024 * heads * tiles ** 2 * tile_len ** 2, 8 * q...  68.6 us
    dot_general x4, matrix products, right_dot(): lax.dot_general(left_mat, right_mat, (((1,), (1,)), ((), ())), preferred_...  65.3 us
  transfers between devices with their start and end apart: 74, of which 34 were waited for; matrix products, arithmetic and copies ran while one was open for 31% of the time, Pallas kernels for 24%

profile of v4, /device:TPU:0, one launch (start us, length us, event | category | flops | bytes accessed | tf_op | source)
XLA Modules:
  0.0 1516.6 jit_solution(14745409400310850675)
XLA Ops:
  15.2 15.3 %collective-permute-done.4 = bf16[352,352]{1,0:T(8,128)(2,1)S(1)} collective-permute-done((bf16[352,352]{1,0:T(8,128)(2,1)}, bf16[352,352]{1,0:T(8,128)(2,1)S(1)}, u32[]{:S(2)}, u32[]{:S(2)}) %collective-permute-start.4) | collective-permute-done | bytes 247840 | tf_op jit(solution)/shard_map/ppermute | solution.py:1067
  36.1 6.9 collective-permute-start.1
  48.8 8.0 collective-permute-done.1
  56.8 5.7 collective-permute-start.14
  63.7 17.8 %all-gather = bf16[8,176,60]{1,2,0:T(8,128)(2,1)S(1)} all-gather(bf16[1,176,60]{1,2,0:T(8,128)(2,1)S(1)} %reshape.636), channel_id=1, replica_groups=mesh['dp'=4,'row'=4,'col'=2] {'row','col'}, dimensions={0}, use_global_device_ids=true | all-gather | bytes 190080 | tf_op jit(solution)/shard_map/all_gather | solution.py:1136
  84.9 9.6 shard_map.314
  117.7 23.2 %collective-permute-start.16 = (bf16[176,1056]{1,0:T(8,128)(2,1)S(1)}, bf16[176,1056]{1,0:T(8,128)(2,1)}, u32[]{:S(2)}, u32[]{:S(2)}) collective-permute-start(bf16[176,1056]{1,0:T(8,128)(2,1)S(1)} %concatenate.103), channel_id=1, source_target_pairs={{0,16},{8,24},{16,0},{24,8},{1,17},{9,25},{17,1},{25,9},{2,18},{10... | collective-permute-start | bytes 1115144 | tf_op jit(solution)/shard_map/ppermute | solution.py:1067
  141.1 14.1 fusion.102
  157.7 20.4 %collective-permute-done.16 = bf16[176,1056]{1,0:T(8,128)(2,1)} collective-permute-done((bf16[176,1056]{1,0:T(8,128)(2,1)S(1)}, bf16[176,1056]{1,0:T(8,128)(2,1)}, u32[]{:S(2)}, u32[]{:S(2)}) %collective-permute-start.16) | collective-permute-done | bytes 371744 | tf_op jit(solution)/shard_map/ppermute | solution.py:1067
  189.6 6.5 collective-permute-done.19
  204.2 14.7 shard_map.315
  227.8 14.7 shard_map.316
  242.5 60.7 %all-to-all-done.query_ref.key_ref.value_ref = bf16[8,3,2,88,512]{4,3,2,1,0:T(8,128)(2,1)} async-done(((bf16[8,3,2,88,512]{4,3,2,1,0:T(8,128)(2,1)}), bf16[8,3,2,88,512]{4,3,2,1,0:T(8,128)(2,1)}, u32[]{:S(2)}, u32[]{:S(2)}) %all-to-all-start) | async-done | bytes 4325408 | tf_op jit(solution)/shard_map/all_to_all | solution.py:1057
  310.8 71.8 %all-to-all-done.2.query_ref.key_ref.value_ref = bf16[8,3,2,88,512]{4,3,2,1,0:T(8,128)(2,1)} async-done(((bf16[8,3,2,88,512]{4,3,2,1,0:T(8,128)(2,1)}), bf16[8,3,2,88,512]{4,3,2,1,0:T(8,128)(2,1)}, u32[]{:S(2)}, u32[]{:S(2)}) %all-to-all-start.2) | async-done | bytes 4325408 | tf_op jit(solution)/shard_map/all_to_all | solution.py:1057
  382.6 34.4 %shard_map.318 = (bf16[8,2,88,512]{3,2,1,0:T(8,128)(2,1)}, f32[8,2,1,512]{3,2,1,0:T(1,128)}) custom-call(bf16[8,3,2,88,512]{4,3,2,1,0:T(8,128)(2,1)} %all-to-all-done.2.query_ref.key_ref.value_ref, bf16[8,3,2,88,512]{4,3,2,1,0:T(8,128)(2,1)} %all-to-all-done.2.query_ref.key_ref.value_ref, ...), custom_call_target="tpu_custom_call" | custom-call | flops 34359738368 | bytes 17301504 | tf_op jit(solution)/shard_map/pallas_call | solution.py:757
  420.6 34.1 %shard_map.317 = (bf16[8,2,88,512]{3,2,1,0:T(8,128)(2,1)}, f32[8,2,1,512]{3,2,1,0:T(1,128)}) custom-call(bf16[8,3,2,88,512]{4,3,2,1,0:T(8,128)(2,1)} %all-to-all-done.query_ref.key_ref.value_ref, bf16[8,3,2,88,512]{4,3,2,1,0:T(8,128)(2,1)} %all-to-all-done.query_ref.key_ref.value_ref, bf16[8,3,2,88,512]{4,3,2,1,0:T(8,128)(2,1)} %all-to-all-done.query_ref.key_ref.value_ref, ...), custom_call_target="tpu_custom_call" | custom-call | flops 34359738368 | bytes 17301504 | tf_op jit(solution)/shard_map/pallas_call | solution.py:757
  464.3 29.0 %all-to-all-done.1 = bf16[8,2,88,512]{3,2,1,0:T(8,128)(2,1)S(1)} async-done(((bf16[8,2,88,512]{3,2,1,0:T(8,128)(2,1)}), bf16[8,2,88,512]{3,2,1,0:T(8,128)(2,1)S(1)}, u32[]{:S(2)}, u32[]{:S(2)}) %all-to-all-start.1) | async-done | bytes 1441824 | tf_op jit(solution)/shard_map/all_to_all | solution.py:1057
  493.3 10.7 fusion.103
  508.9 10.1 fusion.106
  519.8 9.8 fusion.8
  529.7 14.3 shard_map.319
  544.0 8.5 fusion.104
  557.1 39.8 %add_convert_fusion = (bf16[1024,6144]{1,0:T(8,128)(2,1)}, bf16[1024,6144]{1,0:T(8,128)(2,1)}) fusion(bf16[1408,6144]{1,0:T(8,128)(2,1)} %all-gather.16.cloned.1.call-done, f32[1024,1408]{1,0:T(8,128)} %copy-done.3, f32[1408]{0:T(1024)S(1)} %copy-done.75, f32[1408]{0:T(1024)S(1)} %copy-done.52, f32[1024]{0:T(1024)S(1)} %add_rsqrt_fusion.2, ...), kind=kOutput, calls=%fused_computation.1 | convolution fusion | flops 17843486720 | bytes 48253952 | tf_op jit(solution)/shard_map/dot_general | solution.py:72
  596.9 6.8 all-gather.18.cloned.1.call-done
  603.7 28.6 %fusion.105 = (f32[1024]{0:T(1024)S(1)}, f32[1024,1408]{1,0:T(8,128)S(1)}) fusion(f32[1024,1408]{1,0:T(8,128)} %copy-done.3, bf16[1024,6144]{1,0:T(8,128)(2,1)} %get-tuple-element.123, bf16[6144,1408]{0,1:T(8,128)(2,1)} %all-gather.18.cloned.1.call-done), kind=kOutput, calls=%fused_computation.330 | convolution fusion | flops 17719623680 | bytes 41422848 | tf_op jit(solution)/shard_map/dot_general | solution.py:72
  642.6 28.2 %convolution_convert_fusion = bf16[6144,1408]{1,0:T(8,128)(2,1)} fusion(bf16[1024,6144]{1,0:T(8,128)(2,1)} %get-tuple-element.123, bf16[1024,1408]{1,0:T(8,128)(2,1)S(1)} %get-tuple-element.128), kind=kOutput, calls=%fused_computation.5 | convolution fusion | flops 17725390848 | bytes 32768000 | tf_op jit(solution)/shard_map/dot_general | solution.py:76
  672.6 30.5 %multiply_convert_fusion = bf16[1024,6144]{1,0:T(8,128)(2,1)} fusion(bf16[1024,6144]{1,0:T(8,128)(2,1)} %get-tuple-element.129, bf16[1024,1408]{1,0:T(8,128)(2,1)S(1)} %copy-done.18, bf16[6144,1408]{0,1:T(8,128)(2,1)} %all-gather.18.cloned.1.call-done), kind=kOutput, calls=%fused_computation | convolution fusion | flops 17735614464 | bytes 45350912 | tf_op jit(solution)/shard_map/dot_general | solution.py:82
  703.1 26.1 %convolution_convert_fusion.1 = bf16[1408,6144]{1,0:T(8,128)(2,1)} fusion(bf16[1024,6144]{1,0:T(8,128)(2,1)} %multiply_convert_fusion, f32[1024,1408]{1,0:T(8,128)} %copy-done.3, f32[1408]{0:T(1024)S(1)} %copy-done.75, f32[1408]{0:T(1024)S(1)} %copy-done.52, f32[1024]{0:T(1024)S(1)} %add_rsqrt_fusion.2, f32[1024]{0:T(1024)S(1)} %broadcast_multiply_fusion.12), kind=kOutput, calls=%fused_computation.6 | convolution fusion | flops 17732599808 | bytes 35671040 | tf_op jit(solution)/shard_map/dot_general | solution.py:76
  729.2 31.4 %multiply_reduce_fusion.1 = (f32[1408]{0:T(1024)}, f32[1024]{0:T(1024)S(1)}, f32[1024]{0:T(1024)S(1)}, f32[1408]{0:T(1024)}, f32[1024,1408]{1,0:T(8,128)}) fusion(f32[1024,1408]{1,0:T(8,128)} %copy-done.3, f32[1024]{0:T(1024)S(1)} %add_rsqrt_fusion.2, f32[1024]{0:T(1024)S(1)} %broadcast_multiply_fusion.12, f32[1408]{0:T(1024)S(1)} %copy-done.52, ...), kind=kOutput, calls=%fused_computation.19 | convolution fusion | flops 17729710080 | bytes 41452032 | tf_op jit(solution)/shard_map/dot_general | solution.py:82
  760.7 7.7 multiply_add_fusion.1
  768.4 10.5 convolution_convert_fusion.7
  778.9 21.1 %shard_map.320 = (bf16[16,88,1024]{2,1,0:T(8,128)(2,1)}, bf16[16,88,768]{2,1,0:T(8,128)(2,1)}, bf16[16,88,768]{2,1,0:T(8,128)(2,1)}) custom-call(bf16[16,88,1024]{2,1,0:T(8,128)(2,1)} %get-tuple-element.132.query_ref, f32[2,16,88,768]{3,2,1,0:T(8,128)} %bitcast.189, bf16[16,88,1024]{2,1,0:T(8,128)(2,1)} %bitcast.217, ...), custom_call_target="tpu_custom_call" | custom-call | flops 16106127360 | bytes 23068672 | tf_op jit(solution)/shard_map/pallas_call | solution.py:957
  800.1 14.2 multiply_reduce_fusion.2
  814.3 6.3 fusion.89
  820.6 6.7 fusion.15
  832.1 8.6 fusion.2
  840.7 9.8 fusion.1
  850.6 6.6 fusion
  861.2 5.0 all-to-all-done.4.grad_ref
  876.4 6.4 fusion.18
  887.2 89.2 %shard_map.321 = bf16[8,3,2,88,512]{4,3,2,1,0:T(8,128)(2,1)} custom-call(bf16[8,3,2,88,512]{4,3,2,1,0:T(8,128)(2,1)} %all-to-all-done.query_ref.key_ref.value_ref, bf16[8,3,2,88,512]{4,3,2,1,0:T(8,128)(2,1)} %all-to-all-done.query_ref.key_ref.value_ref, bf16[8,3,2,88,512]{4,3,2,1,0:T(8,128)(2,1)} %all-to-all-done.query_ref.key_ref.value_ref, ...), custom_call_target="tpu_custom_call" | custom-call | flops 85899345920 | bytes 17301504 | tf_op jit(solution)/shard_map/pallas_call | solution.py:845
  988.3 89.1 %shard_map.322 = bf16[8,3,2,88,512]{4,3,2,1,0:T(8,128)(2,1)} custom-call(bf16[8,3,2,88,512]{4,3,2,1,0:T(8,128)(2,1)} %all-to-all-done.2.query_ref.key_ref.value_ref, bf16[8,3,2,88,512]{4,3,2,1,0:T(8,128)(2,1)} %all-to-all-done.2.query_ref.key_ref.value_ref, bf16[8,3,2,88,512]{4,3,2,1,0:T(8,128)(2,1)} %all-to-all-done.2.query_ref.key_ref.value_ref, ...), custom_call_target="tpu_custom_call" | custom-call | flops 85899345920 | bytes 17301504 | tf_op jit(solution)/shard_map/pallas_call | solution.py:845
  1088.0 23.0 %collective-permute-done.31 = bf16[176,1536]{1,0:T(8,128)(2,1)S(1)} collective-permute-done((bf16[176,1536]{1,0:T(8,128)(2,1)S(1)}, bf16[176,1536]{1,0:T(8,128)(2,1)S(1)}, u32[]{:S(2)}, u32[]{:S(2)}) %collective-permute-start.31) | collective-permute-done | bytes 540704 | tf_op jit(solution)/shard_map/ppermute | solution.py:1087
  1111.0 12.6 collective-permute-done.32
  1125.1 10.3 shard_map.323.others_0_
  1135.4 16.3 %all-to-all-done.6.grad_ref = bf16[8,3,2,88,512]{4,3,2,1,0:T(8,128)(2,1)} async-done(((bf16[8,3,2,88,512]{4,3,2,1,0:T(8,128)(2,1)}), bf16[8,3,2,88,512]{4,3,2,1,0:T(8,128)(2,1)}, u32[]{:S(2)}, u32[]{:S(2)}) %all-to-all-start.6) | async-done | bytes 4325408 | tf_op jit(solution)/shard_map/all_to_all | solution.py:1057
  1151.7 10.2 shard_map.324
  1161.9 19.9 %convolution_convert_fusion.2 = bf16[1408,4224]{1,0:T(8,128)(2,1)} fusion(bf16[1024,1408]{1,0:T(8,128)(2,1)S(1)} %copy-done.12, bf16[4224,1024]{1,0:T(8,128)(2,1)} %bitcast.169), kind=kOutput, calls=%fused_computation.7 | convolution fusion | flops 12186206208 | bytes 23429120 | tf_op jit(solution)/shard_map/dot_general | solution.py:1144
  1197.2 21.6 %multiply_reduce_fusion.3 = (f32[1408]{0:T(1024)S(1)}, f32[1024]{0:T(1024)S(1)}, f32[1024]{0:T(1024)S(1)}, f32[1408]{0:T(1024)S(1)}, f32[1024,1408]{1,0:T(8,128)}) fusion(f32[1024,1408]{1,0:T(8,128)S(1)} %bitcast.168, f32[1024]{0:T(1024)S(1)} %copy-done.47, f32[1024]{0:T(1024)S(1)} %copy-done.45, f32[1408]{0:T(1024)S(1)} %copy-done.43, ...), kind=kOutput, calls=%fused_computation.21 | convolution fusion | flops 12193230848 | bytes 32113152 | tf_op jit(solution)/shard_map/dot_general | solution.py:1144
  1218.8 6.5 add_convert_fusion.1.low_ref
  1241.0 14.1 convolution_convert_fusion.3
  1255.2 15.2 reduce-scatter.12.cloned.1.call-done
  1270.3 6.4 collective-permute-done.34
  1290.6 24.2 %shard_map.325 = (f32[1024,1408]{1,0:T(8,128)}, bf16[1024,1408]{1,0:T(8,128)(2,1)}, f32[2,2816]{1,0:T(2,128)}) custom-call(bf16[1024,1408]{1,0:T(8,128)(2,1)} %add_convert_fusion.1.low_ref, bf16[2816,1408]{1,0:T(8,128)(2,1)} %all-gather.8.cloned.1.call-done.weight_ref, f32[1024,2816]{1,0:T(8,128)} %get-tuple-element.159.z_ref, ...), custom_call_target="tpu_custom_call" | custom-call | flops 8120172544 | bytes 25952256 | tf_op jit(solution)/shard_map/pallas_call | solution.py:1032
  1349.8 29.2 %collective-permute-done.47 = f32[176,60]{1,0:T(8,128)S(1)} collective-permute-done((f32[176,60]{1,0:T(8,128)S(1)}, f32[176,60]{1,0:T(8,128)S(1)}, u32[]{:S(2)}, u32[]{:S(2)}) %collective-permute-start.47) | collective-permute-done | bytes 42272 | tf_op jit(solution)/shard_map/ppermute | solution.py:1114
  1396.2 7.1 collective-permute-done.37
  1403.3 8.3 collective-permute-done.38
  1423.7 7.8 collective-permute-start.48
  1443.2 10.6 collective-permute-done.50
  1453.7 15.3 %collective-permute-done.49 = bf16[640,352]{1,0:T(8,128)(2,1)S(1)} collective-permute-done((bf16[640,352]{1,0:T(8,128)(2,1)S(1)}, bf16[640,352]{1,0:T(8,128)(2,1)S(1)}, u32[]{:S(2)}, u32[]{:S(2)}) %collective-permute-start.49) | collective-permute-done | bytes 450592 | tf_op jit(solution)/shard_map/ppermute | solution.py:1087
  1476.9 10.0 collective-permute-start.53
  1488.6 5.3 collective-permute-done.53
  1493.9 6.3 collective-permute-done.51
  1500.2 8.3 collective-permute-done.52
  (547 shorter events, 298.8 us)
Async XLA Ops:
  7.2 133.8 %all-gather.8.cloned.1.call-start = ((), (), s32[]{:S(2)}) async-start(), calls=%async_computation.14 | async-start | bytes 8921088 | tf_op jit(solution)/shard_map/all_gather | solution.py:1136
  7.3 23.3 %collective-permute-start.4 = (bf16[352,352]{1,0:T(8,128)(2,1)}, bf16[352,352]{1,0:T(8,128)(2,1)S(1)}, u32[]{:S(2)}, u32[]{:S(2)}) collective-permute-start(bf16[352,352]{1,0:T(8,128)(2,1)} %param.26), channel_id=1, source_target_pairs={{0,16},{8,24},{16,0},{24,8},{1,17},{9,25},{17,1},{25,9},{2,18},{10... | collective-permute-start | bytes 743432 | tf_op jit(solution)/shard_map/ppermute | solution.py:1067
  11.4 19.2 %collective-permute-start.3 = (bf16[352,352]{1,0:T(8,128)(2,1)}, bf16[352,352]{1,0:T(8,128)(2,1)S(1)}, u32[]{:S(2)}, u32[]{:S(2)}) collective-permute-start(bf16[352,352]{1,0:T(8,128)(2,1)} %param.26), channel_id=1, source_target_pairs={{0,8},{8,16},{16,24},{24,0},{1,9},{9,17},{17,25},{25,1},{2,10},{10... | collective-permute-start | bytes 743432 | tf_op jit(solution)/shard_map/ppermute | solution.py:1067
  13.0 18.3 %collective-permute-start.5 = (bf16[352,352]{1,0:T(8,128)(2,1)}, bf16[352,352]{1,0:T(8,128)(2,1)S(1)}, u32[]{:S(2)}, u32[]{:S(2)}) collective-permute-start(bf16[352,352]{1,0:T(8,128)(2,1)} %param.26), channel_id=1, source_target_pairs={{0,24},{8,0},{16,8},{24,16},{1,25},{9,1},{17,9},{25,17},{2,26},{10... | collective-permute-start | bytes 743432 | tf_op jit(solution)/shard_map/ppermute | solution.py:1067
  33.9 170.3 %all-gather.10.cloned.1.call-start = ((), (), s32[]{:S(2)}) async-start(), calls=%async_computation.15 | async-start | bytes 13381632 | tf_op jit(solution)/shard_map/all_gather | solution.py:1136
  36.1 20.7 %collective-permute-start.1 = (bf16[384,352]{0,1:T(8,128)(2,1)S(1)}, bf16[384,352]{0,1:T(8,128)(2,1)S(1)}, u32[]{:S(2)}, u32[]{:S(2)}) collective-permute-start(bf16[384,352]{0,1:T(8,128)(2,1)S(1)} %pad_maximum_fusion.10), channel_id=1, source_target_pairs={{0,16},{8,24},{16,0},{24,8},{1,17},{9,25},{17,1},{25,9},{2,18},{10... | collective-permute-start | bytes 811016 | tf_op jit(solution)/shard_map/ppermute | solution.py:1067
  43.0 19.9 %collective-permute-start.2 = (bf16[384,352]{0,1:T(8,128)(2,1)S(1)}, bf16[384,352]{0,1:T(8,128)(2,1)S(1)}, u32[]{:S(2)}, u32[]{:S(2)}) collective-permute-start(bf16[384,352]{0,1:T(8,128)(2,1)S(1)} %pad_maximum_fusion.10), channel_id=1, source_target_pairs={{0,24},{8,0},{16,8},{24,16},{1,25},{9,1},{17,9},{25,17},{2,26},{10... | collective-permute-start | bytes 811016 | tf_op jit(solution)/shard_map/ppermute | solution.py:1067
  43.5 19.4 %collective-permute-start = (bf16[384,352]{0,1:T(8,128)(2,1)S(1)}, bf16[384,352]{0,1:T(8,128)(2,1)S(1)}, u32[]{:S(2)}, u32[]{:S(2)}) collective-permute-start(bf16[384,352]{0,1:T(8,128)(2,1)S(1)} %pad_maximum_fusion.10), channel_id=1, source_target_pairs={{0,8},{8,16},{16,24},{24,0},{1,9},{9,17},{17,25},{25,1},{2,10},{10... | collective-permute-start | bytes 811016 | tf_op jit(solution)/shard_map/ppermute | solution.py:1067
  45.0 49.5 %collective-permute-start.13 = (bf16[176,1056]{1,0:T(8,128)(2,1)S(1)}, bf16[176,1056]{1,0:T(8,128)(2,1)S(1)}, u32[]{:S(2)}, u32[]{:S(2)}) collective-permute-start(bf16[176,1056]{1,0:T(8,128)(2,1)S(1)} %copy-done.35), channel_id=1, source_target_pairs={{0,16},{8,24},{16,0},{24,8},{1,17},{9,25},{17,1},{25,9},{2,18},{10... | collective-permute-start | bytes 1115144 | tf_op jit(solution)/shard_map/ppermute | solution.py:1067
  45.1 49.4 %collective-permute-start.12 = (bf16[176,1056]{1,0:T(8,128)(2,1)S(1)}, bf16[176,1056]{1,0:T(8,128)(2,1)S(1)}, u32[]{:S(2)}, u32[]{:S(2)}) collective-permute-start(bf16[176,1056]{1,0:T(8,128)(2,1)S(1)} %copy-done.35), channel_id=1, source_target_pairs={{0,8},{8,16},{16,24},{24,0},{1,9},{9,17},{17,25},{25,1},{2,10},{10... | collective-permute-start | bytes 1115144 | tf_op jit(solution)/shard_map/ppermute | solution.py:1067
  56.8 37.8 %collective-permute-start.14 = (bf16[176,1056]{1,0:T(8,128)(2,1)S(1)}, bf16[176,1056]{1,0:T(8,128)(2,1)S(1)}, u32[]{:S(2)}, u32[]{:S(2)}) collective-permute-start(bf16[176,1056]{1,0:T(8,128)(2,1)S(1)} %copy-done.35), channel_id=1, source_target_pairs={{0,24},{8,0},{16,8},{24,16},{1,25},{9,1},{17,9},{25,17},{2,26},{10... | collective-permute-start | bytes 1115144 | tf_op jit(solution)/shard_map/ppermute | solution.py:1067
  100.2 393.1 %all-gather.12.cloned.1.call-start = ((), (), s32[]{:S(2)}) async-start(), calls=%async_computation.16 | async-start | bytes 13381632 | tf_op jit(solution)/shard_map/all_gather | solution.py:1136
  114.9 26.1 %collective-permute-start.11 = (f32[2,1408]{1,0:T(2,128)S(1)}, f32[2,1408]{1,0:T(2,128)S(1)}, u32[]{:S(2)}, u32[]{:S(2)}) collective-permute-start(f32[2,1408]{1,0:T(2,128)S(1)} %add.511), channel_id=1, source_target_pairs={{0,4},{1,5},{2,6},{3,7},{4,0},{5,1},{6,2},{7,3},{8,12},{9,13},{10,... | collective-permute-start | bytes 33800 | tf_op jit(solution)/shard_map/ppermute | solution.py:1124
  117.6 40.0 %collective-permute-start.17 = (bf16[176,1056]{1,0:T(8,128)(2,1)S(1)}, bf16[176,1056]{1,0:T(8,128)(2,1)}, u32[]{:S(2)}, u32[]{:S(2)}) collective-permute-start(bf16[176,1056]{1,0:T(8,128)(2,1)S(1)} %concatenate.103), channel_id=1, source_target_pairs={{0,24},{8,0},{16,8},{24,16},{1,25},{9,1},{17,9},{25,17},{2,26},{10... | collective-permute-start | bytes 1115144 | tf_op jit(solution)/shard_map/ppermute | solution.py:1067
  117.7 60.3 %collective-permute-start.16 = (bf16[176,1056]{1,0:T(8,128)(2,1)S(1)}, bf16[176,1056]{1,0:T(8,128)(2,1)}, u32[]{:S(2)}, u32[]{:S(2)}) collective-permute-start(bf16[176,1056]{1,0:T(8,128)(2,1)S(1)} %concatenate.103), channel_id=1, source_target_pairs={{0,16},{8,24},{16,0},{24,8},{1,17},{9,25},{17,1},{25,9},{2,18},{10... | collective-permute-start | bytes 1115144 | tf_op jit(solution)/shard_map/ppermute | solution.py:1067
  140.8 37.2 %collective-permute-start.15 = (bf16[176,1056]{1,0:T(8,128)(2,1)S(1)}, bf16[176,1056]{1,0:T(8,128)(2,1)}, u32[]{:S(2)}, u32[]{:S(2)}) collective-permute-start(bf16[176,1056]{1,0:T(8,128)(2,1)S(1)} %concatenate.103), channel_id=1, source_target_pairs={{0,8},{8,16},{16,24},{24,0},{1,9},{9,17},{17,25},{25,1},{2,10},{10... | collective-permute-start | bytes 1115144 | tf_op jit(solution)/shard_map/ppermute | solution.py:1067
  185.6 323.4 %all-gather.14.cloned.1.call-start = ((), (), s32[]{:S(2)}) async-start(), calls=%async_computation.17 | async-start | bytes 6488064 | tf_op jit(solution)/shard_map/all_gather | solution.py:1136
  185.6 10.4 collective-permute-start.19
  185.8 12.1 collective-permute-start.20
  218.9 84.3 %all-to-all-start = ((bf16[8,3,2,88,512]{4,3,2,1,0:T(8,128)(2,1)}), bf16[8,3,2,88,512]{4,3,2,1,0:T(8,128)(2,1)}, u32[]{:S(2)}, u32[]{:S(2)}) async-start(bf16[8,3,2,88,512]{4,3,2,1,0:T(8,128)(2,1)} %get-tuple-element.105.own_ref), calls=%async_computation | async-start | bytes 8650752 | tf_op jit(solution)/shard_map/all_to_all | solution.py:1057
  223.6 333.4 %all-gather.16.cloned.1.call-start = ((), (), s32[]{:S(2)}) async-start(), calls=%async_computation.18 | async-start | bytes 19464192 | tf_op jit(solution)/shard_map/all_gather | solution.py:1136
  223.7 79.5 %collective-permute-start.22 = (bf16[176,1536]{1,0:T(8,128)(2,1)S(1)}, bf16[176,1536]{1,0:T(8,128)(2,1)S(1)}, u32[]{:S(2)}, u32[]{:S(2)}) collective-permute-start(bf16[176,1536]{1,0:T(8,128)(2,1)S(1)} %copy-done.31), channel_id=1, source_target_pairs={{0,16},{8,24},{16,0},{24,8},{1,17},{9,25},{17,1},{25,9},{2,18},{10... | collective-permute-start | bytes 1622024 | tf_op jit(solution)/shard_map/ppermute | solution.py:1067
  223.8 79.5 %collective-permute-start.21 = (bf16[176,1536]{1,0:T(8,128)(2,1)S(1)}, bf16[176,1536]{1,0:T(8,128)(2,1)S(1)}, u32[]{:S(2)}, u32[]{:S(2)}) collective-permute-start(bf16[176,1536]{1,0:T(8,128)(2,1)S(1)} %copy-done.31), channel_id=1, source_target_pairs={{0,8},{8,16},{16,24},{24,0},{1,9},{9,17},{17,25},{25,1},{2,10},{10... | collective-permute-start | bytes 1622024 | tf_op jit(solution)/shard_map/ppermute | solution.py:1067
  225.5 77.7 %collective-permute-start.23 = (bf16[176,1536]{1,0:T(8,128)(2,1)S(1)}, bf16[176,1536]{1,0:T(8,128)(2,1)S(1)}, u32[]{:S(2)}, u32[]{:S(2)}) collective-permute-start(bf16[176,1536]{1,0:T(8,128)(2,1)S(1)} %copy-done.31), channel_id=1, source_target_pairs={{0,24},{8,0},{16,8},{24,16},{1,25},{9,1},{17,9},{25,17},{2,26},{10... | collective-permute-start | bytes 1622024 | tf_op jit(solution)/shard_map/ppermute | solution.py:1067
  305.1 77.4 %all-to-all-start.2 = ((bf16[8,3,2,88,512]{4,3,2,1,0:T(8,128)(2,1)}), bf16[8,3,2,88,512]{4,3,2,1,0:T(8,128)(2,1)}, u32[]{:S(2)}, u32[]{:S(2)}) async-start(bf16[8,3,2,88,512]{4,3,2,1,0:T(8,128)(2,1)} %get-tuple-element.154.own_ref), calls=%async_computation.2 | async-start | bytes 8650752 | tf_op jit(solution)/shard_map/all_to_all | solution.py:1057
  417.0 37.7 %all-to-all-start.3 = ((bf16[8,2,88,512]{3,2,1,0:T(8,128)(2,1)}), bf16[8,2,88,512]{3,2,1,0:T(8,128)(2,1)S(1)}, u32[]{:S(2)}, u32[]{:S(2)}) async-start(bf16[8,2,88,512]{3,2,1,0:T(8,128)(2,1)} %get-tuple-element.109.att_ref), calls=%async_computation.3 | async-start | bytes 2883584 | tf_op jit(solution)/shard_map/all_to_all | solution.py:1057
  454.8 38.6 %all-to-all-start.1 = ((bf16[8,2,88,512]{3,2,1,0:T(8,128)(2,1)}), bf16[8,2,88,512]{3,2,1,0:T(8,128)(2,1)S(1)}, u32[]{:S(2)}, u32[]{:S(2)}) async-start(bf16[8,2,88,512]{3,2,1,0:T(8,128)(2,1)} %get-tuple-element.108.att_ref), calls=%async_computation.1 | async-start | bytes 2883584 | tf_op jit(solution)/shard_map/all_to_all | solution.py:1057
  458.9 144.9 %all-gather.18.cloned.1.call-start = ((), (), s32[]{:S(2)}) async-start(), calls=%async_computation.19 | async-start | bytes 19464192 | tf_op jit(solution)/shard_map/all_gather | solution.py:1136
  458.9 45.1 %collective-permute-start.25 = (bf16[768,352]{0,1:T(8,128)(2,1)S(1)}, bf16[768,352]{0,1:T(8,128)(2,1)}, u32[]{:S(2)}, u32[]{:S(2)}) collective-permute-start(bf16[768,352]{0,1:T(8,128)(2,1)S(1)} %copy-done.32), channel_id=1, source_target_pairs={{0,16},{8,24},{16,0},{24,8},{1,17},{9,25},{17,1},{25,9},{2,18},{10... | collective-permute-start | bytes 1622024 | tf_op jit(solution)/shard_map/ppermute | solution.py:1067
  460.5 43.5 %collective-permute-start.24 = (bf16[768,352]{0,1:T(8,128)(2,1)S(1)}, bf16[768,352]{0,1:T(8,128)(2,1)}, u32[]{:S(2)}, u32[]{:S(2)}) collective-permute-start(bf16[768,352]{0,1:T(8,128)(2,1)S(1)} %copy-done.32), channel_id=1, source_target_pairs={{0,8},{8,16},{16,24},{24,0},{1,9},{9,17},{17,25},{25,1},{2,10},{10... | collective-permute-start | bytes 1622024 | tf_op jit(solution)/shard_map/ppermute | solution.py:1067
  462.6 41.4 %collective-permute-start.26 = (bf16[768,352]{0,1:T(8,128)(2,1)S(1)}, bf16[768,352]{0,1:T(8,128)(2,1)}, u32[]{:S(2)}, u32[]{:S(2)}) collective-permute-start(bf16[768,352]{0,1:T(8,128)(2,1)S(1)} %copy-done.32), channel_id=1, source_target_pairs={{0,24},{8,0},{16,8},{24,16},{1,25},{9,1},{17,9},{25,17},{2,26},{10... | collective-permute-start | bytes 1622024 | tf_op jit(solution)/shard_map/ppermute | solution.py:1067
  507.3 292.7 %reduce-scatter.6.cloned.1.call-start = ((), (), s32[]{:S(2)}) async-start(), calls=%async_computation.20 | async-start | bytes 19464192 | tf_op jit(solution)/shard_map/reduce_scatter | solution.py:1131
  670.8 411.3 %reduce-scatter.8.cloned.1.call-start = ((), (), s32[]{:S(2)}) async-start(), calls=%async_computation.21 | async-start | bytes 19464192 | tf_op jit(solution)/shard_map/reduce_scatter | solution.py:1131
  827.4 38.8 %all-to-all-start.4 = ((bf16[8,2,88,512]{3,2,1,0:T(8,128)(2,1)}), bf16[8,2,88,512]{3,2,1,0:T(8,128)(2,1)}, u32[]{:S(2)}, u32[]{:S(2)}) async-start(bf16[8,2,88,512]{3,2,1,0:T(8,128)(2,1)} %bitcast.199), calls=%async_computation.6 | async-start | bytes 2883584 | tf_op jit(solution)/shard_map/all_to_all | solution.py:1057
  831.7 393.6 %reduce-scatter.10.cloned.1.call-start = ((), (), s32[]{:S(2)}) async-start(), calls=%async_computation.22 | async-start | bytes 18247680 | tf_op jit(solution)/shard_map/reduce_scatter | solution.py:1131
  867.9 108.5 %collective-permute-start.28 = (bf16[768,352]{0,1:T(8,128)(2,1)}, bf16[768,352]{0,1:T(8,128)(2,1)}, u32[]{:S(2)}, u32[]{:S(2)}) collective-permute-start(bf16[768,352]{0,1:T(8,128)(2,1)} %copy.126), channel_id=1, source_target_pairs={{0,16},{8,24},{16,0},{24,8},{1,17},{9,25},{17,1},{25,9},{2,18},{10... | collective-permute-start | bytes 1622024 | tf_op jit(solution)/shard_map/ppermute | solution.py:1087
  872.6 103.8 %collective-permute-start.27 = (bf16[768,352]{0,1:T(8,128)(2,1)}, bf16[768,352]{0,1:T(8,128)(2,1)S(1)}, u32[]{:S(2)}, u32[]{:S(2)}) collective-permute-start(bf16[768,352]{0,1:T(8,128)(2,1)} %copy.125), channel_id=1, source_target_pairs={{0,8},{8,16},{16,24},{24,0},{1,9},{9,17},{17,25},{25,1},{2,10},{10... | collective-permute-start | bytes 1622024 | tf_op jit(solution)/shard_map/ppermute | solution.py:1087
  874.1 102.3 %collective-permute-start.29 = (bf16[768,352]{0,1:T(8,128)(2,1)}, bf16[768,352]{0,1:T(8,128)(2,1)}, u32[]{:S(2)}, u32[]{:S(2)}) collective-permute-start(bf16[768,352]{0,1:T(8,128)(2,1)} %copy.127), channel_id=1, source_target_pairs={{0,24},{8,0},{16,8},{24,16},{1,25},{9,1},{17,9},{25,17},{2,26},{10... | collective-permute-start | bytes 1622024 | tf_op jit(solution)/shard_map/ppermute | solution.py:1087
  882.8 100.7 %all-to-all-start.5 = ((bf16[8,2,88,512]{3,2,1,0:T(8,128)(2,1)}), bf16[8,2,88,512]{3,2,1,0:T(8,128)(2,1)}, u32[]{:S(2)}, u32[]{:S(2)}) async-start(bf16[8,2,88,512]{3,2,1,0:T(8,128)(2,1)} %bitcast.198), calls=%async_computation.7 | async-start | bytes 2883584 | tf_op jit(solution)/shard_map/all_to_all | solution.py:1057
  983.5 94.0 %all-to-all-start.7 = ((bf16[8,3,2,88,512]{4,3,2,1,0:T(8,128)(2,1)}), bf16[8,3,2,88,512]{4,3,2,1,0:T(8,128)(2,1)}, u32[]{:S(2)}, u32[]{:S(2)}) async-start(bf16[8,3,2,88,512]{4,3,2,1,0:T(8,128)(2,1)} %shard_map.321), calls=%async_computation.9 | async-start | bytes 8650752 | tf_op jit(solution)/shard_map/all_to_all | solution.py:1057
  1077.4 74.3 %all-to-all-start.6 = ((bf16[8,3,2,88,512]{4,3,2,1,0:T(8,128)(2,1)}), bf16[8,3,2,88,512]{4,3,2,1,0:T(8,128)(2,1)}, u32[]{:S(2)}, u32[]{:S(2)}) async-start(bf16[8,3,2,88,512]{4,3,2,1,0:T(8,128)(2,1)} %shard_map.322), calls=%async_computation.8 | async-start | bytes 8650752 | tf_op jit(solution)/shard_map/all_to_all | solution.py:1057
  1082.0 188.3 %reduce-scatter.12.cloned.1.call-start = ((), (), s32[]{:S(2)}) async-start(), calls=%async_computation.23 | async-start | bytes 13381632 | tf_op jit(solution)/shard_map/reduce_scatter | solution.py:1131
  1083.9 27.1 %collective-permute-start.31 = (bf16[176,1536]{1,0:T(8,128)(2,1)S(1)}, bf16[176,1536]{1,0:T(8,128)(2,1)S(1)}, u32[]{:S(2)}, u32[]{:S(2)}) collective-permute-start(bf16[176,1536]{1,0:T(8,128)(2,1)S(1)} %select_select_fusion.4), channel_id=1, source_target_pairs={{0,16},{8,24},{16,0},{24,8},{1,17},{9,25},{17,1},{25,9},{2,18},{10... | collective-permute-start | bytes 1622024 | tf_op jit(solution)/shard_map/ppermute | solution.py:1087
  1085.6 38.0 %collective-permute-start.32 = (bf16[176,1536]{1,0:T(8,128)(2,1)S(1)}, bf16[176,1536]{1,0:T(8,128)(2,1)S(1)}, u32[]{:S(2)}, u32[]{:S(2)}) collective-permute-start(bf16[176,1536]{1,0:T(8,128)(2,1)S(1)} %get-tuple-element.292), channel_id=1, source_target_pairs={{0,24},{8,0},{16,8},{24,16},{1,25},{9,1},{17,9},{25,17},{2,26},{10... | collective-permute-start | bytes 1622024 | tf_op jit(solution)/shard_map/ppermute | solution.py:1087
  1088.0 35.6 %collective-permute-start.30 = (bf16[176,1536]{1,0:T(8,128)(2,1)S(1)}, bf16[176,1536]{1,0:T(8,128)(2,1)S(1)}, u32[]{:S(2)}, u32[]{:S(2)}) collective-permute-start(bf16[176,1536]{1,0:T(8,128)(2,1)S(1)} %get-tuple-element.293), channel_id=1, source_target_pairs={{0,8},{8,16},{16,24},{24,0},{1,9},{9,17},{17,25},{25,1},{2,10},{10... | collective-permute-start | bytes 1622024 | tf_op jit(solution)/shard_map/ppermute | solution.py:1087
  1181.9 291.1 %reduce-scatter.14.cloned.1.call-start = ((), (), s32[]{:S(2)}) async-start(), calls=%async_computation.24 | async-start | bytes 8921088 | tf_op jit(solution)/shard_map/reduce_scatter | solution.py:1131
  1238.4 32.0 %collective-permute-start.35 = (bf16[176,1056]{1,0:T(8,128)(2,1)}, bf16[176,1056]{1,0:T(8,128)(2,1)}, u32[]{:S(2)}, u32[]{:S(2)}) collective-permute-start(bf16[176,1056]{1,0:T(8,128)(2,1)} %get-tuple-element.319), channel_id=1, source_target_pairs={{0,24},{8,0},{16,8},{24,16},{1,25},{9,1},{17,9},{25,17},{2,26},{10... | collective-permute-start | bytes 1115144 | tf_op jit(solution)/shard_map/ppermute | solution.py:1087
  1239.6 37.1 %collective-permute-start.34 = (bf16[176,1056]{1,0:T(8,128)(2,1)}, bf16[176,1056]{1,0:T(8,128)(2,1)}, u32[]{:S(2)}, u32[]{:S(2)}) collective-permute-start(bf16[176,1056]{1,0:T(8,128)(2,1)} %get-tuple-element.320), channel_id=1, source_target_pairs={{0,16},{8,24},{16,0},{24,8},{1,17},{9,25},{17,1},{25,9},{2,18},{10... | collective-permute-start | bytes 1115144 | tf_op jit(solution)/shard_map/ppermute | solution.py:1087
  1241.0 35.7 %collective-permute-start.33 = (bf16[176,1056]{1,0:T(8,128)(2,1)}, bf16[176,1056]{1,0:T(8,128)(2,1)}, u32[]{:S(2)}, u32[]{:S(2)}) collective-permute-start(bf16[176,1056]{1,0:T(8,128)(2,1)} %get-tuple-element.321), channel_id=1, source_target_pairs={{0,8},{8,16},{16,24},{24,0},{1,9},{9,17},{17,25},{25,1},{2,10},{10... | collective-permute-start | bytes 1115144 | tf_op jit(solution)/shard_map/ppermute | solution.py:1087
  1289.0 29.3 %collective-permute-start.39 = (f32[2,1408]{1,0:T(2,128)S(1)}, f32[2,1408]{1,0:T(2,128)S(1)}, u32[]{:S(2)}, u32[]{:S(2)}) collective-permute-start(f32[2,1408]{1,0:T(2,128)S(1)} %bitcast_reduce_fusion), channel_id=1, source_target_pairs={{0,1},{1,0},{2,3},{3,2},{4,5},{5,4},{6,7},{7,6},{8,9},{9,8},{10,11... | collective-permute-start | bytes 33800 | tf_op jit(solution)/shard_map/ppermute | solution.py:1124
  1320.8 12.8 collective-permute-start.45
  1332.0 16.9 %collective-permute-start.44 = (f32[2,1408]{1,0:T(2,128)S(1)}, f32[2,1408]{1,0:T(2,128)S(1)}, u32[]{:S(2)}, u32[]{:S(2)}) collective-permute-start(f32[2,1408]{1,0:T(2,128)S(1)} %add.580), channel_id=1, source_target_pairs={{0,4},{1,5},{2,6},{3,7},{4,0},{5,1},{6,2},{7,3},{8,12},{9,13},{10,... | collective-permute-start | bytes 33800 | tf_op jit(solution)/shard_map/ppermute | solution.py:1124
  1334.6 12.2 collective-permute-start.46
  1342.5 44.3 %all-to-all-start.8 = ((bf16[8,128,1120]{1,2,0:T(8,128)(2,1)}), bf16[8,128,1120]{1,2,0:T(8,128)(2,1)}, u32[]{:S(2)}, u32[]{:S(2)}) async-start(bf16[8,128,1120]{1,2,0:T(8,128)(2,1)} %copy_bitcast_fusion), calls=%async_computation.11 | async-start | bytes 4587520 | tf_op jit(solution)/shard_map/all_to_all | solution.py:1057
  1346.9 32.1 %collective-permute-start.47 = (f32[176,60]{1,0:T(8,128)S(1)}, f32[176,60]{1,0:T(8,128)S(1)}, u32[]{:S(2)}, u32[]{:S(2)}) collective-permute-start(f32[176,60]{1,0:T(8,128)S(1)} %slice_select_fusion.3), channel_id=1, source_target_pairs={{0,1},{1,0},{2,3},{3,2},{4,5},{5,4},{6,7},{7,6},{8,9},{9,8},{10,11... | collective-permute-start | bytes 126728 | tf_op jit(solution)/shard_map/ppermute | solution.py:1114
  1380.2 23.1 %collective-permute-start.37 = (bf16[176,1056]{1,0:T(8,128)(2,1)}, bf16[176,1056]{1,0:T(8,128)(2,1)S(1)}, u32[]{:S(2)}, u32[]{:S(2)}) collective-permute-start(bf16[176,1056]{1,0:T(8,128)(2,1)} %select_select_fusion.18), channel_id=1, source_target_pairs={{0,16},{8,24},{16,0},{24,8},{1,17},{9,25},{17,1},{25,9},{2,18},{10... | collective-permute-start | bytes 1115144 | tf_op jit(solution)/shard_map/ppermute | solution.py:1087
  1384.0 27.6 %collective-permute-start.38 = (bf16[176,1056]{1,0:T(8,128)(2,1)}, bf16[176,1056]{1,0:T(8,128)(2,1)}, u32[]{:S(2)}, u32[]{:S(2)}) collective-permute-start(bf16[176,1056]{1,0:T(8,128)(2,1)} %get-tuple-element.330), channel_id=1, source_target_pairs={{0,24},{8,0},{16,8},{24,16},{1,25},{9,1},{17,9},{25,17},{2,26},{10... | collective-permute-start | bytes 1115144 | tf_op jit(solution)/shard_map/ppermute | solution.py:1087
  1385.4 26.1 %collective-permute-start.36 = (bf16[176,1056]{1,0:T(8,128)(2,1)}, bf16[176,1056]{1,0:T(8,128)(2,1)}, u32[]{:S(2)}, u32[]{:S(2)}) collective-permute-start(bf16[176,1056]{1,0:T(8,128)(2,1)} %get-tuple-element.331), channel_id=1, source_target_pairs={{0,8},{8,16},{16,24},{24,0},{1,9},{9,17},{17,25},{25,1},{2,10},{10... | collective-permute-start | bytes 1115144 | tf_op jit(solution)/shard_map/ppermute | solution.py:1087
  1423.7 19.4 %collective-permute-start.48 = (bf16[640,352]{1,0:T(8,128)(2,1)S(1)}, bf16[640,352]{1,0:T(8,128)(2,1)S(1)}, u32[]{:S(2)}, u32[]{:S(2)}) collective-permute-start(bf16[640,352]{1,0:T(8,128)(2,1)S(1)} %get-tuple-element.316), channel_id=1, source_target_pairs={{0,8},{8,16},{16,24},{24,0},{1,9},{9,17},{17,25},{25,1},{2,10},{10... | collective-permute-start | bytes 1351688 | tf_op jit(solution)/shard_map/ppermute | solution.py:1087
  1431.5 22.2 %collective-permute-start.50 = (bf16[640,352]{1,0:T(8,128)(2,1)S(1)}, bf16[640,352]{1,0:T(8,128)(2,1)S(1)}, u32[]{:S(2)}, u32[]{:S(2)}) collective-permute-start(bf16[640,352]{1,0:T(8,128)(2,1)S(1)} %get-tuple-element.317), channel_id=1, source_target_pairs={{0,24},{8,0},{16,8},{24,16},{1,25},{9,1},{17,9},{25,17},{2,26},{10... | collective-permute-start | bytes 1351688 | tf_op jit(solution)/shard_map/ppermute | solution.py:1087
  1431.6 37.4 %collective-permute-start.49 = (bf16[640,352]{1,0:T(8,128)(2,1)S(1)}, bf16[640,352]{1,0:T(8,128)(2,1)S(1)}, u32[]{:S(2)}, u32[]{:S(2)}) collective-permute-start(bf16[640,352]{1,0:T(8,128)(2,1)S(1)} %get-tuple-element.318), channel_id=1, source_target_pairs={{0,16},{8,24},{16,0},{24,8},{1,17},{9,25},{17,1},{25,9},{2,18},{10... | collective-permute-start | bytes 1351688 | tf_op jit(solution)/shard_map/ppermute | solution.py:1087
  1476.9 17.0 %collective-permute-start.53 = (bf16[352,352]{1,0:T(8,128)(2,1)S(1)}, bf16[352,352]{1,0:T(8,128)(2,1)S(1)}, u32[]{:S(2)}, u32[]{:S(2)}) collective-permute-start(bf16[352,352]{1,0:T(8,128)(2,1)S(1)} %select_select_fusion.31), channel_id=1, source_target_pairs={{0,24},{8,0},{16,8},{24,16},{1,25},{9,1},{17,9},{25,17},{2,26},{10... | collective-permute-start | bytes 743432 | tf_op jit(solution)/shard_map/ppermute | solution.py:1087
  1487.0 13.3 collective-permute-start.51
  1487.0 21.6 %collective-permute-start.52 = (bf16[352,352]{1,0:T(8,128)(2,1)S(1)}, bf16[352,352]{1,0:T(8,128)(2,1)S(1)}, u32[]{:S(2)}, u32[]{:S(2)}) collective-permute-start(bf16[352,352]{1,0:T(8,128)(2,1)S(1)} %get-tuple-element.341), channel_id=1, source_target_pairs={{0,16},{8,24},{16,0},{24,8},{1,17},{9,25},{17,1},{25,9},{2,18},{10... | collective-permute-start | bytes 743432 | tf_op jit(solution)/shard_map/ppermute | solution.py:1087
  (103 other events, 1248.3 us)
Sparse Core Ops, SparseCore 0:
  34.0 58.6 all-gather.7
  100.3 87.5 all-gather.9
  189.8 115.5 all-gather.11
  307.7 77.6 all-gather.13
  387.0 116.4 all-gather.15
  507.4 96.2 all-gather.17
  670.9 118.5 reduce-scatter.5
  793.6 149.0 reduce-scatter.7
  946.3 203.6 reduce-scatter.9
  1182.0 88.2 reduce-scatter.11
  1279.7 82.9 reduce-scatter.13

commit v5 on v3

--- a/solution.py
+++ b/solution.py
@@ -1031,7 +1031,7 @@
     fixed = lambda shape: pl.BlockSpec(shape, lambda t: (0, 0))
     return kernel_call(
         join_back_body,
-        4 * tokens * width * width,
+        64 * tokens * width * width,
         18 * tokens * width,
         grid=(tokens // block,),
         in_specs=[rows(width), fixed(f_skip.shape), rows(2 * width), rows(1), fixed(gain.shape)],
@@ -1181,10 +1181,7 @@
     row_count = images * tile_len
     out_width = cotangent.shape[3]
 
-    f_skip = lax.all_gather(w_skip, EVERY, axis=0, tiled=True).reshape(
-        dp_devices, -1, w_skip.shape[1]
-    )
-    f_skip = jnp.swapaxes(f_skip, 0, 1).reshape(f_skip.shape[1], -1)
+    f_skip = tiles_whole(widen(fetch(w_skip)))
     small = jnp.concatenate([w_patch, w_final, norm_params], axis=1)
     small_widths = (w_patch.shape[1], w_final.shape[1], norm_params.shape[1])
     cuts = (0, small_widths[0], sum(small_widths[:2]), sum(small_widths))
@@ -1249,8 +1246,7 @@
     bias_skip = jnp.concatenate([norm_f[:, 9], norm_f[:, 11]])[None]
     joined, joined_inv, skip_in = join_norm(patch_rows, skip_rows, f_patch, gain_skip, bias_skip)
     f_qkv = tiles_whole(widen(held_qkv, skip_in))
-    part_three = widen(held_three, skip_in, 3)
-    f_three = tiles_whole(part_three)
+    f_three = tiles_whole(widen(held_three, skip_in, 3))
     f_out, f_query, f_cross = jnp.split(f_three, 3, axis=1)
     residual = plain_dot(skip_in, f_skip)
     first_z, first_inv = layer_norm(residual)
@@ -1408,11 +1404,21 @@
     ck_z, ck_inv = layer_norm(jnp.swapaxes(own_key, 1, 2))
     grad_ckey = jnp.swapaxes(norm_back(jnp.swapaxes(sum_text_kv[0], 1, 2), ck_z, ck_inv), 1, 2)
     grad_kv = jnp.stack([grad_ckey, sum_text_kv[1]]).astype(BF16)
-    grad_kv = tiles_whole(grad_kv.reshape(-1, images * text_pad))
+    grad_kv = grad_kv.reshape(-1, images * text_pad)
+    t_joint, grad_qkv = lax.optimization_barrier((t_joint, grad_qkv))
     grad_qkv = grad_qkv.reshape(3 * model_width, row_count)
     d_qkv = dot_over(first_in, grad_qkv, 0, 1).astype(BF16)
     d_qkv, grad_qkv = lax.optimization_barrier((d_qkv, grad_qkv))
     t_qkv = over_tiles(d_qkv)
+    text_slice = text_states.shape[2] // grid_devices
+    own_cols = lax.dynamic_slice_in_dim(
+        f_text.reshape(f_text.shape[0], 2, -1), grid_at * group_heads * head_dim, group_heads * head_dim, 2
+    ).reshape(f_text.shape[0], -1)
+    text_parts = jnp.concatenate(
+        [dot_over(text_rows, grad_kv, 0, 1).astype(BF16), plain_dot(own_cols, grad_kv).astype(BF16)],
+        axis=1,
+    )
+    text_parts, grad_qkv = lax.optimization_barrier((text_parts, grad_qkv))
     grad_first = dot_over(grad_qkv, f_qkv, 0, 1)
     joint_blocks = by_device(jnp.split(t_joint[:, : 3 * model_width], 3, axis=1), 1)
     joint_grad = narrow_blocks(joint_blocks, grad_first)
@@ -1421,26 +1427,10 @@
     part_shift = jnp.sum(grad_first.reshape(images, tile_len, model_width), axis=1)
     grad_one = grad_two + norm_back(grad_first * norm_f[:, 0], first_z, first_inv)
 
-    low_one = grad_one.astype(BF16)
-    d_skip_w = left_dot(skip_in, low_one).astype(BF16)
-    d_skip_w, low_one = lax.optimization_barrier((d_skip_w, low_one))
-    skip_grad, grad_patch, skip_sums = join_back(low_one, f_skip, joined, joined_inv, gain_skip)
-    t_qkv, d_skip_w, joint_grad, skip_sums = lax.optimization_barrier(
-        (t_qkv, d_skip_w, joint_grad, skip_sums)
-    )
-    out_grad, query_w_grad, cross_grad = jnp.split(joint_grad, 3, axis=1)
-    t_skip = over_tiles(d_skip_w)
-
-    group_shape = (-1, 2, grid_devices, model_width // grid_devices)
-    text_slice = text_states.shape[2] // grid_devices
-    text_cols = lax.dynamic_slice_in_dim(text_rows, grid_at * text_slice, text_slice, 1)
-    d_text = dot_over(text_cols, grad_kv, 0, 1).astype(BF16)
-    d_text = jnp.swapaxes(d_text.reshape(text_slice, grid_devices, 2, -1), 1, 2)
-    d_text = d_text.reshape(text_slice, -1)
-    grouped_text = jnp.swapaxes(part_text.reshape(group_shape), 1, 2).reshape(part_text.shape)
-    text_grad = dot_over(grad_kv, grouped_text, 0, 1).reshape(images, text_pad, text_slice)
-    text_grad = text_grad[:, :text_len]
-
+    text_parts = swap_tiles(text_parts.reshape(grid_devices, text_slice, -1))
+    own_width = own_cols.shape[1]
+    d_text = text_parts[:, :, :own_width].reshape(grid_devices, text_slice, 2, -1)
+    d_text = jnp.transpose(d_text, (1, 2, 0, 3)).reshape(text_slice, -1)
     shift_low = total_tiles(part_shift).astype(BF16)
     d_shift = left_dot(act_cols, shift_low).astype(BF16)
     grad_time_act = total_tiles(
@@ -1450,6 +1440,20 @@
     )
     grad_time_pre = silu_pull(grad_time_act)[0].astype(BF16)
     d_time = left_dot(embed_cols, grad_time_pre).astype(BF16)
+    low_one = grad_one.astype(BF16)
+    d_skip_w = left_dot(skip_in, low_one).astype(BF16)
+    d_skip_w, low_one = lax.optimization_barrier((d_skip_w, low_one))
+    skip_grad, grad_patch, skip_sums = join_back(low_one, f_skip, joined, joined_inv, gain_skip)
+    t_qkv, d_skip_w, joint_grad, d_text, d_time, d_shift = lax.optimization_barrier(
+        (t_qkv, d_skip_w, joint_grad, d_text, d_time, d_shift)
+    )
+    out_grad, query_w_grad, cross_grad = jnp.split(joint_grad, 3, axis=1)
+    t_skip = over_tiles(d_skip_w)
+
+    text_grad = jnp.sum(text_parts[:, :, own_width:].astype(F32), axis=0)
+    text_grad = jnp.transpose(text_grad).reshape(images, text_pad, text_slice)
+    text_grad = text_grad[:, :text_len]
+
     late, width = [], w_shift.shape[1]
     for at in range(dp_devices):
         pair = d_text[:, 2 * at * width : 2 * (at + 1) * width]
@@ -1457,13 +1461,13 @@
         late.append(
             jnp.concatenate([pair[:, :width], pair[:, width:], d_time[:, own], d_shift[:, own]])
         )
-    qkv_grad = narrow(t_qkv, d_text)
-    qkv_grad, *late = lax.optimization_barrier((qkv_grad, *late))
-    late = narrow_blocks(late)
+    late, qkv_grad = narrow_blocks(late, skip_sums), narrow(t_qkv, skip_sums)
+    late, qkv_grad, skip_sums, grad_patch, skip_grad = lax.optimization_barrier(
+        (late, qkv_grad, skip_sums, grad_patch, skip_grad)
+    )
     rows = d_text.shape[0]
     text_w_grad = jnp.concatenate([late[:rows], late[rows : 2 * rows]], axis=1)
     time_w_grad, shift_w_grad = jnp.split(late[2 * rows :], [d_time.shape[0]], axis=0)
-
     skip_grad = skip_grad.reshape(images, rows_tile, cols_tile, model_width)
     gain_skips, bias_skips = skip_sums[0], skip_sums[1]
     d_patch = left_dot(grad_patch, patch_rows)

time: 1470 us -> 1470 us (level)
  local copies, waits for them, and re-layouts: 107 us -> 78.4 us
  waiting for transfers between devices: 338 us -> 363 us
  starting transfers between devices: 153 us -> 173 us
    ppermute x12, waiting for transfers between devices: 14.7 us -> 42.5 us  [total_tiles(): total = total + lax.ppermute(total, TILE, pairs)]
    reshape x2 -> x1, local copies, waits for them, and re-layouts: 27.9 us -> 1.8 us  [local_heads(): text_parts = swap_tiles(text_parts.reshape(grid_devices, text_slice, -1))]
    ppermute x21, waiting for transfers between devices: 95.9 us -> 79.1 us  [narrow_blocks(): received.append(lax.ppermute(sent, 'dp', shift_pairs(devices, step)))]
    ppermute x21, starting transfers between devices: 42.7 us -> 58 us  [narrow_blocks(): received.append(lax.ppermute(sent, 'dp', shift_pairs(devices, step)))]
    all_to_all x8 -> x9, waiting for transfers between devices: 99.3 us -> 109 us  [swap_tiles(): lax.all_to_all(values_in, TILE, split_axis=0, concat_axis=0, tiled=True)]
    dot_general x11 -> x10, matrix products: 118 us -> 111 us  [dot_over(): lax.dot_general(left_mat, right_mat, (((left_axis,), (right_axis,)), ((),...]
    ppermute x18 -> x21, starting transfers between devices: 60.4 us -> 64.4 us  [fetch(): lax.ppermute(weight, 'dp', shift_pairs(devices, step))]
    all_to_all x8 -> x9, starting transfers between devices: 35 us -> 38.7 us  [swap_tiles(): lax.all_to_all(values_in, TILE, split_axis=0, concat_axis=0, tiled=True)]
  transfers between devices with their start and end apart: 74 -> 77, of which waited for: 34 -> 35; matrix products, arithmetic and copies ran while one was open for 33% -> 29% of each run, Pallas kernels for 25% -> 25%
where the time goes in v5:
time: 1470 us; the launch traced here: 1460 us
  matrix products  375 us (26%)
  Pallas kernels  367 us (25%)
  waiting for transfers between devices  363 us (25%)
  starting transfers between devices  173 us (12%)
  local copies, waits for them, and re-layouts  78.4 us (5%)
  other arithmetic  74 us (5%)
  blocking collectives  17.8 us (1%)
  between operations  16.3 us (1%)
    pallas_call x2, Pallas kernels, attend_back(): kernel_call(functools.partial(attend_back_body, score_scale), 2560 * head...  178 us
    dot_general x10, matrix products, dot_over(): lax.dot_general(left_mat, right_mat, (((left_axis,), (right_axis,)), ((),...  111 us
    all_to_all x9, waiting for transfers between devices, swap_tiles(): lax.all_to_all(values_in, TILE, split_axis=0, concat_axis=0, tiled=True)  109 us
    dot_general x10, matrix products, plain_dot(): return jnp.dot(left_mat, right_mat, preferred_element_type=jnp.float32)  107 us
    ppermute x21, waiting for transfers between devices, fetch(): lax.ppermute(weight, 'dp', shift_pairs(devices, step))  96.8 us
    dot_general x9, matrix products, left_dot(): lax.dot_general(left_mat, right_mat, (((0,), (0,)), ((), ())), preferred_...  91.2 us
    ppermute x21, waiting for transfers between devices, narrow_blocks(): received.append(lax.ppermute(sent, 'dp', shift_pairs(devices, step)))  79.1 us
    pallas_call x2, Pallas kernels, attend(): kernel_call(attend_body, 1024 * heads * tiles ** 2 * tile_len ** 2, 8 * q...  68.5 us
  transfers between devices with their start and end apart: 77, of which 35 were waited for; matrix products, arithmetic and copies ran while one was open for 29% of the time, Pallas kernels for 25%

profile of v5, /device:TPU:0, one launch (start us, length us, event | category | flops | bytes accessed | tf_op | source)
XLA Modules:
  0.0 1464.5 jit_solution(13939958953775480090)
XLA Ops:
  15.2 15.3 %collective-permute-done.4 = bf16[352,352]{1,0:T(8,128)(2,1)S(1)} collective-permute-done((bf16[352,352]{1,0:T(8,128)(2,1)}, bf16[352,352]{1,0:T(8,128)(2,1)S(1)}, u32[]{:S(2)}, u32[]{:S(2)}) %collective-permute-start.4) | collective-permute-done | bytes 247840 | tf_op jit(solution)/shard_map/ppermute | solution.py:1067
  36.1 6.9 collective-permute-start.1
  48.8 8.0 collective-permute-done.1
  56.8 5.7 collective-permute-start.14
  63.7 17.8 %all-gather = bf16[8,176,60]{1,2,0:T(8,128)(2,1)S(1)} all-gather(bf16[1,176,60]{1,2,0:T(8,128)(2,1)S(1)} %reshape.636), channel_id=1, replica_groups=mesh['dp'=4,'row'=4,'col'=2] {'row','col'}, dimensions={0}, use_global_device_ids=true | all-gather | bytes 190080 | tf_op jit(solution)/shard_map/all_gather | solution.py:1136
  84.9 9.6 shard_map.314
  101.6 23.2 %collective-permute-start.16 = (bf16[176,1056]{1,0:T(8,128)(2,1)S(1)}, bf16[176,1056]{1,0:T(8,128)(2,1)S(1)}, u32[]{:S(2)}, u32[]{:S(2)}) collective-permute-start(bf16[176,1056]{1,0:T(8,128)(2,1)S(1)} %concatenate.103), channel_id=1, source_target_pairs={{0,16},{8,24},{16,0},{24,8},{1,17},{9,25},{17,1},{25,9},{2,18},{10... | collective-permute-start | bytes 1115144 | tf_op jit(solution)/shard_map/ppermute | solution.py:1067
  124.8 8.5 collective-permute-done.17
  133.3 27.3 %collective-permute-done.16 = bf16[176,1056]{1,0:T(8,128)(2,1)S(1)} collective-permute-done((bf16[176,1056]{1,0:T(8,128)(2,1)S(1)}, bf16[176,1056]{1,0:T(8,128)(2,1)S(1)}, u32[]{:S(2)}, u32[]{:S(2)}) %collective-permute-start.16) | collective-permute-done | bytes 371744 | tf_op jit(solution)/shard_map/ppermute | solution.py:1067
  185.8 14.3 fusion.103
  209.1 14.7 %shard_map.315 = (bf16[8,3,2,88,512]{4,3,2,1,0:T(8,128)(2,1)}, f32[8,3,2,512]{3,2,1,0:T(2,128)}) custom-call(bf16[512,1408]{1,0:T(8,128)(2,1)} %get-tuple-element.306.rows_ref, bf16[1408,4224]{1,0:T(8,128)(2,1)} %all-gather.10.cloned.1.call-done.weight_ref, f32[88,512]{1,0:T(8,128)} %pad_maximum_fusion.16.cos_ref, f32[88,512]{1,0:T(8,128)} %pad_maximum_fusion.17.sin_ref, ...), custom_call_target="tpu_custom_call" | custom-call | flops 6090129408 | bytes 11894784 | tf_op jit(solution)/shard_map/pallas_call | solution.py:652
  223.9 4.7 all-to-all-start
  234.1 32.9 %collective-permute-done.22 = bf16[176,1536]{1,0:T(8,128)(2,1)S(1)} collective-permute-done((bf16[176,1536]{1,0:T(8,128)(2,1)S(1)}, bf16[176,1536]{1,0:T(8,128)(2,1)S(1)}, u32[]{:S(2)}, u32[]{:S(2)}) %collective-permute-start.22) | collective-permute-done | bytes 540704 | tf_op jit(solution)/shard_map/ppermute | solution.py:1067
  267.7 36.0 %all-to-all-done.query_ref.key_ref.value_ref = bf16[8,3,2,88,512]{4,3,2,1,0:T(8,128)(2,1)} async-done(((bf16[8,3,2,88,512]{4,3,2,1,0:T(8,128)(2,1)}), bf16[8,3,2,88,512]{4,3,2,1,0:T(8,128)(2,1)}, u32[]{:S(2)}, u32[]{:S(2)}) %all-to-all-start) | async-done | bytes 4325408 | tf_op jit(solution)/shard_map/all_to_all | solution.py:1057
  305.8 14.7 %shard_map.317 = (bf16[8,3,2,88,512]{4,3,2,1,0:T(8,128)(2,1)}, f32[8,3,2,512]{3,2,1,0:T(2,128)}) custom-call(bf16[512,1408]{1,0:T(8,128)(2,1)} %get-tuple-element.307.rows_ref, bf16[1408,4224]{1,0:T(8,128)(2,1)} %all-gather.10.cloned.1.call-done.weight_ref, f32[88,512]{1,0:T(8,128)} %pad_maximum_fusion.16.cos_ref, f32[88,512]{1,0:T(8,128)} %pad_maximum_fusion.17.sin_ref, ...), custom_call_target="tpu_custom_call" | custom-call | flops 6090129408 | bytes 11894784 | tf_op jit(solution)/shard_map/pallas_call | solution.py:652
  325.9 34.1 %shard_map.316 = (bf16[8,2,88,512]{3,2,1,0:T(8,128)(2,1)}, f32[8,2,1,512]{3,2,1,0:T(1,128)}) custom-call(bf16[8,3,2,88,512]{4,3,2,1,0:T(8,128)(2,1)} %all-to-all-done.query_ref.key_ref.value_ref, bf16[8,3,2,88,512]{4,3,2,1,0:T(8,128)(2,1)} %all-to-all-done.query_ref.key_ref.value_ref, bf16[8,3,2,88,512]{4,3,2,1,0:T(8,128)(2,1)} %all-to-all-done.query_ref.key_ref.value_ref, ...), custom_call_target="tpu_custom_call" | custom-call | flops 34359738368 | bytes 17301504 | tf_op jit(solution)/shard_map/pallas_call | solution.py:757
  360.0 30.1 %all-to-all-done.2.query_ref.key_ref.value_ref = bf16[8,3,2,88,512]{4,3,2,1,0:T(8,128)(2,1)} async-done(((bf16[8,3,2,88,512]{4,3,2,1,0:T(8,128)(2,1)}), bf16[8,3,2,88,512]{4,3,2,1,0:T(8,128)(2,1)}, u32[]{:S(2)}, u32[]{:S(2)}) %all-to-all-start.2) | async-done | bytes 4325408 | tf_op jit(solution)/shard_map/all_to_all | solution.py:1057
  393.7 34.5 %shard_map.318 = (bf16[8,2,88,512]{3,2,1,0:T(8,128)(2,1)}, f32[8,2,1,512]{3,2,1,0:T(1,128)}) custom-call(bf16[8,3,2,88,512]{4,3,2,1,0:T(8,128)(2,1)} %all-to-all-done.2.query_ref.key_ref.value_ref, bf16[8,3,2,88,512]{4,3,2,1,0:T(8,128)(2,1)} %all-to-all-done.2.query_ref.key_ref.value_ref, ...), custom_call_target="tpu_custom_call" | custom-call | flops 34359738368 | bytes 17301504 | tf_op jit(solution)/shard_map/pallas_call | solution.py:757
  438.7 20.5 %all-to-all-done.3 = bf16[8,2,88,512]{3,2,1,0:T(8,128)(2,1)S(1)} async-done(((bf16[8,2,88,512]{3,2,1,0:T(8,128)(2,1)}), bf16[8,2,88,512]{3,2,1,0:T(8,128)(2,1)S(1)}, u32[]{:S(2)}, u32[]{:S(2)}) %all-to-all-start.3) | async-done | bytes 1441824 | tf_op jit(solution)/shard_map/all_to_all | solution.py:1057
  459.2 10.6 fusion.104
  477.5 10.1 fusion.107
  488.4 9.3 fusion.8
  497.7 15.0 %shard_map.319 = (bf16[16,88,1024]{2,1,0:T(8,128)(2,1)}, bf16[16,88,1024]{2,1,0:T(8,128)(2,1)}, f32[16,1,1024]{2,1,0:T(1,128)}, f32[16,1,1024]{2,1,0:T(1,128)}) custom-call(f32[16,88,1024]{2,1,0:T(8,128)} %bitcast.212, f32[2,16,88,768]{3,2,1,0:T(8,128)} %bitcast.188), custom_call_target="tpu_custom_call" | custom-call | flops 6442450944 | bytes 11534336 | tf_op jit(solution)/shard_map/pallas_call | solution.py:897
  512.7 8.7 fusion.105
  524.6 39.7 %add_convert_fusion = (bf16[1024,6144]{1,0:T(8,128)(2,1)}, bf16[1024,6144]{1,0:T(8,128)(2,1)}) fusion(bf16[1408,6144]{1,0:T(8,128)(2,1)} %all-gather.16.cloned.1.call-done, f32[1024,1408]{1,0:T(8,128)} %copy-done.2, f32[1408]{0:T(1024)S(1)} %copy-done.100, f32[1408]{0:T(1024)S(1)} %copy-done.67, f32[1024]{0:T(1024)S(1)} %add_rsqrt_fusion.2, ...), kind=kOutput, calls=%fused_computation.1 | convolution fusion | flops 17843486720 | bytes 48253952 | tf_op jit(solution)/shard_map/dot_general | solution.py:72
  564.4 29.1 %all-gather.18.cloned.1.call-done = bf16[6144,1408]{0,1:T(8,128)(2,1)} async-done(((bf16[768,1408]{0,1:T(8,128)(2,1)}), bf16[6144,1408]{0,1:T(8,128)(2,1)}) %all-gather.18.cloned.1.call-update) | async-done | bytes 17301520 | tf_op jit(solution)/shard_map/all_gather | solution.py:1136
  593.5 28.6 %fusion.106 = (f32[1024]{0:T(1024)S(1)}, f32[1024,1408]{1,0:T(8,128)S(1)}) fusion(f32[1024,1408]{1,0:T(8,128)} %copy-done.2, bf16[1024,6144]{1,0:T(8,128)(2,1)} %get-tuple-element.130, bf16[6144,1408]{0,1:T(8,128)(2,1)} %all-gather.18.cloned.1.call-done), kind=kOutput, calls=%fused_computation.319 | convolution fusion | flops 17719623680 | bytes 41422848 | tf_op jit(solution)/shard_map/dot_general | solution.py:72
  626.2 4.6 fusion.90
  632.4 28.2 %convolution_convert_fusion = bf16[6144,1408]{1,0:T(8,128)(2,1)} fusion(bf16[1024,6144]{1,0:T(8,128)(2,1)} %get-tuple-element.130, bf16[1024,1408]{1,0:T(8,128)(2,1)S(1)} %get-tuple-element.135), kind=kOutput, calls=%fused_computation.5 | convolution fusion | flops 17725390848 | bytes 32768000 | tf_op jit(solution)/shard_map/dot_general | solution.py:76
  662.4 30.5 %multiply_convert_fusion = bf16[1024,6144]{1,0:T(8,128)(2,1)} fusion(bf16[1024,6144]{1,0:T(8,128)(2,1)} %get-tuple-element.136, bf16[1024,1408]{1,0:T(8,128)(2,1)S(1)} %copy-done.26, bf16[6144,1408]{0,1:T(8,128)(2,1)} %all-gather.18.cloned.1.call-done), kind=kOutput, calls=%fused_computation | convolution fusion | flops 17735614464 | bytes 45350912 | tf_op jit(solution)/shard_map/dot_general | solution.py:82
  692.9 25.9 %convolution_convert_fusion.1 = bf16[1408,6144]{1,0:T(8,128)(2,1)} fusion(bf16[1024,6144]{1,0:T(8,128)(2,1)} %multiply_convert_fusion, f32[1024,1408]{1,0:T(8,128)} %copy-done.2, f32[1408]{0:T(1024)S(1)} %copy-done.100, f32[1408]{0:T(1024)S(1)} %copy-done.67, f32[1024]{0:T(1024)S(1)} %add_rsqrt_fusion.2, f32[1024]{0:T(1024)S(1)} %broadcast_multiply_fusion.12), kind=kOutput, calls=%fused_computation.6 | convolution fusion | flops 17732599808 | bytes 35671040 | tf_op jit(solution)/shard_map/dot_general | solution.py:76
  718.8 31.4 %multiply_reduce_fusion.1 = (f32[1408]{0:T(1024)}, f32[1024]{0:T(1024)S(1)}, f32[1024]{0:T(1024)S(1)}, f32[1408]{0:T(1024)}, f32[1024,1408]{1,0:T(8,128)}) fusion(f32[1024,1408]{1,0:T(8,128)} %copy-done.2, f32[1024]{0:T(1024)S(1)} %add_rsqrt_fusion.2, f32[1024]{0:T(1024)S(1)} %broadcast_multiply_fusion.12, f32[1408]{0:T(1024)S(1)} %copy-done.67, ...), kind=kOutput, calls=%fused_computation.19 | convolution fusion | flops 17729710080 | bytes 41452032 | tf_op jit(solution)/shard_map/dot_general | solution.py:82
  750.2 7.7 multiply_add_fusion.1
  757.9 10.4 convolution_convert_fusion.7
  768.3 21.1 %shard_map.320 = (bf16[16,88,1024]{2,1,0:T(8,128)(2,1)}, bf16[16,88,768]{2,1,0:T(8,128)(2,1)}, bf16[16,88,768]{2,1,0:T(8,128)(2,1)}) custom-call(bf16[16,88,1024]{2,1,0:T(8,128)(2,1)} %get-tuple-element.139.query_ref, f32[2,16,88,768]{3,2,1,0:T(8,128)} %bitcast.189, bf16[16,88,1024]{2,1,0:T(8,128)(2,1)} %bitcast.217, ...), custom_call_target="tpu_custom_call" | custom-call | flops 16106127360 | bytes 23068672 | tf_op jit(solution)/shard_map/pallas_call | solution.py:957
  789.5 13.9 multiply_reduce_fusion.2
  803.4 6.4 fusion.89
  809.9 6.8 fusion.15
  821.3 8.6 fusion.2
  829.9 9.8 fusion.1
  839.8 6.7 fusion
  850.4 5.0 all-to-all-done.4.grad_ref
  865.9 6.2 fusion.18
  876.6 89.2 %shard_map.321 = bf16[8,3,2,88,512]{4,3,2,1,0:T(8,128)(2,1)} custom-call(bf16[8,3,2,88,512]{4,3,2,1,0:T(8,128)(2,1)} %all-to-all-done.query_ref.key_ref.value_ref, bf16[8,3,2,88,512]{4,3,2,1,0:T(8,128)(2,1)} %all-to-all-done.query_ref.key_ref.value_ref, bf16[8,3,2,88,512]{4,3,2,1,0:T(8,128)(2,1)} %all-to-all-done.query_ref.key_ref.value_ref, ...), custom_call_target="tpu_custom_call" | custom-call | flops 85899345920 | bytes 17301504 | tf_op jit(solution)/shard_map/pallas_call | solution.py:845
  972.8 4.8 all-to-all-start.7
  977.7 89.1 %shard_map.322 = bf16[8,3,2,88,512]{4,3,2,1,0:T(8,128)(2,1)} custom-call(bf16[8,3,2,88,512]{4,3,2,1,0:T(8,128)(2,1)} %all-to-all-done.2.query_ref.key_ref.value_ref, bf16[8,3,2,88,512]{4,3,2,1,0:T(8,128)(2,1)} %all-to-all-done.2.query_ref.key_ref.value_ref, bf16[8,3,2,88,512]{4,3,2,1,0:T(8,128)(2,1)} %all-to-all-done.2.query_ref.key_ref.value_ref, ...), custom_call_target="tpu_custom_call" | custom-call | flops 85899345920 | bytes 17301504 | tf_op jit(solution)/shard_map/pallas_call | solution.py:845
  1077.3 23.0 %collective-permute-done.31 = bf16[176,1536]{1,0:T(8,128)(2,1)S(1)} collective-permute-done((bf16[176,1536]{1,0:T(8,128)(2,1)S(1)}, bf16[176,1536]{1,0:T(8,128)(2,1)S(1)}, u32[]{:S(2)}, u32[]{:S(2)}) %collective-permute-start.31) | collective-permute-done | bytes 540704 | tf_op jit(solution)/shard_map/ppermute | solution.py:1087
  1100.4 12.4 collective-permute-done.32
  1114.2 10.5 shard_map.323.others_0_
  1124.7 17.1 %all-to-all-done.6.grad_ref = bf16[8,3,2,88,512]{4,3,2,1,0:T(8,128)(2,1)} async-done(((bf16[8,3,2,88,512]{4,3,2,1,0:T(8,128)(2,1)}), bf16[8,3,2,88,512]{4,3,2,1,0:T(8,128)(2,1)}, u32[]{:S(2)}, u32[]{:S(2)}) %all-to-all-start.6) | async-done | bytes 4325408 | tf_op jit(solution)/shard_map/all_to_all | solution.py:1057
  1141.8 10.3 shard_map.324
  1152.1 19.8 %convolution_convert_fusion.2 = bf16[1408,4224]{1,0:T(8,128)(2,1)} fusion(bf16[1024,1408]{1,0:T(8,128)(2,1)S(1)} %copy-done.12, bf16[4224,1024]{1,0:T(8,128)(2,1)} %bitcast.169), kind=kOutput, calls=%fused_computation.7 | convolution fusion | flops 12186206208 | bytes 23429120 | tf_op jit(solution)/shard_map/dot_general | solution.py:1144
  1207.2 23.9 %multiply_reduce_fusion.3 = (f32[1408]{0:T(1024)}, f32[1024]{0:T(1024)S(1)}, f32[1024]{0:T(1024)S(1)}, f32[1408]{0:T(1024)}, f32[1024,1408]{1,0:T(8,128)S(1)}) fusion(f32[1024,1408]{1,0:T(8,128)S(1)} %bitcast.168, f32[1024]{0:T(1024)S(1)} %copy-done.62, f32[1024]{0:T(1024)S(1)} %copy-done.59, f32[1408]{0:T(1024)S(1)} %copy-done.57, ...), kind=kOutput, calls=%fused_computation.21 | convolution fusion | flops 12193230848 | bytes 32113152 | tf_op jit(solution)/shard_map/dot_general | solution.py:1144
  1246.6 8.7 add_convert_fusion.1.low_ref
  1255.4 27.0 %collective-permute-done.39 = f32[2,1408]{1,0:T(2,128)S(1)} collective-permute-done((f32[2,1408]{1,0:T(2,128)S(1)}, f32[2,1408]{1,0:T(2,128)S(1)}, u32[]{:S(2)}, u32[]{:S(2)}) %collective-permute-start.39) | collective-permute-done | bytes 11296 | tf_op jit(solution)/shard_map/ppermute | solution.py:1124
  1282.8 14.1 convolution_convert_fusion.3
  1305.4 24.2 %shard_map.325 = (f32[1024,1408]{1,0:T(8,128)}, bf16[1024,1408]{1,0:T(8,128)(2,1)}, f32[2,2816]{1,0:T(2,128)}) custom-call(bf16[1024,1408]{1,0:T(8,128)(2,1)} %add_convert_fusion.1.low_ref, bf16[2816,1408]{1,0:T(8,128)(2,1)} %all-gather.8.cloned.1.call-done.weight_ref, f32[1024,2816]{1,0:T(8,128)} %get-tuple-element.178.z_ref, ...), custom_call_target="tpu_custom_call" | custom-call | flops 129922760704 | bytes 25952256 | tf_op jit(solution)/shard_map/pallas_call | solution.py:1032
  1344.8 23.9 %collective-permute-start.45 = (bf16[176,1056]{1,0:T(8,128)(2,1)S(1)}, bf16[176,1056]{1,0:T(8,128)(2,1)S(1)}, u32[]{:S(2)}, u32[]{:S(2)}) collective-permute-start(bf16[176,1056]{1,0:T(8,128)(2,1)S(1)} %get-tuple-element.344), channel_id=1, source_target_pairs={{0,8},{8,16},{16,24},{24,0},{1,9},{9,17},{17,25},{25,1},{2,10},{10... | collective-permute-start | bytes 1115144 | tf_op jit(solution)/shard_map/ppermute | solution.py:1087
  1369.9 8.5 collective-permute-done.43
  1378.8 15.4 %collective-permute-done.46 = bf16[176,1056]{1,0:T(8,128)(2,1)S(1)} collective-permute-done((bf16[176,1056]{1,0:T(8,128)(2,1)S(1)}, bf16[176,1056]{1,0:T(8,128)(2,1)S(1)}, u32[]{:S(2)}, u32[]{:S(2)}) %collective-permute-start.46) | collective-permute-done | bytes 371744 | tf_op jit(solution)/shard_map/ppermute | solution.py:1087
  1404.7 4.7 fusion.52
  1417.2 5.9 collective-permute-start.51
  1438.0 7.2 collective-permute-done.56
  1446.7 9.7 collective-permute-done.55
  (584 shorter events, 265.4 us)
Async XLA Ops:
  7.2 178.6 %all-gather.8.cloned.1.call-start = ((), (), s32[]{:S(2)}) async-start(), calls=%async_computation.14 | async-start | bytes 8921088 | tf_op jit(solution)/shard_map/all_gather | solution.py:1136
  7.3 23.3 %collective-permute-start.4 = (bf16[352,352]{1,0:T(8,128)(2,1)}, bf16[352,352]{1,0:T(8,128)(2,1)S(1)}, u32[]{:S(2)}, u32[]{:S(2)}) collective-permute-start(bf16[352,352]{1,0:T(8,128)(2,1)} %param.26), channel_id=1, source_target_pairs={{0,16},{8,24},{16,0},{24,8},{1,17},{9,25},{17,1},{25,9},{2,18},{10... | collective-permute-start | bytes 743432 | tf_op jit(solution)/shard_map/ppermute | solution.py:1067
  11.4 19.2 %collective-permute-start.3 = (bf16[352,352]{1,0:T(8,128)(2,1)}, bf16[352,352]{1,0:T(8,128)(2,1)S(1)}, u32[]{:S(2)}, u32[]{:S(2)}) collective-permute-start(bf16[352,352]{1,0:T(8,128)(2,1)} %param.26), channel_id=1, source_target_pairs={{0,8},{8,16},{16,24},{24,0},{1,9},{9,17},{17,25},{25,1},{2,10},{10... | collective-permute-start | bytes 743432 | tf_op jit(solution)/shard_map/ppermute | solution.py:1067
  13.0 18.3 %collective-permute-start.5 = (bf16[352,352]{1,0:T(8,128)(2,1)}, bf16[352,352]{1,0:T(8,128)(2,1)S(1)}, u32[]{:S(2)}, u32[]{:S(2)}) collective-permute-start(bf16[352,352]{1,0:T(8,128)(2,1)} %param.26), channel_id=1, source_target_pairs={{0,24},{8,0},{16,8},{24,16},{1,25},{9,1},{17,9},{25,17},{2,26},{10... | collective-permute-start | bytes 743432 | tf_op jit(solution)/shard_map/ppermute | solution.py:1067
  33.9 175.2 %all-gather.10.cloned.1.call-start = ((), (), s32[]{:S(2)}) async-start(), calls=%async_computation.15 | async-start | bytes 13381632 | tf_op jit(solution)/shard_map/all_gather | solution.py:1136
  36.1 20.7 %collective-permute-start.1 = (bf16[384,352]{0,1:T(8,128)(2,1)S(1)}, bf16[384,352]{0,1:T(8,128)(2,1)S(1)}, u32[]{:S(2)}, u32[]{:S(2)}) collective-permute-start(bf16[384,352]{0,1:T(8,128)(2,1)S(1)} %pad_maximum_fusion.15), channel_id=1, source_target_pairs={{0,16},{8,24},{16,0},{24,8},{1,17},{9,25},{17,1},{25,9},{2,18},{10... | collective-permute-start | bytes 811016 | tf_op jit(solution)/shard_map/ppermute | solution.py:1067
  43.0 19.9 %collective-permute-start.2 = (bf16[384,352]{0,1:T(8,128)(2,1)S(1)}, bf16[384,352]{0,1:T(8,128)(2,1)S(1)}, u32[]{:S(2)}, u32[]{:S(2)}) collective-permute-start(bf16[384,352]{0,1:T(8,128)(2,1)S(1)} %pad_maximum_fusion.15), channel_id=1, source_target_pairs={{0,24},{8,0},{16,8},{24,16},{1,25},{9,1},{17,9},{25,17},{2,26},{10... | collective-permute-start | bytes 811016 | tf_op jit(solution)/shard_map/ppermute | solution.py:1067
  43.5 19.4 %collective-permute-start = (bf16[384,352]{0,1:T(8,128)(2,1)S(1)}, bf16[384,352]{0,1:T(8,128)(2,1)S(1)}, u32[]{:S(2)}, u32[]{:S(2)}) collective-permute-start(bf16[384,352]{0,1:T(8,128)(2,1)S(1)} %pad_maximum_fusion.15), channel_id=1, source_target_pairs={{0,8},{8,16},{16,24},{24,0},{1,9},{9,17},{17,25},{25,1},{2,10},{10... | collective-permute-start | bytes 811016 | tf_op jit(solution)/shard_map/ppermute | solution.py:1067
  45.0 49.5 %collective-permute-start.13 = (bf16[176,1056]{1,0:T(8,128)(2,1)S(1)}, bf16[176,1056]{1,0:T(8,128)(2,1)S(1)}, u32[]{:S(2)}, u32[]{:S(2)}) collective-permute-start(bf16[176,1056]{1,0:T(8,128)(2,1)S(1)} %copy-done.45), channel_id=1, source_target_pairs={{0,16},{8,24},{16,0},{24,8},{1,17},{9,25},{17,1},{25,9},{2,18},{10... | collective-permute-start | bytes 1115144 | tf_op jit(solution)/shard_map/ppermute | solution.py:1067
  45.1 49.4 %collective-permute-start.12 = (bf16[176,1056]{1,0:T(8,128)(2,1)S(1)}, bf16[176,1056]{1,0:T(8,128)(2,1)S(1)}, u32[]{:S(2)}, u32[]{:S(2)}) collective-permute-start(bf16[176,1056]{1,0:T(8,128)(2,1)S(1)} %copy-done.45), channel_id=1, source_target_pairs={{0,8},{8,16},{16,24},{24,0},{1,9},{9,17},{17,25},{25,1},{2,10},{10... | collective-permute-start | bytes 1115144 | tf_op jit(solution)/shard_map/ppermute | solution.py:1067
  56.8 37.8 %collective-permute-start.14 = (bf16[176,1056]{1,0:T(8,128)(2,1)S(1)}, bf16[176,1056]{1,0:T(8,128)(2,1)S(1)}, u32[]{:S(2)}, u32[]{:S(2)}) collective-permute-start(bf16[176,1056]{1,0:T(8,128)(2,1)S(1)} %copy-done.45), channel_id=1, source_target_pairs={{0,24},{8,0},{16,8},{24,16},{1,25},{9,1},{17,9},{25,17},{2,26},{10... | collective-permute-start | bytes 1115144 | tf_op jit(solution)/shard_map/ppermute | solution.py:1067
  100.2 338.5 %all-gather.12.cloned.1.call-start = ((), (), s32[]{:S(2)}) async-start(), calls=%async_computation.16 | async-start | bytes 13381632 | tf_op jit(solution)/shard_map/all_gather | solution.py:1136
  101.5 31.7 %collective-permute-start.17 = (bf16[176,1056]{1,0:T(8,128)(2,1)S(1)}, bf16[176,1056]{1,0:T(8,128)(2,1)S(1)}, u32[]{:S(2)}, u32[]{:S(2)}) collective-permute-start(bf16[176,1056]{1,0:T(8,128)(2,1)S(1)} %concatenate.103), channel_id=1, source_target_pairs={{0,24},{8,0},{16,8},{24,16},{1,25},{9,1},{17,9},{25,17},{2,26},{10... | collective-permute-start | bytes 1115144 | tf_op jit(solution)/shard_map/ppermute | solution.py:1067
  101.6 58.9 %collective-permute-start.16 = (bf16[176,1056]{1,0:T(8,128)(2,1)S(1)}, bf16[176,1056]{1,0:T(8,128)(2,1)S(1)}, u32[]{:S(2)}, u32[]{:S(2)}) collective-permute-start(bf16[176,1056]{1,0:T(8,128)(2,1)S(1)} %concatenate.103), channel_id=1, source_target_pairs={{0,16},{8,24},{16,0},{24,8},{1,17},{9,25},{17,1},{25,9},{2,18},{10... | collective-permute-start | bytes 1115144 | tf_op jit(solution)/shard_map/ppermute | solution.py:1067
  124.8 35.8 %collective-permute-start.15 = (bf16[176,1056]{1,0:T(8,128)(2,1)S(1)}, bf16[176,1056]{1,0:T(8,128)(2,1)S(1)}, u32[]{:S(2)}, u32[]{:S(2)}) collective-permute-start(bf16[176,1056]{1,0:T(8,128)(2,1)S(1)} %concatenate.103), channel_id=1, source_target_pairs={{0,8},{8,16},{16,24},{24,0},{1,9},{9,17},{17,25},{25,1},{2,10},{10... | collective-permute-start | bytes 1115144 | tf_op jit(solution)/shard_map/ppermute | solution.py:1067
  165.1 312.3 %all-gather.14.cloned.1.call-start = ((), (), s32[]{:S(2)}) async-start(), calls=%async_computation.17 | async-start | bytes 6488064 | tf_op jit(solution)/shard_map/all_gather | solution.py:1136
  181.8 20.8 %collective-permute-start.19 = (bf16[128,704]{0,1:T(8,128)(2,1)S(1)}, bf16[128,704]{0,1:T(8,128)(2,1)S(1)}, u32[]{:S(2)}, u32[]{:S(2)}) collective-permute-start(bf16[128,704]{0,1:T(8,128)(2,1)S(1)} %copy-done.49), channel_id=1, source_target_pairs={{0,16},{8,24},{16,0},{24,8},{1,17},{9,25},{17,1},{25,9},{2,18},{10... | collective-permute-start | bytes 540680 | tf_op jit(solution)/shard_map/ppermute | solution.py:1067
  181.8 20.8 %collective-permute-start.18 = (bf16[128,704]{0,1:T(8,128)(2,1)S(1)}, bf16[128,704]{0,1:T(8,128)(2,1)S(1)}, u32[]{:S(2)}, u32[]{:S(2)}) collective-permute-start(bf16[128,704]{0,1:T(8,128)(2,1)S(1)} %copy-done.49), channel_id=1, source_target_pairs={{0,8},{8,16},{16,24},{24,0},{1,9},{9,17},{17,25},{25,1},{2,10},{10... | collective-permute-start | bytes 540680 | tf_op jit(solution)/shard_map/ppermute | solution.py:1067
  181.8 20.8 %collective-permute-start.20 = (bf16[128,704]{0,1:T(8,128)(2,1)S(1)}, bf16[128,704]{0,1:T(8,128)(2,1)}, u32[]{:S(2)}, u32[]{:S(2)}) collective-permute-start(bf16[128,704]{0,1:T(8,128)(2,1)S(1)} %copy-done.49), channel_id=1, source_target_pairs={{0,24},{8,0},{16,8},{24,16},{1,25},{9,1},{17,9},{25,17},{2,26},{10... | collective-permute-start | bytes 540680 | tf_op jit(solution)/shard_map/ppermute | solution.py:1067
  223.9 79.8 %all-to-all-start = ((bf16[8,3,2,88,512]{4,3,2,1,0:T(8,128)(2,1)}), bf16[8,3,2,88,512]{4,3,2,1,0:T(8,128)(2,1)}, u32[]{:S(2)}, u32[]{:S(2)}) async-start(bf16[8,3,2,88,512]{4,3,2,1,0:T(8,128)(2,1)} %get-tuple-element.113.own_ref), calls=%async_computation | async-start | bytes 8650752 | tf_op jit(solution)/shard_map/all_to_all | solution.py:1057
  228.6 296.0 %all-gather.16.cloned.1.call-start = ((), (), s32[]{:S(2)}) async-start(), calls=%async_computation.18 | async-start | bytes 19464192 | tf_op jit(solution)/shard_map/all_gather | solution.py:1136
  228.6 38.3 %collective-permute-start.22 = (bf16[176,1536]{1,0:T(8,128)(2,1)S(1)}, bf16[176,1536]{1,0:T(8,128)(2,1)S(1)}, u32[]{:S(2)}, u32[]{:S(2)}) collective-permute-start(bf16[176,1536]{1,0:T(8,128)(2,1)S(1)} %copy-done.41), channel_id=1, source_target_pairs={{0,16},{8,24},{16,0},{24,8},{1,17},{9,25},{17,1},{25,9},{2,18},{10... | collective-permute-start | bytes 1622024 | tf_op jit(solution)/shard_map/ppermute | solution.py:1067
  230.0 36.9 %collective-permute-start.21 = (bf16[176,1536]{1,0:T(8,128)(2,1)S(1)}, bf16[176,1536]{1,0:T(8,128)(2,1)S(1)}, u32[]{:S(2)}, u32[]{:S(2)}) collective-permute-start(bf16[176,1536]{1,0:T(8,128)(2,1)S(1)} %copy-done.41), channel_id=1, source_target_pairs={{0,8},{8,16},{16,24},{24,0},{1,9},{9,17},{17,25},{25,1},{2,10},{10... | collective-permute-start | bytes 1622024 | tf_op jit(solution)/shard_map/ppermute | solution.py:1067
  230.0 37.7 %collective-permute-start.23 = (bf16[176,1536]{1,0:T(8,128)(2,1)S(1)}, bf16[176,1536]{1,0:T(8,128)(2,1)S(1)}, u32[]{:S(2)}, u32[]{:S(2)}) collective-permute-start(bf16[176,1536]{1,0:T(8,128)(2,1)S(1)} %copy-done.41), channel_id=1, source_target_pairs={{0,24},{8,0},{16,8},{24,16},{1,25},{9,1},{17,9},{25,17},{2,26},{10... | collective-permute-start | bytes 1622024 | tf_op jit(solution)/shard_map/ppermute | solution.py:1067
  320.4 69.7 %all-to-all-start.2 = ((bf16[8,3,2,88,512]{4,3,2,1,0:T(8,128)(2,1)}), bf16[8,3,2,88,512]{4,3,2,1,0:T(8,128)(2,1)}, u32[]{:S(2)}, u32[]{:S(2)}) async-start(bf16[8,3,2,88,512]{4,3,2,1,0:T(8,128)(2,1)} %get-tuple-element.115.own_ref), calls=%async_computation.2 | async-start | bytes 8650752 | tf_op jit(solution)/shard_map/all_to_all | solution.py:1057
  390.1 38.0 %all-to-all-start.1 = ((bf16[8,2,88,512]{3,2,1,0:T(8,128)(2,1)}), bf16[8,2,88,512]{3,2,1,0:T(8,128)(2,1)S(1)}, u32[]{:S(2)}, u32[]{:S(2)}) async-start(bf16[8,2,88,512]{3,2,1,0:T(8,128)(2,1)} %get-tuple-element.114.att_ref), calls=%async_computation.1 | async-start | bytes 2883584 | tf_op jit(solution)/shard_map/all_to_all | solution.py:1057
  428.2 31.0 %all-to-all-start.3 = ((bf16[8,2,88,512]{3,2,1,0:T(8,128)(2,1)}), bf16[8,2,88,512]{3,2,1,0:T(8,128)(2,1)S(1)}, u32[]{:S(2)}, u32[]{:S(2)}) async-start(bf16[8,2,88,512]{3,2,1,0:T(8,128)(2,1)} %get-tuple-element.116.att_ref), calls=%async_computation.3 | async-start | bytes 2883584 | tf_op jit(solution)/shard_map/all_to_all | solution.py:1057
  432.3 161.2 %all-gather.18.cloned.1.call-start = ((), (), s32[]{:S(2)}) async-start(), calls=%async_computation.19 | async-start | bytes 19464192 | tf_op jit(solution)/shard_map/all_gather | solution.py:1136
  432.4 39.4 %collective-permute-start.25 = (bf16[768,352]{0,1:T(8,128)(2,1)S(1)}, bf16[768,352]{0,1:T(8,128)(2,1)}, u32[]{:S(2)}, u32[]{:S(2)}) collective-permute-start(bf16[768,352]{0,1:T(8,128)(2,1)S(1)} %copy-done.42), channel_id=1, source_target_pairs={{0,16},{8,24},{16,0},{24,8},{1,17},{9,25},{17,1},{25,9},{2,18},{10... | collective-permute-start | bytes 1622024 | tf_op jit(solution)/shard_map/ppermute | solution.py:1067
  434.8 36.9 %collective-permute-start.24 = (bf16[768,352]{0,1:T(8,128)(2,1)S(1)}, bf16[768,352]{0,1:T(8,128)(2,1)}, u32[]{:S(2)}, u32[]{:S(2)}) collective-permute-start(bf16[768,352]{0,1:T(8,128)(2,1)S(1)} %copy-done.42), channel_id=1, source_target_pairs={{0,8},{8,16},{16,24},{24,0},{1,9},{9,17},{17,25},{25,1},{2,10},{10... | collective-permute-start | bytes 1622024 | tf_op jit(solution)/shard_map/ppermute | solution.py:1067
  436.3 36.3 %collective-permute-start.26 = (bf16[768,352]{0,1:T(8,128)(2,1)S(1)}, bf16[768,352]{0,1:T(8,128)(2,1)}, u32[]{:S(2)}, u32[]{:S(2)}) collective-permute-start(bf16[768,352]{0,1:T(8,128)(2,1)S(1)} %copy-done.42), channel_id=1, source_target_pairs={{0,24},{8,0},{16,8},{24,16},{1,25},{9,1},{17,9},{25,17},{2,26},{10... | collective-permute-start | bytes 1622024 | tf_op jit(solution)/shard_map/ppermute | solution.py:1067
  475.8 313.6 %reduce-scatter.6.cloned.1.call-start = ((), (), s32[]{:S(2)}) async-start(), calls=%async_computation.20 | async-start | bytes 19464192 | tf_op jit(solution)/shard_map/reduce_scatter | solution.py:1131
  660.6 410.8 %reduce-scatter.10.cloned.1.call-start = ((), (), s32[]{:S(2)}) async-start(), calls=%async_computation.22 | async-start | bytes 19464192 | tf_op jit(solution)/shard_map/reduce_scatter | solution.py:1131
  816.7 38.7 %all-to-all-start.4 = ((bf16[8,2,88,512]{3,2,1,0:T(8,128)(2,1)}), bf16[8,2,88,512]{3,2,1,0:T(8,128)(2,1)}, u32[]{:S(2)}, u32[]{:S(2)}) async-start(bf16[8,2,88,512]{3,2,1,0:T(8,128)(2,1)} %bitcast.199), calls=%async_computation.5 | async-start | bytes 2883584 | tf_op jit(solution)/shard_map/all_to_all | solution.py:1057
  821.0 331.1 %reduce-scatter.8.cloned.1.call-start = ((), (), s32[]{:S(2)}) async-start(), calls=%async_computation.21 | async-start | bytes 18247680 | tf_op jit(solution)/shard_map/reduce_scatter | solution.py:1131
  857.2 108.6 %collective-permute-start.28 = (bf16[768,352]{0,1:T(8,128)(2,1)}, bf16[768,352]{0,1:T(8,128)(2,1)}, u32[]{:S(2)}, u32[]{:S(2)}) collective-permute-start(bf16[768,352]{0,1:T(8,128)(2,1)} %copy.111), channel_id=1, source_target_pairs={{0,16},{8,24},{16,0},{24,8},{1,17},{9,25},{17,1},{25,9},{2,18},{10... | collective-permute-start | bytes 1622024 | tf_op jit(solution)/shard_map/ppermute | solution.py:1087
  862.1 103.7 %collective-permute-start.27 = (bf16[768,352]{0,1:T(8,128)(2,1)}, bf16[768,352]{0,1:T(8,128)(2,1)S(1)}, u32[]{:S(2)}, u32[]{:S(2)}) collective-permute-start(bf16[768,352]{0,1:T(8,128)(2,1)} %copy.110), channel_id=1, source_target_pairs={{0,8},{8,16},{16,24},{24,0},{1,9},{9,17},{17,25},{25,1},{2,10},{10... | collective-permute-start | bytes 1622024 | tf_op jit(solution)/shard_map/ppermute | solution.py:1087
  863.6 102.2 %collective-permute-start.29 = (bf16[768,352]{0,1:T(8,128)(2,1)}, bf16[768,352]{0,1:T(8,128)(2,1)}, u32[]{:S(2)}, u32[]{:S(2)}) collective-permute-start(bf16[768,352]{0,1:T(8,128)(2,1)} %copy.112), channel_id=1, source_target_pairs={{0,24},{8,0},{16,8},{24,16},{1,25},{9,1},{17,9},{25,17},{2,26},{10... | collective-permute-start | bytes 1622024 | tf_op jit(solution)/shard_map/ppermute | solution.py:1087
  872.1 100.7 %all-to-all-start.5 = ((bf16[8,2,88,512]{3,2,1,0:T(8,128)(2,1)}), bf16[8,2,88,512]{3,2,1,0:T(8,128)(2,1)}, u32[]{:S(2)}, u32[]{:S(2)}) async-start(bf16[8,2,88,512]{3,2,1,0:T(8,128)(2,1)} %bitcast.198), calls=%async_computation.8 | async-start | bytes 2883584 | tf_op jit(solution)/shard_map/all_to_all | solution.py:1057
  972.8 93.9 %all-to-all-start.7 = ((bf16[8,3,2,88,512]{4,3,2,1,0:T(8,128)(2,1)}), bf16[8,3,2,88,512]{4,3,2,1,0:T(8,128)(2,1)}, u32[]{:S(2)}, u32[]{:S(2)}) async-start(bf16[8,3,2,88,512]{4,3,2,1,0:T(8,128)(2,1)} %shard_map.321), calls=%async_computation.10 | async-start | bytes 8650752 | tf_op jit(solution)/shard_map/all_to_all | solution.py:1057
  1066.8 75.0 %all-to-all-start.6 = ((bf16[8,3,2,88,512]{4,3,2,1,0:T(8,128)(2,1)}), bf16[8,3,2,88,512]{4,3,2,1,0:T(8,128)(2,1)}, u32[]{:S(2)}, u32[]{:S(2)}) async-start(bf16[8,3,2,88,512]{4,3,2,1,0:T(8,128)(2,1)} %shard_map.322), calls=%async_computation.9 | async-start | bytes 8650752 | tf_op jit(solution)/shard_map/all_to_all | solution.py:1057
  1071.4 233.4 %reduce-scatter.12.cloned.1.call-start = ((), (), s32[]{:S(2)}) async-start(), calls=%async_computation.23 | async-start | bytes 13381632 | tf_op jit(solution)/shard_map/reduce_scatter | solution.py:1131
  1073.3 27.0 %collective-permute-start.31 = (bf16[176,1536]{1,0:T(8,128)(2,1)S(1)}, bf16[176,1536]{1,0:T(8,128)(2,1)S(1)}, u32[]{:S(2)}, u32[]{:S(2)}) collective-permute-start(bf16[176,1536]{1,0:T(8,128)(2,1)S(1)} %select_select_fusion.4), channel_id=1, source_target_pairs={{0,16},{8,24},{16,0},{24,8},{1,17},{9,25},{17,1},{25,9},{2,18},{10... | collective-permute-start | bytes 1622024 | tf_op jit(solution)/shard_map/ppermute | solution.py:1087
  1075.1 37.7 %collective-permute-start.32 = (bf16[176,1536]{1,0:T(8,128)(2,1)S(1)}, bf16[176,1536]{1,0:T(8,128)(2,1)S(1)}, u32[]{:S(2)}, u32[]{:S(2)}) collective-permute-start(bf16[176,1536]{1,0:T(8,128)(2,1)S(1)} %get-tuple-element.308), channel_id=1, source_target_pairs={{0,24},{8,0},{16,8},{24,16},{1,25},{9,1},{17,9},{25,17},{2,26},{10... | collective-permute-start | bytes 1622024 | tf_op jit(solution)/shard_map/ppermute | solution.py:1087
  1077.3 35.4 %collective-permute-start.30 = (bf16[176,1536]{1,0:T(8,128)(2,1)S(1)}, bf16[176,1536]{1,0:T(8,128)(2,1)S(1)}, u32[]{:S(2)}, u32[]{:S(2)}) collective-permute-start(bf16[176,1536]{1,0:T(8,128)(2,1)S(1)} %get-tuple-element.309), channel_id=1, source_target_pairs={{0,8},{8,16},{16,24},{24,0},{1,9},{9,17},{17,25},{25,1},{2,10},{10... | collective-permute-start | bytes 1622024 | tf_op jit(solution)/shard_map/ppermute | solution.py:1087
  1199.8 101.1 %collective-permute-start.35 = (bf16[176,1056]{1,0:T(8,128)(2,1)}, bf16[176,1056]{1,0:T(8,128)(2,1)}, u32[]{:S(2)}, u32[]{:S(2)}) collective-permute-start(bf16[176,1056]{1,0:T(8,128)(2,1)} %get-tuple-element.332), channel_id=1, source_target_pairs={{0,24},{8,0},{16,8},{24,16},{1,25},{9,1},{17,9},{25,17},{2,26},{10... | collective-permute-start | bytes 1115144 | tf_op jit(solution)/shard_map/ppermute | solution.py:1087
  1199.8 101.1 %collective-permute-start.34 = (bf16[176,1056]{1,0:T(8,128)(2,1)}, bf16[176,1056]{1,0:T(8,128)(2,1)}, u32[]{:S(2)}, u32[]{:S(2)}) collective-permute-start(bf16[176,1056]{1,0:T(8,128)(2,1)} %get-tuple-element.333), channel_id=1, source_target_pairs={{0,16},{8,24},{16,0},{24,8},{1,17},{9,25},{17,1},{25,9},{2,18},{10... | collective-permute-start | bytes 1115144 | tf_op jit(solution)/shard_map/ppermute | solution.py:1087
  1200.9 100.0 %collective-permute-start.33 = (bf16[176,1056]{1,0:T(8,128)(2,1)}, bf16[176,1056]{1,0:T(8,128)(2,1)}, u32[]{:S(2)}, u32[]{:S(2)}) collective-permute-start(bf16[176,1056]{1,0:T(8,128)(2,1)} %get-tuple-element.334), channel_id=1, source_target_pairs={{0,8},{8,16},{16,24},{24,0},{1,9},{9,17},{17,25},{25,1},{2,10},{10... | collective-permute-start | bytes 1115144 | tf_op jit(solution)/shard_map/ppermute | solution.py:1087
  1240.2 63.6 %all-to-all-start.8 = ((bf16[8,128,1120]{1,2,0:T(8,128)(2,1)}), bf16[8,128,1120]{1,2,0:T(8,128)(2,1)S(1)}, u32[]{:S(2)}, u32[]{:S(2)}) async-start(bf16[8,128,1120]{1,2,0:T(8,128)(2,1)} %copy_bitcast_fusion), calls=%async_computation.12 | async-start | bytes 4587520 | tf_op jit(solution)/shard_map/all_to_all | solution.py:1057
  1243.8 183.2 %reduce-scatter.14.cloned.1.call-start = ((), (), s32[]{:S(2)}) async-start(), calls=%async_computation.24 | async-start | bytes 8921088 | tf_op jit(solution)/shard_map/reduce_scatter | solution.py:1131
  1244.6 37.8 %collective-permute-start.39 = (f32[2,1408]{1,0:T(2,128)S(1)}, f32[2,1408]{1,0:T(2,128)S(1)}, u32[]{:S(2)}, u32[]{:S(2)}) collective-permute-start(f32[2,1408]{1,0:T(2,128)S(1)} %dynamic_update_slice.5), channel_id=1, source_target_pairs={{0,1},{1,0},{2,3},{3,2},{4,5},{5,4},{6,7},{7,6},{8,9},{9,8},{10,11... | collective-permute-start | bytes 33800 | tf_op jit(solution)/shard_map/ppermute | solution.py:1124
  1282.7 14.2 collective-permute-start.40
  1333.2 11.7 collective-permute-start.44
  1336.2 42.2 %collective-permute-start.43 = (bf16[464,352]{1,0:T(8,128)(2,1)S(1)}, bf16[464,352]{1,0:T(8,128)(2,1)S(1)}, u32[]{:S(2)}, u32[]{:S(2)}) collective-permute-start(bf16[464,352]{1,0:T(8,128)(2,1)S(1)} %select_select_fusion.29), channel_id=1, source_target_pairs={{0,16},{8,24},{16,0},{24,8},{1,17},{9,25},{17,1},{25,9},{2,18},{10... | collective-permute-start | bytes 979976 | tf_op jit(solution)/shard_map/ppermute | solution.py:1087
  1336.5 41.9 %collective-permute-start.42 = (bf16[464,352]{1,0:T(8,128)(2,1)S(1)}, bf16[464,352]{1,0:T(8,128)(2,1)S(1)}, u32[]{:S(2)}, u32[]{:S(2)}) collective-permute-start(bf16[464,352]{1,0:T(8,128)(2,1)S(1)} %select_select_fusion.30), channel_id=1, source_target_pairs={{0,8},{8,16},{16,24},{24,0},{1,9},{9,17},{17,25},{25,1},{2,10},{10... | collective-permute-start | bytes 979976 | tf_op jit(solution)/shard_map/ppermute | solution.py:1087
  1339.0 55.2 %collective-permute-start.46 = (bf16[176,1056]{1,0:T(8,128)(2,1)S(1)}, bf16[176,1056]{1,0:T(8,128)(2,1)S(1)}, u32[]{:S(2)}, u32[]{:S(2)}) collective-permute-start(bf16[176,1056]{1,0:T(8,128)(2,1)S(1)} %select_select_fusion.15), channel_id=1, source_target_pairs={{0,16},{8,24},{16,0},{24,8},{1,17},{9,25},{17,1},{25,9},{2,18},{10... | collective-permute-start | bytes 1115144 | tf_op jit(solution)/shard_map/ppermute | solution.py:1087
  1340.5 53.6 %collective-permute-start.47 = (bf16[176,1056]{1,0:T(8,128)(2,1)S(1)}, bf16[176,1056]{1,0:T(8,128)(2,1)S(1)}, u32[]{:S(2)}, u32[]{:S(2)}) collective-permute-start(bf16[176,1056]{1,0:T(8,128)(2,1)S(1)} %get-tuple-element.343), channel_id=1, source_target_pairs={{0,24},{8,0},{16,8},{24,16},{1,25},{9,1},{17,9},{25,17},{2,26},{10... | collective-permute-start | bytes 1115144 | tf_op jit(solution)/shard_map/ppermute | solution.py:1087
  1344.8 49.4 %collective-permute-start.45 = (bf16[176,1056]{1,0:T(8,128)(2,1)S(1)}, bf16[176,1056]{1,0:T(8,128)(2,1)S(1)}, u32[]{:S(2)}, u32[]{:S(2)}) collective-permute-start(bf16[176,1056]{1,0:T(8,128)(2,1)S(1)} %get-tuple-element.344), channel_id=1, source_target_pairs={{0,8},{8,16},{16,24},{24,0},{1,9},{9,17},{17,25},{25,1},{2,10},{10... | collective-permute-start | bytes 1115144 | tf_op jit(solution)/shard_map/ppermute | solution.py:1087
  1414.2 19.6 %collective-permute-start.53 = (f32[176,15]{0,1:T(8,128)S(1)}, f32[176,15]{0,1:T(8,128)S(1)}, u32[]{:S(2)}, u32[]{:S(2)}) collective-permute-start(f32[176,15]{0,1:T(8,128)S(1)} %select_select_fusion.46), channel_id=1, source_target_pairs={{0,24},{8,0},{16,8},{24,16},{1,25},{9,1},{17,9},{25,17},{2,26},{10... | collective-permute-start | bytes 31688 | tf_op jit(solution)/shard_map/ppermute | solution.py:1087
  1417.2 19.0 %collective-permute-start.51 = (f32[176,15]{0,1:T(8,128)S(1)}, f32[176,15]{0,1:T(8,128)S(1)}, u32[]{:S(2)}, u32[]{:S(2)}) collective-permute-start(f32[176,15]{0,1:T(8,128)S(1)} %get-tuple-element.396), channel_id=1, source_target_pairs={{0,8},{8,16},{16,24},{24,0},{1,9},{9,17},{17,25},{25,1},{2,10},{10... | collective-permute-start | bytes 31688 | tf_op jit(solution)/shard_map/ppermute | solution.py:1087
  1423.1 13.1 collective-permute-start.52
  1431.8 13.5 collective-permute-start.56
  1432.7 14.0 collective-permute-start.54
  1433.8 22.6 %collective-permute-start.55 = (bf16[352,352]{1,0:T(8,128)(2,1)}, bf16[352,352]{1,0:T(8,128)(2,1)S(1)}, u32[]{:S(2)}, u32[]{:S(2)}) collective-permute-start(bf16[352,352]{1,0:T(8,128)(2,1)} %get-tuple-element.354), channel_id=1, source_target_pairs={{0,16},{8,24},{16,0},{24,8},{1,17},{9,25},{17,1},{25,9},{2,18},{10... | collective-permute-start | bytes 743432 | tf_op jit(solution)/shard_map/ppermute | solution.py:1087
  (131 other events, 1964.4 us)
Sparse Core Ops, SparseCore 0:
  34.0 58.6 all-gather.7
  100.3 87.9 all-gather.9
  190.3 115.5 all-gather.11
  308.2 77.9 all-gather.13
  387.9 112.0 all-gather.15
  501.7 91.7 all-gather.17
  660.7 118.6 reduce-scatter.5
  783.4 149.3 reduce-scatter.9
  936.5 204.7 reduce-scatter.7
  1172.1 110.3 reduce-scatter.11
  1304.9 68.9 reduce-scatter.13

commit v6 on v3

--- a/solution.py
+++ b/solution.py
@@ -1181,10 +1181,7 @@
     row_count = images * tile_len
     out_width = cotangent.shape[3]
 
-    f_skip = lax.all_gather(w_skip, EVERY, axis=0, tiled=True).reshape(
-        dp_devices, -1, w_skip.shape[1]
-    )
-    f_skip = jnp.swapaxes(f_skip, 0, 1).reshape(f_skip.shape[1], -1)
+    f_skip = tiles_whole(widen(fetch(w_skip)))
     small = jnp.concatenate([w_patch, w_final, norm_params], axis=1)
     small_widths = (w_patch.shape[1], w_final.shape[1], norm_params.shape[1])
     cuts = (0, small_widths[0], sum(small_widths[:2]), sum(small_widths))
@@ -1492,8 +1489,16 @@
         ],
         axis=2,
     )
-    small_grads = narrow(sum_tiles(small_grads.reshape(model_width, -1)))
-    skip_w_grad = narrow(t_skip)
+    small_grads = sum_tiles(small_grads.reshape(model_width, -1))
+    last, small_rows, small_width = [], small_grads.shape[0], sum(small_widths)
+    for at in range(dp_devices):
+        few = small_grads[:, at * small_width : (at + 1) * small_width].astype(BF16).reshape(-1)
+        few = jnp.pad(few, (0, -few.shape[0] % width)).reshape(-1, width)
+        last.append(jnp.concatenate([t_skip[:, at * width : (at + 1) * width], few]))
+    last = narrow_blocks(last)
+    skip_w_grad = last[: t_skip.shape[0]]
+    small_grads = last[t_skip.shape[0] :].reshape(-1)[: small_rows * small_width]
+    small_grads = small_grads.reshape(small_rows, small_width)
     patch_grad, final_grad, norms_grad = (
         small_grads[:, cuts[at] : cuts[at + 1]] for at in range(3)
     )

time: 1470 us -> 1450 us (0.986)
  local copies, waits for them, and re-layouts: 107 us -> 81.7 us
    reshape x2 -> x10, local copies, waits for them, and re-layouts: 27.9 us -> 1.53 us  [the longest x4 0.9 us: local_heads(): small_grads[:, at * small_width:(at + 1) * small_width].astype(BF16)]
    ppermute x18 -> x21, starting transfers between devices: 60.4 us -> 67.8 us  [fetch(): lax.ppermute(weight, 'dp', shift_pairs(devices, step))]
    ppermute x18 -> x21, waiting for transfers between devices: 94.9 us -> 89.6 us  [fetch(): lax.ppermute(weight, 'dp', shift_pairs(devices, step))]
    ppermute x21 -> x18, starting transfers between devices: 42.7 us -> 39.4 us  [narrow_blocks(): received.append(lax.ppermute(sent, 'dp', shift_pairs(devices, step)))]
    all_gather x6 -> x7, waiting for transfers between devices: 29 us -> 29.6 us  [tiles_whole(): return lax.all_gather(weight, TILE, axis=0, tiled=True)]
    ppermute x21 -> x18, waiting for transfers between devices: 95.9 us -> 95.6 us  [narrow_blocks(): received.append(lax.ppermute(sent, 'dp', shift_pairs(devices, step)))]
  transfers between devices with their start and end apart: 74 -> 74, of which waited for: 34 -> 37; matrix products, arithmetic and copies ran while one was open for 33% -> 32% of each run, Pallas kernels for 25% -> 26%
where the time goes in v6:
time: 1450 us; the launch traced here: 1430 us
  matrix products  382 us (26%)
  Pallas kernels  366 us (25%)
  waiting for transfers between devices  337 us (23%)
  starting transfers between devices  155 us (11%)
  local copies, waits for them, and re-layouts  81.7 us (6%)
  other arithmetic  76.9 us (5%)
  blocking collectives  17.7 us (1%)
  between operations  16.6 us (1%)
    pallas_call x2, Pallas kernels, attend_back(): kernel_call(functools.partial(attend_back_body, score_scale), 2560 * head...  178 us
    dot_general x11, matrix products, dot_over(): lax.dot_general(left_mat, right_mat, (((left_axis,), (right_axis,)), ((),...  120 us
    dot_general x9, matrix products, plain_dot(): return jnp.dot(left_mat, right_mat, preferred_element_type=jnp.float32)  106 us
    all_to_all x8, waiting for transfers between devices, swap_tiles(): lax.all_to_all(values_in, TILE, split_axis=0, concat_axis=0, tiled=True)  100 us
    ppermute x18, waiting for transfers between devices, narrow_blocks(): received.append(lax.ppermute(sent, 'dp', shift_pairs(devices, step)))  95.6 us
    dot_general x9, matrix products, left_dot(): lax.dot_general(left_mat, right_mat, (((0,), (0,)), ((), ())), preferred_...  90.3 us
    ppermute x21, waiting for transfers between devices, fetch(): lax.ppermute(weight, 'dp', shift_pairs(devices, step))  89.6 us
    pallas_call x2, Pallas kernels, attend(): kernel_call(attend_body, 1024 * heads * tiles ** 2 * tile_len ** 2, 8 * q...  68.5 us
  transfers between devices with their start and end apart: 74, of which 37 were waited for; matrix products, arithmetic and copies ran while one was open for 32% of the time, Pallas kernels for 26%

profile of v6, /device:TPU:0, one launch (start us, length us, event | category | flops | bytes accessed | tf_op | source)
XLA Modules:
  0.0 1432.0 jit_solution(928214675251457545)
XLA Ops:
  14.3 5.7 collective-permute-done.3
  20.1 10.8 collective-permute-done.4
  35.6 6.3 collective-permute-start
  53.7 8.5 collective-permute-done.1
  62.9 17.7 %all-gather = bf16[8,176,60]{1,2,0:T(8,128)(2,1)S(1)} all-gather(bf16[1,176,60]{1,2,0:T(8,128)(2,1)S(1)} %reshape.660), channel_id=1, replica_groups=mesh['dp'=4,'row'=4,'col'=2] {'row','col'}, dimensions={0}, use_global_device_ids=true | all-gather | bytes 190080 | tf_op jit(solution)/shard_map/all_gather | solution.py:1136
  84.1 9.6 shard_map.314
  100.7 21.2 %collective-permute-start.15 = (bf16[176,1056]{1,0:T(8,128)(2,1)S(1)}, bf16[176,1056]{1,0:T(8,128)(2,1)S(1)}, u32[]{:S(2)}, u32[]{:S(2)}) collective-permute-start(bf16[176,1056]{1,0:T(8,128)(2,1)S(1)} %concatenate.112), channel_id=1, source_target_pairs={{0,8},{8,16},{16,24},{24,0},{1,9},{9,17},{17,25},{25,1},{2,10},{10... | collective-permute-start | bytes 1115144 | tf_op jit(solution)/shard_map/ppermute | solution.py:1067
  124.4 7.3 collective-permute-done.15
  131.7 11.3 collective-permute-done.16
  143.0 5.8 collective-permute-done.17
  170.4 8.9 collective-permute-start.18
  183.0 14.3 fusion.109
  206.5 14.7 %shard_map.315 = (bf16[8,3,2,88,512]{4,3,2,1,0:T(8,128)(2,1)}, f32[8,3,2,512]{3,2,1,0:T(2,128)}) custom-call(bf16[512,1408]{1,0:T(8,128)(2,1)} %get-tuple-element.288.rows_ref, bf16[1408,4224]{1,0:T(8,128)(2,1)} %all-gather.11.cloned.1.call-done.weight_ref, f32[88,512]{1,0:T(8,128)} %pad_maximum_fusion.19.cos_ref, f32[88,512]{1,0:T(8,128)} %pad_maximum_fusion.20.sin_ref, ...), custom_call_target="tpu_custom_call" | custom-call | flops 6090129408 | bytes 11894784 | tf_op jit(solution)/shard_map/pallas_call | solution.py:652
  230.9 12.3 collective-permute-done.21
  243.1 22.6 %collective-permute-done.22 = bf16[176,1536]{1,0:T(8,128)(2,1)S(1)} collective-permute-done((bf16[176,1536]{1,0:T(8,128)(2,1)S(1)}, bf16[176,1536]{1,0:T(8,128)(2,1)S(1)}, u32[]{:S(2)}, u32[]{:S(2)}) %collective-permute-start.22) | collective-permute-done | bytes 540704 | tf_op jit(solution)/shard_map/ppermute | solution.py:1067
  265.7 36.8 %all-to-all-done.query_ref.key_ref.value_ref = bf16[8,3,2,88,512]{4,3,2,1,0:T(8,128)(2,1)} async-done(((bf16[8,3,2,88,512]{4,3,2,1,0:T(8,128)(2,1)}), bf16[8,3,2,88,512]{4,3,2,1,0:T(8,128)(2,1)}, u32[]{:S(2)}, u32[]{:S(2)}) %all-to-all-start) | async-done | bytes 4325408 | tf_op jit(solution)/shard_map/all_to_all | solution.py:1057
  304.6 14.7 %shard_map.317 = (bf16[8,3,2,88,512]{4,3,2,1,0:T(8,128)(2,1)}, f32[8,3,2,512]{3,2,1,0:T(2,128)}) custom-call(bf16[512,1408]{1,0:T(8,128)(2,1)} %get-tuple-element.289.rows_ref, bf16[1408,4224]{1,0:T(8,128)(2,1)} %all-gather.11.cloned.1.call-done.weight_ref, f32[88,512]{1,0:T(8,128)} %pad_maximum_fusion.19.cos_ref, f32[88,512]{1,0:T(8,128)} %pad_maximum_fusion.20.sin_ref, ...), custom_call_target="tpu_custom_call" | custom-call | flops 6090129408 | bytes 11894784 | tf_op jit(solution)/shard_map/pallas_call | solution.py:652
  324.8 34.1 %shard_map.316 = (bf16[8,2,88,512]{3,2,1,0:T(8,128)(2,1)}, f32[8,2,1,512]{3,2,1,0:T(1,128)}) custom-call(bf16[8,3,2,88,512]{4,3,2,1,0:T(8,128)(2,1)} %all-to-all-done.query_ref.key_ref.value_ref, bf16[8,3,2,88,512]{4,3,2,1,0:T(8,128)(2,1)} %all-to-all-done.query_ref.key_ref.value_ref, bf16[8,3,2,88,512]{4,3,2,1,0:T(8,128)(2,1)} %all-to-all-done.query_ref.key_ref.value_ref, ...), custom_call_target="tpu_custom_call" | custom-call | flops 34359738368 | bytes 17301504 | tf_op jit(solution)/shard_map/pallas_call | solution.py:757
  358.8 30.2 %all-to-all-done.2.query_ref.key_ref.value_ref = bf16[8,3,2,88,512]{4,3,2,1,0:T(8,128)(2,1)} async-done(((bf16[8,3,2,88,512]{4,3,2,1,0:T(8,128)(2,1)}), bf16[8,3,2,88,512]{4,3,2,1,0:T(8,128)(2,1)}, u32[]{:S(2)}, u32[]{:S(2)}) %all-to-all-start.2) | async-done | bytes 4325408 | tf_op jit(solution)/shard_map/all_to_all | solution.py:1057
  392.6 34.5 %shard_map.318 = (bf16[8,2,88,512]{3,2,1,0:T(8,128)(2,1)}, f32[8,2,1,512]{3,2,1,0:T(1,128)}) custom-call(bf16[8,3,2,88,512]{4,3,2,1,0:T(8,128)(2,1)} %all-to-all-done.2.query_ref.key_ref.value_ref, bf16[8,3,2,88,512]{4,3,2,1,0:T(8,128)(2,1)} %all-to-all-done.2.query_ref.key_ref.value_ref, ...), custom_call_target="tpu_custom_call" | custom-call | flops 34359738368 | bytes 17301504 | tf_op jit(solution)/shard_map/pallas_call | solution.py:757
  436.6 21.5 %all-to-all-done.3 = bf16[8,2,88,512]{3,2,1,0:T(8,128)(2,1)S(1)} async-done(((bf16[8,2,88,512]{3,2,1,0:T(8,128)(2,1)}), bf16[8,2,88,512]{3,2,1,0:T(8,128)(2,1)S(1)}, u32[]{:S(2)}, u32[]{:S(2)}) %all-to-all-start.3) | async-done | bytes 1441824 | tf_op jit(solution)/shard_map/all_to_all | solution.py:1057
  458.1 10.5 fusion.110
  475.9 9.8 fusion.113
  486.5 9.3 fusion.10
  495.8 14.6 %shard_map.319 = (bf16[16,88,1024]{2,1,0:T(8,128)(2,1)}, bf16[16,88,1024]{2,1,0:T(8,128)(2,1)}, f32[16,1,1024]{2,1,0:T(1,128)}, f32[16,1,1024]{2,1,0:T(1,128)}) custom-call(f32[16,88,1024]{2,1,0:T(8,128)} %bitcast.210, f32[2,16,88,768]{3,2,1,0:T(8,128)} %bitcast.187), custom_call_target="tpu_custom_call" | custom-call | flops 6442450944 | bytes 11534336 | tf_op jit(solution)/shard_map/pallas_call | solution.py:897
  510.4 9.2 fusion.111
  522.9 39.9 %add_convert_fusion = (bf16[1024,6144]{1,0:T(8,128)(2,1)}, bf16[1024,6144]{1,0:T(8,128)(2,1)}) fusion(bf16[1408,6144]{1,0:T(8,128)(2,1)} %all-gather.17.cloned.1.call-done, f32[1024,1408]{1,0:T(8,128)} %copy-done.3, f32[1408]{0:T(1024)S(1)} %copy-done.81, f32[1408]{0:T(1024)S(1)} %copy-done.56, f32[1024]{0:T(1024)S(1)} %add_rsqrt_fusion.2, ...), kind=kOutput, calls=%fused_computation.1 | convolution fusion | flops 17843486720 | bytes 48253952 | tf_op jit(solution)/shard_map/dot_general | solution.py:72
  562.8 29.6 %all-gather.19.cloned.1.call-done = bf16[6144,1408]{0,1:T(8,128)(2,1)} async-done(((bf16[768,1408]{0,1:T(8,128)(2,1)}), bf16[6144,1408]{0,1:T(8,128)(2,1)}) %all-gather.19.cloned.1.call-update) | async-done | bytes 17301520 | tf_op jit(solution)/shard_map/all_gather | solution.py:1136
  592.4 28.8 %fusion.112 = (f32[1024]{0:T(1024)S(1)}, f32[1024,1408]{1,0:T(8,128)S(1)}) fusion(f32[1024,1408]{1,0:T(8,128)} %copy-done.3, bf16[1024,6144]{1,0:T(8,128)(2,1)} %get-tuple-element.121, bf16[6144,1408]{0,1:T(8,128)(2,1)} %all-gather.19.cloned.1.call-done), kind=kOutput, calls=%fused_computation.320 | convolution fusion | flops 17719623680 | bytes 41422848 | tf_op jit(solution)/shard_map/dot_general | solution.py:72
  631.4 27.9 %convolution_convert_fusion = bf16[6144,1408]{1,0:T(8,128)(2,1)} fusion(bf16[1024,6144]{1,0:T(8,128)(2,1)} %get-tuple-element.121, bf16[1024,1408]{1,0:T(8,128)(2,1)S(1)} %get-tuple-element.126), kind=kOutput, calls=%fused_computation.5 | convolution fusion | flops 17725390848 | bytes 32768000 | tf_op jit(solution)/shard_map/dot_general | solution.py:76
  661.1 30.5 %multiply_convert_fusion = bf16[1024,6144]{1,0:T(8,128)(2,1)} fusion(bf16[1024,6144]{1,0:T(8,128)(2,1)} %get-tuple-element.127, bf16[1024,1408]{1,0:T(8,128)(2,1)S(1)} %copy-done.18, bf16[6144,1408]{0,1:T(8,128)(2,1)} %all-gather.19.cloned.1.call-done), kind=kOutput, calls=%fused_computation | convolution fusion | flops 17735614464 | bytes 45350912 | tf_op jit(solution)/shard_map/dot_general | solution.py:82
  691.7 26.0 %convolution_convert_fusion.1 = bf16[1408,6144]{1,0:T(8,128)(2,1)} fusion(bf16[1024,6144]{1,0:T(8,128)(2,1)} %multiply_convert_fusion, f32[1024,1408]{1,0:T(8,128)} %copy-done.3, f32[1408]{0:T(1024)S(1)} %copy-done.81, f32[1408]{0:T(1024)S(1)} %copy-done.56, f32[1024]{0:T(1024)S(1)} %add_rsqrt_fusion.2, f32[1024]{0:T(1024)S(1)} %broadcast_multiply_fusion.12), kind=kOutput, calls=%fused_computation.6 | convolution fusion | flops 17732599808 | bytes 35671040 | tf_op jit(solution)/shard_map/dot_general | solution.py:76
  717.7 31.4 %multiply_reduce_fusion.1 = (f32[1408]{0:T(1024)}, f32[1024]{0:T(1024)S(1)}, f32[1024]{0:T(1024)S(1)}, f32[1408]{0:T(1024)}, f32[1024,1408]{1,0:T(8,128)}) fusion(f32[1024,1408]{1,0:T(8,128)} %copy-done.3, f32[1024]{0:T(1024)S(1)} %add_rsqrt_fusion.2, f32[1024]{0:T(1024)S(1)} %broadcast_multiply_fusion.12, f32[1408]{0:T(1024)S(1)} %copy-done.56, ...), kind=kOutput, calls=%fused_computation.19 | convolution fusion | flops 17729710080 | bytes 41452032 | tf_op jit(solution)/shard_map/dot_general | solution.py:82
  749.1 7.7 multiply_add_fusion.1
  756.9 10.5 convolution_convert_fusion.7
  767.3 21.3 %shard_map.320 = (bf16[16,88,1024]{2,1,0:T(8,128)(2,1)}, bf16[16,88,768]{2,1,0:T(8,128)(2,1)}, bf16[16,88,768]{2,1,0:T(8,128)(2,1)}) custom-call(bf16[16,88,1024]{2,1,0:T(8,128)(2,1)} %get-tuple-element.130.query_ref, f32[2,16,88,768]{3,2,1,0:T(8,128)} %bitcast.188, bf16[16,88,1024]{2,1,0:T(8,128)(2,1)} %bitcast.215, ...), custom_call_target="tpu_custom_call" | custom-call | flops 16106127360 | bytes 23068672 | tf_op jit(solution)/shard_map/pallas_call | solution.py:957
  788.7 14.2 multiply_reduce_fusion.2
  802.9 6.3 fusion.93
  809.2 6.8 fusion.17
  820.6 8.6 fusion.2
  829.3 9.8 fusion.1
  839.1 6.2 fusion
  849.2 5.6 all-to-all-done.4.grad_ref
  863.7 6.3 fusion.20
  874.3 89.2 %shard_map.321 = bf16[8,3,2,88,512]{4,3,2,1,0:T(8,128)(2,1)} custom-call(bf16[8,3,2,88,512]{4,3,2,1,0:T(8,128)(2,1)} %all-to-all-done.query_ref.key_ref.value_ref, bf16[8,3,2,88,512]{4,3,2,1,0:T(8,128)(2,1)} %all-to-all-done.query_ref.key_ref.value_ref, bf16[8,3,2,88,512]{4,3,2,1,0:T(8,128)(2,1)} %all-to-all-done.query_ref.key_ref.value_ref, ...), custom_call_target="tpu_custom_call" | custom-call | flops 85899345920 | bytes 17301504 | tf_op jit(solution)/shard_map/pallas_call | solution.py:845
  975.3 89.2 %shard_map.322 = bf16[8,3,2,88,512]{4,3,2,1,0:T(8,128)(2,1)} custom-call(bf16[8,3,2,88,512]{4,3,2,1,0:T(8,128)(2,1)} %all-to-all-done.2.query_ref.key_ref.value_ref, bf16[8,3,2,88,512]{4,3,2,1,0:T(8,128)(2,1)} %all-to-all-done.2.query_ref.key_ref.value_ref, bf16[8,3,2,88,512]{4,3,2,1,0:T(8,128)(2,1)} %all-to-all-done.2.query_ref.key_ref.value_ref, ...), custom_call_target="tpu_custom_call" | custom-call | flops 85899345920 | bytes 17301504 | tf_op jit(solution)/shard_map/pallas_call | solution.py:845
  1078.0 10.5 collective-permute-done.30
  1088.5 11.0 collective-permute-done.32
  1099.5 23.2 %collective-permute-done.31 = bf16[176,1536]{1,0:T(8,128)(2,1)S(1)} collective-permute-done((bf16[176,1536]{1,0:T(8,128)(2,1)S(1)}, bf16[176,1536]{1,0:T(8,128)(2,1)S(1)}, u32[]{:S(2)}, u32[]{:S(2)}) %collective-permute-start.31) | collective-permute-done | bytes 540704 | tf_op jit(solution)/shard_map/ppermute | solution.py:1087
  1124.1 10.1 shard_map.323.others_0_
  1134.2 6.1 all-to-all-done.6.grad_ref
  1140.3 10.3 shard_map.324
  1150.6 19.9 %convolution_convert_fusion.2 = bf16[1408,4224]{1,0:T(8,128)(2,1)} fusion(bf16[1024,1408]{1,0:T(8,128)(2,1)S(1)} %copy-done.12, bf16[4224,1024]{1,0:T(8,128)(2,1)} %bitcast.165), kind=kOutput, calls=%fused_computation.7 | convolution fusion | flops 12186206208 | bytes 23429120 | tf_op jit(solution)/shard_map/dot_general | solution.py:1144
  1180.6 26.4 %multiply_reduce_fusion.3 = (f32[1408]{0:T(1024)S(1)}, f32[1024]{0:T(1024)S(1)}, f32[1024]{0:T(1024)S(1)}, f32[1408]{0:T(1024)S(1)}, f32[1024,1408]{1,0:T(8,128)S(1)}) fusion(f32[1024,1408]{1,0:T(8,128)} %copy-done, f32[1024]{0:T(1024)S(1)} %copy-done.51, f32[1024]{0:T(1024)S(1)} %copy-done.49, f32[1408]{0:T(1024)S(1)} %copy-done.47, ...), kind=kOutput, calls=%fused_computation.21 | convolution fusion | flops 12193230848 | bytes 32113152 | tf_op jit(solution)/shard_map/dot_general | solution.py:1144
  1207.0 7.9 add_convert_fusion.1.low_ref
  1216.5 14.4 %convolution_convert_fusion.3 = bf16[2816,1408]{1,0:T(8,128)(2,1)} fusion(bf16[1024,2816]{1,0:T(8,128)(2,1)} %get-tuple-element.99, bf16[1024,1408]{1,0:T(8,128)(2,1)S(1)} %add_convert_fusion.1.low_ref), kind=kOutput, calls=%fused_computation.8 | convolution fusion | flops 8124137472 | bytes 16580608 | tf_op jit(solution)/shard_map/dot_general | solution.py:76
  1240.7 23.5 %shard_map.325 = (f32[1024,1408]{1,0:T(8,128)}, bf16[1024,1408]{1,0:T(8,128)(2,1)}, f32[2,2816]{1,0:T(2,128)}) custom-call(bf16[1024,1408]{1,0:T(8,128)(2,1)} %copy-done.16, bf16[2816,1408]{1,0:T(8,128)(2,1)} %all-gather.9.cloned.1.call-done.weight_ref, f32[1024,2816]{1,0:T(8,128)} %get-tuple-element.156.z_ref, f32[1024,1]{1,0:T(8,128)} %get-tuple-element.157.inv_ref, ...), custom_call_target="tpu_custom_call" | custom-call | flops 8120172544 | bytes 25952256 | tf_op jit(solution)/shard_map/pallas_call | solution.py:1032
  1312.1 9.2 collective-permute-start.42
  1336.1 5.0 collective-permute-done.44
  1341.1 17.4 %collective-permute-done.43 = bf16[176,1056]{1,0:T(8,128)(2,1)} collective-permute-done((bf16[176,1056]{1,0:T(8,128)(2,1)}, bf16[176,1056]{1,0:T(8,128)(2,1)}, u32[]{:S(2)}, u32[]{:S(2)}) %collective-permute-start.43) | collective-permute-done | bytes 371744 | tf_op jit(solution)/shard_map/ppermute | solution.py:1087
  1368.9 6.5 copy.140
  1379.6 13.1 collective-permute-done.52
  1396.8 7.4 collective-permute-start.39
  1411.3 9.9 collective-permute-done.40
  (563 shorter events, 285.9 us)
Async XLA Ops:
  7.2 175.8 %all-gather.9.cloned.1.call-start = ((), (), s32[]{:S(2)}) async-start(), calls=%async_computation.13 | async-start | bytes 8921088 | tf_op jit(solution)/shard_map/all_gather | solution.py:1136
  7.3 12.8 collective-permute-start.3
  10.4 20.4 %collective-permute-start.4 = (bf16[352,352]{1,0:T(8,128)(2,1)}, bf16[352,352]{1,0:T(8,128)(2,1)S(1)}, u32[]{:S(2)}, u32[]{:S(2)}) collective-permute-start(bf16[352,352]{1,0:T(8,128)(2,1)} %param.26), channel_id=1, source_target_pairs={{0,16},{8,24},{16,0},{24,8},{1,17},{9,25},{17,1},{25,9},{2,18},{10... | collective-permute-start | bytes 743432 | tf_op jit(solution)/shard_map/ppermute | solution.py:1067
  13.0 17.9 %collective-permute-start.5 = (bf16[352,352]{1,0:T(8,128)(2,1)}, bf16[352,352]{1,0:T(8,128)(2,1)S(1)}, u32[]{:S(2)}, u32[]{:S(2)}) collective-permute-start(bf16[352,352]{1,0:T(8,128)(2,1)} %param.26), channel_id=1, source_target_pairs={{0,24},{8,0},{16,8},{24,16},{1,25},{9,1},{17,9},{25,17},{2,26},{10... | collective-permute-start | bytes 743432 | tf_op jit(solution)/shard_map/ppermute | solution.py:1067
  33.5 173.0 %all-gather.11.cloned.1.call-start = ((), (), s32[]{:S(2)}) async-start(), calls=%async_computation.14 | async-start | bytes 13381632 | tf_op jit(solution)/shard_map/all_gather | solution.py:1136
  35.6 14.9 %collective-permute-start = (bf16[384,352]{0,1:T(8,128)(2,1)S(1)}, bf16[384,352]{0,1:T(8,128)(2,1)S(1)}, u32[]{:S(2)}, u32[]{:S(2)}) collective-permute-start(bf16[384,352]{0,1:T(8,128)(2,1)S(1)} %pad_maximum_fusion.18), channel_id=1, source_target_pairs={{0,8},{8,16},{16,24},{24,0},{1,9},{9,17},{17,25},{25,1},{2,10},{10... | collective-permute-start | bytes 811016 | tf_op jit(solution)/shard_map/ppermute | solution.py:1067
  41.9 20.2 %collective-permute-start.1 = (bf16[384,352]{0,1:T(8,128)(2,1)S(1)}, bf16[384,352]{0,1:T(8,128)(2,1)S(1)}, u32[]{:S(2)}, u32[]{:S(2)}) collective-permute-start(bf16[384,352]{0,1:T(8,128)(2,1)S(1)} %pad_maximum_fusion.18), channel_id=1, source_target_pairs={{0,16},{8,24},{16,0},{24,8},{1,17},{9,25},{17,1},{25,9},{2,18},{10... | collective-permute-start | bytes 811016 | tf_op jit(solution)/shard_map/ppermute | solution.py:1067
  43.5 18.6 %collective-permute-start.2 = (bf16[384,352]{0,1:T(8,128)(2,1)S(1)}, bf16[384,352]{0,1:T(8,128)(2,1)S(1)}, u32[]{:S(2)}, u32[]{:S(2)}) collective-permute-start(bf16[384,352]{0,1:T(8,128)(2,1)S(1)} %pad_maximum_fusion.18), channel_id=1, source_target_pairs={{0,24},{8,0},{16,8},{24,16},{1,25},{9,1},{17,9},{25,17},{2,26},{10... | collective-permute-start | bytes 811016 | tf_op jit(solution)/shard_map/ppermute | solution.py:1067
  44.4 49.3 %collective-permute-start.12 = (bf16[176,1056]{1,0:T(8,128)(2,1)S(1)}, bf16[176,1056]{1,0:T(8,128)(2,1)S(1)}, u32[]{:S(2)}, u32[]{:S(2)}) collective-permute-start(bf16[176,1056]{1,0:T(8,128)(2,1)S(1)} %copy-done.39), channel_id=1, source_target_pairs={{0,8},{8,16},{16,24},{24,0},{1,9},{9,17},{17,25},{25,1},{2,10},{10... | collective-permute-start | bytes 1115144 | tf_op jit(solution)/shard_map/ppermute | solution.py:1067
  45.6 48.2 %collective-permute-start.13 = (bf16[176,1056]{1,0:T(8,128)(2,1)S(1)}, bf16[176,1056]{1,0:T(8,128)(2,1)S(1)}, u32[]{:S(2)}, u32[]{:S(2)}) collective-permute-start(bf16[176,1056]{1,0:T(8,128)(2,1)S(1)} %copy-done.39), channel_id=1, source_target_pairs={{0,16},{8,24},{16,0},{24,8},{1,17},{9,25},{17,1},{25,9},{2,18},{10... | collective-permute-start | bytes 1115144 | tf_op jit(solution)/shard_map/ppermute | solution.py:1067
  50.5 43.2 %collective-permute-start.14 = (bf16[176,1056]{1,0:T(8,128)(2,1)S(1)}, bf16[176,1056]{1,0:T(8,128)(2,1)S(1)}, u32[]{:S(2)}, u32[]{:S(2)}) collective-permute-start(bf16[176,1056]{1,0:T(8,128)(2,1)S(1)} %copy-done.39), channel_id=1, source_target_pairs={{0,24},{8,0},{16,8},{24,16},{1,25},{9,1},{17,9},{25,17},{2,26},{10... | collective-permute-start | bytes 1115144 | tf_op jit(solution)/shard_map/ppermute | solution.py:1067
  99.4 337.2 %all-gather.13.cloned.1.call-start = ((), (), s32[]{:S(2)}) async-start(), calls=%async_computation.15 | async-start | bytes 13381632 | tf_op jit(solution)/shard_map/all_gather | solution.py:1136
  100.7 31.0 %collective-permute-start.15 = (bf16[176,1056]{1,0:T(8,128)(2,1)S(1)}, bf16[176,1056]{1,0:T(8,128)(2,1)S(1)}, u32[]{:S(2)}, u32[]{:S(2)}) collective-permute-start(bf16[176,1056]{1,0:T(8,128)(2,1)S(1)} %concatenate.112), channel_id=1, source_target_pairs={{0,8},{8,16},{16,24},{24,0},{1,9},{9,17},{17,25},{25,1},{2,10},{10... | collective-permute-start | bytes 1115144 | tf_op jit(solution)/shard_map/ppermute | solution.py:1067
  121.9 21.1 %collective-permute-start.16 = (bf16[176,1056]{1,0:T(8,128)(2,1)S(1)}, bf16[176,1056]{1,0:T(8,128)(2,1)S(1)}, u32[]{:S(2)}, u32[]{:S(2)}) collective-permute-start(bf16[176,1056]{1,0:T(8,128)(2,1)S(1)} %concatenate.112), channel_id=1, source_target_pairs={{0,16},{8,24},{16,0},{24,8},{1,17},{9,25},{17,1},{25,9},{2,18},{10... | collective-permute-start | bytes 1115144 | tf_op jit(solution)/shard_map/ppermute | solution.py:1067
  121.9 26.9 %collective-permute-start.17 = (bf16[176,1056]{1,0:T(8,128)(2,1)S(1)}, bf16[176,1056]{1,0:T(8,128)(2,1)S(1)}, u32[]{:S(2)}, u32[]{:S(2)}) collective-permute-start(bf16[176,1056]{1,0:T(8,128)(2,1)S(1)} %concatenate.112), channel_id=1, source_target_pairs={{0,24},{8,0},{16,8},{24,16},{1,25},{9,1},{17,9},{25,17},{2,26},{10... | collective-permute-start | bytes 1115144 | tf_op jit(solution)/shard_map/ppermute | solution.py:1067
  153.4 322.5 %all-gather.15.cloned.1.call-start = ((), (), s32[]{:S(2)}) async-start(), calls=%async_computation.16 | async-start | bytes 6488064 | tf_op jit(solution)/shard_map/all_gather | solution.py:1136
  169.2 13.7 collective-permute-start.11
  170.4 29.4 %collective-permute-start.18 = (bf16[128,704]{0,1:T(8,128)(2,1)S(1)}, bf16[128,704]{0,1:T(8,128)(2,1)S(1)}, u32[]{:S(2)}, u32[]{:S(2)}) collective-permute-start(bf16[128,704]{0,1:T(8,128)(2,1)S(1)} %copy-done.43), channel_id=1, source_target_pairs={{0,8},{8,16},{16,24},{24,0},{1,9},{9,17},{17,25},{25,1},{2,10},{10... | collective-permute-start | bytes 540680 | tf_op jit(solution)/shard_map/ppermute | solution.py:1067
  179.4 20.5 %collective-permute-start.19 = (bf16[128,704]{0,1:T(8,128)(2,1)S(1)}, bf16[128,704]{0,1:T(8,128)(2,1)S(1)}, u32[]{:S(2)}, u32[]{:S(2)}) collective-permute-start(bf16[128,704]{0,1:T(8,128)(2,1)S(1)} %copy-done.43), channel_id=1, source_target_pairs={{0,16},{8,24},{16,0},{24,8},{1,17},{9,25},{17,1},{25,9},{2,18},{10... | collective-permute-start | bytes 540680 | tf_op jit(solution)/shard_map/ppermute | solution.py:1067
  182.7 17.1 %collective-permute-start.20 = (bf16[128,704]{0,1:T(8,128)(2,1)S(1)}, bf16[128,704]{0,1:T(8,128)(2,1)}, u32[]{:S(2)}, u32[]{:S(2)}) collective-permute-start(bf16[128,704]{0,1:T(8,128)(2,1)S(1)} %copy-done.43), channel_id=1, source_target_pairs={{0,24},{8,0},{16,8},{24,16},{1,25},{9,1},{17,9},{25,17},{2,26},{10... | collective-permute-start | bytes 540680 | tf_op jit(solution)/shard_map/ppermute | solution.py:1067
  221.1 81.4 %all-to-all-start = ((bf16[8,3,2,88,512]{4,3,2,1,0:T(8,128)(2,1)}), bf16[8,3,2,88,512]{4,3,2,1,0:T(8,128)(2,1)}, u32[]{:S(2)}, u32[]{:S(2)}) async-start(bf16[8,3,2,88,512]{4,3,2,1,0:T(8,128)(2,1)} %get-tuple-element.104.own_ref), calls=%async_computation | async-start | bytes 8650752 | tf_op jit(solution)/shard_map/all_to_all | solution.py:1057
  226.0 296.9 %all-gather.17.cloned.1.call-start = ((), (), s32[]{:S(2)}) async-start(), calls=%async_computation.17 | async-start | bytes 19464192 | tf_op jit(solution)/shard_map/all_gather | solution.py:1136
  226.0 17.1 %collective-permute-start.21 = (bf16[176,1536]{1,0:T(8,128)(2,1)S(1)}, bf16[176,1536]{1,0:T(8,128)(2,1)S(1)}, u32[]{:S(2)}, u32[]{:S(2)}) collective-permute-start(bf16[176,1536]{1,0:T(8,128)(2,1)S(1)} %copy-done.35), channel_id=1, source_target_pairs={{0,8},{8,16},{16,24},{24,0},{1,9},{9,17},{17,25},{25,1},{2,10},{10... | collective-permute-start | bytes 1622024 | tf_op jit(solution)/shard_map/ppermute | solution.py:1067
  228.0 37.7 %collective-permute-start.22 = (bf16[176,1536]{1,0:T(8,128)(2,1)S(1)}, bf16[176,1536]{1,0:T(8,128)(2,1)S(1)}, u32[]{:S(2)}, u32[]{:S(2)}) collective-permute-start(bf16[176,1536]{1,0:T(8,128)(2,1)S(1)} %copy-done.35), channel_id=1, source_target_pairs={{0,16},{8,24},{16,0},{24,8},{1,17},{9,25},{17,1},{25,9},{2,18},{10... | collective-permute-start | bytes 1622024 | tf_op jit(solution)/shard_map/ppermute | solution.py:1067
  228.7 37.0 %collective-permute-start.23 = (bf16[176,1536]{1,0:T(8,128)(2,1)S(1)}, bf16[176,1536]{1,0:T(8,128)(2,1)S(1)}, u32[]{:S(2)}, u32[]{:S(2)}) collective-permute-start(bf16[176,1536]{1,0:T(8,128)(2,1)S(1)} %copy-done.35), channel_id=1, source_target_pairs={{0,24},{8,0},{16,8},{24,16},{1,25},{9,1},{17,9},{25,17},{2,26},{10... | collective-permute-start | bytes 1622024 | tf_op jit(solution)/shard_map/ppermute | solution.py:1067
  319.3 69.7 %all-to-all-start.2 = ((bf16[8,3,2,88,512]{4,3,2,1,0:T(8,128)(2,1)}), bf16[8,3,2,88,512]{4,3,2,1,0:T(8,128)(2,1)}, u32[]{:S(2)}, u32[]{:S(2)}) async-start(bf16[8,3,2,88,512]{4,3,2,1,0:T(8,128)(2,1)} %get-tuple-element.106.own_ref), calls=%async_computation.2 | async-start | bytes 8650752 | tf_op jit(solution)/shard_map/all_to_all | solution.py:1057
  389.0 38.1 %all-to-all-start.1 = ((bf16[8,2,88,512]{3,2,1,0:T(8,128)(2,1)}), bf16[8,2,88,512]{3,2,1,0:T(8,128)(2,1)S(1)}, u32[]{:S(2)}, u32[]{:S(2)}) async-start(bf16[8,2,88,512]{3,2,1,0:T(8,128)(2,1)} %get-tuple-element.105.att_ref), calls=%async_computation.1 | async-start | bytes 2883584 | tf_op jit(solution)/shard_map/all_to_all | solution.py:1057
  427.1 31.0 %all-to-all-start.3 = ((bf16[8,2,88,512]{3,2,1,0:T(8,128)(2,1)}), bf16[8,2,88,512]{3,2,1,0:T(8,128)(2,1)S(1)}, u32[]{:S(2)}, u32[]{:S(2)}) async-start(bf16[8,2,88,512]{3,2,1,0:T(8,128)(2,1)} %get-tuple-element.107.att_ref), calls=%async_computation.3 | async-start | bytes 2883584 | tf_op jit(solution)/shard_map/all_to_all | solution.py:1057
  431.2 161.2 %all-gather.19.cloned.1.call-start = ((), (), s32[]{:S(2)}) async-start(), calls=%async_computation.18 | async-start | bytes 19464192 | tf_op jit(solution)/shard_map/all_gather | solution.py:1136
  431.2 37.3 %collective-permute-start.24 = (bf16[768,352]{0,1:T(8,128)(2,1)S(1)}, bf16[768,352]{0,1:T(8,128)(2,1)}, u32[]{:S(2)}, u32[]{:S(2)}) collective-permute-start(bf16[768,352]{0,1:T(8,128)(2,1)S(1)} %copy-done.36), channel_id=1, source_target_pairs={{0,8},{8,16},{16,24},{24,0},{1,9},{9,17},{17,25},{25,1},{2,10},{10... | collective-permute-start | bytes 1622024 | tf_op jit(solution)/shard_map/ppermute | solution.py:1067
  432.8 38.3 %collective-permute-start.25 = (bf16[768,352]{0,1:T(8,128)(2,1)S(1)}, bf16[768,352]{0,1:T(8,128)(2,1)}, u32[]{:S(2)}, u32[]{:S(2)}) collective-permute-start(bf16[768,352]{0,1:T(8,128)(2,1)S(1)} %copy-done.36), channel_id=1, source_target_pairs={{0,16},{8,24},{16,0},{24,8},{1,17},{9,25},{17,1},{25,9},{2,18},{10... | collective-permute-start | bytes 1622024 | tf_op jit(solution)/shard_map/ppermute | solution.py:1067
  435.2 35.9 %collective-permute-start.26 = (bf16[768,352]{0,1:T(8,128)(2,1)S(1)}, bf16[768,352]{0,1:T(8,128)(2,1)}, u32[]{:S(2)}, u32[]{:S(2)}) collective-permute-start(bf16[768,352]{0,1:T(8,128)(2,1)S(1)} %copy-done.36), channel_id=1, source_target_pairs={{0,24},{8,0},{16,8},{24,16},{1,25},{9,1},{17,9},{25,17},{2,26},{10... | collective-permute-start | bytes 1622024 | tf_op jit(solution)/shard_map/ppermute | solution.py:1067
  474.3 314.4 %reduce-scatter.6.cloned.1.call-start = ((), (), s32[]{:S(2)}) async-start(), calls=%async_computation.19 | async-start | bytes 19464192 | tf_op jit(solution)/shard_map/reduce_scatter | solution.py:1131
  659.4 409.7 %reduce-scatter.8.cloned.1.call-start = ((), (), s32[]{:S(2)}) async-start(), calls=%async_computation.20 | async-start | bytes 19464192 | tf_op jit(solution)/shard_map/reduce_scatter | solution.py:1131
  816.0 38.8 %all-to-all-start.4 = ((bf16[8,2,88,512]{3,2,1,0:T(8,128)(2,1)}), bf16[8,2,88,512]{3,2,1,0:T(8,128)(2,1)}, u32[]{:S(2)}, u32[]{:S(2)}) async-start(bf16[8,2,88,512]{3,2,1,0:T(8,128)(2,1)} %bitcast.199), calls=%async_computation.6 | async-start | bytes 2883584 | tf_op jit(solution)/shard_map/all_to_all | solution.py:1057
  820.4 354.9 %reduce-scatter.10.cloned.1.call-start = ((), (), s32[]{:S(2)}) async-start(), calls=%async_computation.21 | async-start | bytes 18247680 | tf_op jit(solution)/shard_map/reduce_scatter | solution.py:1131
  856.6 106.9 %collective-permute-start.27 = (bf16[768,352]{0,1:T(8,128)(2,1)}, bf16[768,352]{0,1:T(8,128)(2,1)S(1)}, u32[]{:S(2)}, u32[]{:S(2)}) collective-permute-start(bf16[768,352]{0,1:T(8,128)(2,1)} %copy.133), channel_id=1, source_target_pairs={{0,8},{8,16},{16,24},{24,0},{1,9},{9,17},{17,25},{25,1},{2,10},{10... | collective-permute-start | bytes 1622024 | tf_op jit(solution)/shard_map/ppermute | solution.py:1087
  858.7 104.8 %collective-permute-start.29 = (bf16[768,352]{0,1:T(8,128)(2,1)}, bf16[768,352]{0,1:T(8,128)(2,1)}, u32[]{:S(2)}, u32[]{:S(2)}) collective-permute-start(bf16[768,352]{0,1:T(8,128)(2,1)} %copy.135), channel_id=1, source_target_pairs={{0,24},{8,0},{16,8},{24,16},{1,25},{9,1},{17,9},{25,17},{2,26},{10... | collective-permute-start | bytes 1622024 | tf_op jit(solution)/shard_map/ppermute | solution.py:1087
  863.5 100.0 %collective-permute-start.28 = (bf16[768,352]{0,1:T(8,128)(2,1)}, bf16[768,352]{0,1:T(8,128)(2,1)}, u32[]{:S(2)}, u32[]{:S(2)}) collective-permute-start(bf16[768,352]{0,1:T(8,128)(2,1)} %copy.134), channel_id=1, source_target_pairs={{0,16},{8,24},{16,0},{24,8},{1,17},{9,25},{17,1},{25,9},{2,18},{10... | collective-permute-start | bytes 1622024 | tf_op jit(solution)/shard_map/ppermute | solution.py:1087
  870.0 100.5 %all-to-all-start.5 = ((bf16[8,2,88,512]{3,2,1,0:T(8,128)(2,1)}), bf16[8,2,88,512]{3,2,1,0:T(8,128)(2,1)}, u32[]{:S(2)}, u32[]{:S(2)}) async-start(bf16[8,2,88,512]{3,2,1,0:T(8,128)(2,1)} %bitcast.198), calls=%async_computation.7 | async-start | bytes 2883584 | tf_op jit(solution)/shard_map/all_to_all | solution.py:1057
  970.5 93.9 %all-to-all-start.7 = ((bf16[8,3,2,88,512]{4,3,2,1,0:T(8,128)(2,1)}), bf16[8,3,2,88,512]{4,3,2,1,0:T(8,128)(2,1)}, u32[]{:S(2)}, u32[]{:S(2)}) async-start(bf16[8,3,2,88,512]{4,3,2,1,0:T(8,128)(2,1)} %shard_map.321), calls=%async_computation.9 | async-start | bytes 8650752 | tf_op jit(solution)/shard_map/all_to_all | solution.py:1057
  1064.5 75.9 %all-to-all-start.6 = ((bf16[8,3,2,88,512]{4,3,2,1,0:T(8,128)(2,1)}), bf16[8,3,2,88,512]{4,3,2,1,0:T(8,128)(2,1)}, u32[]{:S(2)}, u32[]{:S(2)}) async-start(bf16[8,3,2,88,512]{4,3,2,1,0:T(8,128)(2,1)} %shard_map.322), calls=%async_computation.8 | async-start | bytes 8650752 | tf_op jit(solution)/shard_map/all_to_all | solution.py:1057
  1069.0 195.3 %reduce-scatter.12.cloned.1.call-start = ((), (), s32[]{:S(2)}) async-start(), calls=%async_computation.23 | async-start | bytes 13381632 | tf_op jit(solution)/shard_map/reduce_scatter | solution.py:1131
  1071.5 17.0 %collective-permute-start.30 = (bf16[176,1536]{1,0:T(8,128)(2,1)S(1)}, bf16[176,1536]{1,0:T(8,128)(2,1)S(1)}, u32[]{:S(2)}, u32[]{:S(2)}) collective-permute-start(bf16[176,1536]{1,0:T(8,128)(2,1)S(1)} %get-tuple-element.291), channel_id=1, source_target_pairs={{0,8},{8,16},{16,24},{24,0},{1,9},{9,17},{17,25},{25,1},{2,10},{10... | collective-permute-start | bytes 1622024 | tf_op jit(solution)/shard_map/ppermute | solution.py:1087
  1074.5 25.0 %collective-permute-start.32 = (bf16[176,1536]{1,0:T(8,128)(2,1)S(1)}, bf16[176,1536]{1,0:T(8,128)(2,1)S(1)}, u32[]{:S(2)}, u32[]{:S(2)}) collective-permute-start(bf16[176,1536]{1,0:T(8,128)(2,1)S(1)} %get-tuple-element.290), channel_id=1, source_target_pairs={{0,24},{8,0},{16,8},{24,16},{1,25},{9,1},{17,9},{25,17},{2,26},{10... | collective-permute-start | bytes 1622024 | tf_op jit(solution)/shard_map/ppermute | solution.py:1087
  1077.1 45.6 %collective-permute-start.31 = (bf16[176,1536]{1,0:T(8,128)(2,1)S(1)}, bf16[176,1536]{1,0:T(8,128)(2,1)S(1)}, u32[]{:S(2)}, u32[]{:S(2)}) collective-permute-start(bf16[176,1536]{1,0:T(8,128)(2,1)S(1)} %select_select_fusion.4), channel_id=1, source_target_pairs={{0,16},{8,24},{16,0},{24,8},{1,17},{9,25},{17,1},{25,9},{2,18},{10... | collective-permute-start | bytes 1622024 | tf_op jit(solution)/shard_map/ppermute | solution.py:1087
  1170.6 158.9 %all-gather.21.cloned.1.call-start = ((), (), s32[]{:S(2)}) async-start(), calls=%async_computation.22 | async-start | bytes 4866048 | tf_op jit(solution)/shard_map/all_gather | solution.py:1136
  1180.1 214.5 %reduce-scatter.14.cloned.1.call-start = ((), (), s32[]{:S(2)}) async-start(), calls=%async_computation.24 | async-start | bytes 8921088 | tf_op jit(solution)/shard_map/reduce_scatter | solution.py:1131
  1235.1 29.3 %collective-permute-start.33 = (bf16[176,1056]{1,0:T(8,128)(2,1)}, bf16[176,1056]{1,0:T(8,128)(2,1)S(1)}, u32[]{:S(2)}, u32[]{:S(2)}) collective-permute-start(bf16[176,1056]{1,0:T(8,128)(2,1)} %get-tuple-element.316), channel_id=1, source_target_pairs={{0,8},{8,16},{16,24},{24,0},{1,9},{9,17},{17,25},{25,1},{2,10},{10... | collective-permute-start | bytes 1115144 | tf_op jit(solution)/shard_map/ppermute | solution.py:1087
  1236.7 29.4 %collective-permute-start.34 = (bf16[176,1056]{1,0:T(8,128)(2,1)}, bf16[176,1056]{1,0:T(8,128)(2,1)S(1)}, u32[]{:S(2)}, u32[]{:S(2)}) collective-permute-start(bf16[176,1056]{1,0:T(8,128)(2,1)} %get-tuple-element.315), channel_id=1, source_target_pairs={{0,16},{8,24},{16,0},{24,8},{1,17},{9,25},{17,1},{25,9},{2,18},{10... | collective-permute-start | bytes 1115144 | tf_op jit(solution)/shard_map/ppermute | solution.py:1087
  1237.7 28.4 %collective-permute-start.35 = (bf16[176,1056]{1,0:T(8,128)(2,1)S(1)}, bf16[176,1056]{1,0:T(8,128)(2,1)}, u32[]{:S(2)}, u32[]{:S(2)}) collective-permute-start(bf16[176,1056]{1,0:T(8,128)(2,1)S(1)} %get-tuple-element.314), channel_id=1, source_target_pairs={{0,24},{8,0},{16,8},{24,16},{1,25},{9,1},{17,9},{25,17},{2,26},{10... | collective-permute-start | bytes 1115144 | tf_op jit(solution)/shard_map/ppermute | solution.py:1087
  1278.2 7.0 collective-permute-start.46
  1289.7 6.0 collective-permute-start.48
  1303.9 5.9 collective-permute-start.36
  1310.9 12.1 collective-permute-start.37
  1312.1 23.9 %collective-permute-start.42 = (bf16[176,1056]{1,0:T(8,128)(2,1)}, bf16[176,1056]{1,0:T(8,128)(2,1)}, u32[]{:S(2)}, u32[]{:S(2)}) collective-permute-start(bf16[176,1056]{1,0:T(8,128)(2,1)} %get-tuple-element.326), channel_id=1, source_target_pairs={{0,8},{8,16},{16,24},{24,0},{1,9},{9,17},{17,25},{25,1},{2,10},{10... | collective-permute-start | bytes 1115144 | tf_op jit(solution)/shard_map/ppermute | solution.py:1087
  1321.3 19.8 %collective-permute-start.44 = (bf16[176,1056]{1,0:T(8,128)(2,1)}, bf16[176,1056]{1,0:T(8,128)(2,1)}, u32[]{:S(2)}, u32[]{:S(2)}) collective-permute-start(bf16[176,1056]{1,0:T(8,128)(2,1)} %get-tuple-element.325), channel_id=1, source_target_pairs={{0,24},{8,0},{16,8},{24,16},{1,25},{9,1},{17,9},{25,17},{2,26},{10... | collective-permute-start | bytes 1115144 | tf_op jit(solution)/shard_map/ppermute | solution.py:1087
  1322.3 36.2 %collective-permute-start.43 = (bf16[176,1056]{1,0:T(8,128)(2,1)}, bf16[176,1056]{1,0:T(8,128)(2,1)}, u32[]{:S(2)}, u32[]{:S(2)}) collective-permute-start(bf16[176,1056]{1,0:T(8,128)(2,1)} %select_select_fusion.15), channel_id=1, source_target_pairs={{0,16},{8,24},{16,0},{24,8},{1,17},{9,25},{17,1},{25,9},{2,18},{10... | collective-permute-start | bytes 1115144 | tf_op jit(solution)/shard_map/ppermute | solution.py:1087
  1365.1 14.5 %collective-permute-start.51 = (bf16[464,352]{1,0:T(8,128)(2,1)}, bf16[464,352]{1,0:T(8,128)(2,1)S(1)}, u32[]{:S(2)}, u32[]{:S(2)}) collective-permute-start(bf16[464,352]{1,0:T(8,128)(2,1)} %get-tuple-element.327), channel_id=1, source_target_pairs={{0,8},{8,16},{16,24},{24,0},{1,9},{9,17},{17,25},{25,1},{2,10},{10... | collective-permute-start | bytes 979976 | tf_op jit(solution)/shard_map/ppermute | solution.py:1087
  1365.1 27.6 %collective-permute-start.52 = (bf16[464,352]{1,0:T(8,128)(2,1)}, bf16[464,352]{1,0:T(8,128)(2,1)S(1)}, u32[]{:S(2)}, u32[]{:S(2)}) collective-permute-start(bf16[464,352]{1,0:T(8,128)(2,1)} %get-tuple-element.329), channel_id=1, source_target_pairs={{0,16},{8,24},{16,0},{24,8},{1,17},{9,25},{17,1},{25,9},{2,18},{10... | collective-permute-start | bytes 979976 | tf_op jit(solution)/shard_map/ppermute | solution.py:1087
  1367.4 25.4 %collective-permute-start.53 = (bf16[464,352]{1,0:T(8,128)(2,1)}, bf16[464,352]{1,0:T(8,128)(2,1)S(1)}, u32[]{:S(2)}, u32[]{:S(2)}) collective-permute-start(bf16[464,352]{1,0:T(8,128)(2,1)} %get-tuple-element.328), channel_id=1, source_target_pairs={{0,24},{8,0},{16,8},{24,16},{1,25},{9,1},{17,9},{25,17},{2,26},{10... | collective-permute-start | bytes 979976 | tf_op jit(solution)/shard_map/ppermute | solution.py:1087
  1396.8 14.4 %collective-permute-start.39 = (bf16[360,352]{1,0:T(8,128)(2,1)S(1)}, bf16[360,352]{1,0:T(8,128)(2,1)S(1)}, u32[]{:S(2)}, u32[]{:S(2)}) collective-permute-start(bf16[360,352]{1,0:T(8,128)(2,1)S(1)} %select_select_fusion.33), channel_id=1, source_target_pairs={{0,8},{8,16},{16,24},{24,0},{1,9},{9,17},{17,25},{25,1},{2,10},{10... | collective-permute-start | bytes 760328 | tf_op jit(solution)/shard_map/ppermute | solution.py:1087
  1404.2 17.0 %collective-permute-start.40 = (bf16[360,352]{1,0:T(8,128)(2,1)S(1)}, bf16[360,352]{1,0:T(8,128)(2,1)S(1)}, u32[]{:S(2)}, u32[]{:S(2)}) collective-permute-start(bf16[360,352]{1,0:T(8,128)(2,1)S(1)} %select_select_fusion.32), channel_id=1, source_target_pairs={{0,16},{8,24},{16,0},{24,8},{1,17},{9,25},{17,1},{25,9},{2,18},{10... | collective-permute-start | bytes 760328 | tf_op jit(solution)/shard_map/ppermute | solution.py:1087
  1404.2 17.2 %collective-permute-start.41 = (bf16[360,352]{1,0:T(8,128)(2,1)S(1)}, bf16[360,352]{1,0:T(8,128)(2,1)S(1)}, u32[]{:S(2)}, u32[]{:S(2)}) collective-permute-start(bf16[360,352]{1,0:T(8,128)(2,1)S(1)} %select_select_fusion.31), channel_id=1, source_target_pairs={{0,24},{8,0},{16,8},{24,16},{1,25},{9,1},{17,9},{25,17},{2,26},{10... | collective-permute-start | bytes 760328 | tf_op jit(solution)/shard_map/ppermute | solution.py:1087
  (106 other events, 1303.0 us)
Sparse Core Ops, SparseCore 0:
  33.6 59.1 all-gather.8
  99.5 87.6 all-gather.10
  189.1 115.5 all-gather.12
  307.0 77.9 all-gather.14
  386.7 112.0 all-gather.16
  500.6 91.7 all-gather.18
  659.5 118.5 reduce-scatter.5
  782.2 148.9 reduce-scatter.7
  934.9 205.3 reduce-scatter.9
  1170.7 88.8 reduce-scatter.11
  1262.0 37.4 all-gather.20
  1303.0 68.9 reduce-scatter.13

commit v7 on v6

--- a/solution.py
+++ b/solution.py
@@ -1418,12 +1418,25 @@
     part_shift = jnp.sum(grad_first.reshape(images, tile_len, model_width), axis=1)
     grad_one = grad_two + norm_back(grad_first * norm_f[:, 0], first_z, first_inv)
 
+    shift_low = total_tiles(part_shift).astype(BF16)
+    d_shift = left_dot(act_cols, shift_low).astype(BF16)
+    grad_time_act = total_tiles(
+        lax.dynamic_update_slice_in_dim(
+            jnp.zeros_like(time_pre), right_dot(shift_low, part_shift_w), grid_at * shift_slice, 1
+        )
+    )
+    grad_time_pre = silu_pull(grad_time_act)[0].astype(BF16)
+    d_time = left_dot(embed_cols, grad_time_pre).astype(BF16)
     low_one = grad_one.astype(BF16)
     d_skip_w = left_dot(skip_in, low_one).astype(BF16)
     d_skip_w, low_one = lax.optimization_barrier((d_skip_w, low_one))
-    skip_grad, grad_patch, skip_sums = join_back(low_one, f_skip, joined, joined_inv, gain_skip)
-    t_qkv, d_skip_w, joint_grad, skip_sums = lax.optimization_barrier(
-        (t_qkv, d_skip_w, joint_grad, skip_sums)
+    t_qkv, d_skip_w, joint_grad, low_join, d_time, d_shift = lax.optimization_barrier(
+        (t_qkv, d_skip_w, joint_grad, low_one, d_time, d_shift)
+    )
+    skip_grad, grad_patch, skip_sums = join_back(low_join, f_skip, joined, joined_inv, gain_skip)
+    qkv_grad = narrow(t_qkv, skip_sums)
+    qkv_grad, grad_kv, grad_patch, skip_grad, skip_sums = lax.optimization_barrier(
+        (qkv_grad, grad_kv, grad_patch, skip_grad, skip_sums)
     )
     out_grad, query_w_grad, cross_grad = jnp.split(joint_grad, 3, axis=1)
     t_skip = over_tiles(d_skip_w)
@@ -1438,15 +1451,6 @@
     text_grad = dot_over(grad_kv, grouped_text, 0, 1).reshape(images, text_pad, text_slice)
     text_grad = text_grad[:, :text_len]
 
-    shift_low = total_tiles(part_shift).astype(BF16)
-    d_shift = left_dot(act_cols, shift_low).astype(BF16)
-    grad_time_act = total_tiles(
-        lax.dynamic_update_slice_in_dim(
-            jnp.zeros_like(time_pre), right_dot(shift_low, part_shift_w), grid_at * shift_slice, 1
-        )
-    )
-    grad_time_pre = silu_pull(grad_time_act)[0].astype(BF16)
-    d_time = left_dot(embed_cols, grad_time_pre).astype(BF16)
     late, width = [], w_shift.shape[1]
     for at in range(dp_devices):
         pair = d_text[:, 2 * at * width : 2 * (at + 1) * width]
@@ -1454,13 +1458,7 @@
         late.append(
             jnp.concatenate([pair[:, :width], pair[:, width:], d_time[:, own], d_shift[:, own]])
         )
-    qkv_grad = narrow(t_qkv, d_text)
-    qkv_grad, *late = lax.optimization_barrier((qkv_grad, *late))
-    late = narrow_blocks(late)
-    rows = d_text.shape[0]
-    text_w_grad = jnp.concatenate([late[:rows], late[rows : 2 * rows]], axis=1)
-    time_w_grad, shift_w_grad = jnp.split(late[2 * rows :], [d_time.shape[0]], axis=0)
-
+    late_blocks = late
     skip_grad = skip_grad.reshape(images, rows_tile, cols_tile, model_width)
     gain_skips, bias_skips = skip_sums[0], skip_sums[1]
     d_patch = left_dot(grad_patch, patch_rows)
@@ -1490,6 +1488,10 @@
         axis=2,
     )
     small_grads = sum_tiles(small_grads.reshape(model_width, -1))
+    late = narrow_blocks(late_blocks, small_grads)
+    rows = d_text.shape[0]
+    text_w_grad = jnp.concatenate([late[:rows], late[rows : 2 * rows]], axis=1)
+    time_w_grad, shift_w_grad = jnp.split(late[2 * rows :], [d_time.shape[0]], axis=0)
     last, small_rows, small_width = [], small_grads.shape[0], sum(small_widths)
     for at in range(dp_devices):
         few = small_grads[:, at * small_width : (at + 1) * small_width].astype(BF16).reshape(-1)

time: 1450 us -> 1440 us (level)
  transfers between devices with their start and end apart: 74 -> 74, of which waited for: 37 -> 35; matrix products, arithmetic and copies ran while one was open for 32% -> 31% of each run, Pallas kernels for 26% -> 26%
where the time goes in v7:
time: 1440 us; the launch traced here: 1420 us
  matrix products  384 us (27%)
  Pallas kernels  368 us (26%)
  waiting for transfers between devices  333 us (23%)
  starting transfers between devices  152 us (11%)
  local copies, waits for them, and re-layouts  78.7 us (5%)
  other arithmetic  74.4 us (5%)
  blocking collectives  17.7 us (1%)
  between operations  16.5 us (1%)
    pallas_call x2, Pallas kernels, attend_back(): kernel_call(functools.partial(attend_back_body, score_scale), 2560 * head...  178 us
    dot_general x11, matrix products, dot_over(): lax.dot_general(left_mat, right_mat, (((left_axis,), (right_axis,)), ((),...  121 us
    dot_general x9, matrix products, plain_dot(): return jnp.dot(left_mat, right_mat, preferred_element_type=jnp.float32)  105 us
    all_to_all x8, waiting for transfers between devices, swap_tiles(): lax.all_to_all(values_in, TILE, split_axis=0, concat_axis=0, tiled=True)  100 us
    dot_general x9, matrix products, left_dot(): lax.dot_general(left_mat, right_mat, (((0,), (0,)), ((), ())), preferred_...  92.9 us
    ppermute x18, waiting for transfers between devices, narrow_blocks(): received.append(lax.ppermute(sent, 'dp', shift_pairs(devices, step)))  92.2 us
    ppermute x21, waiting for transfers between devices, fetch(): lax.ppermute(weight, 'dp', shift_pairs(devices, step))  89.6 us
    pallas_call x2, Pallas kernels, attend(): kernel_call(attend_body, 1024 * heads * tiles ** 2 * tile_len ** 2, 8 * q...  68.5 us
  transfers between devices with their start and end apart: 74, of which 35 were waited for; matrix products, arithmetic and copies ran while one was open for 31% of the time, Pallas kernels for 26%

profile of v7, /device:TPU:0, one launch (start us, length us, event | category | flops | bytes accessed | tf_op | source)
XLA Modules:
  0.0 1423.4 jit_solution(14156675971052734183)
XLA Ops:
  14.3 5.7 collective-permute-done.3
  20.1 10.8 collective-permute-done.4
  35.6 6.3 collective-permute-start
  53.7 8.5 collective-permute-done.1
  62.9 17.7 %all-gather = bf16[8,176,60]{1,2,0:T(8,128)(2,1)S(1)} all-gather(bf16[1,176,60]{1,2,0:T(8,128)(2,1)S(1)} %reshape.660), channel_id=1, replica_groups=mesh['dp'=4,'row'=4,'col'=2] {'row','col'}, dimensions={0}, use_global_device_ids=true | all-gather | bytes 190080 | tf_op jit(solution)/shard_map/all_gather | solution.py:1136
  84.1 9.6 shard_map.314
  100.7 21.2 %collective-permute-start.15 = (bf16[176,1056]{1,0:T(8,128)(2,1)S(1)}, bf16[176,1056]{1,0:T(8,128)(2,1)S(1)}, u32[]{:S(2)}, u32[]{:S(2)}) collective-permute-start(bf16[176,1056]{1,0:T(8,128)(2,1)S(1)} %concatenate.112), channel_id=1, source_target_pairs={{0,8},{8,16},{16,24},{24,0},{1,9},{9,17},{17,25},{25,1},{2,10},{10... | collective-permute-start | bytes 1115144 | tf_op jit(solution)/shard_map/ppermute | solution.py:1067
  124.4 7.3 collective-permute-done.15
  131.7 11.3 collective-permute-done.16
  143.0 5.8 collective-permute-done.17
  170.4 8.9 collective-permute-start.18
  183.0 14.3 %fusion.109 = (f32[1024]{0:T(1024)S(1)}, f32[1024,1408]{1,0:T(8,128)S(1)}) fusion(bf16[1024,2816]{1,0:T(8,128)(2,1)} %get-tuple-element.104, bf16[2816,1408]{1,0:T(8,128)(2,1)} %all-gather.9.cloned.1.call-done.weight_ref), kind=kOutput, calls=%fused_computation.317 | convolution fusion | flops 8121613312 | bytes 19468288 | tf_op jit(solution)/shard_map/dot_general | solution.py:72
  206.4 14.7 %shard_map.315 = (bf16[8,3,2,88,512]{4,3,2,1,0:T(8,128)(2,1)}, f32[8,3,2,512]{3,2,1,0:T(2,128)}) custom-call(bf16[512,1408]{1,0:T(8,128)(2,1)} %get-tuple-element.298.rows_ref, bf16[1408,4224]{1,0:T(8,128)(2,1)} %all-gather.11.cloned.1.call-done.weight_ref, f32[88,512]{1,0:T(8,128)} %pad_maximum_fusion.19.cos_ref, f32[88,512]{1,0:T(8,128)} %pad_maximum_fusion.20.sin_ref, ...), custom_call_target="tpu_custom_call" | custom-call | flops 6090129408 | bytes 11894784 | tf_op jit(solution)/shard_map/pallas_call | solution.py:652
  221.1 4.9 all-to-all-start
  230.8 12.3 collective-permute-done.21
  243.1 22.6 %collective-permute-done.22 = bf16[176,1536]{1,0:T(8,128)(2,1)S(1)} collective-permute-done((bf16[176,1536]{1,0:T(8,128)(2,1)S(1)}, bf16[176,1536]{1,0:T(8,128)(2,1)S(1)}, u32[]{:S(2)}, u32[]{:S(2)}) %collective-permute-start.22) | collective-permute-done | bytes 540704 | tf_op jit(solution)/shard_map/ppermute | solution.py:1067
  265.7 36.8 %all-to-all-done.query_ref.key_ref.value_ref = bf16[8,3,2,88,512]{4,3,2,1,0:T(8,128)(2,1)} async-done(((bf16[8,3,2,88,512]{4,3,2,1,0:T(8,128)(2,1)}), bf16[8,3,2,88,512]{4,3,2,1,0:T(8,128)(2,1)}, u32[]{:S(2)}, u32[]{:S(2)}) %all-to-all-start) | async-done | bytes 4325408 | tf_op jit(solution)/shard_map/all_to_all | solution.py:1057
  304.6 14.7 %shard_map.317 = (bf16[8,3,2,88,512]{4,3,2,1,0:T(8,128)(2,1)}, f32[8,3,2,512]{3,2,1,0:T(2,128)}) custom-call(bf16[512,1408]{1,0:T(8,128)(2,1)} %get-tuple-element.299.rows_ref, bf16[1408,4224]{1,0:T(8,128)(2,1)} %all-gather.11.cloned.1.call-done.weight_ref, f32[88,512]{1,0:T(8,128)} %pad_maximum_fusion.19.cos_ref, f32[88,512]{1,0:T(8,128)} %pad_maximum_fusion.20.sin_ref, ...), custom_call_target="tpu_custom_call" | custom-call | flops 6090129408 | bytes 11894784 | tf_op jit(solution)/shard_map/pallas_call | solution.py:652
  324.7 34.0 %shard_map.316 = (bf16[8,2,88,512]{3,2,1,0:T(8,128)(2,1)}, f32[8,2,1,512]{3,2,1,0:T(1,128)}) custom-call(bf16[8,3,2,88,512]{4,3,2,1,0:T(8,128)(2,1)} %all-to-all-done.query_ref.key_ref.value_ref, bf16[8,3,2,88,512]{4,3,2,1,0:T(8,128)(2,1)} %all-to-all-done.query_ref.key_ref.value_ref, bf16[8,3,2,88,512]{4,3,2,1,0:T(8,128)(2,1)} %all-to-all-done.query_ref.key_ref.value_ref, ...), custom_call_target="tpu_custom_call" | custom-call | flops 34359738368 | bytes 17301504 | tf_op jit(solution)/shard_map/pallas_call | solution.py:757
  358.8 30.2 %all-to-all-done.2.query_ref.key_ref.value_ref = bf16[8,3,2,88,512]{4,3,2,1,0:T(8,128)(2,1)} async-done(((bf16[8,3,2,88,512]{4,3,2,1,0:T(8,128)(2,1)}), bf16[8,3,2,88,512]{4,3,2,1,0:T(8,128)(2,1)}, u32[]{:S(2)}, u32[]{:S(2)}) %all-to-all-start.2) | async-done | bytes 4325408 | tf_op jit(solution)/shard_map/all_to_all | solution.py:1057
  392.6 34.5 %shard_map.318 = (bf16[8,2,88,512]{3,2,1,0:T(8,128)(2,1)}, f32[8,2,1,512]{3,2,1,0:T(1,128)}) custom-call(bf16[8,3,2,88,512]{4,3,2,1,0:T(8,128)(2,1)} %all-to-all-done.2.query_ref.key_ref.value_ref, bf16[8,3,2,88,512]{4,3,2,1,0:T(8,128)(2,1)} %all-to-all-done.2.query_ref.key_ref.value_ref, ...), custom_call_target="tpu_custom_call" | custom-call | flops 34359738368 | bytes 17301504 | tf_op jit(solution)/shard_map/pallas_call | solution.py:757
  436.6 21.4 %all-to-all-done.3 = bf16[8,2,88,512]{3,2,1,0:T(8,128)(2,1)S(1)} async-done(((bf16[8,2,88,512]{3,2,1,0:T(8,128)(2,1)}), bf16[8,2,88,512]{3,2,1,0:T(8,128)(2,1)S(1)}, u32[]{:S(2)}, u32[]{:S(2)}) %all-to-all-start.3) | async-done | bytes 1441824 | tf_op jit(solution)/shard_map/all_to_all | solution.py:1057
  458.0 10.5 fusion.110
  475.9 9.8 fusion.113
  486.4 9.3 fusion.10
  495.8 14.5 %shard_map.319 = (bf16[16,88,1024]{2,1,0:T(8,128)(2,1)}, bf16[16,88,1024]{2,1,0:T(8,128)(2,1)}, f32[16,1,1024]{2,1,0:T(1,128)}, f32[16,1,1024]{2,1,0:T(1,128)}) custom-call(f32[16,88,1024]{2,1,0:T(8,128)} %bitcast.210, f32[2,16,88,768]{3,2,1,0:T(8,128)} %bitcast.187), custom_call_target="tpu_custom_call" | custom-call | flops 6442450944 | bytes 11534336 | tf_op jit(solution)/shard_map/pallas_call | solution.py:897
  510.3 9.2 fusion.111
  522.9 39.8 %add_convert_fusion = (bf16[1024,6144]{1,0:T(8,128)(2,1)}, bf16[1024,6144]{1,0:T(8,128)(2,1)}) fusion(bf16[1408,6144]{1,0:T(8,128)(2,1)} %all-gather.17.cloned.1.call-done, f32[1024,1408]{1,0:T(8,128)} %copy-done.2, f32[1408]{0:T(1024)S(1)} %copy-done.79, f32[1408]{0:T(1024)S(1)} %copy-done.55, f32[1024]{0:T(1024)S(1)} %add_rsqrt_fusion.2, ...), kind=kOutput, calls=%fused_computation.1 | convolution fusion | flops 17843486720 | bytes 48253952 | tf_op jit(solution)/shard_map/dot_general | solution.py:72
  562.7 29.7 %all-gather.19.cloned.1.call-done = bf16[6144,1408]{0,1:T(8,128)(2,1)} async-done(((bf16[768,1408]{0,1:T(8,128)(2,1)}), bf16[6144,1408]{0,1:T(8,128)(2,1)}) %all-gather.19.cloned.1.call-update) | async-done | bytes 17301520 | tf_op jit(solution)/shard_map/all_gather | solution.py:1136
  592.4 28.8 %fusion.112 = (f32[1024]{0:T(1024)S(1)}, f32[1024,1408]{1,0:T(8,128)S(1)}) fusion(f32[1024,1408]{1,0:T(8,128)} %copy-done.2, bf16[1024,6144]{1,0:T(8,128)(2,1)} %get-tuple-element.126, bf16[6144,1408]{0,1:T(8,128)(2,1)} %all-gather.19.cloned.1.call-done), kind=kOutput, calls=%fused_computation.320 | convolution fusion | flops 17719623680 | bytes 41422848 | tf_op jit(solution)/shard_map/dot_general | solution.py:72
  631.4 27.9 %convolution_convert_fusion = bf16[6144,1408]{1,0:T(8,128)(2,1)} fusion(bf16[1024,6144]{1,0:T(8,128)(2,1)} %get-tuple-element.126, bf16[1024,1408]{1,0:T(8,128)(2,1)S(1)} %get-tuple-element.131), kind=kOutput, calls=%fused_computation.5 | convolution fusion | flops 17725390848 | bytes 32768000 | tf_op jit(solution)/shard_map/dot_general | solution.py:76
  661.1 30.5 %multiply_convert_fusion = bf16[1024,6144]{1,0:T(8,128)(2,1)} fusion(bf16[1024,6144]{1,0:T(8,128)(2,1)} %get-tuple-element.132, bf16[1024,1408]{1,0:T(8,128)(2,1)S(1)} %copy-done.19, bf16[6144,1408]{0,1:T(8,128)(2,1)} %all-gather.19.cloned.1.call-done), kind=kOutput, calls=%fused_computation | convolution fusion | flops 17735614464 | bytes 45350912 | tf_op jit(solution)/shard_map/dot_general | solution.py:82
  691.7 25.9 %convolution_convert_fusion.1 = bf16[1408,6144]{1,0:T(8,128)(2,1)} fusion(bf16[1024,6144]{1,0:T(8,128)(2,1)} %multiply_convert_fusion, f32[1024,1408]{1,0:T(8,128)} %copy-done.2, f32[1408]{0:T(1024)S(1)} %copy-done.79, f32[1408]{0:T(1024)S(1)} %copy-done.55, f32[1024]{0:T(1024)S(1)} %add_rsqrt_fusion.2, f32[1024]{0:T(1024)S(1)} %broadcast_multiply_fusion.12), kind=kOutput, calls=%fused_computation.6 | convolution fusion | flops 17732599808 | bytes 35671040 | tf_op jit(solution)/shard_map/dot_general | solution.py:76
  717.6 31.4 %multiply_reduce_fusion.1 = (f32[1408]{0:T(1024)}, f32[1024]{0:T(1024)S(1)}, f32[1024]{0:T(1024)S(1)}, f32[1408]{0:T(1024)}, f32[1024,1408]{1,0:T(8,128)}) fusion(f32[1024,1408]{1,0:T(8,128)} %copy-done.2, f32[1024]{0:T(1024)S(1)} %add_rsqrt_fusion.2, f32[1024]{0:T(1024)S(1)} %broadcast_multiply_fusion.12, f32[1408]{0:T(1024)S(1)} %copy-done.55, ...), kind=kOutput, calls=%fused_computation.19 | convolution fusion | flops 17729710080 | bytes 41452032 | tf_op jit(solution)/shard_map/dot_general | solution.py:82
  749.0 7.7 multiply_add_fusion.1
  756.7 10.4 convolution_convert_fusion.7
  767.2 21.3 %shard_map.320 = (bf16[16,88,1024]{2,1,0:T(8,128)(2,1)}, bf16[16,88,768]{2,1,0:T(8,128)(2,1)}, bf16[16,88,768]{2,1,0:T(8,128)(2,1)}) custom-call(bf16[16,88,1024]{2,1,0:T(8,128)(2,1)} %get-tuple-element.135.query_ref, f32[2,16,88,768]{3,2,1,0:T(8,128)} %bitcast.188, bf16[16,88,1024]{2,1,0:T(8,128)(2,1)} %bitcast.215, ...), custom_call_target="tpu_custom_call" | custom-call | flops 16106127360 | bytes 23068672 | tf_op jit(solution)/shard_map/pallas_call | solution.py:957
  788.6 14.1 multiply_reduce_fusion.2
  802.7 6.3 fusion.93
  809.0 6.8 fusion.17
  820.4 8.6 fusion.2
  829.0 10.0 fusion.1
  839.0 6.2 fusion
  849.1 5.4 all-to-all-done.4.grad_ref
  863.6 6.3 fusion.20
  874.2 89.2 %shard_map.321 = bf16[8,3,2,88,512]{4,3,2,1,0:T(8,128)(2,1)} custom-call(bf16[8,3,2,88,512]{4,3,2,1,0:T(8,128)(2,1)} %all-to-all-done.query_ref.key_ref.value_ref, bf16[8,3,2,88,512]{4,3,2,1,0:T(8,128)(2,1)} %all-to-all-done.query_ref.key_ref.value_ref, bf16[8,3,2,88,512]{4,3,2,1,0:T(8,128)(2,1)} %all-to-all-done.query_ref.key_ref.value_ref, ...), custom_call_target="tpu_custom_call" | custom-call | flops 85899345920 | bytes 17301504 | tf_op jit(solution)/shard_map/pallas_call | solution.py:845
  975.2 89.1 %shard_map.322 = bf16[8,3,2,88,512]{4,3,2,1,0:T(8,128)(2,1)} custom-call(bf16[8,3,2,88,512]{4,3,2,1,0:T(8,128)(2,1)} %all-to-all-done.2.query_ref.key_ref.value_ref, bf16[8,3,2,88,512]{4,3,2,1,0:T(8,128)(2,1)} %all-to-all-done.2.query_ref.key_ref.value_ref, bf16[8,3,2,88,512]{4,3,2,1,0:T(8,128)(2,1)} %all-to-all-done.2.query_ref.key_ref.value_ref, ...), custom_call_target="tpu_custom_call" | custom-call | flops 85899345920 | bytes 17301504 | tf_op jit(solution)/shard_map/pallas_call | solution.py:845
  1077.6 10.8 collective-permute-done.30
  1088.4 11.0 collective-permute-done.32
  1099.4 23.2 %collective-permute-done.31 = bf16[176,1536]{1,0:T(8,128)(2,1)S(1)} collective-permute-done((bf16[176,1536]{1,0:T(8,128)(2,1)S(1)}, bf16[176,1536]{1,0:T(8,128)(2,1)S(1)}, u32[]{:S(2)}, u32[]{:S(2)}) %collective-permute-start.31) | collective-permute-done | bytes 540704 | tf_op jit(solution)/shard_map/ppermute | solution.py:1087
  1124.0 10.1 shard_map.323.others_0_
  1134.1 6.1 all-to-all-done.6.grad_ref
  1140.2 10.2 shard_map.324
  1150.5 19.9 %convolution_convert_fusion.2 = bf16[1408,4224]{1,0:T(8,128)(2,1)} fusion(bf16[1024,1408]{1,0:T(8,128)(2,1)S(1)} %copy-done.12, bf16[4224,1024]{1,0:T(8,128)(2,1)} %bitcast.165), kind=kOutput, calls=%fused_computation.7 | convolution fusion | flops 12186206208 | bytes 23429120 | tf_op jit(solution)/shard_map/dot_general | solution.py:1144
  1180.5 27.0 %multiply_reduce_fusion.3 = (f32[1408]{0:T(1024)}, f32[1024]{0:T(1024)S(1)}, f32[1024]{0:T(1024)S(1)}, f32[1408]{0:T(1024)}, f32[1024,1408]{1,0:T(8,128)S(1)}) fusion(f32[1024,1408]{1,0:T(8,128)} %copy-done, f32[1024]{0:T(1024)S(1)} %copy-done.50, f32[1024]{0:T(1024)S(1)} %copy-done.48, f32[1408]{0:T(1024)S(1)} %copy-done.46, ...), kind=kOutput, calls=%fused_computation.21 | convolution fusion | flops 12193230848 | bytes 32113152 | tf_op jit(solution)/shard_map/dot_general | solution.py:1144
  1221.6 7.1 add_convert_fusion.1.low_ref
  1229.0 14.6 %convolution_convert_fusion.3 = bf16[2816,1408]{1,0:T(8,128)(2,1)} fusion(bf16[1024,2816]{1,0:T(8,128)(2,1)} %get-tuple-element.104, bf16[1024,1408]{1,0:T(8,128)(2,1)S(1)} %add_convert_fusion.1.low_ref), kind=kOutput, calls=%fused_computation.8 | convolution fusion | flops 8124137472 | bytes 16580608 | tf_op jit(solution)/shard_map/dot_general | solution.py:76
  1262.9 15.9 %collective-permute-done.34 = bf16[176,1056]{1,0:T(8,128)(2,1)S(1)} collective-permute-done((bf16[176,1056]{1,0:T(8,128)(2,1)}, bf16[176,1056]{1,0:T(8,128)(2,1)S(1)}, u32[]{:S(2)}, u32[]{:S(2)}) %collective-permute-start.34) | collective-permute-done | bytes 371744 | tf_op jit(solution)/shard_map/ppermute | solution.py:1087
  1295.4 9.3 collective-permute-start.42
  1306.9 25.9 %shard_map.325 = (f32[1024,1408]{1,0:T(8,128)}, bf16[1024,1408]{1,0:T(8,128)(2,1)}, f32[2,2816]{1,0:T(2,128)}) custom-call(bf16[1024,1408]{1,0:T(8,128)(2,1)} %copy-done.16, bf16[2816,1408]{1,0:T(8,128)(2,1)} %all-gather.9.cloned.1.call-done.weight_ref, f32[1024,2816]{1,0:T(8,128)} %get-tuple-element.169.z_ref, f32[1024,1]{1,0:T(8,128)} %get-tuple-element.170.inv_ref, ...), custom_call_target="tpu_custom_call" | custom-call | flops 8120172544 | bytes 25952256 | tf_op jit(solution)/shard_map/pallas_call | solution.py:1032
  1334.0 6.0 collective-permute-done.43
  1357.9 6.9 copy.172
  1376.0 9.3 collective-permute-done.52
  1402.3 9.2 collective-permute-done.49
  (557 shorter events, 281.8 us)
Async XLA Ops:
  7.2 175.7 %all-gather.9.cloned.1.call-start = ((), (), s32[]{:S(2)}) async-start(), calls=%async_computation.13 | async-start | bytes 8921088 | tf_op jit(solution)/shard_map/all_gather | solution.py:1136
  7.3 12.8 collective-permute-start.3
  10.4 20.4 %collective-permute-start.4 = (bf16[352,352]{1,0:T(8,128)(2,1)}, bf16[352,352]{1,0:T(8,128)(2,1)S(1)}, u32[]{:S(2)}, u32[]{:S(2)}) collective-permute-start(bf16[352,352]{1,0:T(8,128)(2,1)} %param.26), channel_id=1, source_target_pairs={{0,16},{8,24},{16,0},{24,8},{1,17},{9,25},{17,1},{25,9},{2,18},{10... | collective-permute-start | bytes 743432 | tf_op jit(solution)/shard_map/ppermute | solution.py:1067
  13.0 17.9 %collective-permute-start.5 = (bf16[352,352]{1,0:T(8,128)(2,1)}, bf16[352,352]{1,0:T(8,128)(2,1)S(1)}, u32[]{:S(2)}, u32[]{:S(2)}) collective-permute-start(bf16[352,352]{1,0:T(8,128)(2,1)} %param.26), channel_id=1, source_target_pairs={{0,24},{8,0},{16,8},{24,16},{1,25},{9,1},{17,9},{25,17},{2,26},{10... | collective-permute-start | bytes 743432 | tf_op jit(solution)/shard_map/ppermute | solution.py:1067
  33.5 172.9 %all-gather.11.cloned.1.call-start = ((), (), s32[]{:S(2)}) async-start(), calls=%async_computation.14 | async-start | bytes 13381632 | tf_op jit(solution)/shard_map/all_gather | solution.py:1136
  35.6 14.9 %collective-permute-start = (bf16[384,352]{0,1:T(8,128)(2,1)S(1)}, bf16[384,352]{0,1:T(8,128)(2,1)S(1)}, u32[]{:S(2)}, u32[]{:S(2)}) collective-permute-start(bf16[384,352]{0,1:T(8,128)(2,1)S(1)} %pad_maximum_fusion.18), channel_id=1, source_target_pairs={{0,8},{8,16},{16,24},{24,0},{1,9},{9,17},{17,25},{25,1},{2,10},{10... | collective-permute-start | bytes 811016 | tf_op jit(solution)/shard_map/ppermute | solution.py:1067
  41.9 20.2 %collective-permute-start.1 = (bf16[384,352]{0,1:T(8,128)(2,1)S(1)}, bf16[384,352]{0,1:T(8,128)(2,1)S(1)}, u32[]{:S(2)}, u32[]{:S(2)}) collective-permute-start(bf16[384,352]{0,1:T(8,128)(2,1)S(1)} %pad_maximum_fusion.18), channel_id=1, source_target_pairs={{0,16},{8,24},{16,0},{24,8},{1,17},{9,25},{17,1},{25,9},{2,18},{10... | collective-permute-start | bytes 811016 | tf_op jit(solution)/shard_map/ppermute | solution.py:1067
  43.5 18.6 %collective-permute-start.2 = (bf16[384,352]{0,1:T(8,128)(2,1)S(1)}, bf16[384,352]{0,1:T(8,128)(2,1)S(1)}, u32[]{:S(2)}, u32[]{:S(2)}) collective-permute-start(bf16[384,352]{0,1:T(8,128)(2,1)S(1)} %pad_maximum_fusion.18), channel_id=1, source_target_pairs={{0,24},{8,0},{16,8},{24,16},{1,25},{9,1},{17,9},{25,17},{2,26},{10... | collective-permute-start | bytes 811016 | tf_op jit(solution)/shard_map/ppermute | solution.py:1067
  44.4 49.3 %collective-permute-start.12 = (bf16[176,1056]{1,0:T(8,128)(2,1)S(1)}, bf16[176,1056]{1,0:T(8,128)(2,1)S(1)}, u32[]{:S(2)}, u32[]{:S(2)}) collective-permute-start(bf16[176,1056]{1,0:T(8,128)(2,1)S(1)} %copy-done.37), channel_id=1, source_target_pairs={{0,8},{8,16},{16,24},{24,0},{1,9},{9,17},{17,25},{25,1},{2,10},{10... | collective-permute-start | bytes 1115144 | tf_op jit(solution)/shard_map/ppermute | solution.py:1067
  45.6 48.2 %collective-permute-start.13 = (bf16[176,1056]{1,0:T(8,128)(2,1)S(1)}, bf16[176,1056]{1,0:T(8,128)(2,1)S(1)}, u32[]{:S(2)}, u32[]{:S(2)}) collective-permute-start(bf16[176,1056]{1,0:T(8,128)(2,1)S(1)} %copy-done.37), channel_id=1, source_target_pairs={{0,16},{8,24},{16,0},{24,8},{1,17},{9,25},{17,1},{25,9},{2,18},{10... | collective-permute-start | bytes 1115144 | tf_op jit(solution)/shard_map/ppermute | solution.py:1067
  50.5 43.2 %collective-permute-start.14 = (bf16[176,1056]{1,0:T(8,128)(2,1)S(1)}, bf16[176,1056]{1,0:T(8,128)(2,1)S(1)}, u32[]{:S(2)}, u32[]{:S(2)}) collective-permute-start(bf16[176,1056]{1,0:T(8,128)(2,1)S(1)} %copy-done.37), channel_id=1, source_target_pairs={{0,24},{8,0},{16,8},{24,16},{1,25},{9,1},{17,9},{25,17},{2,26},{10... | collective-permute-start | bytes 1115144 | tf_op jit(solution)/shard_map/ppermute | solution.py:1067
  99.4 337.2 %all-gather.13.cloned.1.call-start = ((), (), s32[]{:S(2)}) async-start(), calls=%async_computation.15 | async-start | bytes 13381632 | tf_op jit(solution)/shard_map/all_gather | solution.py:1136
  100.7 31.0 %collective-permute-start.15 = (bf16[176,1056]{1,0:T(8,128)(2,1)S(1)}, bf16[176,1056]{1,0:T(8,128)(2,1)S(1)}, u32[]{:S(2)}, u32[]{:S(2)}) collective-permute-start(bf16[176,1056]{1,0:T(8,128)(2,1)S(1)} %concatenate.112), channel_id=1, source_target_pairs={{0,8},{8,16},{16,24},{24,0},{1,9},{9,17},{17,25},{25,1},{2,10},{10... | collective-permute-start | bytes 1115144 | tf_op jit(solution)/shard_map/ppermute | solution.py:1067
  121.9 21.1 %collective-permute-start.16 = (bf16[176,1056]{1,0:T(8,128)(2,1)S(1)}, bf16[176,1056]{1,0:T(8,128)(2,1)S(1)}, u32[]{:S(2)}, u32[]{:S(2)}) collective-permute-start(bf16[176,1056]{1,0:T(8,128)(2,1)S(1)} %concatenate.112), channel_id=1, source_target_pairs={{0,16},{8,24},{16,0},{24,8},{1,17},{9,25},{17,1},{25,9},{2,18},{10... | collective-permute-start | bytes 1115144 | tf_op jit(solution)/shard_map/ppermute | solution.py:1067
  121.9 26.9 %collective-permute-start.17 = (bf16[176,1056]{1,0:T(8,128)(2,1)S(1)}, bf16[176,1056]{1,0:T(8,128)(2,1)S(1)}, u32[]{:S(2)}, u32[]{:S(2)}) collective-permute-start(bf16[176,1056]{1,0:T(8,128)(2,1)S(1)} %concatenate.112), channel_id=1, source_target_pairs={{0,24},{8,0},{16,8},{24,16},{1,25},{9,1},{17,9},{25,17},{2,26},{10... | collective-permute-start | bytes 1115144 | tf_op jit(solution)/shard_map/ppermute | solution.py:1067
  153.4 322.5 %all-gather.15.cloned.1.call-start = ((), (), s32[]{:S(2)}) async-start(), calls=%async_computation.16 | async-start | bytes 6488064 | tf_op jit(solution)/shard_map/all_gather | solution.py:1136
  169.2 13.7 collective-permute-start.11
  170.4 29.4 %collective-permute-start.18 = (bf16[128,704]{0,1:T(8,128)(2,1)S(1)}, bf16[128,704]{0,1:T(8,128)(2,1)S(1)}, u32[]{:S(2)}, u32[]{:S(2)}) collective-permute-start(bf16[128,704]{0,1:T(8,128)(2,1)S(1)} %copy-done.41), channel_id=1, source_target_pairs={{0,8},{8,16},{16,24},{24,0},{1,9},{9,17},{17,25},{25,1},{2,10},{10... | collective-permute-start | bytes 540680 | tf_op jit(solution)/shard_map/ppermute | solution.py:1067
  179.3 20.5 %collective-permute-start.19 = (bf16[128,704]{0,1:T(8,128)(2,1)S(1)}, bf16[128,704]{0,1:T(8,128)(2,1)S(1)}, u32[]{:S(2)}, u32[]{:S(2)}) collective-permute-start(bf16[128,704]{0,1:T(8,128)(2,1)S(1)} %copy-done.41), channel_id=1, source_target_pairs={{0,16},{8,24},{16,0},{24,8},{1,17},{9,25},{17,1},{25,9},{2,18},{10... | collective-permute-start | bytes 540680 | tf_op jit(solution)/shard_map/ppermute | solution.py:1067
  182.7 17.1 %collective-permute-start.20 = (bf16[128,704]{0,1:T(8,128)(2,1)S(1)}, bf16[128,704]{0,1:T(8,128)(2,1)}, u32[]{:S(2)}, u32[]{:S(2)}) collective-permute-start(bf16[128,704]{0,1:T(8,128)(2,1)S(1)} %copy-done.41), channel_id=1, source_target_pairs={{0,24},{8,0},{16,8},{24,16},{1,25},{9,1},{17,9},{25,17},{2,26},{10... | collective-permute-start | bytes 540680 | tf_op jit(solution)/shard_map/ppermute | solution.py:1067
  221.1 81.4 %all-to-all-start = ((bf16[8,3,2,88,512]{4,3,2,1,0:T(8,128)(2,1)}), bf16[8,3,2,88,512]{4,3,2,1,0:T(8,128)(2,1)}, u32[]{:S(2)}, u32[]{:S(2)}) async-start(bf16[8,3,2,88,512]{4,3,2,1,0:T(8,128)(2,1)} %get-tuple-element.109.own_ref), calls=%async_computation | async-start | bytes 8650752 | tf_op jit(solution)/shard_map/all_to_all | solution.py:1057
  226.0 296.8 %all-gather.17.cloned.1.call-start = ((), (), s32[]{:S(2)}) async-start(), calls=%async_computation.17 | async-start | bytes 19464192 | tf_op jit(solution)/shard_map/all_gather | solution.py:1136
  226.1 17.1 %collective-permute-start.21 = (bf16[176,1536]{1,0:T(8,128)(2,1)S(1)}, bf16[176,1536]{1,0:T(8,128)(2,1)S(1)}, u32[]{:S(2)}, u32[]{:S(2)}) collective-permute-start(bf16[176,1536]{1,0:T(8,128)(2,1)S(1)} %copy-done.33), channel_id=1, source_target_pairs={{0,8},{8,16},{16,24},{24,0},{1,9},{9,17},{17,25},{25,1},{2,10},{10... | collective-permute-start | bytes 1622024 | tf_op jit(solution)/shard_map/ppermute | solution.py:1067
  228.0 37.7 %collective-permute-start.22 = (bf16[176,1536]{1,0:T(8,128)(2,1)S(1)}, bf16[176,1536]{1,0:T(8,128)(2,1)S(1)}, u32[]{:S(2)}, u32[]{:S(2)}) collective-permute-start(bf16[176,1536]{1,0:T(8,128)(2,1)S(1)} %copy-done.33), channel_id=1, source_target_pairs={{0,16},{8,24},{16,0},{24,8},{1,17},{9,25},{17,1},{25,9},{2,18},{10... | collective-permute-start | bytes 1622024 | tf_op jit(solution)/shard_map/ppermute | solution.py:1067
  228.7 37.1 %collective-permute-start.23 = (bf16[176,1536]{1,0:T(8,128)(2,1)S(1)}, bf16[176,1536]{1,0:T(8,128)(2,1)S(1)}, u32[]{:S(2)}, u32[]{:S(2)}) collective-permute-start(bf16[176,1536]{1,0:T(8,128)(2,1)S(1)} %copy-done.33), channel_id=1, source_target_pairs={{0,24},{8,0},{16,8},{24,16},{1,25},{9,1},{17,9},{25,17},{2,26},{10... | collective-permute-start | bytes 1622024 | tf_op jit(solution)/shard_map/ppermute | solution.py:1067
  319.3 69.7 %all-to-all-start.2 = ((bf16[8,3,2,88,512]{4,3,2,1,0:T(8,128)(2,1)}), bf16[8,3,2,88,512]{4,3,2,1,0:T(8,128)(2,1)}, u32[]{:S(2)}, u32[]{:S(2)}) async-start(bf16[8,3,2,88,512]{4,3,2,1,0:T(8,128)(2,1)} %get-tuple-element.111.own_ref), calls=%async_computation.2 | async-start | bytes 8650752 | tf_op jit(solution)/shard_map/all_to_all | solution.py:1057
  389.0 38.0 %all-to-all-start.1 = ((bf16[8,2,88,512]{3,2,1,0:T(8,128)(2,1)}), bf16[8,2,88,512]{3,2,1,0:T(8,128)(2,1)S(1)}, u32[]{:S(2)}, u32[]{:S(2)}) async-start(bf16[8,2,88,512]{3,2,1,0:T(8,128)(2,1)} %get-tuple-element.110.att_ref), calls=%async_computation.1 | async-start | bytes 2883584 | tf_op jit(solution)/shard_map/all_to_all | solution.py:1057
  427.0 31.0 %all-to-all-start.3 = ((bf16[8,2,88,512]{3,2,1,0:T(8,128)(2,1)}), bf16[8,2,88,512]{3,2,1,0:T(8,128)(2,1)S(1)}, u32[]{:S(2)}, u32[]{:S(2)}) async-start(bf16[8,2,88,512]{3,2,1,0:T(8,128)(2,1)} %get-tuple-element.112.att_ref), calls=%async_computation.3 | async-start | bytes 2883584 | tf_op jit(solution)/shard_map/all_to_all | solution.py:1057
  431.1 161.2 %all-gather.19.cloned.1.call-start = ((), (), s32[]{:S(2)}) async-start(), calls=%async_computation.18 | async-start | bytes 19464192 | tf_op jit(solution)/shard_map/all_gather | solution.py:1136
  431.2 37.3 %collective-permute-start.24 = (bf16[768,352]{0,1:T(8,128)(2,1)S(1)}, bf16[768,352]{0,1:T(8,128)(2,1)}, u32[]{:S(2)}, u32[]{:S(2)}) collective-permute-start(bf16[768,352]{0,1:T(8,128)(2,1)S(1)} %copy-done.34), channel_id=1, source_target_pairs={{0,8},{8,16},{16,24},{24,0},{1,9},{9,17},{17,25},{25,1},{2,10},{10... | collective-permute-start | bytes 1622024 | tf_op jit(solution)/shard_map/ppermute | solution.py:1067
  432.7 38.3 %collective-permute-start.25 = (bf16[768,352]{0,1:T(8,128)(2,1)S(1)}, bf16[768,352]{0,1:T(8,128)(2,1)}, u32[]{:S(2)}, u32[]{:S(2)}) collective-permute-start(bf16[768,352]{0,1:T(8,128)(2,1)S(1)} %copy-done.34), channel_id=1, source_target_pairs={{0,16},{8,24},{16,0},{24,8},{1,17},{9,25},{17,1},{25,9},{2,18},{10... | collective-permute-start | bytes 1622024 | tf_op jit(solution)/shard_map/ppermute | solution.py:1067
  435.1 36.0 %collective-permute-start.26 = (bf16[768,352]{0,1:T(8,128)(2,1)S(1)}, bf16[768,352]{0,1:T(8,128)(2,1)}, u32[]{:S(2)}, u32[]{:S(2)}) collective-permute-start(bf16[768,352]{0,1:T(8,128)(2,1)S(1)} %copy-done.34), channel_id=1, source_target_pairs={{0,24},{8,0},{16,8},{24,16},{1,25},{9,1},{17,9},{25,17},{2,26},{10... | collective-permute-start | bytes 1622024 | tf_op jit(solution)/shard_map/ppermute | solution.py:1067
  474.2 314.3 %reduce-scatter.8.cloned.1.call-start = ((), (), s32[]{:S(2)}) async-start(), calls=%async_computation.20 | async-start | bytes 19464192 | tf_op jit(solution)/shard_map/reduce_scatter | solution.py:1131
  659.3 409.6 %reduce-scatter.6.cloned.1.call-start = ((), (), s32[]{:S(2)}) async-start(), calls=%async_computation.19 | async-start | bytes 19464192 | tf_op jit(solution)/shard_map/reduce_scatter | solution.py:1131
  815.8 38.7 %all-to-all-start.4 = ((bf16[8,2,88,512]{3,2,1,0:T(8,128)(2,1)}), bf16[8,2,88,512]{3,2,1,0:T(8,128)(2,1)}, u32[]{:S(2)}, u32[]{:S(2)}) async-start(bf16[8,2,88,512]{3,2,1,0:T(8,128)(2,1)} %bitcast.199), calls=%async_computation.6 | async-start | bytes 2883584 | tf_op jit(solution)/shard_map/all_to_all | solution.py:1057
  820.1 354.9 %reduce-scatter.12.cloned.1.call-start = ((), (), s32[]{:S(2)}) async-start(), calls=%async_computation.22 | async-start | bytes 18247680 | tf_op jit(solution)/shard_map/reduce_scatter | solution.py:1131
  856.4 107.0 %collective-permute-start.27 = (bf16[768,352]{0,1:T(8,128)(2,1)}, bf16[768,352]{0,1:T(8,128)(2,1)S(1)}, u32[]{:S(2)}, u32[]{:S(2)}) collective-permute-start(bf16[768,352]{0,1:T(8,128)(2,1)} %copy.133), channel_id=1, source_target_pairs={{0,8},{8,16},{16,24},{24,0},{1,9},{9,17},{17,25},{25,1},{2,10},{10... | collective-permute-start | bytes 1622024 | tf_op jit(solution)/shard_map/ppermute | solution.py:1087
  858.6 104.8 %collective-permute-start.29 = (bf16[768,352]{0,1:T(8,128)(2,1)}, bf16[768,352]{0,1:T(8,128)(2,1)}, u32[]{:S(2)}, u32[]{:S(2)}) collective-permute-start(bf16[768,352]{0,1:T(8,128)(2,1)} %copy.135), channel_id=1, source_target_pairs={{0,24},{8,0},{16,8},{24,16},{1,25},{9,1},{17,9},{25,17},{2,26},{10... | collective-permute-start | bytes 1622024 | tf_op jit(solution)/shard_map/ppermute | solution.py:1087
  863.3 100.1 %collective-permute-start.28 = (bf16[768,352]{0,1:T(8,128)(2,1)}, bf16[768,352]{0,1:T(8,128)(2,1)}, u32[]{:S(2)}, u32[]{:S(2)}) collective-permute-start(bf16[768,352]{0,1:T(8,128)(2,1)} %copy.134), channel_id=1, source_target_pairs={{0,16},{8,24},{16,0},{24,8},{1,17},{9,25},{17,1},{25,9},{2,18},{10... | collective-permute-start | bytes 1622024 | tf_op jit(solution)/shard_map/ppermute | solution.py:1087
  869.9 100.5 %all-to-all-start.5 = ((bf16[8,2,88,512]{3,2,1,0:T(8,128)(2,1)}), bf16[8,2,88,512]{3,2,1,0:T(8,128)(2,1)}, u32[]{:S(2)}, u32[]{:S(2)}) async-start(bf16[8,2,88,512]{3,2,1,0:T(8,128)(2,1)} %bitcast.198), calls=%async_computation.7 | async-start | bytes 2883584 | tf_op jit(solution)/shard_map/all_to_all | solution.py:1057
  970.4 93.9 %all-to-all-start.7 = ((bf16[8,3,2,88,512]{4,3,2,1,0:T(8,128)(2,1)}), bf16[8,3,2,88,512]{4,3,2,1,0:T(8,128)(2,1)}, u32[]{:S(2)}, u32[]{:S(2)}) async-start(bf16[8,3,2,88,512]{4,3,2,1,0:T(8,128)(2,1)} %shard_map.321), calls=%async_computation.9 | async-start | bytes 8650752 | tf_op jit(solution)/shard_map/all_to_all | solution.py:1057
  1064.3 75.9 %all-to-all-start.6 = ((bf16[8,3,2,88,512]{4,3,2,1,0:T(8,128)(2,1)}), bf16[8,3,2,88,512]{4,3,2,1,0:T(8,128)(2,1)}, u32[]{:S(2)}, u32[]{:S(2)}) async-start(bf16[8,3,2,88,512]{4,3,2,1,0:T(8,128)(2,1)} %shard_map.322), calls=%async_computation.8 | async-start | bytes 8650752 | tf_op jit(solution)/shard_map/all_to_all | solution.py:1057
  1068.9 190.9 %reduce-scatter.10.cloned.1.call-start = ((), (), s32[]{:S(2)}) async-start(), calls=%async_computation.21 | async-start | bytes 13381632 | tf_op jit(solution)/shard_map/reduce_scatter | solution.py:1131
  1071.4 17.0 %collective-permute-start.30 = (bf16[176,1536]{1,0:T(8,128)(2,1)S(1)}, bf16[176,1536]{1,0:T(8,128)(2,1)S(1)}, u32[]{:S(2)}, u32[]{:S(2)}) collective-permute-start(bf16[176,1536]{1,0:T(8,128)(2,1)S(1)} %get-tuple-element.301), channel_id=1, source_target_pairs={{0,8},{8,16},{16,24},{24,0},{1,9},{9,17},{17,25},{25,1},{2,10},{10... | collective-permute-start | bytes 1622024 | tf_op jit(solution)/shard_map/ppermute | solution.py:1087
  1074.3 25.1 %collective-permute-start.32 = (bf16[176,1536]{1,0:T(8,128)(2,1)S(1)}, bf16[176,1536]{1,0:T(8,128)(2,1)S(1)}, u32[]{:S(2)}, u32[]{:S(2)}) collective-permute-start(bf16[176,1536]{1,0:T(8,128)(2,1)S(1)} %get-tuple-element.300), channel_id=1, source_target_pairs={{0,24},{8,0},{16,8},{24,16},{1,25},{9,1},{17,9},{25,17},{2,26},{10... | collective-permute-start | bytes 1622024 | tf_op jit(solution)/shard_map/ppermute | solution.py:1087
  1077.0 45.6 %collective-permute-start.31 = (bf16[176,1536]{1,0:T(8,128)(2,1)S(1)}, bf16[176,1536]{1,0:T(8,128)(2,1)S(1)}, u32[]{:S(2)}, u32[]{:S(2)}) collective-permute-start(bf16[176,1536]{1,0:T(8,128)(2,1)S(1)} %select_select_fusion.4), channel_id=1, source_target_pairs={{0,16},{8,24},{16,0},{24,8},{1,17},{9,25},{17,1},{25,9},{2,18},{10... | collective-permute-start | bytes 1622024 | tf_op jit(solution)/shard_map/ppermute | solution.py:1087
  1170.4 171.2 %all-gather.21.cloned.1.call-start = ((), (), s32[]{:S(2)}) async-start(), calls=%async_computation.23 | async-start | bytes 4866048 | tf_op jit(solution)/shard_map/all_gather | solution.py:1136
  1180.0 208.1 %reduce-scatter.14.cloned.1.call-start = ((), (), s32[]{:S(2)}) async-start(), calls=%async_computation.24 | async-start | bytes 8921088 | tf_op jit(solution)/shard_map/reduce_scatter | solution.py:1131
  1219.9 8.8 collective-permute-start.39
  1228.9 14.8 %collective-permute-start.40 = (f32[2,1408]{1,0:T(2,128)S(1)}, f32[2,1408]{1,0:T(2,128)S(1)}, u32[]{:S(2)}, u32[]{:S(2)}) collective-permute-start(f32[2,1408]{1,0:T(2,128)S(1)} %add.575), channel_id=1, source_target_pairs={{0,2},{1,3},{2,0},{3,1},{4,6},{5,7},{6,4},{7,5},{8,10},{9,11},{10,... | collective-permute-start | bytes 33800 | tf_op jit(solution)/shard_map/ppermute | solution.py:1124
  1243.7 11.3 collective-permute-start.41
  1248.4 14.5 %collective-permute-start.33 = (bf16[176,1056]{1,0:T(8,128)(2,1)}, bf16[176,1056]{1,0:T(8,128)(2,1)S(1)}, u32[]{:S(2)}, u32[]{:S(2)}) collective-permute-start(bf16[176,1056]{1,0:T(8,128)(2,1)} %get-tuple-element.326), channel_id=1, source_target_pairs={{0,8},{8,16},{16,24},{24,0},{1,9},{9,17},{17,25},{25,1},{2,10},{10... | collective-permute-start | bytes 1115144 | tf_op jit(solution)/shard_map/ppermute | solution.py:1087
  1249.9 28.9 %collective-permute-start.34 = (bf16[176,1056]{1,0:T(8,128)(2,1)}, bf16[176,1056]{1,0:T(8,128)(2,1)S(1)}, u32[]{:S(2)}, u32[]{:S(2)}) collective-permute-start(bf16[176,1056]{1,0:T(8,128)(2,1)} %get-tuple-element.325), channel_id=1, source_target_pairs={{0,16},{8,24},{16,0},{24,8},{1,17},{9,25},{17,1},{25,9},{2,18},{10... | collective-permute-start | bytes 1115144 | tf_op jit(solution)/shard_map/ppermute | solution.py:1087
  1251.3 27.5 %collective-permute-start.35 = (bf16[176,1056]{1,0:T(8,128)(2,1)S(1)}, bf16[176,1056]{1,0:T(8,128)(2,1)}, u32[]{:S(2)}, u32[]{:S(2)}) collective-permute-start(bf16[176,1056]{1,0:T(8,128)(2,1)S(1)} %get-tuple-element.324), channel_id=1, source_target_pairs={{0,24},{8,0},{16,8},{24,16},{1,25},{9,1},{17,9},{25,17},{2,26},{10... | collective-permute-start | bytes 1115144 | tf_op jit(solution)/shard_map/ppermute | solution.py:1087
  1295.4 38.6 %collective-permute-start.42 = (bf16[176,1056]{1,0:T(8,128)(2,1)S(1)}, bf16[176,1056]{1,0:T(8,128)(2,1)S(1)}, u32[]{:S(2)}, u32[]{:S(2)}) collective-permute-start(bf16[176,1056]{1,0:T(8,128)(2,1)S(1)} %get-tuple-element.336), channel_id=1, source_target_pairs={{0,8},{8,16},{16,24},{24,0},{1,9},{9,17},{17,25},{25,1},{2,10},{10... | collective-permute-start | bytes 1115144 | tf_op jit(solution)/shard_map/ppermute | solution.py:1087
  1304.7 29.3 %collective-permute-start.44 = (bf16[176,1056]{1,0:T(8,128)(2,1)S(1)}, bf16[176,1056]{1,0:T(8,128)(2,1)S(1)}, u32[]{:S(2)}, u32[]{:S(2)}) collective-permute-start(bf16[176,1056]{1,0:T(8,128)(2,1)S(1)} %get-tuple-element.335), channel_id=1, source_target_pairs={{0,24},{8,0},{16,8},{24,16},{1,25},{9,1},{17,9},{25,17},{2,26},{10... | collective-permute-start | bytes 1115144 | tf_op jit(solution)/shard_map/ppermute | solution.py:1087
  1306.1 33.9 %collective-permute-start.43 = (bf16[176,1056]{1,0:T(8,128)(2,1)S(1)}, bf16[176,1056]{1,0:T(8,128)(2,1)S(1)}, u32[]{:S(2)}, u32[]{:S(2)}) collective-permute-start(bf16[176,1056]{1,0:T(8,128)(2,1)S(1)} %select_select_fusion.15), channel_id=1, source_target_pairs={{0,16},{8,24},{16,0},{24,8},{1,17},{9,25},{17,1},{25,9},{2,18},{10... | collective-permute-start | bytes 1115144 | tf_op jit(solution)/shard_map/ppermute | solution.py:1087
  1350.0 14.7 %collective-permute-start.45 = (f32[704,60]{0,1:T(8,128)S(1)}, f32[704,60]{0,1:T(8,128)}, u32[]{:S(2)}, u32[]{:S(2)}) collective-permute-start(f32[704,60]{0,1:T(8,128)S(1)} %select_n.1636), channel_id=1, source_target_pairs={{0,4},{1,5},{2,6},{3,7},{4,0},{5,1},{6,2},{7,3},{8,12},{9,13},{10,... | collective-permute-start | bytes 506888 | tf_op jit(solution)/shard_map/ppermute | solution.py:1114
  1353.4 22.6 %collective-permute-start.53 = (bf16[464,352]{1,0:T(8,128)(2,1)}, bf16[464,352]{1,0:T(8,128)(2,1)S(1)}, u32[]{:S(2)}, u32[]{:S(2)}) collective-permute-start(bf16[464,352]{1,0:T(8,128)(2,1)} %select_select_fusion.28), channel_id=1, source_target_pairs={{0,24},{8,0},{16,8},{24,16},{1,25},{9,1},{17,9},{25,17},{2,26},{10... | collective-permute-start | bytes 979976 | tf_op jit(solution)/shard_map/ppermute | solution.py:1087
  1356.3 29.0 %collective-permute-start.52 = (bf16[464,352]{1,0:T(8,128)(2,1)}, bf16[464,352]{1,0:T(8,128)(2,1)}, u32[]{:S(2)}, u32[]{:S(2)}) collective-permute-start(bf16[464,352]{1,0:T(8,128)(2,1)} %select_select_fusion.29), channel_id=1, source_target_pairs={{0,16},{8,24},{16,0},{24,8},{1,17},{9,25},{17,1},{25,9},{2,18},{10... | collective-permute-start | bytes 979976 | tf_op jit(solution)/shard_map/ppermute | solution.py:1087
  1357.3 28.0 %collective-permute-start.51 = (bf16[464,352]{1,0:T(8,128)(2,1)}, bf16[464,352]{1,0:T(8,128)(2,1)}, u32[]{:S(2)}, u32[]{:S(2)}) collective-permute-start(bf16[464,352]{1,0:T(8,128)(2,1)} %select_select_fusion.30), channel_id=1, source_target_pairs={{0,8},{8,16},{16,24},{24,0},{1,9},{9,17},{17,25},{25,1},{2,10},{10... | collective-permute-start | bytes 979976 | tf_op jit(solution)/shard_map/ppermute | solution.py:1087
  1390.9 11.4 collective-permute-start.48
  1392.8 18.8 %collective-permute-start.49 = (bf16[360,352]{1,0:T(8,128)(2,1)S(1)}, bf16[360,352]{1,0:T(8,128)(2,1)}, u32[]{:S(2)}, u32[]{:S(2)}) collective-permute-start(bf16[360,352]{1,0:T(8,128)(2,1)S(1)} %select_select_fusion.32), channel_id=1, source_target_pairs={{0,16},{8,24},{16,0},{24,8},{1,17},{9,25},{17,1},{25,9},{2,18},{10... | collective-permute-start | bytes 760328 | tf_op jit(solution)/shard_map/ppermute | solution.py:1087
  1394.7 16.9 %collective-permute-start.50 = (bf16[360,352]{1,0:T(8,128)(2,1)}, bf16[360,352]{1,0:T(8,128)(2,1)}, u32[]{:S(2)}, u32[]{:S(2)}) collective-permute-start(bf16[360,352]{1,0:T(8,128)(2,1)} %select_select_fusion.31), channel_id=1, source_target_pairs={{0,24},{8,0},{16,8},{24,16},{1,25},{9,1},{17,9},{25,17},{2,26},{10... | collective-permute-start | bytes 760328 | tf_op jit(solution)/shard_map/ppermute | solution.py:1087
  (104 other events, 1410.9 us)
Sparse Core Ops, SparseCore 0:
  33.6 59.1 all-gather.8
  99.5 87.6 all-gather.10
  189.1 115.5 all-gather.12
  306.4 78.5 all-gather.14
  386.7 112.0 all-gather.16
  500.5 91.7 all-gather.18
  659.5 118.5 reduce-scatter.7
  782.1 149.0 reduce-scatter.5
  934.9 205.3 reduce-scatter.11
  1170.5 89.2 reduce-scatter.9
  1262.3 37.2 all-gather.20
  1303.0 69.4 reduce-scatter.13

commit v8 on v7

--- a/solution.py
+++ b/solution.py
@@ -1418,6 +1418,7 @@
     part_shift = jnp.sum(grad_first.reshape(images, tile_len, model_width), axis=1)
     grad_one = grad_two + norm_back(grad_first * norm_f[:, 0], first_z, first_inv)
 
+    joint_grad, part_shift = lax.optimization_barrier((joint_grad, part_shift))
     shift_low = total_tiles(part_shift).astype(BF16)
     d_shift = left_dot(act_cols, shift_low).astype(BF16)
     grad_time_act = total_tiles(
@@ -1430,8 +1431,8 @@
     low_one = grad_one.astype(BF16)
     d_skip_w = left_dot(skip_in, low_one).astype(BF16)
     d_skip_w, low_one = lax.optimization_barrier((d_skip_w, low_one))
-    t_qkv, d_skip_w, joint_grad, low_join, d_time, d_shift = lax.optimization_barrier(
-        (t_qkv, d_skip_w, joint_grad, low_one, d_time, d_shift)
+    t_qkv, d_skip_w, low_join, d_time, d_shift = lax.optimization_barrier(
+        (t_qkv, d_skip_w, low_one, d_time, d_shift)
     )
     skip_grad, grad_patch, skip_sums = join_back(low_join, f_skip, joined, joined_inv, gain_skip)
     qkv_grad = narrow(t_qkv, skip_sums)

time: 1440 us -> 1420 us (0.986)
    ppermute x18, waiting for transfers between devices: 92.2 us -> 77.5 us  [narrow_blocks(): received.append(lax.ppermute(sent, 'dp', shift_pairs(devices, step)))]
  transfers between devices with their start and end apart: 74 -> 74, of which waited for: 35 -> 35; matrix products, arithmetic and copies ran while one was open for 31% -> 32% of each run, Pallas kernels for 26% -> 26%
where the time goes in v8:
time: 1420 us; the launch traced here: 1410 us
  matrix products  380 us (27%)
  Pallas kernels  366 us (26%)
  waiting for transfers between devices  331 us (23%)
  starting transfers between devices  144 us (10%)
  local copies, waits for them, and re-layouts  81.2 us (6%)
  other arithmetic  74.2 us (5%)
  blocking collectives  17.7 us (1%)
  between operations  16.5 us (1%)
    pallas_call x2, Pallas kernels, attend_back(): kernel_call(functools.partial(attend_back_body, score_scale), 2560 * head...  178 us
    dot_general x11, matrix products, dot_over(): lax.dot_general(left_mat, right_mat, (((left_axis,), (right_axis,)), ((),...  118 us
    dot_general x9, matrix products, plain_dot(): return jnp.dot(left_mat, right_mat, preferred_element_type=jnp.float32)  105 us
    all_to_all x8, waiting for transfers between devices, swap_tiles(): lax.all_to_all(values_in, TILE, split_axis=0, concat_axis=0, tiled=True)  99.9 us
    dot_general x9, matrix products, left_dot(): lax.dot_general(left_mat, right_mat, (((0,), (0,)), ((), ())), preferred_...  91.5 us
    ppermute x21, waiting for transfers between devices, fetch(): lax.ppermute(weight, 'dp', shift_pairs(devices, step))  89.6 us
    ppermute x18, waiting for transfers between devices, narrow_blocks(): received.append(lax.ppermute(sent, 'dp', shift_pairs(devices, step)))  77.5 us
    pallas_call x2, Pallas kernels, attend(): kernel_call(attend_body, 1024 * heads * tiles ** 2 * tile_len ** 2, 8 * q...  68.5 us
  transfers between devices with their start and end apart: 74, of which 35 were waited for; matrix products, arithmetic and copies ran while one was open for 32% of the time, Pallas kernels for 26%

profile of v8, /device:TPU:0, one launch (start us, length us, event | category | flops | bytes accessed | tf_op | source)
XLA Modules:
  0.0 1410.4 jit_solution(6353259681770750884)
XLA Ops:
  14.3 5.7 collective-permute-done.3
  20.1 10.8 collective-permute-done.4
  35.6 6.3 collective-permute-start
  53.7 8.5 collective-permute-done.1
  62.9 17.7 %all-gather = bf16[8,176,60]{1,2,0:T(8,128)(2,1)S(1)} all-gather(bf16[1,176,60]{1,2,0:T(8,128)(2,1)S(1)} %reshape.660), channel_id=1, replica_groups=mesh['dp'=4,'row'=4,'col'=2] {'row','col'}, dimensions={0}, use_global_device_ids=true | all-gather | bytes 190080 | tf_op jit(solution)/shard_map/all_gather | solution.py:1136
  84.1 9.6 shard_map.314
  100.7 21.2 %collective-permute-start.15 = (bf16[176,1056]{1,0:T(8,128)(2,1)S(1)}, bf16[176,1056]{1,0:T(8,128)(2,1)S(1)}, u32[]{:S(2)}, u32[]{:S(2)}) collective-permute-start(bf16[176,1056]{1,0:T(8,128)(2,1)S(1)} %concatenate.112), channel_id=1, source_target_pairs={{0,8},{8,16},{16,24},{24,0},{1,9},{9,17},{17,25},{25,1},{2,10},{10... | collective-permute-start | bytes 1115144 | tf_op jit(solution)/shard_map/ppermute | solution.py:1067
  124.4 7.3 collective-permute-done.15
  131.7 11.3 collective-permute-done.16
  143.0 5.8 collective-permute-done.17
  170.4 8.9 collective-permute-start.18
  183.0 14.3 %fusion.109 = (f32[1024]{0:T(1024)S(1)}, f32[1024,1408]{1,0:T(8,128)S(1)}) fusion(bf16[1024,2816]{1,0:T(8,128)(2,1)} %get-tuple-element.105, bf16[2816,1408]{1,0:T(8,128)(2,1)} %all-gather.9.cloned.1.call-done.weight_ref), kind=kOutput, calls=%fused_computation.317 | convolution fusion | flops 8121613312 | bytes 19468288 | tf_op jit(solution)/shard_map/dot_general | solution.py:72
  206.4 14.7 %shard_map.315 = (bf16[8,3,2,88,512]{4,3,2,1,0:T(8,128)(2,1)}, f32[8,3,2,512]{3,2,1,0:T(2,128)}) custom-call(bf16[512,1408]{1,0:T(8,128)(2,1)} %get-tuple-element.300.rows_ref, bf16[1408,4224]{1,0:T(8,128)(2,1)} %all-gather.11.cloned.1.call-done.weight_ref, f32[88,512]{1,0:T(8,128)} %pad_maximum_fusion.19.cos_ref, f32[88,512]{1,0:T(8,128)} %pad_maximum_fusion.20.sin_ref, ...), custom_call_target="tpu_custom_call" | custom-call | flops 6090129408 | bytes 11894784 | tf_op jit(solution)/shard_map/pallas_call | solution.py:652
  230.8 12.3 collective-permute-done.21
  243.1 22.6 %collective-permute-done.22 = bf16[176,1536]{1,0:T(8,128)(2,1)S(1)} collective-permute-done((bf16[176,1536]{1,0:T(8,128)(2,1)S(1)}, bf16[176,1536]{1,0:T(8,128)(2,1)S(1)}, u32[]{:S(2)}, u32[]{:S(2)}) %collective-permute-start.22) | collective-permute-done | bytes 540704 | tf_op jit(solution)/shard_map/ppermute | solution.py:1067
  265.7 36.8 %all-to-all-done.query_ref.key_ref.value_ref = bf16[8,3,2,88,512]{4,3,2,1,0:T(8,128)(2,1)} async-done(((bf16[8,3,2,88,512]{4,3,2,1,0:T(8,128)(2,1)}), bf16[8,3,2,88,512]{4,3,2,1,0:T(8,128)(2,1)}, u32[]{:S(2)}, u32[]{:S(2)}) %all-to-all-start) | async-done | bytes 4325408 | tf_op jit(solution)/shard_map/all_to_all | solution.py:1057
  304.6 14.7 %shard_map.317 = (bf16[8,3,2,88,512]{4,3,2,1,0:T(8,128)(2,1)}, f32[8,3,2,512]{3,2,1,0:T(2,128)}) custom-call(bf16[512,1408]{1,0:T(8,128)(2,1)} %get-tuple-element.301.rows_ref, bf16[1408,4224]{1,0:T(8,128)(2,1)} %all-gather.11.cloned.1.call-done.weight_ref, f32[88,512]{1,0:T(8,128)} %pad_maximum_fusion.19.cos_ref, f32[88,512]{1,0:T(8,128)} %pad_maximum_fusion.20.sin_ref, ...), custom_call_target="tpu_custom_call" | custom-call | flops 6090129408 | bytes 11894784 | tf_op jit(solution)/shard_map/pallas_call | solution.py:652
  324.7 34.0 %shard_map.316 = (bf16[8,2,88,512]{3,2,1,0:T(8,128)(2,1)}, f32[8,2,1,512]{3,2,1,0:T(1,128)}) custom-call(bf16[8,3,2,88,512]{4,3,2,1,0:T(8,128)(2,1)} %all-to-all-done.query_ref.key_ref.value_ref, bf16[8,3,2,88,512]{4,3,2,1,0:T(8,128)(2,1)} %all-to-all-done.query_ref.key_ref.value_ref, bf16[8,3,2,88,512]{4,3,2,1,0:T(8,128)(2,1)} %all-to-all-done.query_ref.key_ref.value_ref, ...), custom_call_target="tpu_custom_call" | custom-call | flops 34359738368 | bytes 17301504 | tf_op jit(solution)/shard_map/pallas_call | solution.py:757
  358.8 30.2 %all-to-all-done.2.query_ref.key_ref.value_ref = bf16[8,3,2,88,512]{4,3,2,1,0:T(8,128)(2,1)} async-done(((bf16[8,3,2,88,512]{4,3,2,1,0:T(8,128)(2,1)}), bf16[8,3,2,88,512]{4,3,2,1,0:T(8,128)(2,1)}, u32[]{:S(2)}, u32[]{:S(2)}) %all-to-all-start.2) | async-done | bytes 4325408 | tf_op jit(solution)/shard_map/all_to_all | solution.py:1057
  392.6 34.5 %shard_map.318 = (bf16[8,2,88,512]{3,2,1,0:T(8,128)(2,1)}, f32[8,2,1,512]{3,2,1,0:T(1,128)}) custom-call(bf16[8,3,2,88,512]{4,3,2,1,0:T(8,128)(2,1)} %all-to-all-done.2.query_ref.key_ref.value_ref, bf16[8,3,2,88,512]{4,3,2,1,0:T(8,128)(2,1)} %all-to-all-done.2.query_ref.key_ref.value_ref, ...), custom_call_target="tpu_custom_call" | custom-call | flops 34359738368 | bytes 17301504 | tf_op jit(solution)/shard_map/pallas_call | solution.py:757
  436.6 21.5 %all-to-all-done.3 = bf16[8,2,88,512]{3,2,1,0:T(8,128)(2,1)S(1)} async-done(((bf16[8,2,88,512]{3,2,1,0:T(8,128)(2,1)}), bf16[8,2,88,512]{3,2,1,0:T(8,128)(2,1)S(1)}, u32[]{:S(2)}, u32[]{:S(2)}) %all-to-all-start.3) | async-done | bytes 1441824 | tf_op jit(solution)/shard_map/all_to_all | solution.py:1057
  458.1 10.5 fusion.110
  475.9 9.8 fusion.113
  486.4 9.3 fusion.10
  495.7 14.6 %shard_map.319 = (bf16[16,88,1024]{2,1,0:T(8,128)(2,1)}, bf16[16,88,1024]{2,1,0:T(8,128)(2,1)}, f32[16,1,1024]{2,1,0:T(1,128)}, f32[16,1,1024]{2,1,0:T(1,128)}) custom-call(f32[16,88,1024]{2,1,0:T(8,128)} %bitcast.210, f32[2,16,88,768]{3,2,1,0:T(8,128)} %bitcast.187), custom_call_target="tpu_custom_call" | custom-call | flops 6442450944 | bytes 11534336 | tf_op jit(solution)/shard_map/pallas_call | solution.py:897
  510.3 9.2 fusion.111
  522.8 39.8 %add_convert_fusion = (bf16[1024,6144]{1,0:T(8,128)(2,1)}, bf16[1024,6144]{1,0:T(8,128)(2,1)}) fusion(bf16[1408,6144]{1,0:T(8,128)(2,1)} %all-gather.17.cloned.1.call-done, f32[1024,1408]{1,0:T(8,128)} %copy-done.2, f32[1408]{0:T(1024)S(1)} %copy-done.78, f32[1408]{0:T(1024)S(1)} %copy-done.54, f32[1024]{0:T(1024)S(1)} %add_rsqrt_fusion.2, ...), kind=kOutput, calls=%fused_computation.1 | convolution fusion | flops 17843486720 | bytes 48253952 | tf_op jit(solution)/shard_map/dot_general | solution.py:72
  562.7 29.7 %all-gather.19.cloned.1.call-done = bf16[6144,1408]{0,1:T(8,128)(2,1)} async-done(((bf16[768,1408]{0,1:T(8,128)(2,1)}), bf16[6144,1408]{0,1:T(8,128)(2,1)}) %all-gather.19.cloned.1.call-update) | async-done | bytes 17301520 | tf_op jit(solution)/shard_map/all_gather | solution.py:1136
  592.3 28.8 %fusion.112 = (f32[1024]{0:T(1024)S(1)}, f32[1024,1408]{1,0:T(8,128)S(1)}) fusion(f32[1024,1408]{1,0:T(8,128)} %copy-done.2, bf16[1024,6144]{1,0:T(8,128)(2,1)} %get-tuple-element.127, bf16[6144,1408]{0,1:T(8,128)(2,1)} %all-gather.19.cloned.1.call-done), kind=kOutput, calls=%fused_computation.320 | convolution fusion | flops 17719623680 | bytes 41422848 | tf_op jit(solution)/shard_map/dot_general | solution.py:72
  631.4 27.9 %convolution_convert_fusion = bf16[6144,1408]{1,0:T(8,128)(2,1)} fusion(bf16[1024,6144]{1,0:T(8,128)(2,1)} %get-tuple-element.127, bf16[1024,1408]{1,0:T(8,128)(2,1)S(1)} %get-tuple-element.132), kind=kOutput, calls=%fused_computation.5 | convolution fusion | flops 17725390848 | bytes 32768000 | tf_op jit(solution)/shard_map/dot_general | solution.py:76
  661.1 30.5 %multiply_convert_fusion = bf16[1024,6144]{1,0:T(8,128)(2,1)} fusion(bf16[1024,6144]{1,0:T(8,128)(2,1)} %get-tuple-element.133, bf16[1024,1408]{1,0:T(8,128)(2,1)S(1)} %copy-done.18, bf16[6144,1408]{0,1:T(8,128)(2,1)} %all-gather.19.cloned.1.call-done), kind=kOutput, calls=%fused_computation | convolution fusion | flops 17735614464 | bytes 45350912 | tf_op jit(solution)/shard_map/dot_general | solution.py:82
  691.6 26.1 %convolution_convert_fusion.1 = bf16[1408,6144]{1,0:T(8,128)(2,1)} fusion(bf16[1024,6144]{1,0:T(8,128)(2,1)} %multiply_convert_fusion, f32[1024,1408]{1,0:T(8,128)} %copy-done.2, f32[1408]{0:T(1024)S(1)} %copy-done.78, f32[1408]{0:T(1024)S(1)} %copy-done.54, f32[1024]{0:T(1024)S(1)} %add_rsqrt_fusion.2, f32[1024]{0:T(1024)S(1)} %broadcast_multiply_fusion.12), kind=kOutput, calls=%fused_computation.6 | convolution fusion | flops 17732599808 | bytes 35671040 | tf_op jit(solution)/shard_map/dot_general | solution.py:76
  717.8 31.5 %multiply_reduce_fusion.1 = (f32[1408]{0:T(1024)}, f32[1024]{0:T(1024)S(1)}, f32[1024]{0:T(1024)S(1)}, f32[1408]{0:T(1024)}, f32[1024,1408]{1,0:T(8,128)}) fusion(f32[1024,1408]{1,0:T(8,128)} %copy-done.2, f32[1024]{0:T(1024)S(1)} %add_rsqrt_fusion.2, f32[1024]{0:T(1024)S(1)} %broadcast_multiply_fusion.12, f32[1408]{0:T(1024)S(1)} %copy-done.54, ...), kind=kOutput, calls=%fused_computation.19 | convolution fusion | flops 17729710080 | bytes 41452032 | tf_op jit(solution)/shard_map/dot_general | solution.py:82
  749.2 7.7 multiply_add_fusion.1
  756.9 10.6 convolution_convert_fusion.7
  767.5 21.3 %shard_map.320 = (bf16[16,88,1024]{2,1,0:T(8,128)(2,1)}, bf16[16,88,768]{2,1,0:T(8,128)(2,1)}, bf16[16,88,768]{2,1,0:T(8,128)(2,1)}) custom-call(bf16[16,88,1024]{2,1,0:T(8,128)(2,1)} %get-tuple-element.136.query_ref, f32[2,16,88,768]{3,2,1,0:T(8,128)} %bitcast.188, bf16[16,88,1024]{2,1,0:T(8,128)(2,1)} %bitcast.215, ...), custom_call_target="tpu_custom_call" | custom-call | flops 16106127360 | bytes 23068672 | tf_op jit(solution)/shard_map/pallas_call | solution.py:957
  788.9 14.3 %multiply_reduce_fusion.2 = (f32[1408]{0:T(1024)}, f32[1024]{0:T(1024)S(1)}, f32[1024]{0:T(1024)S(1)}, f32[1408]{0:T(1024)}, f32[1024,1408]{1,0:T(8,128)S(1)}) fusion(f32[1024,1408]{1,0:T(8,128)} %get-tuple-element.416, f32[1024]{0:T(1024)S(1)} %copy-done.63, f32[1024]{0:T(1024)S(1)} %copy-done.51, f32[1408]{0:T(1024)S(1)} %copy-done.53, ...), kind=kOutput, calls=%fused_computation.20 | convolution fusion | flops 4073057280 | bytes 18416128 | tf_op jit(solution)/shard_map/dot_general | solution.py:1144
  803.2 6.3 fusion.93
  809.5 6.8 fusion.17
  820.9 8.6 fusion.2
  829.5 9.8 fusion.1
  839.4 6.2 fusion
  849.5 5.6 all-to-all-done.4.grad_ref
  863.7 6.3 fusion.20
  874.3 89.2 %shard_map.321 = bf16[8,3,2,88,512]{4,3,2,1,0:T(8,128)(2,1)} custom-call(bf16[8,3,2,88,512]{4,3,2,1,0:T(8,128)(2,1)} %all-to-all-done.query_ref.key_ref.value_ref, bf16[8,3,2,88,512]{4,3,2,1,0:T(8,128)(2,1)} %all-to-all-done.query_ref.key_ref.value_ref, bf16[8,3,2,88,512]{4,3,2,1,0:T(8,128)(2,1)} %all-to-all-done.query_ref.key_ref.value_ref, ...), custom_call_target="tpu_custom_call" | custom-call | flops 85899345920 | bytes 17301504 | tf_op jit(solution)/shard_map/pallas_call | solution.py:845
  975.5 89.1 %shard_map.322 = bf16[8,3,2,88,512]{4,3,2,1,0:T(8,128)(2,1)} custom-call(bf16[8,3,2,88,512]{4,3,2,1,0:T(8,128)(2,1)} %all-to-all-done.2.query_ref.key_ref.value_ref, bf16[8,3,2,88,512]{4,3,2,1,0:T(8,128)(2,1)} %all-to-all-done.2.query_ref.key_ref.value_ref, bf16[8,3,2,88,512]{4,3,2,1,0:T(8,128)(2,1)} %all-to-all-done.2.query_ref.key_ref.value_ref, ...), custom_call_target="tpu_custom_call" | custom-call | flops 85899345920 | bytes 17301504 | tf_op jit(solution)/shard_map/pallas_call | solution.py:845
  1078.2 10.3 collective-permute-done.30
  1088.4 11.0 collective-permute-done.32
  1099.4 23.2 %collective-permute-done.31 = bf16[176,1536]{1,0:T(8,128)(2,1)S(1)} collective-permute-done((bf16[176,1536]{1,0:T(8,128)(2,1)S(1)}, bf16[176,1536]{1,0:T(8,128)(2,1)S(1)}, u32[]{:S(2)}, u32[]{:S(2)}) %collective-permute-start.31) | collective-permute-done | bytes 540704 | tf_op jit(solution)/shard_map/ppermute | solution.py:1087
  1124.0 10.1 shard_map.323.others_0_
  1134.1 5.9 all-to-all-done.6.grad_ref
  1140.0 10.2 shard_map.324
  1150.3 19.9 %convolution_convert_fusion.2 = bf16[1408,4224]{1,0:T(8,128)(2,1)} fusion(bf16[1024,1408]{1,0:T(8,128)(2,1)S(1)} %copy-done.12, bf16[4224,1024]{1,0:T(8,128)(2,1)} %bitcast.165), kind=kOutput, calls=%fused_computation.7 | convolution fusion | flops 12186206208 | bytes 23429120 | tf_op jit(solution)/shard_map/dot_general | solution.py:1144
  1189.9 23.9 %multiply_reduce_fusion.3 = (f32[1408]{0:T(1024)}, f32[1024]{0:T(1024)S(1)}, f32[1024]{0:T(1024)S(1)}, f32[1408]{0:T(1024)}, f32[1024,1408]{1,0:T(8,128)S(1)}) fusion(f32[1024,1408]{1,0:T(8,128)} %copy-done, f32[1024]{0:T(1024)S(1)} %copy-done.49, f32[1024]{0:T(1024)S(1)} %copy-done.47, f32[1408]{0:T(1024)S(1)} %copy-done.45, ...), kind=kOutput, calls=%fused_computation.21 | convolution fusion | flops 12193230848 | bytes 32113152 | tf_op jit(solution)/shard_map/dot_general | solution.py:1144
  1230.1 7.1 add_convert_fusion.1.low_ref
  1238.7 14.8 %convolution_convert_fusion.3 = bf16[2816,1408]{1,0:T(8,128)(2,1)} fusion(bf16[1024,2816]{1,0:T(8,128)(2,1)} %get-tuple-element.105, bf16[1024,1408]{1,0:T(8,128)(2,1)S(1)} %add_convert_fusion.1.low_ref), kind=kOutput, calls=%fused_computation.8 | convolution fusion | flops 8124137472 | bytes 16580608 | tf_op jit(solution)/shard_map/dot_general | solution.py:76
  1253.6 5.8 reduce-scatter.10.cloned.1.call-done
  1284.1 23.7 %shard_map.325 = (f32[1024,1408]{1,0:T(8,128)}, bf16[1024,1408]{1,0:T(8,128)(2,1)}, f32[2,2816]{1,0:T(2,128)}) custom-call(bf16[1024,1408]{1,0:T(8,128)(2,1)} %copy-done.15, bf16[2816,1408]{1,0:T(8,128)(2,1)} %all-gather.9.cloned.1.call-done.weight_ref, f32[1024,2816]{1,0:T(8,128)} %get-tuple-element.171.z_ref, f32[1024,1]{1,0:T(8,128)} %get-tuple-element.172.inv_ref, ...), custom_call_target="tpu_custom_call" | custom-call | flops 8120172544 | bytes 25952256 | tf_op jit(solution)/shard_map/pallas_call | solution.py:1032
  1308.2 8.8 collective-permute-done.43
  1333.6 6.8 copy.172
  1353.5 8.4 collective-permute-done.52
  1364.7 8.9 reduce-scatter.14.cloned.1.call-done
  1382.8 5.1 collective-permute-done.48
  1388.0 10.7 collective-permute-done.49
  (555 shorter events, 281.3 us)
Async XLA Ops:
  7.2 175.7 %all-gather.9.cloned.1.call-start = ((), (), s32[]{:S(2)}) async-start(), calls=%async_computation.13 | async-start | bytes 8921088 | tf_op jit(solution)/shard_map/all_gather | solution.py:1136
  7.3 12.8 collective-permute-start.3
  10.4 20.4 %collective-permute-start.4 = (bf16[352,352]{1,0:T(8,128)(2,1)}, bf16[352,352]{1,0:T(8,128)(2,1)S(1)}, u32[]{:S(2)}, u32[]{:S(2)}) collective-permute-start(bf16[352,352]{1,0:T(8,128)(2,1)} %param.26), channel_id=1, source_target_pairs={{0,16},{8,24},{16,0},{24,8},{1,17},{9,25},{17,1},{25,9},{2,18},{10... | collective-permute-start | bytes 743432 | tf_op jit(solution)/shard_map/ppermute | solution.py:1067
  13.0 17.9 %collective-permute-start.5 = (bf16[352,352]{1,0:T(8,128)(2,1)}, bf16[352,352]{1,0:T(8,128)(2,1)S(1)}, u32[]{:S(2)}, u32[]{:S(2)}) collective-permute-start(bf16[352,352]{1,0:T(8,128)(2,1)} %param.26), channel_id=1, source_target_pairs={{0,24},{8,0},{16,8},{24,16},{1,25},{9,1},{17,9},{25,17},{2,26},{10... | collective-permute-start | bytes 743432 | tf_op jit(solution)/shard_map/ppermute | solution.py:1067
  33.5 172.9 %all-gather.11.cloned.1.call-start = ((), (), s32[]{:S(2)}) async-start(), calls=%async_computation.14 | async-start | bytes 13381632 | tf_op jit(solution)/shard_map/all_gather | solution.py:1136
  35.6 14.9 %collective-permute-start = (bf16[384,352]{0,1:T(8,128)(2,1)S(1)}, bf16[384,352]{0,1:T(8,128)(2,1)S(1)}, u32[]{:S(2)}, u32[]{:S(2)}) collective-permute-start(bf16[384,352]{0,1:T(8,128)(2,1)S(1)} %pad_maximum_fusion.18), channel_id=1, source_target_pairs={{0,8},{8,16},{16,24},{24,0},{1,9},{9,17},{17,25},{25,1},{2,10},{10... | collective-permute-start | bytes 811016 | tf_op jit(solution)/shard_map/ppermute | solution.py:1067
  41.9 20.2 %collective-permute-start.1 = (bf16[384,352]{0,1:T(8,128)(2,1)S(1)}, bf16[384,352]{0,1:T(8,128)(2,1)S(1)}, u32[]{:S(2)}, u32[]{:S(2)}) collective-permute-start(bf16[384,352]{0,1:T(8,128)(2,1)S(1)} %pad_maximum_fusion.18), channel_id=1, source_target_pairs={{0,16},{8,24},{16,0},{24,8},{1,17},{9,25},{17,1},{25,9},{2,18},{10... | collective-permute-start | bytes 811016 | tf_op jit(solution)/shard_map/ppermute | solution.py:1067
  43.5 18.6 %collective-permute-start.2 = (bf16[384,352]{0,1:T(8,128)(2,1)S(1)}, bf16[384,352]{0,1:T(8,128)(2,1)S(1)}, u32[]{:S(2)}, u32[]{:S(2)}) collective-permute-start(bf16[384,352]{0,1:T(8,128)(2,1)S(1)} %pad_maximum_fusion.18), channel_id=1, source_target_pairs={{0,24},{8,0},{16,8},{24,16},{1,25},{9,1},{17,9},{25,17},{2,26},{10... | collective-permute-start | bytes 811016 | tf_op jit(solution)/shard_map/ppermute | solution.py:1067
  44.4 49.3 %collective-permute-start.12 = (bf16[176,1056]{1,0:T(8,128)(2,1)S(1)}, bf16[176,1056]{1,0:T(8,128)(2,1)S(1)}, u32[]{:S(2)}, u32[]{:S(2)}) collective-permute-start(bf16[176,1056]{1,0:T(8,128)(2,1)S(1)} %copy-done.36), channel_id=1, source_target_pairs={{0,8},{8,16},{16,24},{24,0},{1,9},{9,17},{17,25},{25,1},{2,10},{10... | collective-permute-start | bytes 1115144 | tf_op jit(solution)/shard_map/ppermute | solution.py:1067
  45.6 48.2 %collective-permute-start.13 = (bf16[176,1056]{1,0:T(8,128)(2,1)S(1)}, bf16[176,1056]{1,0:T(8,128)(2,1)S(1)}, u32[]{:S(2)}, u32[]{:S(2)}) collective-permute-start(bf16[176,1056]{1,0:T(8,128)(2,1)S(1)} %copy-done.36), channel_id=1, source_target_pairs={{0,16},{8,24},{16,0},{24,8},{1,17},{9,25},{17,1},{25,9},{2,18},{10... | collective-permute-start | bytes 1115144 | tf_op jit(solution)/shard_map/ppermute | solution.py:1067
  50.5 43.2 %collective-permute-start.14 = (bf16[176,1056]{1,0:T(8,128)(2,1)S(1)}, bf16[176,1056]{1,0:T(8,128)(2,1)S(1)}, u32[]{:S(2)}, u32[]{:S(2)}) collective-permute-start(bf16[176,1056]{1,0:T(8,128)(2,1)S(1)} %copy-done.36), channel_id=1, source_target_pairs={{0,24},{8,0},{16,8},{24,16},{1,25},{9,1},{17,9},{25,17},{2,26},{10... | collective-permute-start | bytes 1115144 | tf_op jit(solution)/shard_map/ppermute | solution.py:1067
  99.4 337.2 %all-gather.13.cloned.1.call-start = ((), (), s32[]{:S(2)}) async-start(), calls=%async_computation.15 | async-start | bytes 13381632 | tf_op jit(solution)/shard_map/all_gather | solution.py:1136
  100.7 31.0 %collective-permute-start.15 = (bf16[176,1056]{1,0:T(8,128)(2,1)S(1)}, bf16[176,1056]{1,0:T(8,128)(2,1)S(1)}, u32[]{:S(2)}, u32[]{:S(2)}) collective-permute-start(bf16[176,1056]{1,0:T(8,128)(2,1)S(1)} %concatenate.112), channel_id=1, source_target_pairs={{0,8},{8,16},{16,24},{24,0},{1,9},{9,17},{17,25},{25,1},{2,10},{10... | collective-permute-start | bytes 1115144 | tf_op jit(solution)/shard_map/ppermute | solution.py:1067
  121.9 21.1 %collective-permute-start.16 = (bf16[176,1056]{1,0:T(8,128)(2,1)S(1)}, bf16[176,1056]{1,0:T(8,128)(2,1)S(1)}, u32[]{:S(2)}, u32[]{:S(2)}) collective-permute-start(bf16[176,1056]{1,0:T(8,128)(2,1)S(1)} %concatenate.112), channel_id=1, source_target_pairs={{0,16},{8,24},{16,0},{24,8},{1,17},{9,25},{17,1},{25,9},{2,18},{10... | collective-permute-start | bytes 1115144 | tf_op jit(solution)/shard_map/ppermute | solution.py:1067
  121.9 26.9 %collective-permute-start.17 = (bf16[176,1056]{1,0:T(8,128)(2,1)S(1)}, bf16[176,1056]{1,0:T(8,128)(2,1)S(1)}, u32[]{:S(2)}, u32[]{:S(2)}) collective-permute-start(bf16[176,1056]{1,0:T(8,128)(2,1)S(1)} %concatenate.112), channel_id=1, source_target_pairs={{0,24},{8,0},{16,8},{24,16},{1,25},{9,1},{17,9},{25,17},{2,26},{10... | collective-permute-start | bytes 1115144 | tf_op jit(solution)/shard_map/ppermute | solution.py:1067
  153.4 322.5 %all-gather.15.cloned.1.call-start = ((), (), s32[]{:S(2)}) async-start(), calls=%async_computation.16 | async-start | bytes 6488064 | tf_op jit(solution)/shard_map/all_gather | solution.py:1136
  169.2 13.7 collective-permute-start.11
  170.4 29.4 %collective-permute-start.18 = (bf16[128,704]{0,1:T(8,128)(2,1)S(1)}, bf16[128,704]{0,1:T(8,128)(2,1)S(1)}, u32[]{:S(2)}, u32[]{:S(2)}) collective-permute-start(bf16[128,704]{0,1:T(8,128)(2,1)S(1)} %copy-done.40), channel_id=1, source_target_pairs={{0,8},{8,16},{16,24},{24,0},{1,9},{9,17},{17,25},{25,1},{2,10},{10... | collective-permute-start | bytes 540680 | tf_op jit(solution)/shard_map/ppermute | solution.py:1067
  179.3 20.5 %collective-permute-start.19 = (bf16[128,704]{0,1:T(8,128)(2,1)S(1)}, bf16[128,704]{0,1:T(8,128)(2,1)S(1)}, u32[]{:S(2)}, u32[]{:S(2)}) collective-permute-start(bf16[128,704]{0,1:T(8,128)(2,1)S(1)} %copy-done.40), channel_id=1, source_target_pairs={{0,16},{8,24},{16,0},{24,8},{1,17},{9,25},{17,1},{25,9},{2,18},{10... | collective-permute-start | bytes 540680 | tf_op jit(solution)/shard_map/ppermute | solution.py:1067
  182.7 17.1 %collective-permute-start.20 = (bf16[128,704]{0,1:T(8,128)(2,1)S(1)}, bf16[128,704]{0,1:T(8,128)(2,1)}, u32[]{:S(2)}, u32[]{:S(2)}) collective-permute-start(bf16[128,704]{0,1:T(8,128)(2,1)S(1)} %copy-done.40), channel_id=1, source_target_pairs={{0,24},{8,0},{16,8},{24,16},{1,25},{9,1},{17,9},{25,17},{2,26},{10... | collective-permute-start | bytes 540680 | tf_op jit(solution)/shard_map/ppermute | solution.py:1067
  221.1 81.4 %all-to-all-start = ((bf16[8,3,2,88,512]{4,3,2,1,0:T(8,128)(2,1)}), bf16[8,3,2,88,512]{4,3,2,1,0:T(8,128)(2,1)}, u32[]{:S(2)}, u32[]{:S(2)}) async-start(bf16[8,3,2,88,512]{4,3,2,1,0:T(8,128)(2,1)} %get-tuple-element.110.own_ref), calls=%async_computation | async-start | bytes 8650752 | tf_op jit(solution)/shard_map/all_to_all | solution.py:1057
  226.0 296.8 %all-gather.17.cloned.1.call-start = ((), (), s32[]{:S(2)}) async-start(), calls=%async_computation.17 | async-start | bytes 19464192 | tf_op jit(solution)/shard_map/all_gather | solution.py:1136
  226.0 17.1 %collective-permute-start.21 = (bf16[176,1536]{1,0:T(8,128)(2,1)S(1)}, bf16[176,1536]{1,0:T(8,128)(2,1)S(1)}, u32[]{:S(2)}, u32[]{:S(2)}) collective-permute-start(bf16[176,1536]{1,0:T(8,128)(2,1)S(1)} %copy-done.32), channel_id=1, source_target_pairs={{0,8},{8,16},{16,24},{24,0},{1,9},{9,17},{17,25},{25,1},{2,10},{10... | collective-permute-start | bytes 1622024 | tf_op jit(solution)/shard_map/ppermute | solution.py:1067
  228.0 37.7 %collective-permute-start.22 = (bf16[176,1536]{1,0:T(8,128)(2,1)S(1)}, bf16[176,1536]{1,0:T(8,128)(2,1)S(1)}, u32[]{:S(2)}, u32[]{:S(2)}) collective-permute-start(bf16[176,1536]{1,0:T(8,128)(2,1)S(1)} %copy-done.32), channel_id=1, source_target_pairs={{0,16},{8,24},{16,0},{24,8},{1,17},{9,25},{17,1},{25,9},{2,18},{10... | collective-permute-start | bytes 1622024 | tf_op jit(solution)/shard_map/ppermute | solution.py:1067
  228.7 37.0 %collective-permute-start.23 = (bf16[176,1536]{1,0:T(8,128)(2,1)S(1)}, bf16[176,1536]{1,0:T(8,128)(2,1)S(1)}, u32[]{:S(2)}, u32[]{:S(2)}) collective-permute-start(bf16[176,1536]{1,0:T(8,128)(2,1)S(1)} %copy-done.32), channel_id=1, source_target_pairs={{0,24},{8,0},{16,8},{24,16},{1,25},{9,1},{17,9},{25,17},{2,26},{10... | collective-permute-start | bytes 1622024 | tf_op jit(solution)/shard_map/ppermute | solution.py:1067
  319.3 69.7 %all-to-all-start.2 = ((bf16[8,3,2,88,512]{4,3,2,1,0:T(8,128)(2,1)}), bf16[8,3,2,88,512]{4,3,2,1,0:T(8,128)(2,1)}, u32[]{:S(2)}, u32[]{:S(2)}) async-start(bf16[8,3,2,88,512]{4,3,2,1,0:T(8,128)(2,1)} %get-tuple-element.112.own_ref), calls=%async_computation.2 | async-start | bytes 8650752 | tf_op jit(solution)/shard_map/all_to_all | solution.py:1057
  389.0 38.1 %all-to-all-start.1 = ((bf16[8,2,88,512]{3,2,1,0:T(8,128)(2,1)}), bf16[8,2,88,512]{3,2,1,0:T(8,128)(2,1)S(1)}, u32[]{:S(2)}, u32[]{:S(2)}) async-start(bf16[8,2,88,512]{3,2,1,0:T(8,128)(2,1)} %get-tuple-element.111.att_ref), calls=%async_computation.1 | async-start | bytes 2883584 | tf_op jit(solution)/shard_map/all_to_all | solution.py:1057
  427.0 31.0 %all-to-all-start.3 = ((bf16[8,2,88,512]{3,2,1,0:T(8,128)(2,1)}), bf16[8,2,88,512]{3,2,1,0:T(8,128)(2,1)S(1)}, u32[]{:S(2)}, u32[]{:S(2)}) async-start(bf16[8,2,88,512]{3,2,1,0:T(8,128)(2,1)} %get-tuple-element.113.att_ref), calls=%async_computation.3 | async-start | bytes 2883584 | tf_op jit(solution)/shard_map/all_to_all | solution.py:1057
  431.2 161.2 %all-gather.19.cloned.1.call-start = ((), (), s32[]{:S(2)}) async-start(), calls=%async_computation.18 | async-start | bytes 19464192 | tf_op jit(solution)/shard_map/all_gather | solution.py:1136
  431.2 37.3 %collective-permute-start.24 = (bf16[768,352]{0,1:T(8,128)(2,1)S(1)}, bf16[768,352]{0,1:T(8,128)(2,1)}, u32[]{:S(2)}, u32[]{:S(2)}) collective-permute-start(bf16[768,352]{0,1:T(8,128)(2,1)S(1)} %copy-done.33), channel_id=1, source_target_pairs={{0,8},{8,16},{16,24},{24,0},{1,9},{9,17},{17,25},{25,1},{2,10},{10... | collective-permute-start | bytes 1622024 | tf_op jit(solution)/shard_map/ppermute | solution.py:1067
  432.7 38.4 %collective-permute-start.25 = (bf16[768,352]{0,1:T(8,128)(2,1)S(1)}, bf16[768,352]{0,1:T(8,128)(2,1)}, u32[]{:S(2)}, u32[]{:S(2)}) collective-permute-start(bf16[768,352]{0,1:T(8,128)(2,1)S(1)} %copy-done.33), channel_id=1, source_target_pairs={{0,16},{8,24},{16,0},{24,8},{1,17},{9,25},{17,1},{25,9},{2,18},{10... | collective-permute-start | bytes 1622024 | tf_op jit(solution)/shard_map/ppermute | solution.py:1067
  435.2 35.9 %collective-permute-start.26 = (bf16[768,352]{0,1:T(8,128)(2,1)S(1)}, bf16[768,352]{0,1:T(8,128)(2,1)}, u32[]{:S(2)}, u32[]{:S(2)}) collective-permute-start(bf16[768,352]{0,1:T(8,128)(2,1)S(1)} %copy-done.33), channel_id=1, source_target_pairs={{0,24},{8,0},{16,8},{24,16},{1,25},{9,1},{17,9},{25,17},{2,26},{10... | collective-permute-start | bytes 1622024 | tf_op jit(solution)/shard_map/ppermute | solution.py:1067
  474.2 314.6 %reduce-scatter.8.cloned.1.call-start = ((), (), s32[]{:S(2)}) async-start(), calls=%async_computation.20 | async-start | bytes 19464192 | tf_op jit(solution)/shard_map/reduce_scatter | solution.py:1131
  659.3 410.0 %reduce-scatter.6.cloned.1.call-start = ((), (), s32[]{:S(2)}) async-start(), calls=%async_computation.19 | async-start | bytes 19464192 | tf_op jit(solution)/shard_map/reduce_scatter | solution.py:1131
  816.2 38.8 %all-to-all-start.4 = ((bf16[8,2,88,512]{3,2,1,0:T(8,128)(2,1)}), bf16[8,2,88,512]{3,2,1,0:T(8,128)(2,1)}, u32[]{:S(2)}, u32[]{:S(2)}) async-start(bf16[8,2,88,512]{3,2,1,0:T(8,128)(2,1)} %bitcast.199), calls=%async_computation.6 | async-start | bytes 2883584 | tf_op jit(solution)/shard_map/all_to_all | solution.py:1057
  820.6 354.2 %reduce-scatter.12.cloned.1.call-start = ((), (), s32[]{:S(2)}) async-start(), calls=%async_computation.22 | async-start | bytes 18247680 | tf_op jit(solution)/shard_map/reduce_scatter | solution.py:1131
  856.9 106.6 %collective-permute-start.27 = (bf16[768,352]{0,1:T(8,128)(2,1)}, bf16[768,352]{0,1:T(8,128)(2,1)S(1)}, u32[]{:S(2)}, u32[]{:S(2)}) collective-permute-start(bf16[768,352]{0,1:T(8,128)(2,1)} %copy.133), channel_id=1, source_target_pairs={{0,8},{8,16},{16,24},{24,0},{1,9},{9,17},{17,25},{25,1},{2,10},{10... | collective-permute-start | bytes 1622024 | tf_op jit(solution)/shard_map/ppermute | solution.py:1087
  858.9 104.6 %collective-permute-start.29 = (bf16[768,352]{0,1:T(8,128)(2,1)}, bf16[768,352]{0,1:T(8,128)(2,1)}, u32[]{:S(2)}, u32[]{:S(2)}) collective-permute-start(bf16[768,352]{0,1:T(8,128)(2,1)} %copy.135), channel_id=1, source_target_pairs={{0,24},{8,0},{16,8},{24,16},{1,25},{9,1},{17,9},{25,17},{2,26},{10... | collective-permute-start | bytes 1622024 | tf_op jit(solution)/shard_map/ppermute | solution.py:1087
  863.6 99.9 %collective-permute-start.28 = (bf16[768,352]{0,1:T(8,128)(2,1)}, bf16[768,352]{0,1:T(8,128)(2,1)}, u32[]{:S(2)}, u32[]{:S(2)}) collective-permute-start(bf16[768,352]{0,1:T(8,128)(2,1)} %copy.134), channel_id=1, source_target_pairs={{0,16},{8,24},{16,0},{24,8},{1,17},{9,25},{17,1},{25,9},{2,18},{10... | collective-permute-start | bytes 1622024 | tf_op jit(solution)/shard_map/ppermute | solution.py:1087
  870.0 100.6 %all-to-all-start.5 = ((bf16[8,2,88,512]{3,2,1,0:T(8,128)(2,1)}), bf16[8,2,88,512]{3,2,1,0:T(8,128)(2,1)}, u32[]{:S(2)}, u32[]{:S(2)}) async-start(bf16[8,2,88,512]{3,2,1,0:T(8,128)(2,1)} %bitcast.198), calls=%async_computation.7 | async-start | bytes 2883584 | tf_op jit(solution)/shard_map/all_to_all | solution.py:1057
  970.5 94.1 %all-to-all-start.7 = ((bf16[8,3,2,88,512]{4,3,2,1,0:T(8,128)(2,1)}), bf16[8,3,2,88,512]{4,3,2,1,0:T(8,128)(2,1)}, u32[]{:S(2)}, u32[]{:S(2)}) async-start(bf16[8,3,2,88,512]{4,3,2,1,0:T(8,128)(2,1)} %shard_map.321), calls=%async_computation.9 | async-start | bytes 8650752 | tf_op jit(solution)/shard_map/all_to_all | solution.py:1057
  1064.6 75.4 %all-to-all-start.6 = ((bf16[8,3,2,88,512]{4,3,2,1,0:T(8,128)(2,1)}), bf16[8,3,2,88,512]{4,3,2,1,0:T(8,128)(2,1)}, u32[]{:S(2)}, u32[]{:S(2)}) async-start(bf16[8,3,2,88,512]{4,3,2,1,0:T(8,128)(2,1)} %shard_map.322), calls=%async_computation.8 | async-start | bytes 8650752 | tf_op jit(solution)/shard_map/all_to_all | solution.py:1057
  1069.2 190.2 %reduce-scatter.10.cloned.1.call-start = ((), (), s32[]{:S(2)}) async-start(), calls=%async_computation.21 | async-start | bytes 13381632 | tf_op jit(solution)/shard_map/reduce_scatter | solution.py:1131
  1071.4 17.0 %collective-permute-start.30 = (bf16[176,1536]{1,0:T(8,128)(2,1)S(1)}, bf16[176,1536]{1,0:T(8,128)(2,1)S(1)}, u32[]{:S(2)}, u32[]{:S(2)}) collective-permute-start(bf16[176,1536]{1,0:T(8,128)(2,1)S(1)} %get-tuple-element.303), channel_id=1, source_target_pairs={{0,8},{8,16},{16,24},{24,0},{1,9},{9,17},{17,25},{25,1},{2,10},{10... | collective-permute-start | bytes 1622024 | tf_op jit(solution)/shard_map/ppermute | solution.py:1087
  1074.8 24.6 %collective-permute-start.32 = (bf16[176,1536]{1,0:T(8,128)(2,1)S(1)}, bf16[176,1536]{1,0:T(8,128)(2,1)S(1)}, u32[]{:S(2)}, u32[]{:S(2)}) collective-permute-start(bf16[176,1536]{1,0:T(8,128)(2,1)S(1)} %get-tuple-element.302), channel_id=1, source_target_pairs={{0,24},{8,0},{16,8},{24,16},{1,25},{9,1},{17,9},{25,17},{2,26},{10... | collective-permute-start | bytes 1622024 | tf_op jit(solution)/shard_map/ppermute | solution.py:1087
  1077.2 45.4 %collective-permute-start.31 = (bf16[176,1536]{1,0:T(8,128)(2,1)S(1)}, bf16[176,1536]{1,0:T(8,128)(2,1)S(1)}, u32[]{:S(2)}, u32[]{:S(2)}) collective-permute-start(bf16[176,1536]{1,0:T(8,128)(2,1)S(1)} %select_select_fusion.4), channel_id=1, source_target_pairs={{0,16},{8,24},{16,0},{24,8},{1,17},{9,25},{17,1},{25,9},{2,18},{10... | collective-permute-start | bytes 1622024 | tf_op jit(solution)/shard_map/ppermute | solution.py:1087
  1170.2 148.5 %all-gather.21.cloned.1.call-start = ((), (), s32[]{:S(2)}) async-start(), calls=%async_computation.23 | async-start | bytes 4866048 | tf_op jit(solution)/shard_map/all_gather | solution.py:1136
  1180.9 35.6 %collective-permute-start.33 = (bf16[176,1056]{1,0:T(8,128)(2,1)}, bf16[176,1056]{1,0:T(8,128)(2,1)S(1)}, u32[]{:S(2)}, u32[]{:S(2)}) collective-permute-start(bf16[176,1056]{1,0:T(8,128)(2,1)} %get-tuple-element.328), channel_id=1, source_target_pairs={{0,8},{8,16},{16,24},{24,0},{1,9},{9,17},{17,25},{25,1},{2,10},{10... | collective-permute-start | bytes 1115144 | tf_op jit(solution)/shard_map/ppermute | solution.py:1087
  1182.3 34.3 %collective-permute-start.34 = (bf16[176,1056]{1,0:T(8,128)(2,1)}, bf16[176,1056]{1,0:T(8,128)(2,1)S(1)}, u32[]{:S(2)}, u32[]{:S(2)}) collective-permute-start(bf16[176,1056]{1,0:T(8,128)(2,1)} %get-tuple-element.327), channel_id=1, source_target_pairs={{0,16},{8,24},{16,0},{24,8},{1,17},{9,25},{17,1},{25,9},{2,18},{10... | collective-permute-start | bytes 1115144 | tf_op jit(solution)/shard_map/ppermute | solution.py:1087
  1183.7 32.9 %collective-permute-start.35 = (bf16[176,1056]{1,0:T(8,128)(2,1)}, bf16[176,1056]{1,0:T(8,128)(2,1)}, u32[]{:S(2)}, u32[]{:S(2)}) collective-permute-start(bf16[176,1056]{1,0:T(8,128)(2,1)} %get-tuple-element.326), channel_id=1, source_target_pairs={{0,24},{8,0},{16,8},{24,16},{1,25},{9,1},{17,9},{25,17},{2,26},{10... | collective-permute-start | bytes 1115144 | tf_op jit(solution)/shard_map/ppermute | solution.py:1087
  1189.6 184.0 %reduce-scatter.14.cloned.1.call-start = ((), (), s32[]{:S(2)}) async-start(), calls=%async_computation.24 | async-start | bytes 8921088 | tf_op jit(solution)/shard_map/reduce_scatter | solution.py:1131
  1228.5 8.8 collective-permute-start.39
  1237.5 21.9 %collective-permute-start.40 = (f32[2,1408]{1,0:T(2,128)S(1)}, f32[2,1408]{1,0:T(2,128)S(1)}, u32[]{:S(2)}, u32[]{:S(2)}) collective-permute-start(f32[2,1408]{1,0:T(2,128)S(1)} %add.575), channel_id=1, source_target_pairs={{0,2},{1,3},{2,0},{3,1},{4,6},{5,7},{6,4},{7,5},{8,10},{9,11},{10,... | collective-permute-start | bytes 33800 | tf_op jit(solution)/shard_map/ppermute | solution.py:1124
  1279.1 29.0 %collective-permute-start.42 = (bf16[176,1056]{1,0:T(8,128)(2,1)S(1)}, bf16[176,1056]{1,0:T(8,128)(2,1)S(1)}, u32[]{:S(2)}, u32[]{:S(2)}) collective-permute-start(bf16[176,1056]{1,0:T(8,128)(2,1)S(1)} %get-tuple-element.338), channel_id=1, source_target_pairs={{0,8},{8,16},{16,24},{24,0},{1,9},{9,17},{17,25},{25,1},{2,10},{10... | collective-permute-start | bytes 1115144 | tf_op jit(solution)/shard_map/ppermute | solution.py:1087
  1280.7 27.5 %collective-permute-start.44 = (bf16[176,1056]{1,0:T(8,128)(2,1)S(1)}, bf16[176,1056]{1,0:T(8,128)(2,1)S(1)}, u32[]{:S(2)}, u32[]{:S(2)}) collective-permute-start(bf16[176,1056]{1,0:T(8,128)(2,1)S(1)} %get-tuple-element.337), channel_id=1, source_target_pairs={{0,24},{8,0},{16,8},{24,16},{1,25},{9,1},{17,9},{25,17},{2,26},{10... | collective-permute-start | bytes 1115144 | tf_op jit(solution)/shard_map/ppermute | solution.py:1087
  1283.4 33.6 %collective-permute-start.43 = (bf16[176,1056]{1,0:T(8,128)(2,1)S(1)}, bf16[176,1056]{1,0:T(8,128)(2,1)S(1)}, u32[]{:S(2)}, u32[]{:S(2)}) collective-permute-start(bf16[176,1056]{1,0:T(8,128)(2,1)S(1)} %select_select_fusion.15), channel_id=1, source_target_pairs={{0,16},{8,24},{16,0},{24,8},{1,17},{9,25},{17,1},{25,9},{2,18},{10... | collective-permute-start | bytes 1115144 | tf_op jit(solution)/shard_map/ppermute | solution.py:1087
  1327.0 13.4 collective-permute-start.45
  1330.3 23.2 %collective-permute-start.53 = (bf16[464,352]{1,0:T(8,128)(2,1)}, bf16[464,352]{1,0:T(8,128)(2,1)S(1)}, u32[]{:S(2)}, u32[]{:S(2)}) collective-permute-start(bf16[464,352]{1,0:T(8,128)(2,1)} %select_select_fusion.28), channel_id=1, source_target_pairs={{0,24},{8,0},{16,8},{24,16},{1,25},{9,1},{17,9},{25,17},{2,26},{10... | collective-permute-start | bytes 979976 | tf_op jit(solution)/shard_map/ppermute | solution.py:1087
  1332.0 29.9 %collective-permute-start.52 = (bf16[464,352]{1,0:T(8,128)(2,1)}, bf16[464,352]{1,0:T(8,128)(2,1)}, u32[]{:S(2)}, u32[]{:S(2)}) collective-permute-start(bf16[464,352]{1,0:T(8,128)(2,1)} %select_select_fusion.29), channel_id=1, source_target_pairs={{0,16},{8,24},{16,0},{24,8},{1,17},{9,25},{17,1},{25,9},{2,18},{10... | collective-permute-start | bytes 979976 | tf_op jit(solution)/shard_map/ppermute | solution.py:1087
  1333.0 28.9 %collective-permute-start.51 = (bf16[464,352]{1,0:T(8,128)(2,1)}, bf16[464,352]{1,0:T(8,128)(2,1)}, u32[]{:S(2)}, u32[]{:S(2)}) collective-permute-start(bf16[464,352]{1,0:T(8,128)(2,1)} %select_select_fusion.30), channel_id=1, source_target_pairs={{0,8},{8,16},{16,24},{24,0},{1,9},{9,17},{17,25},{25,1},{2,10},{10... | collective-permute-start | bytes 979976 | tf_op jit(solution)/shard_map/ppermute | solution.py:1087
  1345.3 6.3 collective-permute-start.47
  1376.4 11.6 collective-permute-start.48
  1377.9 20.8 %collective-permute-start.49 = (bf16[360,352]{1,0:T(8,128)(2,1)S(1)}, bf16[360,352]{1,0:T(8,128)(2,1)}, u32[]{:S(2)}, u32[]{:S(2)}) collective-permute-start(bf16[360,352]{1,0:T(8,128)(2,1)S(1)} %select_select_fusion.32), channel_id=1, source_target_pairs={{0,16},{8,24},{16,0},{24,8},{1,17},{9,25},{17,1},{25,9},{2,18},{10... | collective-permute-start | bytes 760328 | tf_op jit(solution)/shard_map/ppermute | solution.py:1087
  1380.3 18.4 %collective-permute-start.50 = (bf16[360,352]{1,0:T(8,128)(2,1)}, bf16[360,352]{1,0:T(8,128)(2,1)}, u32[]{:S(2)}, u32[]{:S(2)}) collective-permute-start(bf16[360,352]{1,0:T(8,128)(2,1)} %select_select_fusion.31), channel_id=1, source_target_pairs={{0,24},{8,0},{16,8},{24,16},{1,25},{9,1},{17,9},{25,17},{2,26},{10... | collective-permute-start | bytes 760328 | tf_op jit(solution)/shard_map/ppermute | solution.py:1087
  (103 other events, 1386.4 us)
Sparse Core Ops, SparseCore 0:
  33.6 59.1 all-gather.8
  99.5 87.6 all-gather.10
  189.1 115.5 all-gather.12
  306.4 78.5 all-gather.14
  386.7 112.0 all-gather.16
  500.5 91.7 all-gather.18
  659.4 118.5 reduce-scatter.7
  782.1 148.7 reduce-scatter.5
  934.6 205.2 reduce-scatter.11
  1170.3 89.0 reduce-scatter.9
  1261.9 37.2 all-gather.20
  1302.6 70.9 reduce-scatter.13
